TPU v7x, 32 devices: a whole 2x2x4 slice. The times are simulated.
32 devices in a mesh: tile: 8 (over z, core), bank: 4 (over y, x).
Axes of the slice: x: 2, y: 2, z: 4, core: 2. Of those that a mesh axis runs over, the one named last changes fastest.
Arguments:
- volume: bfloat16 [512, 256, 128], P('tile', 'bank'), may hold values from -6 to 6
- pick_list: int32 [3, 8, 4, 16], P(None, 'tile', 'bank'), may hold values from 0 to 511, as said below
- box_counts: int32 [8, 4], P('tile', 'bank'), may hold values from 1 to 16, as said below
- orientations: int32 [8, 4, 16, 128], P('tile', 'bank'), may hold values from 0 to 255, all different within a row
- orient_weight: int32 [8, 4, 16, 128], P('tile', 'bank'), may hold values from 1 to 4
- reference_bank: bfloat16 [256, 20, 4096], P('bank'), may hold values from -6 to 6
Outputs:
- class_sums: float32 [256, 20, 4096], P('bank')
- weight_sums: float32 [256, 20], P('bank')
Inputs may be any that keep to these rules, and one draw needn't show every extreme that they name: pick_list[0, t, b, s] lies in [t * 64, (t + 1) * 64), pick_list[1, t, b, s] in [b * 64, (b + 1) * 64), and pick_list[2, t, b, s] in [0, 32]. `box_counts`: every device has at least one live slot and some device has all 16. The 128 orientations of a slot are distinct.
All inputs are finite; a program needn't handle non-finite values.
Results may differ from a plain program's by a relative error of at most 0.012.
Values may be sent and summed in bfloat16 or wider, within the bound.
No kernel may reach another device: no remote copies, remote signals or barrier semaphores. Data moves between devices by JAX's collectives and lax.ppermute only.
A program may use at most 128 MiB of HBM per device.

v0:
```python
import jax
import jax.numpy as jnp
from jax import lax
from jax.sharding import PartitionSpec as P

B = 96
L = 16
R = 256
F = 4096


EPSILON = 1e-06


def extended(block, sides, width):
    for axis, dim in sides:
        count = lax.axis_size(axis)
        forward = [(i, i + 1) for i in range(count - 1)]
        backward = [(target, source) for source, target in forward]
        low = lax.ppermute(
            lax.slice_in_dim(block, block.shape[dim] - width, None, axis=dim), axis, forward
        )
        high = lax.ppermute(lax.slice_in_dim(block, 0, width, axis=dim), axis, backward)
        block = jnp.concatenate([low, block, high], axis=dim)
    return block


def fourier_table():
    samples = jnp.arange(B).astype(jnp.float32)
    terms = jnp.arange(L)
    frequency = jnp.where(terms <= L // 2, terms, terms - L // 2).astype(jnp.float32)
    angles = 2.0 * jnp.pi * frequency[:, None] * samples[None, :] / B
    table = jnp.where((terms <= L // 2)[:, None], jnp.cos(angles), jnp.sin(angles)) / jnp.sqrt(
        jnp.float32(B)
    )
    table_half = table.astype(jnp.bfloat16)
    return (table_half, table_half.astype(jnp.float32))


def box_features(box_cube, table_half, table_full):
    first = jnp.dot(
        box_cube.reshape(B * B, B), table_half.T, preferred_element_type=jnp.float32
    ).reshape(B, B, L)
    second = jnp.einsum("xyc,by->xbc", first, table_full, precision=lax.Precision.HIGHEST)
    third = jnp.einsum("xbc,ax->abc", second, table_full, precision=lax.Precision.HIGHEST)
    return third.reshape(L * L * L).astype(jnp.bfloat16)


def norms_of(features):
    feature_wide = features.astype(jnp.float32)
    return jnp.sqrt(jnp.mean(feature_wide * feature_wide, axis=1) + EPSILON)


def correlate(features, box_norm, bank_rows):
    scores = jnp.einsum("if,rcf->irc", features, bank_rows, preferred_element_type=jnp.float32)
    bank_wide = bank_rows.astype(jnp.float32)
    ref_norm = jnp.sqrt(jnp.mean(bank_wide * bank_wide, axis=2) + EPSILON)
    return scores / (F * box_norm[:, None, None] * ref_norm[None])


def accumulate(multiplicity, correl, features):
    weights = (multiplicity.astype(jnp.float32)[:, :, None] * jnp.maximum(correl, 0.0)).astype(
        jnp.bfloat16
    )
    class_sums = jnp.einsum("irc,if->rcf", weights, features, preferred_element_type=jnp.float32)
    weight_sums = jnp.sum(weights.astype(jnp.float32), axis=0)
    return (class_sums, weight_sums)


def score_local(box_rows, box_multiplicity, reference_bank):
    local_rows = reference_bank.shape[0]
    row_start = lax.axis_index("bank") * local_rows
    local_multiplicity = lax.dynamic_slice_in_dim(box_multiplicity, row_start, local_rows, 1)
    box_norm = norms_of(box_rows)
    correl = correlate(box_rows, box_norm, reference_bank)
    return accumulate(local_multiplicity, correl, box_rows)


def body(volume, pick_list, box_counts, orientations, orient_weight, reference_bank):
    table_half, table_full = fourier_table()
    half_box = B // 2
    padded = extended(volume, (("tile", 0), ("bank", 1)), half_box)
    offset_x = lax.axis_index("tile") * volume.shape[0]
    offset_y = lax.axis_index("bank") * volume.shape[1]
    coords = jnp.stack(
        [pick_list[0, 0, 0] - offset_x, pick_list[1, 0, 0] - offset_y, pick_list[2, 0, 0]], axis=1
    )

    def extract_one(corner):
        box_cube = lax.dynamic_slice(padded, (corner[0], corner[1], corner[2]), (B, B, B))
        return box_features(box_cube, table_half, table_full)

    features = lax.map(extract_one, coords)
    slots = pick_list.shape[3]
    live_slots = jnp.arange(slots) < box_counts[0, 0]
    matches = orientations[0, 0][:, :, None] == jnp.arange(R)[None, None, :]
    multiplicity = jnp.sum(
        jnp.where(matches, orient_weight[0, 0][:, :, None].astype(jnp.float32), 0.0), axis=1
    )
    multiplicity = jnp.where(live_slots[:, None], multiplicity, 0.0).astype(jnp.bfloat16)
    every_features, every_multiplicity = (
        lax.all_gather(features, ("tile", "bank"), axis=0, tiled=True),
        lax.all_gather(multiplicity, ("tile", "bank"), axis=0, tiled=True),
    )
    class_sums, weight_sums = score_local(every_features, every_multiplicity, reference_bank)
    return (class_sums, weight_sums)


def solution(mesh):
    in_specs = (
        P("tile", "bank", None),
        P(None, "tile", "bank", None),
        P("tile", "bank"),
        P("tile", "bank", None, None),
        P("tile", "bank", None, None),
        P("bank", None, None),
    )
    out_specs = (P("bank", None, None), P("bank", None))
    return jax.shard_map(body, mesh=mesh, in_specs=in_specs, out_specs=out_specs, check_vma=False)
```

profile of v0, /device:TPU:0, one launch (start us, length us, event | category | flops | bytes accessed | tf_op | source)
XLA Modules:
  0.0 437.1 jit_solution(13327008595162852058)
XLA Ops:
  13.3 4.3 collective-permute-done.1
  20.3 4.7 %collective-permute-start.2 = (bf16[160,48,128]{2,1,0:T(8,128)(2,1)}, bf16[160,48,128]{2,1,0:T(8,128)(2,1)}, u32[]{:S(2)}, u32[]{:S(2)}) collective-permute-start(bf16[160,48,128]{2,1,0:T(8,128)(2,1)} %get-tuple-element.123), channel_id=1, source_target_pairs={{0,1},{1,2},{2,3},{4,5},{5,6},{6,7},{8,9},{9,10},{10,11},{12,13},{... | collective-permute-start | bytes 5898248 | tf_op jit(solution)/shard_map/ppermute | solution.py:20
  26.4 31.7 %collective-permute-done.2 = bf16[160,48,128]{2,1,0:T(8,128)(2,1)} collective-permute-done((bf16[160,48,128]{2,1,0:T(8,128)(2,1)}, bf16[160,48,128]{2,1,0:T(8,128)(2,1)}, u32[]{:S(2)}, u32[]{:S(2)}) %collective-permute-start.2) | collective-permute-done | bytes 1966112 | tf_op jit(solution)/shard_map/ppermute | solution.py:20
  58.1 44.1 %collective-permute-done.3 = bf16[160,48,128]{2,1,0:T(8,128)(2,1)} collective-permute-done((bf16[160,48,128]{2,1,0:T(8,128)(2,1)}, bf16[160,48,128]{2,1,0:T(8,128)(2,1)}, u32[]{:S(2)}, u32[]{:S(2)}) %collective-permute-start.3) | collective-permute-done | bytes 1966112 | tf_op jit(solution)/shard_map/ppermute | solution.py:23
  102.2 5.3 %pad_maximum_fusion = bf16[160,160,128]{2,1,0:T(8,128)(2,1)} fusion(bf16[160,48,128]{2,1,0:T(8,128)(2,1)} %collective-permute-done.3, bf16[160,64,128]{2,1,0:T(8,128)(2,1)S(1)} %constant_dynamic-update-slice_fusion, bf16[160,48,128]{2,1,0:T(8,128)(2,1)} %collective-permute-done.2), kind=kLoop, calls=%fused_computation.31 | loop fusion | flops 19660800 | bytes 13107200 | tf_op jit(solution)/shard_map/concatenate | solution.py:24
  107.4 219.0 %while.13 = (s32[]{:T(128)}, bf16[16,4096]{1,0:T(8,128)(2,1)}, s32[16,3]{0,1:T(4,128)S(1)}, bf16[160,160,128]{2,1,0:T(8,128)(2,1)}, f32[96]{0:T(128)S(1)}, /*ind...) while((s32[]{:T(128)}, bf16[16,4096]{1,0:T(8,128)(2,1)}, ...), condition=%wide.region_2.3_spmd.clone.clone.clone, body=%wide.region_1.2_spmd.clone.clone.clone.sunk | while | flops 61371912 | bytes 3794575 | solution.py:93
  113.9 3.4 fusion.59
  127.6 3.4 fusion.59
  141.3 3.4 fusion.59
  155.0 3.4 fusion.59
  168.6 3.4 fusion.59
  182.3 3.4 fusion.59
  196.0 3.4 fusion.59
  209.7 3.4 fusion.59
  223.3 3.4 fusion.59
  237.0 3.4 fusion.59
  250.7 3.4 fusion.59
  264.4 3.4 fusion.59
  278.1 3.4 fusion.59
  291.8 3.4 fusion.59
  327.9 72.5 %all_gather.6 = bf16[512,256]{1,0:T(8,128)(2,1)S(1)} all-gather(bf16[16,256]{1,0:T(8,128)(2,1)S(1)} %select_convert_fusion), channel_id=1, replica_groups=mesh['tile'=8,'bank'=4] {'tile','bank'}, dimensions={0}, use_global_device_ids=true | all-gather | bytes 270336 | tf_op jit(solution)/shard_map/all_gather | solution.py:103
  400.7 6.3 %multiply_reduce_fusion = f32[64,20]{0,1:T(8,128)S(1)} fusion(bf16[64,20,4096]{2,0,1:T(8,128)(2,1)} %param.13), kind=kLoop, calls=%fused_computation.29 | loop fusion | flops 15727360 | bytes 10490880 | tf_op jit(solution)/shard_map/reduce_sum | solution.py:57
  410.5 9.3 %convert_reduce_fusion = (f32[64,20]{0,1:T(8,128)}, bf16[512,64,20]{0,1,2:T(8,128)(2,1)S(1)}) fusion(f32[64,20]{0,1:T(8,128)S(1)} %add_sqrt_fusion, f32[512]{0:T(512)S(1)} %sqrt_multiply_fusion, bf16[64,20,4096]{2,0,1:T(8,128)(2,1)} %param.13, bf16[512,4096]{1,0:T(8,128)(2,1)S(1)} %copy-done.1, f32[512,64]{0,1:T(8,128)S(1)} %convert_element_type.82), kind=kOutput, calls=%fused_computation.36 | convolution fusion | flops 5373295616 | bytes 16134144 | tf_op jit(solution)/shard_map/if,rcf->irc/dot_general | solution.py:55
  419.8 10.5 %fusion.30 = f32[64,20,4096]{2,0,1:T(8,128)} fusion(bf16[512,64,20]{0,1,2:T(8,128)(2,1)S(1)} %get-tuple-element.131, bf16[512,4096]{1,0:T(8,128)(2,1)S(1)} %copy-done.1), kind=kOutput, calls=%fused_computation.32 | convolution fusion | flops 5368709120 | bytes 26476544 | tf_op jit(solution)/shard_map/irc,if->rcf/dot_general | solution.py:65
  (152 shorter events, 93.5 us)
Async XLA Ops:
  7.2 399.9 %all-gather.2.cloned.1.call-start = ((), (), s32[]{:S(2)}) async-start(), calls=%async_computation | async-start | bytes 4325376 | tf_op jit(solution)/shard_map/all_gather | solution.py:102
  7.2 5.9 %copy-start = (bf16[64,64,128]{2,1,0:T(8,128)(2,1)S(1)}, bf16[64,64,128]{2,1,0:T(8,128)(2,1)}, u32[]{:S(2)}) copy-start(bf16[64,64,128]{2,1,0:T(8,128)(2,1)} %param.8) | copy-start | bytes 3145732
  8.8 4.3 collective-permute-start
  11.2 6.3 %collective-permute-start.1 = (bf16[48,64,128]{2,1,0:T(8,128)(2,1)S(1)}, bf16[48,64,128]{2,1,0:T(8,128)(2,1)S(1)}, u32[]{:S(2)}, u32[]{:S(2)}) collective-permute-start(bf16[48,64,128]{2,1,0:T(8,128)(2,1)S(1)} %get-tuple-element.125), channel_id=1, source_target_pairs={{4,0},{8,4},{12,8},{16,12},{20,16},{24,20},{28,24},{5,1},{9,5},{13... | collective-permute-start | bytes 2359304 | tf_op jit(solution)/shard_map/ppermute | solution.py:23
  17.6 8.7 %copy-start.4 = (s32[3,1,1,16]{3,2,1,0:T(1,128)S(1)}, s32[3,1,1,16]{3,2,1,0:T(1,128)}, u32[]{:S(2)}) copy-start(s32[3,1,1,16]{3,2,1,0:T(1,128)} %param.9) | copy-start | bytes 580
  20.3 37.8 %collective-permute-start.2 = (bf16[160,48,128]{2,1,0:T(8,128)(2,1)}, bf16[160,48,128]{2,1,0:T(8,128)(2,1)}, u32[]{:S(2)}, u32[]{:S(2)}) collective-permute-start(bf16[160,48,128]{2,1,0:T(8,128)(2,1)} %get-tuple-element.123), channel_id=1, source_target_pairs={{0,1},{1,2},{2,3},{4,5},{5,6},{6,7},{8,9},{9,10},{10,11},{12,13},{... | collective-permute-start | bytes 5898248 | tf_op jit(solution)/shard_map/ppermute | solution.py:20
  25.0 77.2 %collective-permute-start.3 = (bf16[160,48,128]{2,1,0:T(8,128)(2,1)}, bf16[160,48,128]{2,1,0:T(8,128)(2,1)}, u32[]{:S(2)}, u32[]{:S(2)}) collective-permute-start(bf16[160,48,128]{2,1,0:T(8,128)(2,1)} %get-tuple-element.124), channel_id=1, source_target_pairs={{1,0},{2,1},{3,2},{5,4},{6,5},{7,6},{9,8},{10,9},{11,10},{13,12},{... | collective-permute-start | bytes 5898248 | tf_op jit(solution)/shard_map/ppermute | solution.py:23
  107.4 219.7 %copy-start.3 = (s32[1,1,16,128]{3,2,1,0:T(8,128)S(1)}, s32[1,1,16,128]{3,2,1,0:T(8,128)}, u32[]{:S(2)}) copy-start(s32[1,1,16,128]{3,2,1,0:T(8,128)} %param.12) | copy-start | bytes 24580
  107.4 219.7 %copy-start.2 = (s32[1,1,16,128]{3,2,1,0:T(8,128)S(1)}, s32[1,1,16,128]{3,2,1,0:T(8,128)}, u32[]{:S(2)}) copy-start(s32[1,1,16,128]{3,2,1,0:T(8,128)} %param.11) | copy-start | bytes 24580
  407.0 3.5 copy-start.1
Sparse Core Ops, SparseCore 0:
  326.6 78.6 all-gather.1
where the time goes:
time: 440 us; the launch traced here: 437 us
  matrix products  107 us (24%)
  loops' own time  93 us (21%)
  waiting for transfers between devices  80.6 us (18%)
  blocking collectives  72.5 us (16%)
  local copies, waits for them, and re-layouts  44 us (10%)
  other arithmetic  15.7 us (4%)
  between operations  14.9 us (3%)
  starting transfers between devices  9.72 us (2%)
    another operation x1, loops' own time, body(): features = lax.map(extract_one, coords)  93 us
    all_gather x1, blocking collectives, body(): lax.all_gather(multiplicity, ('tile', 'bank'), axis=0, tiled=True)  72.5 us
    dot_general x16, matrix products, box_features(): jnp.dot(box_cube.reshape(B * B, B), table_half.T, preferred_element_type=...  53.8 us
    ppermute x2, waiting for transfers between devices, extended(): lax.ppermute(lax.slice_in_dim(block, 0, width, axis=dim), axis, backward)  48.3 us
    ppermute x2, waiting for transfers between devices, extended(): lax.ppermute(lax.slice_in_dim(block, block.shape[dim] - width, None, axis...  32.2 us
    dot_general x16, matrix products, box_features(): jnp.einsum('xyc,by->xbc', first, table_full, precision=lax.Precision.HIGH...  27.1 us
    dynamic_update_slice x16, local copies, waits for them, and re-layouts, body(): features = lax.map(extract_one, coords)  24.6 us
    dot_general x1, matrix products, accumulate(): jnp.einsum('irc,if->rcf', weights, features, preferred_element_type=jnp.f...  10.5 us
  transfers between devices with their start and end apart: 5, of which 4 were waited for; matrix products, arithmetic and copies ran while one was open for 2% of the time, Pallas kernels for 0%

commit v1 on v0

v1 whole, which is shorter than its diff:
```python
import functools

import jax
import jax.numpy as jnp
import numpy as np
from jax import lax
from jax.experimental import pallas as pl
from jax.experimental.pallas import tpu as pltpu
from jax.sharding import PartitionSpec as P

B = 96
L = 16
R = 256
F = L * L * L
HALF = B // 2
TERMS = L // 2
EPSILON = 1e-06
LIMIT = 60 * 1024 * 1024


def waves(count):
    steps = 2.0 * np.pi * np.outer(np.arange(TERMS + 1), np.arange(count)) / B
    return np.cos(steps) / np.sqrt(B), np.sin(steps) / np.sqrt(B)


def depth_tables(depth):
    cos, sin = waves(depth)
    first = np.concatenate([cos, sin[1:TERMS]], axis=0)
    second = np.concatenate([sin, -cos[1:TERMS]], axis=0)
    repeat = 128 // L
    return (
        np.tile(first.T, (1, repeat)).astype(np.float32),
        np.tile(second.T, (1, repeat)).astype(np.float32),
    )


def plane_table(wide, high):
    cos_x, sin_x = waves(wide)
    cos_y, sin_y = waves(high)
    along_x = np.concatenate([cos_x, sin_x[1:]], axis=0)
    along_y = np.concatenate([cos_y[1:], sin_y[1:]], axis=0)
    main = np.einsum("ax,by->abxy", along_x, along_y).reshape(-1, wide * high)
    order = np.concatenate([along_x[1:], along_x[:1]], axis=0)
    flat = np.einsum("ax,y->axy", order, cos_y[0]).reshape(-1, wide * high)
    rows = np.concatenate([main, flat], axis=0)
    pad = -rows.shape[0] % 16
    return np.concatenate([rows, np.zeros((pad, rows.shape[1]))], axis=0).astype(np.float32)


def spread(corners, lanes):
    boxes = corners.shape[1]
    box = lax.broadcasted_iota(jnp.int32, (boxes, lanes), 0)
    lane = lax.broadcasted_iota(jnp.int32, (boxes, lanes), 1)
    pick = jnp.where(lane // L == box, 1.0, 0.0).astype(jnp.bfloat16)
    return jnp.dot(corners, pick, preferred_element_type=jnp.float32)


def turns(terms, shift):
    turn = (terms * shift).astype(jnp.int32)
    turn = lax.rem(turn, B)
    angle = turn.astype(jnp.float32) * (2.0 * np.pi / B)
    return jnp.cos(angle), jnp.sin(angle)


def prepare(corners_ref, first_ref, second_ref, depth_ref, high_ref):
    depth, lanes = depth_ref.shape
    where = spread(corners_ref[...], lanes)
    start_y, start_z = where[1:2], where[2:3]
    lane = lax.rem(lax.broadcasted_iota(jnp.int32, (1, lanes), 1), L)
    term = jnp.where(lane <= TERMS, lane, lane - TERMS).astype(jnp.float32)
    cos, sin = turns(term, start_z)
    copies = lanes // first_ref.shape[1]
    first = jnp.concatenate([first_ref[...]] * copies, axis=1)
    second = jnp.concatenate([second_ref[...]] * copies, axis=1)
    z = lax.broadcasted_iota(jnp.int32, (depth, lanes), 0).astype(jnp.float32) - start_z
    table = jnp.where((z >= 0) & (z < B), first * cos + second * sin, 0.0)
    depth_ref[...] = table.astype(jnp.bfloat16)
    y = lax.broadcasted_iota(jnp.int32, high_ref.shape, 0).astype(jnp.float32) - start_y
    high_ref[...] = jnp.where((y >= 0) & (y < B), 1.0, 0.0)
    return where[0:1]


def add_rows(voxels, base, start_x, depth_ref, high_ref, part_ref, plane):
    count, high, depth = voxels.shape
    for x in range(0, count, 4):
        rows = voxels[x : x + 4].reshape(4 * high, depth)
        first = jnp.dot(rows, depth_ref[...], preferred_element_type=jnp.float32)
        for i in range(4):
            at = (base + (x + i)).astype(jnp.float32) - start_x
            live = high_ref[...] * jnp.where((at >= 0) & (at < B), 1.0, 0.0)
            kept = first[i * high : (i + 1) * high] * live
            part_ref[pl.ds((x + i) * high, high), :] = kept.astype(jnp.bfloat16)
    return jnp.dot(plane, part_ref[...], preferred_element_type=jnp.float32)


def near_kernel(
    corners_ref, first_ref, second_ref, volume_ref, plane_ref, total_ref,
    depth_ref, high_ref, start_ref, part_ref, *, offset,
):
    step = pl.program_id(0)

    @pl.when(step == 0)
    def _():
        start_ref[...] = prepare(corners_ref, first_ref, second_ref, depth_ref, high_ref)

    base = offset + step * volume_ref.shape[0]
    added = add_rows(
        volume_ref[...], base, start_ref[...], depth_ref, high_ref, part_ref, plane_ref[...]
    )

    @pl.when(step == 0)
    def _():
        total_ref[...] = added

    @pl.when(step > 0)
    def _():
        total_ref[...] += added


def rotate(total, start_x, start_y):
    lanes = total.shape[1]
    term = (lax.broadcasted_iota(jnp.int32, (TERMS, lanes), 0) + 1).astype(jnp.float32)
    cos_x, sin_x = turns(term, start_x)
    cos_y, sin_y = turns(term, start_y)
    blocks = 2 * TERMS + 1
    main = blocks * 2 * TERMS
    flat_cos = total[main : main + TERMS]
    flat_sin = total[main + TERMS : main + 2 * TERMS]
    flat_zero = total[main + 2 * TERMS : main + 2 * TERMS + 1]
    flats = (
        [flat_zero]
        + [flat_cos[j : j + 1] for j in range(TERMS)]
        + [flat_sin[j : j + 1] for j in range(TERMS)]
    )
    last = lax.broadcasted_iota(jnp.int32, (TERMS, lanes), 0) == TERMS - 1
    turned = []
    for a in range(blocks):
        cos = total[a * 2 * TERMS : a * 2 * TERMS + TERMS]
        sin = total[a * 2 * TERMS + TERMS : (a + 1) * 2 * TERMS]
        low = cos * cos_y + sin * sin_y
        high = sin * cos_y - cos * sin_y
        turned.append((low, jnp.where(last, flats[a], high)))
    rows = [None] * (2 * TERMS)
    rows[0] = turned[0]
    for j in range(1, TERMS + 1):
        c, s = cos_x[j - 1 : j], sin_x[j - 1 : j]
        cos, sin = turned[j], turned[TERMS + j]
        rows[j] = tuple(u * c + v * s for u, v in zip(cos, sin))
        if j < TERMS:
            rows[TERMS + j] = tuple(v * c - u * s for u, v in zip(cos, sin))
    return jnp.concatenate([half for pair in rows for half in pair], axis=0)


def far_kernel(
    corners_ref, first_ref, second_ref, low_ref, high_voxels_ref, plane_ref, near_ref,
    left_ref, own_ref, right_ref,
    depth_ref, high_ref, start_ref, part_ref, total_ref, *, half, gap,
):
    step = pl.program_id(0)

    @pl.when(step == 0)
    def _():
        start_ref[...] = prepare(corners_ref, first_ref, second_ref, depth_ref, high_ref)
        total_ref[...] = near_ref[...]

    count = low_ref.shape[0]
    base = step * count + jnp.where(step < half, 0, gap)
    voxels = jnp.where(step < half, low_ref[...], high_voxels_ref[...])
    total_ref[...] += add_rows(
        voxels, base, start_ref[...], depth_ref, high_ref, part_ref, plane_ref[...]
    )

    @pl.when(step == 2 * half - 1)
    def _():
        where = spread(corners_ref[...], total_ref.shape[1])
        rows = rotate(total_ref[...], where[0:1], where[1:2])
        width = left_ref.shape[1]
        left_ref[...] = rows[:, :width].astype(jnp.bfloat16)
        own_ref[...] = rows[:, width : 2 * width]
        right_ref[...] = rows[:, 2 * width :].astype(jnp.bfloat16)


def join_kernel(own_ref, left_ref, right_ref, multiplicity_ref, out_ref, wide_ref):
    total = own_ref[...] + left_ref[...].astype(jnp.float32) + right_ref[...].astype(jnp.float32)
    total = total.astype(jnp.bfloat16)
    rows, lanes = total.shape
    slots = lanes // L
    k = lax.broadcasted_iota(jnp.int32, (lanes, L * L), 0)
    lane = lax.broadcasted_iota(jnp.int32, (lanes, L * L), 1)
    gap = k - lax.rem(lane, L)
    row = lax.rem(lax.broadcasted_iota(jnp.int32, (rows, L * L), 0), L)
    place = jnp.where(row == L - 1, 0, row + 1)
    keep = jnp.where(
        place == lax.broadcasted_iota(jnp.int32, (rows, L * L), 1) // L, 1.0, 0.0
    )
    sums = jnp.where(
        lax.broadcasted_iota(jnp.int32, (L, rows), 1) // L
        == lax.broadcasted_iota(jnp.int32, (L, rows), 0),
        1.0,
        0.0,
    ).astype(jnp.bfloat16)
    for s in range(slots):
        copies = jnp.where(gap == s * L, 1.0, 0.0).astype(jnp.bfloat16)
        spread_rows = jnp.dot(total, copies, preferred_element_type=jnp.float32) * keep
        feature = jnp.dot(
            sums, spread_rows.astype(jnp.bfloat16), preferred_element_type=jnp.float32
        )
        for a in range(L):
            wide_ref[s : s + 1, a * L * L : (a + 1) * L * L] = feature[a : a + 1]
    wide = wide_ref[...]
    norm = jnp.sqrt(jnp.mean(wide * wide, axis=1, keepdims=True) + EPSILON)
    high = norm.astype(jnp.bfloat16).astype(jnp.float32)
    tail = lax.broadcasted_iota(jnp.int32, (slots, 128), 1)
    tail = jnp.where(tail == 0, high, jnp.where(tail == 1, norm - high, 0.0))
    out_ref[:, :F] = wide.astype(jnp.bfloat16)
    out_ref[:, F : F + R] = multiplicity_ref[...]
    out_ref[:, F + R :] = tail.astype(jnp.bfloat16)


def score_kernel(
    rows_ref, multiplicity_ref, norm_ref, bank_ref, out_ref, sums_ref, turned_ref,
):
    step = pl.program_id(0)

    @pl.when(step == 0)
    def _():
        turned_ref[...] = rows_ref[...].T

    count, orients, width = bank_ref.shape
    bank = bank_ref[...].reshape(count * orients, width)
    scores = jnp.dot(bank, turned_ref[...], preferred_element_type=jnp.float32)
    wide = bank.astype(jnp.float32)
    bank_norm = jnp.sqrt(jnp.mean(wide * wide, axis=1, keepdims=True) + EPSILON)
    correl = scores / (F * norm_ref[...] * bank_norm)
    multiplicity = jnp.concatenate([multiplicity_ref[...].astype(jnp.float32)] * count, axis=0)
    weights = (multiplicity * jnp.maximum(correl, 0.0)).astype(jnp.bfloat16)
    total = jnp.dot(weights, rows_ref[...], preferred_element_type=jnp.float32)
    out_ref[...] = total.reshape(out_ref.shape)
    sums = jnp.sum(weights.astype(jnp.float32), axis=1, keepdims=True)
    sums_ref[...] = sums.reshape(sums_ref.shape)


def score_plain(rows, multiplicity, norm, bank):
    scores = jnp.einsum("if,rcf->irc", rows, bank, preferred_element_type=jnp.float32)
    wide = bank.astype(jnp.float32)
    bank_norm = jnp.sqrt(jnp.mean(wide * wide, axis=2) + EPSILON)
    correl = scores / (F * norm[:, None, None] * bank_norm[None])
    weights = (multiplicity.astype(jnp.float32)[:, :, None] * jnp.maximum(correl, 0.0)).astype(
        jnp.bfloat16
    )
    class_sums = jnp.einsum("irc,if->rcf", weights, rows, preferred_element_type=jnp.float32)
    return class_sums, jnp.sum(weights.astype(jnp.float32), axis=0)


def steps_of(axis, by):
    count = lax.axis_size(axis)
    return [(i, i + by) for i in range(count) if 0 <= i + by < count]


def shifted(value, axis, by):
    return lax.ppermute(value, axis, steps_of(axis, by))


def gather_rows(mine):
    tiles, banks = lax.axis_size("tile"), lax.axis_size("bank")
    blocks = [mine]
    if tiles % 2 == 0:
        for by in range(2, tiles, 2):
            blocks.append(
                lax.ppermute(mine, "tile", [(i, (i + by) % tiles) for i in range(tiles)])
            )
    line = jnp.concatenate(blocks, axis=0)
    if banks == 4:
        along_x = lax.ppermute(line, "bank", [(0, 1), (1, 0), (2, 3), (3, 2)])
        along_y = lax.ppermute(line, "bank", [(0, 2), (2, 0), (1, 3), (3, 1)])
        half = line.shape[0] // 2
        across_y = lax.ppermute(along_x[:half], "bank", [(0, 2), (2, 0), (1, 3), (3, 1)])
        across_x = lax.ppermute(along_y[half:], "bank", [(0, 1), (1, 0), (2, 3), (3, 2)])
        line = jnp.concatenate([line, along_x, along_y, across_y, across_x], axis=0)
    else:
        line = lax.all_gather(line, "bank", axis=0, tiled=True)
    if tiles % 2 == 0:
        other = lax.ppermute(line, "tile", [(i, i ^ 1) for i in range(tiles)])
        return jnp.concatenate([line, other], axis=0)
    return lax.all_gather(line, "tile", axis=0, tiled=True)


def score_local(rows, reference_bank):
    local_rows, classes, width = reference_bank.shape
    row_start = lax.axis_index("bank") * local_rows
    multiplicity = lax.dynamic_slice_in_dim(rows, F + row_start, local_rows, 1)
    norm = rows[:, F + R].astype(jnp.float32) + rows[:, F + R + 1].astype(jnp.float32)
    features = rows[:, :F]
    boxes = rows.shape[0]
    if boxes > 1024 or classes % 4:
        return score_plain(features, multiplicity, norm, reference_bank)
    group = 4
    out, sums = pl.pallas_call(
        score_kernel,
        grid=(classes // group,),
        in_specs=[
            pl.BlockSpec((boxes, F), lambda i: (0, 0)),
            pl.BlockSpec((local_rows, boxes), lambda i: (0, 0)),
            pl.BlockSpec((1, boxes), lambda i: (0, 0)),
            pl.BlockSpec((group, local_rows, width), lambda i: (i, 0, 0)),
        ],
        out_specs=[
            pl.BlockSpec((group, local_rows, width), lambda i: (i, 0, 0)),
            pl.BlockSpec((group, local_rows, 1), lambda i: (i, 0, 0)),
        ],
        out_shape=[
            jax.ShapeDtypeStruct((classes, local_rows, width), jnp.float32),
            jax.ShapeDtypeStruct((classes, local_rows, 1), jnp.float32),
        ],
        scratch_shapes=[pltpu.VMEM((F, boxes), jnp.bfloat16)],
        compiler_params=pltpu.CompilerParams(vmem_limit_bytes=LIMIT),
        cost_estimate=pl.CostEstimate(
            flops=4 * boxes * classes * local_rows * width,
            bytes_accessed=6 * classes * local_rows * width,
            transcendentals=0,
        ),
        name="score",
    )(features, multiplicity.T, norm[None], jnp.transpose(reference_bank, (1, 0, 2)))
    return jnp.transpose(out, (1, 0, 2)), jnp.transpose(sums[:, :, 0], (1, 0))


def body(volume, pick_list, box_counts, orientations, orient_weight, reference_bank):
    wide, high, depth = volume.shape
    slots = pick_list.shape[3]
    low = shifted(volume[wide - HALF :], "tile", 1)
    top = shifted(volume[:HALF], "tile", -1)

    corner_x = pick_list[0, 0, 0] - lax.axis_index("tile") * wide
    corner_y = pick_list[1, 0, 0] - lax.axis_index("bank") * high - HALF
    own = jnp.stack([corner_x, corner_y, pick_list[2, 0, 0]])
    before = shifted(own, "bank", 1)
    after = shifted(own, "bank", -1)
    step = jnp.array([0, high, 0], jnp.int32)[:, None]
    corners = jnp.concatenate([before - step, own, after + step], axis=1)
    corners = jnp.pad(corners, ((0, 5), (0, 128 - 3 * slots))).astype(jnp.bfloat16)

    first, second = depth_tables(depth)
    plane = jnp.asarray(plane_table(wide + 2 * HALF, high), jnp.bfloat16)
    modes, lanes = plane.shape[0], 3 * slots * L
    unit = 16
    scratch = [
        pltpu.VMEM((depth, lanes), jnp.bfloat16),
        pltpu.VMEM((high, lanes), jnp.float32),
        pltpu.VMEM((1, lanes), jnp.float32),
        pltpu.VMEM((unit * high, lanes), jnp.bfloat16),
    ]
    whole = [
        pl.BlockSpec((8, 128), lambda i: (0, 0)),
        pl.BlockSpec((depth, 128), lambda i: (0, 0)),
        pl.BlockSpec((depth, 128), lambda i: (0, 0)),
    ]
    params = pltpu.CompilerParams(vmem_limit_bytes=LIMIT)
    near = pl.pallas_call(
        functools.partial(near_kernel, offset=HALF),
        grid=(wide // unit,),
        in_specs=whole
        + [
            pl.BlockSpec((unit, high, depth), lambda i: (i, 0, 0)),
            pl.BlockSpec((modes, unit * high), lambda i: (0, HALF // unit + i)),
        ],
        out_specs=pl.BlockSpec((modes, lanes), lambda i: (0, 0)),
        out_shape=jax.ShapeDtypeStruct((modes, lanes), jnp.float32),
        scratch_shapes=scratch,
        compiler_params=params,
        cost_estimate=pl.CostEstimate(
            flops=2 * wide * high * lanes * (depth + modes), bytes_accessed=8000000, transcendentals=0
        ),
        name="near_rows",
    )(corners, first, second, volume, plane)
    half = HALF // unit
    skip = wide // unit
    left, mid, right = pl.pallas_call(
        functools.partial(far_kernel, half=half, gap=wide),
        grid=(2 * half,),
        in_specs=whole
        + [
            pl.BlockSpec((unit, high, depth), lambda i: (jnp.minimum(i, half - 1), 0, 0)),
            pl.BlockSpec((unit, high, depth), lambda i: (jnp.maximum(i - half, 0), 0, 0)),
            pl.BlockSpec(
                (modes, unit * high), lambda i: (0, jnp.where(i < half, i, i + skip))
            ),
            pl.BlockSpec((modes, lanes), lambda i: (0, 0)),
        ],
        out_specs=[pl.BlockSpec((L * L, slots * L), lambda i: (0, 0))] * 3,
        out_shape=[
            jax.ShapeDtypeStruct((L * L, slots * L), jnp.bfloat16),
            jax.ShapeDtypeStruct((L * L, slots * L), jnp.float32),
            jax.ShapeDtypeStruct((L * L, slots * L), jnp.bfloat16),
        ],
        scratch_shapes=scratch + [pltpu.VMEM((modes, lanes), jnp.float32)],
        compiler_params=params,
        name="far_rows",
    )(corners, first, second, low, top, plane, near)
    from_after = shifted(left, "bank", -1)
    from_before = shifted(right, "bank", 1)

    live_slots = jnp.arange(slots) < box_counts[0, 0]
    matches = orientations[0, 0][:, :, None] == jnp.arange(R)[None, None, :]
    multiplicity = jnp.sum(
        jnp.where(matches, orient_weight[0, 0][:, :, None].astype(jnp.float32), 0.0), axis=1
    )
    multiplicity = jnp.where(live_slots[:, None], multiplicity, 0.0).astype(jnp.bfloat16)
    mine = pl.pallas_call(
        join_kernel,
        out_shape=jax.ShapeDtypeStruct((slots, F + R + 128), jnp.bfloat16),
        scratch_shapes=[pltpu.VMEM((slots, F), jnp.float32)],
        compiler_params=params,
        name="join",
    )(mid, from_after, from_before, multiplicity)
    return score_local(gather_rows(mine), reference_bank)


def solution(mesh):
    in_specs = (
        P("tile", "bank", None),
        P(None, "tile", "bank", None),
        P("tile", "bank"),
        P("tile", "bank", None, None),
        P("tile", "bank", None, None),
        P("bank", None, None),
    )
    out_specs = (P("bank", None, None), P("bank", None))
    return jax.shard_map(body, mesh=mesh, in_specs=in_specs, out_specs=out_specs, check_vma=False)
```

time: 440 us -> 168 us (0.38)
  matrix products: 107 us -> 0 us
  loops' own time: 93 us -> 0 us
  blocking collectives: 72.5 us -> 0 us
  waiting for transfers between devices: 80.6 us -> 28.8 us
  Pallas kernels: 0 us -> 41.9 us
  starting transfers between devices: 9.72 us -> 32 us
  between operations: 14.9 us -> 1.48 us
  local copies, waits for them, and re-layouts: 44 us -> 55.2 us
  other arithmetic: 15.7 us -> 7.21 us
    dot_general x50 -> x0, matrix products: 107 us -> none  [the longest x16 53.8 us: box_features(): jnp.dot(box_cube.reshape(B * B, B), table_half.T, preferred_element_type=...]
    another operation x1 -> x0, loops' own time: 93 us -> none  [body(): features = lax.map(extract_one, coords)]
    all_gather x1 -> x0, blocking collectives: 72.5 us -> none  [body(): lax.all_gather(multiplicity, ('tile', 'bank'), axis=0, tiled=True)]
    ppermute x4 -> x14, waiting for transfers between devices: 80.6 us -> 28.8 us  [the longest x3 11.3 us: gather_rows(): lax.ppermute(mine, 'tile', [(i, (i + by) % tiles) for i in range(tiles)])]
    pallas_call x0 -> x4, Pallas kernels: none -> 41.9 us  [the longest x1 19.8 us: score_local(): pl.pallas_call(score_kernel, grid=(classes // group,), in_specs=[pl.Block...]
    dynamic_update_slice x16 -> x0, local copies, waits for them, and re-layouts: 24.6 us -> none  [body(): features = lax.map(extract_one, coords)]
    concatenate x1 -> x2, local copies, waits for them, and re-layouts: 0.1 us -> 22.9 us  [the longest x1 12.6 us: gather_rows(): return jnp.concatenate([line, other], axis=0)]
    ppermute x4 -> x14, starting transfers between devices: 9.68 us -> 32 us  [the longest x6 17.9 us: shifted(): return lax.ppermute(value, axis, steps_of(axis, by))]
  transfers between devices with their start and end apart: 5 -> 14, of which waited for: 4 -> 6; matrix products, arithmetic and copies ran while one was open for 2% -> 10% of each run, Pallas kernels for 0% -> 4%
where the time goes in v1:
time: 168 us; the launch traced here: 167 us
  local copies, waits for them, and re-layouts  55.2 us (33%)
  Pallas kernels  41.9 us (25%)
  starting transfers between devices  32 us (19%)
  waiting for transfers between devices  28.8 us (17%)
  other arithmetic  7.21 us (4%)
    pallas_call x1, Pallas kernels, score_local(): pl.pallas_call(score_kernel, grid=(classes // group,), in_specs=[pl.Block...  19.8 us
    ppermute x6, starting transfers between devices, shifted(): return lax.ppermute(value, axis, steps_of(axis, by))  17.9 us
    concatenate x1, local copies, waits for them, and re-layouts, gather_rows(): return jnp.concatenate([line, other], axis=0)  12.6 us
    ppermute x3, waiting for transfers between devices, gather_rows(): lax.ppermute(mine, 'tile', [(i, (i + by) % tiles) for i in range(tiles)])  11.3 us
    slice x2, local copies, waits for them, and re-layouts, score_local(): features = rows[:, :F]  10.9 us
    concatenate x1, local copies, waits for them, and re-layouts, gather_rows(): line = jnp.concatenate([line, along_x, along_y, across_y, across_x], axis=0)  10.3 us
    pallas_call x1, Pallas kernels, body(): pl.pallas_call(functools.partial(far_kernel, half=half, gap=wide), grid=(...  9.99 us
    ppermute x1, waiting for transfers between devices, gather_rows(): along_x = lax.ppermute(line, 'bank', [(0, 1), (1, 0), (2, 3), (3, 2)])  9.4 us
  transfers between devices with their start and end apart: 14, of which 6 were waited for; matrix products, arithmetic and copies ran while one was open for 10% of the time, Pallas kernels for 4%

profile of v1, /device:TPU:0, one launch (start us, length us, event | category | flops | bytes accessed | tf_op | source)
XLA Modules:
  0.0 166.6 jit_solution(8179405617204554150)
XLA Ops:
  2.7 5.5 %collective-permute-start = (s32[3,16]{1,0:T(4,128)S(1)}, s32[3,16]{1,0:T(4,128)S(1)}, u32[]{:S(2)}, u32[]{:S(2)}) collective-permute-start(s32[3,16]{1,0:T(4,128)S(1)} %get-tuple-element.15), channel_id=1, source_target_pairs={{0,1},{1,2},{2,3},{4,5},{5,6},{6,7},{8,9},{9,10},{10,11},{12,13},{... | collective-permute-start | bytes 584 | tf_op jit(solution)/shard_map/ppermute | solution.py:261
  11.0 3.1 %collective-permute-start.2 = (bf16[48,64,128]{2,1,0:T(8,128)(2,1)S(1)}, bf16[48,64,128]{2,1,0:T(8,128)(2,1)S(1)}, u32[]{:S(2)}, u32[]{:S(2)}) collective-permute-start(bf16[48,64,128]{2,1,0:T(8,128)(2,1)S(1)} %get-tuple-element.13), channel_id=1, source_target_pairs={{0,4},{4,8},{8,12},{12,16},{16,20},{20,24},{24,28},{1,5},{5,9},{9,... | collective-permute-start | bytes 2359304 | tf_op jit(solution)/shard_map/ppermute | solution.py:261
  16.3 7.1 %near_rows.1.near_ref = f32[304,768]{1,0:T(8,128)} custom-call(bf16[8,128]{1,0:T(8,128)(2,1)} %fusion.8.corners_ref, f32[128,128]{1,0:T(8,128)} %constant.35.clone.first_ref, f32[128,128]{1,0:T(8,128)} %constant.36.clone.second_ref, bf16[64,64,128]{2,1,0:T(8,128)(2,1)} %volume_ref.1, bf16[304,10240]{1,0:T(8,128)(2,1)} %constant.34.clone.plane_ref), custom_call_target="tpu_custom_call" | custom-call | flops 2717908992 | bytes 8000000 | tf_op jit(solution)/shard_map/near_rows/pallas_call | solution.py:358
  25.2 10.0 %far_rows.1 = (bf16[256,256]{1,0:T(8,128)(2,1)}, f32[256,256]{1,0:T(8,128)}, bf16[256,256]{1,0:T(8,128)(2,1)}) custom-call(bf16[8,128]{1,0:T(8,128)(2,1)} %fusion.8.corners_ref, f32[128,128]{1,0:T(8,128)} %constant.35.clone.first_ref, f32[128,128]{1,0:T(8,128)} %constant.36.clone.second_ref, bf16[48,64,128]{2,1,0:T(8,128)(2,1)} %copy-done.4, ...), custom_call_target="tpu_custom_call" | custom-call | tf_op jit(solution)/shard_map/far_rows/pallas_call | solution.py:377
  36.5 5.5 %collective-permute-start.5 = (bf16[256,256]{1,0:T(8,128)(2,1)}, bf16[256,256]{1,0:T(8,128)(2,1)S(1)}, u32[]{:S(2)}, u32[]{:S(2)}) collective-permute-start(bf16[256,256]{1,0:T(8,128)(2,1)} %get-tuple-element.9), channel_id=1, source_target_pairs={{0,1},{1,2},{2,3},{4,5},{5,6},{6,7},{8,9},{9,10},{10,11},{12,13},{... | collective-permute-start | bytes 393224 | tf_op jit(solution)/shard_map/ppermute | solution.py:261
  46.6 5.0 %join.1 = bf16[16,4480]{1,0:T(8,128)(2,1)} custom-call(f32[256,256]{1,0:T(8,128)} %get-tuple-element.7.own_ref, bf16[256,256]{1,0:T(8,128)(2,1)} %copy-done.7, bf16[256,256]{1,0:T(8,128)(2,1)} %copy-done.8, bf16[16,256]{1,0:T(8,128)(2,1)} %select_convert_fusion.multiplicity_ref), custom_call_target="tpu_custom_call" | custom-call | tf_op jit(solution)/shard_map/join/pallas_call | solution.py:408
  51.6 3.0 %collective-permute-start.8 = (bf16[16,4480]{1,0:T(8,128)(2,1)}, bf16[16,4480]{1,0:T(8,128)(2,1)S(1)}, u32[]{:S(2)}, u32[]{:S(2)}) collective-permute-start(bf16[16,4480]{1,0:T(8,128)(2,1)} %join.1), channel_id=1, source_target_pairs={{0,24},{4,28},{8,0},{12,4},{16,8},{20,12},{24,16},{28,20},{1,25},{... | collective-permute-start | bytes 430088 | tf_op jit(solution)/shard_map/ppermute | solution.py:270
  56.6 2.6 %collective-permute-done.8 = bf16[16,4480]{1,0:T(8,128)(2,1)S(1)} collective-permute-done((bf16[16,4480]{1,0:T(8,128)(2,1)}, bf16[16,4480]{1,0:T(8,128)(2,1)S(1)}, u32[]{:S(2)}, u32[]{:S(2)}) %collective-permute-start.8) | collective-permute-done | bytes 143392 | tf_op jit(solution)/shard_map/ppermute | solution.py:270
  59.2 8.7 %collective-permute-done.7 = bf16[16,4480]{1,0:T(8,128)(2,1)S(1)} collective-permute-done((bf16[16,4480]{1,0:T(8,128)(2,1)}, bf16[16,4480]{1,0:T(8,128)(2,1)S(1)}, u32[]{:S(2)}, u32[]{:S(2)}) %collective-permute-start.7) | collective-permute-done | bytes 143392 | tf_op jit(solution)/shard_map/ppermute | solution.py:270
  68.9 2.4 %collective-permute-start.9 = (bf16[64,4480]{1,0:T(8,128)(2,1)S(1)}, bf16[64,4480]{1,0:T(8,128)(2,1)S(1)}, u32[]{:S(2)}, u32[]{:S(2)}) collective-permute-start(bf16[64,4480]{1,0:T(8,128)(2,1)S(1)} %pad_maximum_fusion), channel_id=1, source_target_pairs={{0,1},{1,0},{2,3},{3,2},{4,5},{5,4},{6,7},{7,6},{8,9},{9,8},{10,11... | collective-permute-start | bytes 1720328 | tf_op jit(solution)/shard_map/ppermute | solution.py:274
  71.3 2.3 %collective-permute-start.10 = (bf16[64,4480]{1,0:T(8,128)(2,1)S(1)}, bf16[64,4480]{1,0:T(8,128)(2,1)S(1)}, u32[]{:S(2)}, u32[]{:S(2)}) collective-permute-start(bf16[64,4480]{1,0:T(8,128)(2,1)S(1)} %pad_maximum_fusion), channel_id=1, source_target_pairs={{0,2},{2,0},{1,3},{3,1},{4,6},{6,4},{5,7},{7,5},{8,10},{10,8},{9,1... | collective-permute-start | bytes 1720328 | tf_op jit(solution)/shard_map/ppermute | solution.py:275
  73.7 9.4 %collective-permute-done.9 = bf16[64,4480]{1,0:T(8,128)(2,1)S(1)} collective-permute-done((bf16[64,4480]{1,0:T(8,128)(2,1)S(1)}, bf16[64,4480]{1,0:T(8,128)(2,1)S(1)}, u32[]{:S(2)}, u32[]{:S(2)}) %collective-permute-start.9) | collective-permute-done | bytes 573472 | tf_op jit(solution)/shard_map/ppermute | solution.py:274
  83.8 3.1 %collective-permute-start.11 = (bf16[32,4480]{1,0:T(8,128)(2,1)}, bf16[32,4480]{1,0:T(8,128)(2,1)}, u32[]{:S(2)}, u32[]{:S(2)}) collective-permute-start(bf16[32,4480]{1,0:T(8,128)(2,1)} %slice.40), channel_id=1, source_target_pairs={{0,2},{2,0},{1,3},{3,1},{4,6},{6,4},{5,7},{7,5},{8,10},{10,8},{9,1... | collective-permute-start | bytes 860168 | tf_op jit(solution)/shard_map/ppermute | solution.py:277
  92.0 2.3 %copy.54 = bf16[16,4480]{0,1:T(8,128)(2,1)} copy(bf16[16,4480]{1,0:T(8,128)(2,1)} %copy-done.5) | data formatting | bytes 286720 | tf_op jit(solution)/shard_map/ppermute | solution.py:270
  94.3 2.3 %copy.56 = bf16[64,4480]{0,1:T(8,128)(2,1)} copy(bf16[64,4480]{1,0:T(8,128)(2,1)} %copy-done.2) | data formatting | bytes 1146880 | tf_op jit(solution)/shard_map/ppermute | solution.py:275
  96.5 2.3 %copy.55 = bf16[64,4480]{0,1:T(8,128)(2,1)} copy(bf16[64,4480]{1,0:T(8,128)(2,1)} %copy-done.1) | data formatting | bytes 1146880 | tf_op jit(solution)/shard_map/ppermute | solution.py:274
  98.8 2.4 %copy.57 = bf16[32,4480]{0,1:T(8,128)(2,1)} copy(bf16[32,4480]{1,0:T(8,128)(2,1)} %collective-permute-done.11) | data formatting | bytes 573440 | tf_op jit(solution)/shard_map/ppermute | solution.py:277
  101.2 2.4 %copy.58 = bf16[32,4480]{0,1:T(8,128)(2,1)} copy(bf16[32,4480]{1,0:T(8,128)(2,1)} %collective-permute-done.12) | data formatting | bytes 573440 | tf_op jit(solution)/shard_map/ppermute | solution.py:278
  103.5 10.3 %concatenate.17 = bf16[256,4480]{0,1:T(8,128)(2,1)} concatenate(bf16[16,4480]{0,1:T(8,128)(2,1)S(1)} %copy.51, bf16[16,4480]{0,1:T(8,128)(2,1)S(1)} %copy.52, bf16[16,4480]{0,1:T(8,128)(2,1)S(1)} %copy.53, bf16[16,4480]{0,1:T(8,128)(2,1)} %copy.54, bf16[64,4480]{0,1:T(8,128)(2,1)} %copy.55, bf16[64,4480]{0,1:T(8,128)(2,1)} %copy.56, bf16[32,4480]{0,1:T(8,128)(2,1)} %copy.57, ...), dimensions={0} | concatenate | bytes 4587520 | tf_op jit(solution)/shard_map/concatenate | solution.py:279
  113.9 4.8 %collective-permute-done.13 = bf16[256,4480]{0,1:T(8,128)(2,1)} collective-permute-done((bf16[256,4480]{0,1:T(8,128)(2,1)}, bf16[256,4480]{0,1:T(8,128)(2,1)}, u32[]{:S(2)}, u32[]{:S(2)}) %collective-permute-start.13) | collective-permute-done | bytes 2293792 | tf_op jit(solution)/shard_map/ppermute | solution.py:283
  118.6 12.6 %concatenate.18 = bf16[512,4480]{0,1:T(8,128)(2,1)} concatenate(bf16[16,4480]{0,1:T(8,128)(2,1)S(1)} %copy.51, bf16[16,4480]{0,1:T(8,128)(2,1)S(1)} %copy.52, bf16[16,4480]{0,1:T(8,128)(2,1)S(1)} %copy.53, bf16[16,4480]{0,1:T(8,128)(2,1)} %copy.54, bf16[64,4480]{0,1:T(8,128)(2,1)} %copy.55, bf16[64,4480]{0,1:T(8,128)(2,1)} %copy.56, bf16[32,4480]{0,1:T(8,128)(2,1)} %copy.57, ...), dimensions={0} | concatenate | bytes 9175040 | tf_op jit(solution)/shard_map/concatenate | solution.py:284
  132.5 4.5 %slice.42 = bf16[512,4096]{0,1:T(8,128)(2,1)} slice(bf16[512,4480]{0,1:T(8,128)(2,1)} %concatenate.18), slice={[0:512], [0:4096]} | slice | bytes 8388608 | tf_op jit(solution)/shard_map/slice | solution.py:293
  138.5 6.4 %copy.59.rows_ref = bf16[512,4096]{1,0:T(8,128)(2,1)} copy(bf16[512,4096]{0,1:T(8,128)(2,1)} %slice.42) | data formatting | bytes 8388608 | tf_op jit(solution)/shard_map/slice | solution.py:293
  144.9 19.8 %score.1 = (f32[20,64,4096]{2,1,0:T(8,128)}, f32[20,64,1]{2,1,0:T(8,128)}) custom-call(bf16[512,4096]{1,0:T(8,128)(2,1)} %copy.59.rows_ref, bf16[64,512]{1,0:T(8,128)(2,1)} %dynamic-slice_bitcast_fusion.multiplicity_ref, f32[1,512]{1,0:T(1,128)} %fusion.10.norm_ref, bf16[20,64,4096]{2,1,0:T(8,128)(2,1)} %bitcast.20), custom_call_target="tpu_custom_call" | custom-call | flops 10737418240 | bytes 31457280 | tf_op jit(solution)/shard_map/score/pallas_call | solution.py:298
  (62 shorter events, 27.6 us)
Async XLA Ops:
  0.6 14.8 %copy-start.12 = (s32[3]{0:T(128)S(1)}, s32[3]{0:T(128)}, u32[]{:S(2)}) copy-start(s32[3]{0:T(128)} %constant.33.clone) | copy-start | bytes 40
  0.6 14.9 %copy-start.11 = (s32[3]{0:T(128)S(1)}, s32[3]{0:T(128)}, u32[]{:S(2)}) copy-start(s32[3]{0:T(128)} %constant.43) | copy-start | bytes 40
  0.7 14.1 %copy-start.10 = (s32[1,1,16,128]{3,2,1,0:T(8,128)S(1)}, s32[1,1,16,128]{3,2,1,0:T(8,128)}, u32[]{:S(2)}) copy-start(s32[1,1,16,128]{3,2,1,0:T(8,128)} %param.14) | copy-start | bytes 24580
  0.7 14.1 %copy-start.9 = (s32[1,1,16,128]{3,2,1,0:T(8,128)S(1)}, s32[1,1,16,128]{3,2,1,0:T(8,128)}, u32[]{:S(2)}) copy-start(s32[1,1,16,128]{3,2,1,0:T(8,128)} %param.13) | copy-start | bytes 24580
  1.4 14.1 %collective-permute-start.1 = (s32[3,16]{1,0:T(4,128)S(1)}, s32[3,16]{1,0:T(4,128)S(1)}, u32[]{:S(2)}, u32[]{:S(2)}) collective-permute-start(s32[3,16]{1,0:T(4,128)S(1)} %get-tuple-element.15), channel_id=1, source_target_pairs={{1,0},{2,1},{3,2},{5,4},{6,5},{7,6},{9,8},{10,9},{11,10},{13,12},{... | collective-permute-start | bytes 584 | tf_op jit(solution)/shard_map/ppermute | solution.py:261
  2.7 12.9 %collective-permute-start = (s32[3,16]{1,0:T(4,128)S(1)}, s32[3,16]{1,0:T(4,128)S(1)}, u32[]{:S(2)}, u32[]{:S(2)}) collective-permute-start(s32[3,16]{1,0:T(4,128)S(1)} %get-tuple-element.15), channel_id=1, source_target_pairs={{0,1},{1,2},{2,3},{4,5},{5,6},{6,7},{8,9},{9,10},{10,11},{12,13},{... | collective-permute-start | bytes 584 | tf_op jit(solution)/shard_map/ppermute | solution.py:261
  9.7 13.7 %collective-permute-start.3 = (bf16[48,64,128]{2,1,0:T(8,128)(2,1)S(1)}, bf16[48,64,128]{2,1,0:T(8,128)(2,1)S(1)}, u32[]{:S(2)}, u32[]{:S(2)}) collective-permute-start(bf16[48,64,128]{2,1,0:T(8,128)(2,1)S(1)} %get-tuple-element.12), channel_id=1, source_target_pairs={{4,0},{8,4},{12,8},{16,12},{20,16},{24,20},{28,24},{5,1},{9,5},{13... | collective-permute-start | bytes 2359304 | tf_op jit(solution)/shard_map/ppermute | solution.py:261
  11.0 12.4 %collective-permute-start.2 = (bf16[48,64,128]{2,1,0:T(8,128)(2,1)S(1)}, bf16[48,64,128]{2,1,0:T(8,128)(2,1)S(1)}, u32[]{:S(2)}, u32[]{:S(2)}) collective-permute-start(bf16[48,64,128]{2,1,0:T(8,128)(2,1)S(1)} %get-tuple-element.13), channel_id=1, source_target_pairs={{0,4},{4,8},{8,12},{12,16},{16,20},{20,24},{24,28},{1,5},{5,9},{9,... | collective-permute-start | bytes 2359304 | tf_op jit(solution)/shard_map/ppermute | solution.py:261
  23.4 0.9 copy-start.3
  35.2 9.0 %collective-permute-start.4 = (bf16[256,256]{1,0:T(8,128)(2,1)}, bf16[256,256]{1,0:T(8,128)(2,1)S(1)}, u32[]{:S(2)}, u32[]{:S(2)}) collective-permute-start(bf16[256,256]{1,0:T(8,128)(2,1)} %get-tuple-element.8), channel_id=1, source_target_pairs={{1,0},{2,1},{3,2},{5,4},{6,5},{7,6},{9,8},{10,9},{11,10},{13,12},{... | collective-permute-start | bytes 393224 | tf_op jit(solution)/shard_map/ppermute | solution.py:261
  36.5 9.5 %collective-permute-start.5 = (bf16[256,256]{1,0:T(8,128)(2,1)}, bf16[256,256]{1,0:T(8,128)(2,1)S(1)}, u32[]{:S(2)}, u32[]{:S(2)}) collective-permute-start(bf16[256,256]{1,0:T(8,128)(2,1)} %get-tuple-element.9), channel_id=1, source_target_pairs={{0,1},{1,2},{2,3},{4,5},{5,6},{6,7},{8,9},{9,10},{10,11},{12,13},{... | collective-permute-start | bytes 393224 | tf_op jit(solution)/shard_map/ppermute | solution.py:261
  44.2 1.8 %copy-start.7 = (bf16[256,256]{1,0:T(8,128)(2,1)}, bf16[256,256]{1,0:T(8,128)(2,1)S(1)}, u32[]{:S(2)}) copy-start(bf16[256,256]{1,0:T(8,128)(2,1)S(1)} %collective-permute-done.4.left_ref) | copy-start | bytes 393220
  51.6 37.5 %copy-start = (bf16[16,4480]{1,0:T(8,128)(2,1)S(1)}, bf16[16,4480]{1,0:T(8,128)(2,1)}, u32[]{:S(2)}) copy-start(bf16[16,4480]{1,0:T(8,128)(2,1)} %join.1) | copy-start | bytes 430084
  51.6 7.5 %collective-permute-start.8 = (bf16[16,4480]{1,0:T(8,128)(2,1)}, bf16[16,4480]{1,0:T(8,128)(2,1)S(1)}, u32[]{:S(2)}, u32[]{:S(2)}) collective-permute-start(bf16[16,4480]{1,0:T(8,128)(2,1)} %join.1), channel_id=1, source_target_pairs={{0,24},{4,28},{8,0},{12,4},{16,8},{20,12},{24,16},{28,20},{1,25},{... | collective-permute-start | bytes 430088 | tf_op jit(solution)/shard_map/ppermute | solution.py:270
  54.6 13.2 %collective-permute-start.7 = (bf16[16,4480]{1,0:T(8,128)(2,1)}, bf16[16,4480]{1,0:T(8,128)(2,1)S(1)}, u32[]{:S(2)}, u32[]{:S(2)}) collective-permute-start(bf16[16,4480]{1,0:T(8,128)(2,1)} %join.1), channel_id=1, source_target_pairs={{0,16},{4,20},{8,24},{12,28},{16,0},{20,4},{24,8},{28,12},{1,17},{... | collective-permute-start | bytes 430088 | tf_op jit(solution)/shard_map/ppermute | solution.py:270
  55.0 12.8 %collective-permute-start.6 = (bf16[16,4480]{1,0:T(8,128)(2,1)}, bf16[16,4480]{1,0:T(8,128)(2,1)S(1)}, u32[]{:S(2)}, u32[]{:S(2)}) collective-permute-start(bf16[16,4480]{1,0:T(8,128)(2,1)} %join.1), channel_id=1, source_target_pairs={{0,8},{4,12},{8,16},{12,20},{16,24},{20,28},{24,0},{28,4},{1,9},{5... | collective-permute-start | bytes 430088 | tf_op jit(solution)/shard_map/ppermute | solution.py:270
  59.2 28.6 %copy-start.5 = (bf16[16,4480]{1,0:T(8,128)(2,1)}, bf16[16,4480]{1,0:T(8,128)(2,1)S(1)}, u32[]{:S(2)}) copy-start(bf16[16,4480]{1,0:T(8,128)(2,1)S(1)} %collective-permute-done.8) | copy-start | bytes 430084
  67.9 19.9 %copy-start.6 = (bf16[16,4480]{1,0:T(8,128)(2,1)}, bf16[16,4480]{1,0:T(8,128)(2,1)S(1)}, u32[]{:S(2)}) copy-start(bf16[16,4480]{1,0:T(8,128)(2,1)S(1)} %collective-permute-done.7) | copy-start | bytes 430084
  68.9 14.2 %collective-permute-start.9 = (bf16[64,4480]{1,0:T(8,128)(2,1)S(1)}, bf16[64,4480]{1,0:T(8,128)(2,1)S(1)}, u32[]{:S(2)}, u32[]{:S(2)}) collective-permute-start(bf16[64,4480]{1,0:T(8,128)(2,1)S(1)} %pad_maximum_fusion), channel_id=1, source_target_pairs={{0,1},{1,0},{2,3},{3,2},{4,5},{5,4},{6,7},{7,6},{8,9},{9,8},{10,11... | collective-permute-start | bytes 1720328 | tf_op jit(solution)/shard_map/ppermute | solution.py:274
  71.3 15.6 %collective-permute-start.10 = (bf16[64,4480]{1,0:T(8,128)(2,1)S(1)}, bf16[64,4480]{1,0:T(8,128)(2,1)S(1)}, u32[]{:S(2)}, u32[]{:S(2)}) collective-permute-start(bf16[64,4480]{1,0:T(8,128)(2,1)S(1)} %pad_maximum_fusion), channel_id=1, source_target_pairs={{0,2},{2,0},{1,3},{3,1},{4,6},{6,4},{5,7},{7,5},{8,10},{10,8},{9,1... | collective-permute-start | bytes 1720328 | tf_op jit(solution)/shard_map/ppermute | solution.py:275
  83.1 4.7 %copy-start.1 = (bf16[64,4480]{1,0:T(8,128)(2,1)}, bf16[64,4480]{1,0:T(8,128)(2,1)S(1)}, u32[]{:S(2)}) copy-start(bf16[64,4480]{1,0:T(8,128)(2,1)S(1)} %collective-permute-done.9) | copy-start | bytes 1720324
  83.8 15.0 %collective-permute-start.11 = (bf16[32,4480]{1,0:T(8,128)(2,1)}, bf16[32,4480]{1,0:T(8,128)(2,1)}, u32[]{:S(2)}, u32[]{:S(2)}) collective-permute-start(bf16[32,4480]{1,0:T(8,128)(2,1)} %slice.40), channel_id=1, source_target_pairs={{0,2},{2,0},{1,3},{3,1},{4,6},{6,4},{5,7},{7,5},{8,10},{10,8},{9,1... | collective-permute-start | bytes 860168 | tf_op jit(solution)/shard_map/ppermute | solution.py:277
  87.9 13.3 %collective-permute-start.12 = (bf16[32,4480]{1,0:T(8,128)(2,1)}, bf16[32,4480]{1,0:T(8,128)(2,1)}, u32[]{:S(2)}, u32[]{:S(2)}) collective-permute-start(bf16[32,4480]{1,0:T(8,128)(2,1)} %slice.41), channel_id=1, source_target_pairs={{0,1},{1,0},{2,3},{3,2},{4,5},{5,4},{6,7},{7,6},{8,9},{9,8},{10,11... | collective-permute-start | bytes 860168 | tf_op jit(solution)/shard_map/ppermute | solution.py:278
  113.9 4.8 %collective-permute-start.13 = (bf16[256,4480]{0,1:T(8,128)(2,1)}, bf16[256,4480]{0,1:T(8,128)(2,1)}, u32[]{:S(2)}, u32[]{:S(2)}) collective-permute-start(bf16[256,4480]{0,1:T(8,128)(2,1)} %concatenate.17), channel_id=1, source_target_pairs={{0,4},{4,0},{8,12},{12,8},{16,20},{20,16},{24,28},{28,24},{1,5},{5... | collective-permute-start | bytes 6881288 | tf_op jit(solution)/shard_map/ppermute | solution.py:283
  (3 other events, 2.5 us)

commit v2 on v1

--- a/solution.py
+++ b/solution.py
@@ -15,7 +15,7 @@
 HALF = B // 2
 TERMS = L // 2
 EPSILON = 1e-06
-LIMIT = 60 * 1024 * 1024
+MIB = 1024 * 1024
 
 
 def waves(count):
@@ -217,38 +217,102 @@
     out_ref[:, F + R :] = tail.astype(jnp.bfloat16)
 
 
-def score_kernel(
-    rows_ref, multiplicity_ref, norm_ref, bank_ref, out_ref, sums_ref, turned_ref,
-):
+def load_blocks(blocks, rows_ref, tail_ref, sems):
+    copies, at = [], 0
+    for k, block in enumerate(blocks):
+        count = block.shape[0]
+        place = pl.ds(at, count)
+        copies.append(
+            pltpu.make_async_copy(block.at[:, pl.ds(0, F)], rows_ref.at[place], sems.at[2 * k])
+        )
+        copies.append(
+            pltpu.make_async_copy(
+                block.at[:, pl.ds(F, block.shape[1] - F)], tail_ref.at[place], sems.at[2 * k + 1]
+            )
+        )
+        at += count
+    for copy in copies:
+        copy.start()
+    for copy in copies:
+        copy.wait()
+
+
+def read_tail(bank_ref, tail, tail_ref, multiplicity_ref, norm_ref, orients):
+    tail_ref[...] = tail.astype(jnp.float32).T
+    start = pl.multiple_of(bank_ref[0] * orients, orients)
+    multiplicity_ref[...] = tail_ref[pl.ds(start, orients), :]
+    norm_ref[...] = tail_ref[R : R + 1, :] + tail_ref[R + 1 : R + 2, :]
+
+
+def weigh(bank_rows, rows, multiplicity, norm, count):
+    scores = lax.dot_general(
+        bank_rows, rows, (((1,), (1,)), ((), ())), preferred_element_type=jnp.float32
+    )
+    wide = bank_rows.astype(jnp.float32)
+    bank_norm = jnp.sqrt(jnp.mean(wide * wide, axis=1, keepdims=True) + EPSILON)
+    correl = scores / (F * norm * bank_norm)
+    multiplicity = jnp.concatenate([multiplicity] * count, axis=0)
+    return (multiplicity * jnp.maximum(correl, 0.0)).astype(jnp.bfloat16)
+
+
+def weigh_kernel(index_ref, *refs, blocks):
+    sources, (bank_ref, out_ref) = refs[:blocks], refs[blocks : blocks + 2]
+    rows_ref, tail_ref, turned_ref, multiplicity_ref, norm_ref, sems = refs[blocks + 2 :]
+    count, orients, width = bank_ref.shape
+
+    @pl.when(pl.program_id(0) == 0)
+    def _():
+        load_blocks(sources, rows_ref, tail_ref, sems)
+        read_tail(index_ref, tail_ref[...], turned_ref, multiplicity_ref, norm_ref, orients)
+
+    bank = bank_ref[...].reshape(count * orients, width)
+    weights = weigh(bank, rows_ref[...], multiplicity_ref[...], norm_ref[...], count)
+    out_ref[...] = weights.reshape(out_ref.shape)
+
+
+def sum_kernel(index_ref, *refs, early, blocks, late):
+    parts, sources = refs[:early], refs[early : early + blocks]
+    bank_ref, out_ref, sums_ref = refs[early + blocks : early + blocks + 3]
+    rows_ref, tail_ref, turned_ref, multiplicity_ref, norm_ref, sems = refs[early + blocks + 3 :]
+    count, orients, width = bank_ref.shape
+    boxes = rows_ref.shape[0]
     step = pl.program_id(0)
 
     @pl.when(step == 0)
     def _():
-        turned_ref[...] = rows_ref[...].T
-
-    count, orients, width = bank_ref.shape
+        load_blocks(sources, rows_ref, tail_ref, sems)
+        read_tail(
+            index_ref, tail_ref[boxes - late :], turned_ref, multiplicity_ref, norm_ref, orients
+        )
+
     bank = bank_ref[...].reshape(count * orients, width)
-    scores = jnp.dot(bank, turned_ref[...], preferred_element_type=jnp.float32)
-    wide = bank.astype(jnp.float32)
-    bank_norm = jnp.sqrt(jnp.mean(wide * wide, axis=1, keepdims=True) + EPSILON)
-    correl = scores / (F * norm_ref[...] * bank_norm)
-    multiplicity = jnp.concatenate([multiplicity_ref[...].astype(jnp.float32)] * count, axis=0)
-    weights = (multiplicity * jnp.maximum(correl, 0.0)).astype(jnp.bfloat16)
+    weights = weigh(
+        bank, rows_ref[boxes - late :, :], multiplicity_ref[...], norm_ref[...], count
+    )
+    known = [part[...].reshape(count * orients, part.shape[2]) for part in parts]
+    weights = jnp.concatenate(known + [weights], axis=1)
     total = jnp.dot(weights, rows_ref[...], preferred_element_type=jnp.float32)
     out_ref[...] = total.reshape(out_ref.shape)
-    sums = jnp.sum(weights.astype(jnp.float32), axis=1, keepdims=True)
-    sums_ref[...] = sums.reshape(sums_ref.shape)
-
-
-def score_plain(rows, multiplicity, norm, bank):
-    scores = jnp.einsum("if,rcf->irc", rows, bank, preferred_element_type=jnp.float32)
+    ones = jnp.ones((8, boxes), jnp.bfloat16)
+    sums = lax.dot_general(
+        ones, weights, (((1,), (1,)), ((), ())), preferred_element_type=jnp.float32
+    )
+    for c in range(count):
+        sums_ref[pl.ds(step * count + c, 1), :] = sums[:1, c * orients : (c + 1) * orients]
+
+
+def score_plain(rows, bank):
+    local_rows = bank.shape[0]
+    start = F + lax.axis_index("bank") * local_rows
+    multiplicity = lax.dynamic_slice_in_dim(rows, start, local_rows, 1).astype(jnp.float32)
+    norm = rows[:, F + R].astype(jnp.float32) + rows[:, F + R + 1].astype(jnp.float32)
+    features = rows[:, :F]
+    scores = jnp.einsum("if,rcf->irc", features, bank, preferred_element_type=jnp.float32)
     wide = bank.astype(jnp.float32)
     bank_norm = jnp.sqrt(jnp.mean(wide * wide, axis=2) + EPSILON)
     correl = scores / (F * norm[:, None, None] * bank_norm[None])
-    weights = (multiplicity.astype(jnp.float32)[:, :, None] * jnp.maximum(correl, 0.0)).astype(
-        jnp.bfloat16
-    )
-    class_sums = jnp.einsum("irc,if->rcf", weights, rows, preferred_element_type=jnp.float32)
+    weights = (multiplicity[:, :, None] * jnp.maximum(correl, 0.0)).astype(jnp.bfloat16)
+    class_sums = jnp.einsum("irc,if->rcf", weights, features, preferred_element_type=jnp.float32)
     return class_sums, jnp.sum(weights.astype(jnp.float32), axis=0)
 
 
@@ -261,67 +325,114 @@
     return lax.ppermute(value, axis, steps_of(axis, by))
 
 
-def gather_rows(mine):
+def gather_score(mine, reference_bank):
     tiles, banks = lax.axis_size("tile"), lax.axis_size("bank")
-    blocks = [mine]
-    if tiles % 2 == 0:
-        for by in range(2, tiles, 2):
-            blocks.append(
-                lax.ppermute(mine, "tile", [(i, (i + by) % tiles) for i in range(tiles)])
-            )
-    line = jnp.concatenate(blocks, axis=0)
-    if banks == 4:
-        along_x = lax.ppermute(line, "bank", [(0, 1), (1, 0), (2, 3), (3, 2)])
-        along_y = lax.ppermute(line, "bank", [(0, 2), (2, 0), (1, 3), (3, 1)])
-        half = line.shape[0] // 2
-        across_y = lax.ppermute(along_x[:half], "bank", [(0, 2), (2, 0), (1, 3), (3, 1)])
-        across_x = lax.ppermute(along_y[half:], "bank", [(0, 1), (1, 0), (2, 3), (3, 2)])
-        line = jnp.concatenate([line, along_x, along_y, across_y, across_x], axis=0)
-    else:
-        line = lax.all_gather(line, "bank", axis=0, tiled=True)
-    if tiles % 2 == 0:
-        other = lax.ppermute(line, "tile", [(i, i ^ 1) for i in range(tiles)])
-        return jnp.concatenate([line, other], axis=0)
-    return lax.all_gather(line, "tile", axis=0, tiled=True)
-
-
-def score_local(rows, reference_bank):
     local_rows, classes, width = reference_bank.shape
-    row_start = lax.axis_index("bank") * local_rows
-    multiplicity = lax.dynamic_slice_in_dim(rows, F + row_start, local_rows, 1)
-    norm = rows[:, F + R].astype(jnp.float32) + rows[:, F + R + 1].astype(jnp.float32)
-    features = rows[:, :F]
-    boxes = rows.shape[0]
-    if boxes > 1024 or classes % 4:
-        return score_plain(features, multiplicity, norm, reference_bank)
-    group = 4
-    out, sums = pl.pallas_call(
-        score_kernel,
-        grid=(classes // group,),
-        in_specs=[
-            pl.BlockSpec((boxes, F), lambda i: (0, 0)),
-            pl.BlockSpec((local_rows, boxes), lambda i: (0, 0)),
-            pl.BlockSpec((1, boxes), lambda i: (0, 0)),
-            pl.BlockSpec((group, local_rows, width), lambda i: (i, 0, 0)),
+    if banks != 4 or tiles % 2 or tiles * banks * mine.shape[0] > 1024 or classes % 5:
+        return score_plain(
+            lax.all_gather(lax.all_gather(mine, "bank", axis=0, tiled=True), "tile", axis=0, tiled=True),
+            reference_bank,
+        )
+    bank = jnp.transpose(reference_bank, (1, 0, 2))
+
+    def along(value, pairs):
+        return lax.ppermute(value, "bank", pairs)
+
+    def swap(value):
+        return lax.ppermute(value, "tile", [(i, i ^ 1) for i in range(tiles)])
+
+    x_pairs, y_pairs = [(0, 1), (1, 0), (2, 3), (3, 2)], [(0, 2), (2, 0), (1, 3), (3, 1)]
+    line = jnp.concatenate(
+        [mine]
+        + [
+            lax.ppermute(mine, "tile", [(i, (i + by) % tiles) for i in range(tiles)])
+            for by in range(2, tiles, 2)
         ],
+        axis=0,
+    )
+    half = line.shape[0] // 2
+    from_x, from_y = along(line, x_pairs), along(line, y_pairs)
+    near = [line, swap(line)]
+    first = weigh_blocks(near, bank)
+    part_x, part_y, first = lax.optimization_barrier((from_x[:half], from_y[half:], first))
+    across_y, across_x = along(part_x, y_pairs), along(part_y, x_pairs)
+    middle = [from_x, from_y, swap(from_x), swap(from_y)]
+    second = weigh_blocks(middle, bank)
+    across_y, across_x, second = lax.optimization_barrier((across_y, across_x, second))
+    last = [across_y, across_x, swap(across_y), swap(across_x)]
+    out, sums = sum_blocks([first, second], near + middle + last, 2 * line.shape[0], bank)
+    return jnp.transpose(out, (1, 0, 2)), jnp.transpose(sums, (1, 0))
+
+
+def scratch_of(boxes, scored, blocks, orients, tail):
+    return [
+        pltpu.VMEM((boxes, F), jnp.bfloat16),
+        pltpu.VMEM((boxes, tail), jnp.bfloat16),
+        pltpu.VMEM((tail, scored), jnp.float32),
+        pltpu.VMEM((orients, scored), jnp.float32),
+        pltpu.VMEM((1, scored), jnp.float32),
+        pltpu.SemaphoreType.DMA((2 * blocks,)),
+    ]
+
+
+CLASSES = 5
+
+
+def bank_index():
+    return lax.axis_index("bank").astype(jnp.int32)[None]
+
+
+def weigh_blocks(blocks, bank):
+    classes, orients, width = bank.shape
+    boxes = sum(block.shape[0] for block in blocks)
+    tail = blocks[0].shape[1] - F
+    return pl.pallas_call(
+        functools.partial(weigh_kernel, blocks=len(blocks)),
+        grid=(classes // CLASSES,),
+        in_specs=[pl.BlockSpec(memory_space=pltpu.SMEM)]
+        + [pl.BlockSpec(memory_space=pl.ANY)] * len(blocks)
+        + [pl.BlockSpec((CLASSES, orients, width), lambda i: (i, 0, 0))],
+        out_specs=pl.BlockSpec((CLASSES, orients, boxes), lambda i: (i, 0, 0)),
+        out_shape=jax.ShapeDtypeStruct((classes, orients, boxes), jnp.bfloat16),
+        scratch_shapes=scratch_of(boxes, boxes, len(blocks), orients, tail),
+        compiler_params=pltpu.CompilerParams(vmem_limit_bytes=18 * MIB),
+        cost_estimate=pl.CostEstimate(
+            flops=2 * boxes * classes * orients * width,
+            bytes_accessed=2 * classes * orients * width,
+            transcendentals=0,
+        ),
+        name="weigh",
+    )(bank_index(), *blocks, bank)
+
+
+def sum_blocks(parts, blocks, late, bank):
+    classes, orients, width = bank.shape
+    boxes = sum(block.shape[0] for block in blocks)
+    tail = blocks[0].shape[1] - F
+    return pl.pallas_call(
+        functools.partial(sum_kernel, early=len(parts), blocks=len(blocks), late=late),
+        grid=(classes // CLASSES,),
+        in_specs=[pl.BlockSpec(memory_space=pltpu.SMEM)]
+        + [pl.BlockSpec((CLASSES, orients, part.shape[2]), lambda i: (i, 0, 0)) for part in parts]
+        + [pl.BlockSpec(memory_space=pl.ANY)] * len(blocks)
+        + [pl.BlockSpec((CLASSES, orients, width), lambda i: (i, 0, 0))],
         out_specs=[
-            pl.BlockSpec((group, local_rows, width), lambda i: (i, 0, 0)),
-            pl.BlockSpec((group, local_rows, 1), lambda i: (i, 0, 0)),
+            pl.BlockSpec((CLASSES, orients, width), lambda i: (i, 0, 0)),
+            pl.BlockSpec((classes, orients), lambda i: (0, 0)),
         ],
         out_shape=[
-            jax.ShapeDtypeStruct((classes, local_rows, width), jnp.float32),
-            jax.ShapeDtypeStruct((classes, local_rows, 1), jnp.float32),
+            jax.ShapeDtypeStruct((classes, orients, width), jnp.float32),
+            jax.ShapeDtypeStruct((classes, orients), jnp.float32),
         ],
-        scratch_shapes=[pltpu.VMEM((F, boxes), jnp.bfloat16)],
-        compiler_params=pltpu.CompilerParams(vmem_limit_bytes=LIMIT),
+        scratch_shapes=scratch_of(boxes, late, len(blocks), orients, tail),
+        compiler_params=pltpu.CompilerParams(vmem_limit_bytes=36 * MIB),
         cost_estimate=pl.CostEstimate(
-            flops=4 * boxes * classes * local_rows * width,
-            bytes_accessed=6 * classes * local_rows * width,
+            flops=2 * (boxes + late) * classes * orients * width,
+            bytes_accessed=6 * classes * orients * width,
             transcendentals=0,
         ),
-        name="score",
-    )(features, multiplicity.T, norm[None], jnp.transpose(reference_bank, (1, 0, 2)))
-    return jnp.transpose(out, (1, 0, 2)), jnp.transpose(sums[:, :, 0], (1, 0))
+        name="class_sums",
+    )(bank_index(), *parts, *blocks, bank)
 
 
 def body(volume, pick_list, box_counts, orientations, orient_weight, reference_bank):
@@ -354,7 +465,7 @@
         pl.BlockSpec((depth, 128), lambda i: (0, 0)),
         pl.BlockSpec((depth, 128), lambda i: (0, 0)),
     ]
-    params = pltpu.CompilerParams(vmem_limit_bytes=LIMIT)
+    params = pltpu.CompilerParams(vmem_limit_bytes=16 * MIB)
     near = pl.pallas_call(
         functools.partial(near_kernel, offset=HALF),
         grid=(wide // unit,),
@@ -412,7 +523,7 @@
         compiler_params=params,
         name="join",
     )(mid, from_after, from_before, multiplicity)
-    return score_local(gather_rows(mine), reference_bank)
+    return gather_score(mine, reference_bank)
 
 
 def solution(mesh):

time: 168 us -> 114 us (0.68)
  local copies, waits for them, and re-layouts: 55.2 us -> 7.26 us
  other arithmetic: 7.21 us -> 1.87 us
    concatenate x2 -> x0, local copies, waits for them, and re-layouts: 22.9 us -> none  [the longest x1 12.6 us: gather_rows(): return jnp.concatenate([line, other], axis=0)]
    ppermute x7 -> x0, local copies, waits for them, and re-layouts: 13.8 us -> none  [the longest x3 4.49 us: gather_rows(): lax.ppermute(mine, 'tile', [(i, (i + by) % tiles) for i in range(tiles)])]
    slice x4 -> x2, local copies, waits for them, and re-layouts: 12.4 us -> 0.04 us  [the longest x1 0.02 us: gather_score(): from_x[:half]]
    pallas_call x1 -> x3, Pallas kernels: 19.8 us -> 26.8 us  [the longest x1 17.5 us: sum_blocks(): pl.pallas_call(functools.partial(sum_kernel, early=len(parts), blocks=len...]
    unnamed x26 -> x24, local copies, waits for them, and re-layouts: 2.65 us -> 5.72 us
    pallas_call x1, Pallas kernels: 9.99 us -> 7.72 us  [body(): pl.pallas_call(functools.partial(far_kernel, half=half, gap=wide), grid=(...]
    pallas_call x1 -> x0, other arithmetic: 1.93 us -> none  [score_local(): pl.pallas_call(score_kernel, grid=(classes // group,), in_specs=[pl.Block...]
    pallas_call x1, Pallas kernels: 7.07 us -> 5.17 us  [body(): pl.pallas_call(functools.partial(near_kernel, offset=HALF), grid=(wide //...]
  transfers between devices with their start and end apart: 14 -> 18, of which waited for: 6 -> 10; matrix products, arithmetic and copies ran while one was open for 10% -> 2% of each run, Pallas kernels for 4% -> 13%
where the time goes in v2:
time: 114 us; the launch traced here: 113 us
  Pallas kernels  43 us (38%)
  starting transfers between devices  30.9 us (27%)
  waiting for transfers between devices  28.4 us (25%)
  local copies, waits for them, and re-layouts  7.26 us (6%)
  other arithmetic  1.87 us (2%)
  between operations  1.76 us (2%)
    ppermute x6, starting transfers between devices, shifted(): return lax.ppermute(value, axis, steps_of(axis, by))  17.9 us
    pallas_call x1, Pallas kernels, sum_blocks(): pl.pallas_call(functools.partial(sum_kernel, early=len(parts), blocks=len...  17.5 us
    ppermute x4, waiting for transfers between devices, along(): return lax.ppermute(value, 'bank', pairs)  12.7 us
    ppermute x3, waiting for transfers between devices, gather_score(): lax.ppermute(mine, 'tile', [(i, (i + by) % tiles) for i in range(tiles)])  10.6 us
    pallas_call x2, Pallas kernels, weigh_blocks(): pl.pallas_call(functools.partial(weigh_kernel, blocks=len(blocks)), grid=...  9.29 us
    pallas_call x1, Pallas kernels, body(): pl.pallas_call(functools.partial(far_kernel, half=half, gap=wide), grid=(...  7.72 us
    ppermute x4, starting transfers between devices, along(): return lax.ppermute(value, 'bank', pairs)  7.48 us
    unnamed x24, local copies, waits for them, and re-layouts  5.72 us
  transfers between devices with their start and end apart: 18, of which 10 were waited for; matrix products, arithmetic and copies ran while one was open for 2% of the time, Pallas kernels for 13%

profile of v2, /device:TPU:0, one launch (start us, length us, event | category | flops | bytes accessed | tf_op | source)
XLA Modules:
  0.0 113.1 jit_solution(305096984257262501)
XLA Ops:
  2.8 5.5 %collective-permute-start = (s32[3,16]{1,0:T(4,128)S(1)}, s32[3,16]{1,0:T(4,128)S(1)}, u32[]{:S(2)}, u32[]{:S(2)}) collective-permute-start(s32[3,16]{1,0:T(4,128)S(1)} %get-tuple-element.27), channel_id=1, source_target_pairs={{0,1},{1,2},{2,3},{4,5},{5,6},{6,7},{8,9},{9,10},{10,11},{12,13},{... | collective-permute-start | bytes 584 | tf_op jit(solution)/shard_map/ppermute | solution.py:325
  8.3 1.5 %fusion.10 = (bf16[48,64,128]{2,1,0:T(8,128)(2,1)S(1)}, bf16[48,64,128]{2,1,0:T(8,128)(2,1)S(1)}) fusion(bf16[64,64,128]{2,1,0:T(8,128)(2,1)} %volume_ref.1), kind=kLoop, calls=%fused_computation.24 | loop fusion | bytes 3145728 | tf_op jit(solution)/shard_map/slice | solution.py:442
  9.8 1.3 %collective-permute-start.3 = (bf16[48,64,128]{2,1,0:T(8,128)(2,1)S(1)}, bf16[48,64,128]{2,1,0:T(8,128)(2,1)S(1)}, u32[]{:S(2)}, u32[]{:S(2)}) collective-permute-start(bf16[48,64,128]{2,1,0:T(8,128)(2,1)S(1)} %get-tuple-element.24), channel_id=1, source_target_pairs={{4,0},{8,4},{12,8},{16,12},{20,16},{24,20},{28,24},{5,1},{9,5},{13... | collective-permute-start | bytes 2359304 | tf_op jit(solution)/shard_map/ppermute | solution.py:325
  11.1 3.1 %collective-permute-start.2 = (bf16[48,64,128]{2,1,0:T(8,128)(2,1)S(1)}, bf16[48,64,128]{2,1,0:T(8,128)(2,1)S(1)}, u32[]{:S(2)}, u32[]{:S(2)}) collective-permute-start(bf16[48,64,128]{2,1,0:T(8,128)(2,1)S(1)} %get-tuple-element.25), channel_id=1, source_target_pairs={{0,4},{4,8},{8,12},{12,16},{16,20},{20,24},{24,28},{1,5},{5,9},{9,... | collective-permute-start | bytes 2359304 | tf_op jit(solution)/shard_map/ppermute | solution.py:325
  15.9 2.8 %copy-done = bf16[304,10240]{1,0:T(8,128)(2,1)S(1)} copy-done((bf16[304,10240]{1,0:T(8,128)(2,1)S(1)}, bf16[304,10240]{1,0:T(8,128)(2,1)}, u32[]{:S(2)}) %copy-start) | copy-done | bytes 6225944
  18.6 5.2 %near_rows.1.near_ref = f32[304,768]{1,0:T(8,128)S(1)} custom-call(bf16[8,128]{1,0:T(8,128)(2,1)S(1)} %fusion.8.corners_ref, f32[128,128]{1,0:T(8,128)S(1)} %copy-done.4, f32[128,128]{1,0:T(8,128)S(1)} %copy-done.3, bf16[64,64,128]{2,1,0:T(8,128)(2,1)S(1)} %copy-done.2, bf16[304,10240]{1,0:T(8,128)(2,1)S(1)} %copy-done), custom_call_target="tpu_custom_call" | custom-call | flops 2717908992 | bytes 8000000 | tf_op jit(solution)/shard_map/near_rows/pallas_call | solution.py:469
  23.9 2.9 %copy-done.1 = bf16[304,10240]{1,0:T(8,128)(2,1)S(1)} copy-done((bf16[304,10240]{1,0:T(8,128)(2,1)S(1)}, bf16[304,10240]{1,0:T(8,128)(2,1)}, u32[]{:S(2)}) %copy-start.1) | copy-done | bytes 6225944
  26.8 7.7 %far_rows.1 = (bf16[256,256]{1,0:T(8,128)(2,1)S(1)}, f32[256,256]{1,0:T(8,128)S(1)}, bf16[256,256]{1,0:T(8,128)(2,1)S(1)}) custom-call(bf16[8,128]{1,0:T(8,128)(2,1)S(1)} %fusion.8.corners_ref, f32[128,128]{1,0:T(8,128)S(1)} %copy-done.4, f32[128,128]{1,0:T(8,128)S(1)} %copy-done.3, bf16[48,64,128]{2,1,0:T(8,128)(2,1)S(1)} %collective-permute-done.2.low_ref, ...), custom_call_target="tpu_custom_call" | custom-call | tf_op jit(solution)/shard_map/far_rows/pallas_call | solution.py:488
  35.8 5.5 %collective-permute-start.5 = (bf16[256,256]{1,0:T(8,128)(2,1)S(1)}, bf16[256,256]{1,0:T(8,128)(2,1)S(1)}, u32[]{:S(2)}, u32[]{:S(2)}) collective-permute-start(bf16[256,256]{1,0:T(8,128)(2,1)S(1)} %get-tuple-element.15), channel_id=1, source_target_pairs={{0,1},{1,2},{2,3},{4,5},{5,6},{6,7},{8,9},{9,10},{10,11},{12,13},{... | collective-permute-start | bytes 393224 | tf_op jit(solution)/shard_map/ppermute | solution.py:325
  41.3 2.0 %collective-permute-done.4.left_ref = bf16[256,256]{1,0:T(8,128)(2,1)S(1)} collective-permute-done((bf16[256,256]{1,0:T(8,128)(2,1)S(1)}, bf16[256,256]{1,0:T(8,128)(2,1)S(1)}, u32[]{:S(2)}, u32[]{:S(2)}) %collective-permute-start.4) | collective-permute-done | bytes 131104 | tf_op jit(solution)/shard_map/ppermute | solution.py:325
  43.3 1.7 %collective-permute-done.5.right_ref = bf16[256,256]{1,0:T(8,128)(2,1)S(1)} collective-permute-done((bf16[256,256]{1,0:T(8,128)(2,1)S(1)}, bf16[256,256]{1,0:T(8,128)(2,1)S(1)}, u32[]{:S(2)}, u32[]{:S(2)}) %collective-permute-start.5) | collective-permute-done | bytes 131104 | tf_op jit(solution)/shard_map/ppermute | solution.py:325
  44.9 3.3 %join.1 = bf16[16,4480]{1,0:T(8,128)(2,1)S(1)} custom-call(f32[256,256]{1,0:T(8,128)S(1)} %get-tuple-element.13.own_ref, bf16[256,256]{1,0:T(8,128)(2,1)S(1)} %collective-permute-done.4.left_ref, bf16[256,256]{1,0:T(8,128)(2,1)S(1)} %collective-permute-done.5.right_ref, bf16[16,256]{1,0:T(8,128)(2,1)S(1)} %select_convert_fusion.multiplicity_ref), custom_call_target="tpu_custom_call" | custom-call | tf_op jit(solution)/shard_map/join/pallas_call | solution.py:519
  48.3 3.5 %collective-permute-start.8 = (bf16[16,4480]{1,0:T(8,128)(2,1)S(1)}, bf16[16,4480]{1,0:T(8,128)(2,1)S(1)}, u32[]{:S(2)}, u32[]{:S(2)}) collective-permute-start(bf16[16,4480]{1,0:T(8,128)(2,1)S(1)} %join.1), channel_id=1, source_target_pairs={{0,24},{4,28},{8,0},{12,4},{16,8},{20,12},{24,16},{28,20},{1,25},{... | collective-permute-start | bytes 430088 | tf_op jit(solution)/shard_map/ppermute | solution.py:348
  51.7 1.5 %collective-permute-start.6 = (bf16[16,4480]{1,0:T(8,128)(2,1)S(1)}, bf16[16,4480]{1,0:T(8,128)(2,1)S(1)}, u32[]{:S(2)}, u32[]{:S(2)}) collective-permute-start(bf16[16,4480]{1,0:T(8,128)(2,1)S(1)} %join.1), channel_id=1, source_target_pairs={{0,8},{4,12},{8,16},{12,20},{16,24},{20,28},{24,0},{28,4},{1,9},{5... | collective-permute-start | bytes 430088 | tf_op jit(solution)/shard_map/ppermute | solution.py:348
  53.2 2.2 %collective-permute-done.8 = bf16[16,4480]{1,0:T(8,128)(2,1)S(1)} collective-permute-done((bf16[16,4480]{1,0:T(8,128)(2,1)S(1)}, bf16[16,4480]{1,0:T(8,128)(2,1)S(1)}, u32[]{:S(2)}, u32[]{:S(2)}) %collective-permute-start.8) | collective-permute-done | bytes 143392 | tf_op jit(solution)/shard_map/ppermute | solution.py:348
  55.5 8.3 %collective-permute-done.7 = bf16[16,4480]{1,0:T(8,128)(2,1)S(1)} collective-permute-done((bf16[16,4480]{1,0:T(8,128)(2,1)S(1)}, bf16[16,4480]{1,0:T(8,128)(2,1)S(1)}, u32[]{:S(2)}, u32[]{:S(2)}) %collective-permute-start.7) | collective-permute-done | bytes 143392 | tf_op jit(solution)/shard_map/ppermute | solution.py:348
  63.8 4.3 %collective-permute-start.10 = (bf16[64,4480]{1,0:T(8,128)(2,1)S(1)}, bf16[64,4480]{1,0:T(8,128)(2,1)S(1)}, u32[]{:S(2)}, u32[]{:S(2)}) collective-permute-start(bf16[64,4480]{1,0:T(8,128)(2,1)S(1)} %pad_maximum_fusion.refs_0_.refs_2_), channel_id=1, source_target_pairs={{0,2},{2,0},{1,3},{3,1},{4,6},{6,4},{5,7},{7,5},{8,10},{10,8},{9,1... | collective-permute-start | bytes 1720328 | tf_op jit(solution)/shard_map/ppermute | solution.py:339
  68.7 8.3 %collective-permute-done.10.refs_1_.refs_5_ = bf16[64,4480]{1,0:T(8,128)(2,1)S(1)} collective-permute-done((bf16[64,4480]{1,0:T(8,128)(2,1)S(1)}, bf16[64,4480]{1,0:T(8,128)(2,1)S(1)}, u32[]{:S(2)}, u32[]{:S(2)}) %collective-permute-start.10) | collective-permute-done | bytes 573472 | tf_op jit(solution)/shard_map/ppermute | solution.py:339
  77.0 2.6 %collective-permute-done.9.refs_0_.refs_4_ = bf16[64,4480]{1,0:T(8,128)(2,1)S(1)} collective-permute-done((bf16[64,4480]{1,0:T(8,128)(2,1)S(1)}, bf16[64,4480]{1,0:T(8,128)(2,1)S(1)}, u32[]{:S(2)}, u32[]{:S(2)}) %collective-permute-start.9) | collective-permute-done | bytes 573472 | tf_op jit(solution)/shard_map/ppermute | solution.py:339
  79.7 4.3 %weigh.2.refs_0_ = bf16[20,64,128]{2,1,0:T(8,128)(2,1)S(1)} custom-call(s32[1]{0:T(128)} %bitcast.index_ref, bf16[64,4480]{1,0:T(8,128)(2,1)S(1)} %pad_maximum_fusion.refs_0_.refs_2_, bf16[64,4480]{1,0:T(8,128)(2,1)S(1)} %collective-permute-done.11.refs_1_.refs_3_, bf16[20,64,4096]{2,1,0:T(8,128)(2,1)S(1)} %bitcast.17), custom_call_target="tpu_custom_call" | custom-call | flops 1342177280 | bytes 10485760 | tf_op jit(solution)/shard_map/weigh/pallas_call | solution.py:389
  84.5 2.2 %collective-permute-start.13 = (bf16[32,4480]{1,0:T(8,128)(2,1)S(1)}, bf16[32,4480]{1,0:T(8,128)(2,1)S(1)}, u32[]{:S(2)}, u32[]{:S(2)}) collective-permute-start(bf16[32,4480]{1,0:T(8,128)(2,1)S(1)} %slice.29), channel_id=1, source_target_pairs={{0,1},{1,0},{2,3},{3,2},{4,5},{5,4},{6,7},{7,6},{8,9},{9,8},{10,11... | collective-permute-start | bytes 860168 | tf_op jit(solution)/shard_map/ppermute | solution.py:339
  86.7 5.0 %weigh.3.refs_1_ = bf16[20,64,256]{2,1,0:T(8,128)(2,1)S(1)} custom-call(s32[1]{0:T(128)} %bitcast.index_ref, bf16[64,4480]{1,0:T(8,128)(2,1)S(1)} %collective-permute-done.9.refs_0_.refs_4_, bf16[64,4480]{1,0:T(8,128)(2,1)S(1)} %collective-permute-done.10.refs_1_.refs_5_, bf16[64,4480]{1,0:T(8,128)(2,1)S(1)} %collective-permute-done.14.refs_2_.refs_6_, ...), custom_call_target="tpu_custom_call" | custom-call | flops 2684354560 | bytes 10485760 | tf_op jit(solution)/shard_map/weigh/pallas_call | solution.py:389
  91.7 1.7 %collective-permute-done.12.refs_8_ = bf16[32,4480]{1,0:T(8,128)(2,1)S(1)} collective-permute-done((bf16[32,4480]{1,0:T(8,128)(2,1)S(1)}, bf16[32,4480]{1,0:T(8,128)(2,1)S(1)}, u32[]{:S(2)}, u32[]{:S(2)}) %collective-permute-start.12) | collective-permute-done | bytes 286752 | tf_op jit(solution)/shard_map/ppermute | solution.py:339
  95.5 17.5 %class_sums.1 = (f32[20,64,4096]{2,1,0:T(8,128)}, f32[20,64]{1,0:T(8,128)}) custom-call(s32[1]{0:T(128)} %bitcast.index_ref, bf16[20,64,128]{2,1,0:T(8,128)(2,1)S(1)} %weigh.2.refs_0_, bf16[20,64,256]{2,1,0:T(8,128)(2,1)S(1)} %weigh.3.refs_1_, bf16[64,4480]{1,0:T(8,128)(2,1)S(1)} %pad_maximum_fusion.refs_0_.refs_2_, ...), custom_call_target="tpu_custom_call" | custom-call | flops 6710886400 | bytes 31457280 | tf_op jit(solution)/shard_map/class_sums/pallas_call | solution.py:412
  (56 shorter events, 7.7 us)
Async XLA Ops:
  0.7 15.2 %copy-start.3 = (f32[128,128]{1,0:T(8,128)S(1)}, f32[128,128]{1,0:T(8,128)}, u32[]{:S(2)}) copy-start(f32[128,128]{1,0:T(8,128)} %constant.30.clone.second_ref) | copy-start | bytes 196612
  0.7 15.2 %copy-start.4 = (f32[128,128]{1,0:T(8,128)S(1)}, f32[128,128]{1,0:T(8,128)}, u32[]{:S(2)}) copy-start(f32[128,128]{1,0:T(8,128)} %constant.29.clone.first_ref) | copy-start | bytes 196612
  0.7 15.2 %copy-start.2 = (bf16[64,64,128]{2,1,0:T(8,128)(2,1)S(1)}, bf16[64,64,128]{2,1,0:T(8,128)(2,1)}, u32[]{:S(2)}) copy-start(bf16[64,64,128]{2,1,0:T(8,128)(2,1)} %volume_ref.1) | copy-start | bytes 3145732
  1.5 14.1 %collective-permute-start.1 = (s32[3,16]{1,0:T(4,128)S(1)}, s32[3,16]{1,0:T(4,128)S(1)}, u32[]{:S(2)}, u32[]{:S(2)}) collective-permute-start(s32[3,16]{1,0:T(4,128)S(1)} %get-tuple-element.27), channel_id=1, source_target_pairs={{1,0},{2,1},{3,2},{5,4},{6,5},{7,6},{9,8},{10,9},{11,10},{13,12},{... | collective-permute-start | bytes 584 | tf_op jit(solution)/shard_map/ppermute | solution.py:325
  2.8 12.9 %collective-permute-start = (s32[3,16]{1,0:T(4,128)S(1)}, s32[3,16]{1,0:T(4,128)S(1)}, u32[]{:S(2)}, u32[]{:S(2)}) collective-permute-start(s32[3,16]{1,0:T(4,128)S(1)} %get-tuple-element.27), channel_id=1, source_target_pairs={{0,1},{1,2},{2,3},{4,5},{5,6},{6,7},{8,9},{9,10},{10,11},{12,13},{... | collective-permute-start | bytes 584 | tf_op jit(solution)/shard_map/ppermute | solution.py:325
  9.8 14.0 %collective-permute-start.3 = (bf16[48,64,128]{2,1,0:T(8,128)(2,1)S(1)}, bf16[48,64,128]{2,1,0:T(8,128)(2,1)S(1)}, u32[]{:S(2)}, u32[]{:S(2)}) collective-permute-start(bf16[48,64,128]{2,1,0:T(8,128)(2,1)S(1)} %get-tuple-element.24), channel_id=1, source_target_pairs={{4,0},{8,4},{12,8},{16,12},{20,16},{24,20},{28,24},{5,1},{9,5},{13... | collective-permute-start | bytes 2359304 | tf_op jit(solution)/shard_map/ppermute | solution.py:325
  11.1 12.7 %collective-permute-start.2 = (bf16[48,64,128]{2,1,0:T(8,128)(2,1)S(1)}, bf16[48,64,128]{2,1,0:T(8,128)(2,1)S(1)}, u32[]{:S(2)}, u32[]{:S(2)}) collective-permute-start(bf16[48,64,128]{2,1,0:T(8,128)(2,1)S(1)} %get-tuple-element.25), channel_id=1, source_target_pairs={{0,4},{4,8},{8,12},{12,16},{16,20},{20,24},{24,28},{1,5},{5,9},{9,... | collective-permute-start | bytes 2359304 | tf_op jit(solution)/shard_map/ppermute | solution.py:325
  18.6 61.1 %slice-start = ((s8[10485760]{0:T(1024)(128)(4,1)}), s8[4194304]{0:T(1024)(128)(4,1)S(1)}, s32[]{:S(2)}) async-start(s8[10485760]{0:T(1024)(128)(4,1)} %bitcast.15), calls=%async_computation | async-start | bytes 8388608
  18.6 61.1 %slice-start.1 = ((s8[10485760]{0:T(1024)(128)(4,1)}), s8[4194304]{0:T(1024)(128)(4,1)S(1)}, s32[]{:S(2)}) async-start(s8[10485760]{0:T(1024)(128)(4,1)} %bitcast.15), calls=%async_computation.1 | async-start | bytes 8388608
  23.8 55.9 %slice-start.2 = ((s8[10485760]{0:T(1024)(128)(4,1)}), s8[2097152]{0:T(1024)(128)(4,1)S(1)}, s32[]{:S(2)}) async-start(s8[10485760]{0:T(1024)(128)(4,1)} %bitcast.15), calls=%async_computation.2 | async-start | bytes 4194304
  34.5 8.8 %collective-permute-start.4 = (bf16[256,256]{1,0:T(8,128)(2,1)S(1)}, bf16[256,256]{1,0:T(8,128)(2,1)S(1)}, u32[]{:S(2)}, u32[]{:S(2)}) collective-permute-start(bf16[256,256]{1,0:T(8,128)(2,1)S(1)} %get-tuple-element.14), channel_id=1, source_target_pairs={{1,0},{2,1},{3,2},{5,4},{6,5},{7,6},{9,8},{10,9},{11,10},{13,12},{... | collective-permute-start | bytes 393224 | tf_op jit(solution)/shard_map/ppermute | solution.py:325
  35.8 9.2 %collective-permute-start.5 = (bf16[256,256]{1,0:T(8,128)(2,1)S(1)}, bf16[256,256]{1,0:T(8,128)(2,1)S(1)}, u32[]{:S(2)}, u32[]{:S(2)}) collective-permute-start(bf16[256,256]{1,0:T(8,128)(2,1)S(1)} %get-tuple-element.15), channel_id=1, source_target_pairs={{0,1},{1,2},{2,3},{4,5},{5,6},{6,7},{8,9},{9,10},{10,11},{12,13},{... | collective-permute-start | bytes 393224 | tf_op jit(solution)/shard_map/ppermute | solution.py:325
  48.3 7.2 %collective-permute-start.8 = (bf16[16,4480]{1,0:T(8,128)(2,1)S(1)}, bf16[16,4480]{1,0:T(8,128)(2,1)S(1)}, u32[]{:S(2)}, u32[]{:S(2)}) collective-permute-start(bf16[16,4480]{1,0:T(8,128)(2,1)S(1)} %join.1), channel_id=1, source_target_pairs={{0,24},{4,28},{8,0},{12,4},{16,8},{20,12},{24,16},{28,20},{1,25},{... | collective-permute-start | bytes 430088 | tf_op jit(solution)/shard_map/ppermute | solution.py:348
  51.7 12.1 %collective-permute-start.7 = (bf16[16,4480]{1,0:T(8,128)(2,1)S(1)}, bf16[16,4480]{1,0:T(8,128)(2,1)S(1)}, u32[]{:S(2)}, u32[]{:S(2)}) collective-permute-start(bf16[16,4480]{1,0:T(8,128)(2,1)S(1)} %join.1), channel_id=1, source_target_pairs={{0,16},{4,20},{8,24},{12,28},{16,0},{20,4},{24,8},{28,12},{1,17},{... | collective-permute-start | bytes 430088 | tf_op jit(solution)/shard_map/ppermute | solution.py:348
  51.7 12.1 %collective-permute-start.6 = (bf16[16,4480]{1,0:T(8,128)(2,1)S(1)}, bf16[16,4480]{1,0:T(8,128)(2,1)S(1)}, u32[]{:S(2)}, u32[]{:S(2)}) collective-permute-start(bf16[16,4480]{1,0:T(8,128)(2,1)S(1)} %join.1), channel_id=1, source_target_pairs={{0,8},{4,12},{8,16},{12,20},{16,24},{20,28},{24,0},{28,4},{1,9},{5... | collective-permute-start | bytes 430088 | tf_op jit(solution)/shard_map/ppermute | solution.py:348
  63.8 13.2 %collective-permute-start.10 = (bf16[64,4480]{1,0:T(8,128)(2,1)S(1)}, bf16[64,4480]{1,0:T(8,128)(2,1)S(1)}, u32[]{:S(2)}, u32[]{:S(2)}) collective-permute-start(bf16[64,4480]{1,0:T(8,128)(2,1)S(1)} %pad_maximum_fusion.refs_0_.refs_2_), channel_id=1, source_target_pairs={{0,2},{2,0},{1,3},{3,1},{4,6},{6,4},{5,7},{7,5},{8,10},{10,8},{9,1... | collective-permute-start | bytes 1720328 | tf_op jit(solution)/shard_map/ppermute | solution.py:339
  68.1 11.5 %collective-permute-start.9 = (bf16[64,4480]{1,0:T(8,128)(2,1)S(1)}, bf16[64,4480]{1,0:T(8,128)(2,1)S(1)}, u32[]{:S(2)}, u32[]{:S(2)}) collective-permute-start(bf16[64,4480]{1,0:T(8,128)(2,1)S(1)} %pad_maximum_fusion.refs_0_.refs_2_), channel_id=1, source_target_pairs={{0,1},{1,0},{2,3},{3,2},{4,5},{5,4},{6,7},{7,6},{8,9},{9,8},{10,11... | collective-permute-start | bytes 1720328 | tf_op jit(solution)/shard_map/ppermute | solution.py:339
  68.7 11.0 %collective-permute-start.11 = (bf16[64,4480]{1,0:T(8,128)(2,1)S(1)}, bf16[64,4480]{1,0:T(8,128)(2,1)S(1)}, u32[]{:S(2)}, u32[]{:S(2)}) collective-permute-start(bf16[64,4480]{1,0:T(8,128)(2,1)S(1)} %pad_maximum_fusion.refs_0_.refs_2_), channel_id=1, source_target_pairs={{0,4},{4,0},{8,12},{12,8},{16,20},{20,16},{24,28},{28,24},{1,5},{5... | collective-permute-start | bytes 1720328 | tf_op jit(solution)/shard_map/ppermute | solution.py:342
  77.0 9.7 %collective-permute-start.15 = (bf16[64,4480]{1,0:T(8,128)(2,1)S(1)}, bf16[64,4480]{1,0:T(8,128)(2,1)S(1)}, u32[]{:S(2)}, u32[]{:S(2)}) collective-permute-start(bf16[64,4480]{1,0:T(8,128)(2,1)S(1)} %collective-permute-done.10.refs_1_.refs_5_), channel_id=1, source_target_pairs={{0,4},{4,0},{8,12},{12,8},{16,20},{20,16},{24,28},{28,24},{1,5},{5... | collective-permute-start | bytes 1720328 | tf_op jit(solution)/shard_map/ppermute | solution.py:342
  79.6 7.1 %collective-permute-start.14 = (bf16[64,4480]{1,0:T(8,128)(2,1)S(1)}, bf16[64,4480]{1,0:T(8,128)(2,1)S(1)}, u32[]{:S(2)}, u32[]{:S(2)}) collective-permute-start(bf16[64,4480]{1,0:T(8,128)(2,1)S(1)} %collective-permute-done.9.refs_0_.refs_4_), channel_id=1, source_target_pairs={{0,4},{4,0},{8,12},{12,8},{16,20},{20,16},{24,28},{28,24},{1,5},{5... | collective-permute-start | bytes 1720328 | tf_op jit(solution)/shard_map/ppermute | solution.py:342
  84.1 9.3 %collective-permute-start.12 = (bf16[32,4480]{1,0:T(8,128)(2,1)S(1)}, bf16[32,4480]{1,0:T(8,128)(2,1)S(1)}, u32[]{:S(2)}, u32[]{:S(2)}) collective-permute-start(bf16[32,4480]{1,0:T(8,128)(2,1)S(1)} %slice.28), channel_id=1, source_target_pairs={{0,2},{2,0},{1,3},{3,1},{4,6},{6,4},{5,7},{7,5},{8,10},{10,8},{9,1... | collective-permute-start | bytes 860168 | tf_op jit(solution)/shard_map/ppermute | solution.py:339
  84.5 9.0 %collective-permute-start.13 = (bf16[32,4480]{1,0:T(8,128)(2,1)S(1)}, bf16[32,4480]{1,0:T(8,128)(2,1)S(1)}, u32[]{:S(2)}, u32[]{:S(2)}) collective-permute-start(bf16[32,4480]{1,0:T(8,128)(2,1)S(1)} %slice.29), channel_id=1, source_target_pairs={{0,1},{1,0},{2,3},{3,2},{4,5},{5,4},{6,7},{7,6},{8,9},{9,8},{10,11... | collective-permute-start | bytes 860168 | tf_op jit(solution)/shard_map/ppermute | solution.py:339
  93.5 1.6 %collective-permute-start.16 = (bf16[32,4480]{1,0:T(8,128)(2,1)S(1)}, bf16[32,4480]{1,0:T(8,128)(2,1)S(1)}, u32[]{:S(2)}, u32[]{:S(2)}) collective-permute-start(bf16[32,4480]{1,0:T(8,128)(2,1)S(1)} %collective-permute-done.12.refs_8_), channel_id=1, source_target_pairs={{0,4},{4,0},{8,12},{12,8},{16,20},{20,16},{24,28},{28,24},{1,5},{5... | collective-permute-start | bytes 860168 | tf_op jit(solution)/shard_map/ppermute | solution.py:342
  93.5 2.0 %collective-permute-start.17 = (bf16[32,4480]{1,0:T(8,128)(2,1)S(1)}, bf16[32,4480]{1,0:T(8,128)(2,1)S(1)}, u32[]{:S(2)}, u32[]{:S(2)}) collective-permute-start(bf16[32,4480]{1,0:T(8,128)(2,1)S(1)} %collective-permute-done.13.refs_9_), channel_id=1, source_target_pairs={{0,4},{4,0},{8,12},{12,8},{16,20},{20,16},{24,28},{28,24},{1,5},{5... | collective-permute-start | bytes 860168 | tf_op jit(solution)/shard_map/ppermute | solution.py:342
  (6 other events, 64.0 us)

commit v3 on v2

--- a/solution.py
+++ b/solution.py
@@ -47,12 +47,21 @@
     return np.concatenate([rows, np.zeros((pad, rows.shape[1]))], axis=0).astype(np.float32)
 
 
-def spread(corners, lanes):
-    boxes = corners.shape[1]
-    box = lax.broadcasted_iota(jnp.int32, (boxes, lanes), 0)
-    lane = lax.broadcasted_iota(jnp.int32, (boxes, lanes), 1)
-    pick = jnp.where(lane // L == box, 1.0, 0.0).astype(jnp.bfloat16)
-    return jnp.dot(corners, pick, preferred_element_type=jnp.float32)
+def spread(origin_ref, corner_refs, lanes):
+    slots = corner_refs[0].shape[3]
+    box = lax.broadcasted_iota(jnp.int32, (slots, lanes), 0)
+    lane = lax.broadcasted_iota(jnp.int32, (slots, lanes), 1)
+    row = lax.broadcasted_iota(jnp.int32, (8, slots), 0)
+    origin = jnp.where(row == 0, origin_ref[0], jnp.where(row == 1, origin_ref[1], 0))
+    total = jnp.zeros((8, lanes), jnp.float32)
+    for k, corner_ref in enumerate(corner_refs):
+        corners = jnp.zeros((8, slots), jnp.int32)
+        for axis in range(3):
+            corners = jnp.where(row == axis, corner_ref[axis, 0], corners)
+        corners = (corners - origin).astype(jnp.float32).astype(jnp.bfloat16)
+        pick = jnp.where(lane // L == box + k * slots, 1.0, 0.0).astype(jnp.bfloat16)
+        total += jnp.dot(corners, pick, preferred_element_type=jnp.float32)
+    return total
 
 
 def turns(terms, shift):
@@ -62,9 +71,9 @@
     return jnp.cos(angle), jnp.sin(angle)
 
 
-def prepare(corners_ref, first_ref, second_ref, depth_ref, high_ref):
+def prepare(origin_ref, corner_refs, first_ref, second_ref, depth_ref, high_ref):
     depth, lanes = depth_ref.shape
-    where = spread(corners_ref[...], lanes)
+    where = spread(origin_ref, corner_refs, lanes)
     start_y, start_z = where[1:2], where[2:3]
     lane = lax.rem(lax.broadcasted_iota(jnp.int32, (1, lanes), 1), L)
     term = jnp.where(lane <= TERMS, lane, lane - TERMS).astype(jnp.float32)
@@ -80,41 +89,67 @@
     return where[0:1]
 
 
-def add_rows(voxels, base, start_x, depth_ref, high_ref, part_ref, plane):
+def block_modes(voxels, at_x, turn, start_x, depth_ref, high_ref, part_ref, plane_ref):
     count, high, depth = voxels.shape
+    offset = at_x - start_x
     for x in range(0, count, 4):
         rows = voxels[x : x + 4].reshape(4 * high, depth)
         first = jnp.dot(rows, depth_ref[...], preferred_element_type=jnp.float32)
         for i in range(4):
-            at = (base + (x + i)).astype(jnp.float32) - start_x
+            at = offset + float(x + i)
             live = high_ref[...] * jnp.where((at >= 0) & (at < B), 1.0, 0.0)
             kept = first[i * high : (i + 1) * high] * live
             part_ref[pl.ds((x + i) * high, high), :] = kept.astype(jnp.bfloat16)
-    return jnp.dot(plane, part_ref[...], preferred_element_type=jnp.float32)
+    length = count * high
+    total = jnp.dot(
+        plane_ref[:, :length], part_ref[:length], preferred_element_type=jnp.float32
+    )
+    return total if turn is None else moved(total, turn)
+
+
+def turn_of(at_x):
+    angles = 2.0 * np.pi * np.arange(1, TERMS + 1) * at_x / B
+    return [float(c) for c in np.cos(angles)], [float(s) for s in np.sin(angles)]
+
+
+def either(flag, one, other):
+    return tuple([jnp.where(flag, a, b) for a, b in zip(u, v)] for u, v in zip(one, other))
+
+
+def moved(total, turn):
+    group, blocks = 2 * TERMS, 2 * TERMS + 1
+    rows = [total[a * group : (a + 1) * group] for a in range(blocks)]
+    main = blocks * group
+    flat_cos, flat_sin = total[main : main + TERMS], total[main + TERMS : main + group]
+    out = list(rows)
+    term = lax.broadcasted_iota(jnp.int32, flat_cos.shape, 0)
+    flat_c, flat_s = jnp.zeros_like(flat_cos), jnp.zeros_like(flat_cos)
+    for j, (c, s) in enumerate(zip(*turn)):
+        out[1 + j] = rows[1 + j] * c - rows[1 + TERMS + j] * s
+        out[1 + TERMS + j] = rows[1 + j] * s + rows[1 + TERMS + j] * c
+        flat_c = jnp.where(term == j, c, flat_c)
+        flat_s = jnp.where(term == j, s, flat_s)
+    out += [
+        flat_cos * flat_c - flat_sin * flat_s,
+        flat_cos * flat_s + flat_sin * flat_c,
+        total[main + group :],
+    ]
+    return jnp.concatenate(out, axis=0)
 
 
 def near_kernel(
-    corners_ref, first_ref, second_ref, volume_ref, plane_ref, total_ref,
-    depth_ref, high_ref, start_ref, part_ref, *, offset,
+    origin_ref, first_pick_ref, pick_ref, second_pick_ref, first_ref, second_ref, volume_ref, plane_ref,
+    total_ref, depth_ref, high_ref, part_ref,
 ):
-    step = pl.program_id(0)
-
-    @pl.when(step == 0)
-    def _():
-        start_ref[...] = prepare(corners_ref, first_ref, second_ref, depth_ref, high_ref)
-
-    base = offset + step * volume_ref.shape[0]
-    added = add_rows(
-        volume_ref[...], base, start_ref[...], depth_ref, high_ref, part_ref, plane_ref[...]
-    )
-
-    @pl.when(step == 0)
-    def _():
-        total_ref[...] = added
-
-    @pl.when(step > 0)
-    def _():
-        total_ref[...] += added
+    corner_refs = (first_pick_ref, pick_ref, second_pick_ref)
+    start_x = prepare(origin_ref, corner_refs, first_ref, second_ref, depth_ref, high_ref)
+    unit = part_ref.shape[0] // volume_ref.shape[1]
+    for x in range(0, volume_ref.shape[0], unit):
+        added = block_modes(
+            volume_ref[x : x + unit], float(x), turn_of(x) if x else None, start_x,
+            depth_ref, high_ref, part_ref, plane_ref,
+        )
+        total_ref[...] = added if x == 0 else total_ref[...] + added
 
 
 def rotate(total, start_x, start_y):
@@ -152,32 +187,29 @@
 
 
 def far_kernel(
-    corners_ref, first_ref, second_ref, low_ref, high_voxels_ref, plane_ref, near_ref,
-    left_ref, own_ref, right_ref,
-    depth_ref, high_ref, start_ref, part_ref, total_ref, *, half, gap,
+    origin_ref, first_pick_ref, pick_ref, second_pick_ref, first_ref, second_ref, first_halo_ref, second_halo_ref, plane_ref,
+    near_ref, first_out_ref, own_ref, second_out_ref, depth_ref, high_ref, part_ref, total_ref, *, wide,
 ):
-    step = pl.program_id(0)
-
-    @pl.when(step == 0)
-    def _():
-        start_ref[...] = prepare(corners_ref, first_ref, second_ref, depth_ref, high_ref)
-        total_ref[...] = near_ref[...]
-
-    count = low_ref.shape[0]
-    base = step * count + jnp.where(step < half, 0, gap)
-    voxels = jnp.where(step < half, low_ref[...], high_voxels_ref[...])
-    total_ref[...] += add_rows(
-        voxels, base, start_ref[...], depth_ref, high_ref, part_ref, plane_ref[...]
-    )
-
-    @pl.when(step == 2 * half - 1)
-    def _():
-        where = spread(corners_ref[...], total_ref.shape[1])
-        rows = rotate(total_ref[...], where[0:1], where[1:2])
-        width = left_ref.shape[1]
-        left_ref[...] = rows[:, :width].astype(jnp.bfloat16)
-        own_ref[...] = rows[:, width : 2 * width]
-        right_ref[...] = rows[:, 2 * width :].astype(jnp.bfloat16)
+    corner_refs = (first_pick_ref, pick_ref, second_pick_ref)
+    start_x = prepare(origin_ref, corner_refs, first_ref, second_ref, depth_ref, high_ref)
+    where = spread(origin_ref, corner_refs, total_ref.shape[1])
+    total_ref[...] = near_ref[...]
+    even = origin_ref[2] == 0
+    below, above = turn_of(-HALF), turn_of(wide)
+    sides = (
+        (first_halo_ref, jnp.where(even, wide, -HALF), either(even, above, below)),
+        (second_halo_ref, jnp.where(even, -HALF, wide), either(even, below, above)),
+    )
+    for voxels_ref, at_x, turn in sides:
+        total_ref[...] += block_modes(
+            voxels_ref[...], at_x.astype(jnp.float32), turn, start_x,
+            depth_ref, high_ref, part_ref, plane_ref,
+        )
+    rows = rotate(total_ref[...], start_x, where[1:2])
+    width = own_ref.shape[1]
+    first_out_ref[...] = rows[:, :width].astype(jnp.bfloat16)
+    own_ref[...] = rows[:, width : 2 * width]
+    second_out_ref[...] = rows[:, 2 * width :].astype(jnp.bfloat16)
 
 
 def join_kernel(own_ref, left_ref, right_ref, multiplicity_ref, out_ref, wide_ref):
@@ -316,19 +348,18 @@
     return class_sums, jnp.sum(weights.astype(jnp.float32), axis=0)
 
 
-def steps_of(axis, by):
+def exchange(value, axis, first):
     count = lax.axis_size(axis)
-    return [(i, i + by) for i in range(count) if 0 <= i + by < count]
-
-
-def shifted(value, axis, by):
-    return lax.ppermute(value, axis, steps_of(axis, by))
+    pairs = []
+    for i in range(0 if first else 1, count - 1, 2):
+        pairs += [(i, i + 1), (i + 1, i)]
+    return lax.ppermute(value, axis, pairs)
 
 
 def gather_score(mine, reference_bank):
     tiles, banks = lax.axis_size("tile"), lax.axis_size("bank")
     local_rows, classes, width = reference_bank.shape
-    if banks != 4 or tiles % 2 or tiles * banks * mine.shape[0] > 1024 or classes % 5:
+    if banks != 4 or tiles & (tiles - 1) or tiles < 2 or tiles * banks * mine.shape[0] > 1024 or classes % 5:
         return score_plain(
             lax.all_gather(lax.all_gather(mine, "bank", axis=0, tiled=True), "tile", axis=0, tiled=True),
             reference_bank,
@@ -345,7 +376,7 @@
     line = jnp.concatenate(
         [mine]
         + [
-            lax.ppermute(mine, "tile", [(i, (i + by) % tiles) for i in range(tiles)])
+            lax.ppermute(mine, "tile", [(i, i ^ by) for i in range(tiles)])
             for by in range(2, tiles, 2)
         ],
         axis=0,
@@ -354,8 +385,8 @@
     from_x, from_y = along(line, x_pairs), along(line, y_pairs)
     near = [line, swap(line)]
     first = weigh_blocks(near, bank)
-    part_x, part_y, first = lax.optimization_barrier((from_x[:half], from_y[half:], first))
-    across_y, across_x = along(part_x, y_pairs), along(part_y, x_pairs)
+    from_x, from_y, first = lax.optimization_barrier((from_x, from_y, first))
+    across_y, across_x = along(from_x[:half], y_pairs), along(from_y[half:], x_pairs)
     middle = [from_x, from_y, swap(from_x), swap(from_y)]
     second = weigh_blocks(middle, bank)
     across_y, across_x, second = lax.optimization_barrier((across_y, across_x, second))
@@ -438,77 +469,60 @@
 def body(volume, pick_list, box_counts, orientations, orient_weight, reference_bank):
     wide, high, depth = volume.shape
     slots = pick_list.shape[3]
-    low = shifted(volume[wide - HALF :], "tile", 1)
-    top = shifted(volume[:HALF], "tile", -1)
-
-    corner_x = pick_list[0, 0, 0] - lax.axis_index("tile") * wide
-    corner_y = pick_list[1, 0, 0] - lax.axis_index("bank") * high - HALF
-    own = jnp.stack([corner_x, corner_y, pick_list[2, 0, 0]])
-    before = shifted(own, "bank", 1)
-    after = shifted(own, "bank", -1)
-    step = jnp.array([0, high, 0], jnp.int32)[:, None]
-    corners = jnp.concatenate([before - step, own, after + step], axis=1)
-    corners = jnp.pad(corners, ((0, 5), (0, 128 - 3 * slots))).astype(jnp.bfloat16)
+    tile, bank = lax.axis_index("tile"), lax.axis_index("bank")
+    side = lax.rem(tile, 2)
+    upper, lower = volume[wide - HALF :], volume[:HALF]
+    to_first = jnp.where(side == 0, upper, lower)
+    to_second = jnp.where(side == 0, lower, upper)
+    to_first, to_second, picks = lax.optimization_barrier((to_first, to_second, pick_list))
+    first_halo = exchange(to_first, "tile", True)
+    second_halo = exchange(to_second, "tile", False)
+    first_picks, second_picks = exchange(picks, "bank", True), exchange(picks, "bank", False)
+    origin = jnp.stack([tile * wide + HALF, bank * high + HALF, side]).astype(jnp.int32)
 
     first, second = depth_tables(depth)
-    plane = jnp.asarray(plane_table(wide + 2 * HALF, high), jnp.bfloat16)
+    plane = jnp.asarray(plane_table(HALF, high), jnp.bfloat16)
     modes, lanes = plane.shape[0], 3 * slots * L
-    unit = 16
-    scratch = [
-        pltpu.VMEM((depth, lanes), jnp.bfloat16),
-        pltpu.VMEM((high, lanes), jnp.float32),
-        pltpu.VMEM((1, lanes), jnp.float32),
-        pltpu.VMEM((unit * high, lanes), jnp.bfloat16),
-    ]
-    whole = [
-        pl.BlockSpec((8, 128), lambda i: (0, 0)),
-        pl.BlockSpec((depth, 128), lambda i: (0, 0)),
-        pl.BlockSpec((depth, 128), lambda i: (0, 0)),
-    ]
-    params = pltpu.CompilerParams(vmem_limit_bytes=16 * MIB)
+    unit = 32
+
+    def scratch(count):
+        return [
+            pltpu.VMEM((depth, lanes), jnp.bfloat16),
+            pltpu.VMEM((high, lanes), jnp.float32),
+            pltpu.VMEM((count * high, lanes), jnp.bfloat16),
+        ]
+
+    params = pltpu.CompilerParams(vmem_limit_bytes=24 * MIB)
+    vmem = pl.BlockSpec(memory_space=pltpu.VMEM)
+    given = [pl.BlockSpec(memory_space=pltpu.SMEM)] + [vmem] * 5
     near = pl.pallas_call(
-        functools.partial(near_kernel, offset=HALF),
-        grid=(wide // unit,),
-        in_specs=whole
-        + [
-            pl.BlockSpec((unit, high, depth), lambda i: (i, 0, 0)),
-            pl.BlockSpec((modes, unit * high), lambda i: (0, HALF // unit + i)),
-        ],
-        out_specs=pl.BlockSpec((modes, lanes), lambda i: (0, 0)),
+        near_kernel,
+        in_specs=given + [vmem] * 2,
+        out_specs=vmem,
         out_shape=jax.ShapeDtypeStruct((modes, lanes), jnp.float32),
-        scratch_shapes=scratch,
+        scratch_shapes=scratch(unit),
         compiler_params=params,
         cost_estimate=pl.CostEstimate(
             flops=2 * wide * high * lanes * (depth + modes), bytes_accessed=8000000, transcendentals=0
         ),
         name="near_rows",
-    )(corners, first, second, volume, plane)
-    half = HALF // unit
-    skip = wide // unit
-    left, mid, right = pl.pallas_call(
-        functools.partial(far_kernel, half=half, gap=wide),
-        grid=(2 * half,),
-        in_specs=whole
-        + [
-            pl.BlockSpec((unit, high, depth), lambda i: (jnp.minimum(i, half - 1), 0, 0)),
-            pl.BlockSpec((unit, high, depth), lambda i: (jnp.maximum(i - half, 0), 0, 0)),
-            pl.BlockSpec(
-                (modes, unit * high), lambda i: (0, jnp.where(i < half, i, i + skip))
-            ),
-            pl.BlockSpec((modes, lanes), lambda i: (0, 0)),
-        ],
-        out_specs=[pl.BlockSpec((L * L, slots * L), lambda i: (0, 0))] * 3,
+    )(origin, first_picks, picks, second_picks, first, second, volume, plane)
+    for_first, mid, for_second = pl.pallas_call(
+        functools.partial(far_kernel, wide=wide),
+        in_specs=given + [vmem] * 4,
+        out_specs=[vmem] * 3,
         out_shape=[
             jax.ShapeDtypeStruct((L * L, slots * L), jnp.bfloat16),
             jax.ShapeDtypeStruct((L * L, slots * L), jnp.float32),
             jax.ShapeDtypeStruct((L * L, slots * L), jnp.bfloat16),
         ],
-        scratch_shapes=scratch + [pltpu.VMEM((modes, lanes), jnp.float32)],
+        scratch_shapes=scratch(HALF) + [pltpu.VMEM((modes, lanes), jnp.float32)],
         compiler_params=params,
         name="far_rows",
-    )(corners, first, second, low, top, plane, near)
-    from_after = shifted(left, "bank", -1)
-    from_before = shifted(right, "bank", 1)
+    )(
+        origin, first_picks, picks, second_picks, first, second, first_halo, second_halo, plane, near
+    )
+    from_first, from_second = exchange(for_first, "bank", True), exchange(for_second, "bank", False)
 
     live_slots = jnp.arange(slots) < box_counts[0, 0]
     matches = orientations[0, 0][:, :, None] == jnp.arange(R)[None, None, :]
@@ -522,7 +536,7 @@
         scratch_shapes=[pltpu.VMEM((slots, F), jnp.float32)],
         compiler_params=params,
         name="join",
-    )(mid, from_after, from_before, multiplicity)
+    )(mid, from_first, from_second, multiplicity)
     return gather_score(mine, reference_bank)
 
 

time: 114 us -> 105 us (0.921)
  starting transfers between devices: 30.9 us -> 25 us
  local copies, waits for them, and re-layouts: 7.26 us -> 3.35 us
  other arithmetic: 1.87 us -> 3.71 us
  Pallas kernels: 43 us -> 41.4 us
    ppermute x9, starting transfers between devices: 22.9 us -> 17.2 us  [the longest x6 9.37 us: exchange(): return lax.ppermute(value, axis, pairs)]
    select_n x0 -> x1, other arithmetic: none -> 2.79 us  [body(): to_second = jnp.where(side == 0, lower, upper)]
    unnamed x24 -> x20, local copies, waits for them, and re-layouts: 5.72 us -> 3.31 us
    slice x1 -> x0, local copies, waits for them, and re-layouts: 1.49 us -> none  [body(): top = shifted(volume[:HALF], 'tile', -1)]
    pallas_call x2, Pallas kernels: 9.29 us -> 8.12 us  [weigh_blocks(): pl.pallas_call(functools.partial(weigh_kernel, blocks=len(blocks)), grid=...]
  transfers between devices with their start and end apart: 18 -> 18, of which waited for: 10 -> 10; matrix products, arithmetic and copies ran while one was open for 2% -> 1% of each run, Pallas kernels for 13% -> 12%
where the time goes in v3:
time: 105 us; the launch traced here: 104 us
  Pallas kernels  41.4 us (39%)
  waiting for transfers between devices  29.2 us (28%)
  starting transfers between devices  25 us (24%)
  other arithmetic  3.71 us (4%)
  local copies, waits for them, and re-layouts  3.35 us (3%)
  between operations  1.7 us (2%)
    pallas_call x1, Pallas kernels, sum_blocks(): pl.pallas_call(functools.partial(sum_kernel, early=len(parts), blocks=len...  17.3 us
    ppermute x4, waiting for transfers between devices, along(): return lax.ppermute(value, 'bank', pairs)  13.4 us
    ppermute x3, waiting for transfers between devices, gather_score(): lax.ppermute(mine, 'tile', [(i, i ^ by) for i in range(tiles)])  10.6 us
    ppermute x6, starting transfers between devices, exchange(): return lax.ppermute(value, axis, pairs)  9.37 us
    pallas_call x2, Pallas kernels, weigh_blocks(): pl.pallas_call(functools.partial(weigh_kernel, blocks=len(blocks)), grid=...  8.12 us
    ppermute x3, starting transfers between devices, gather_score(): lax.ppermute(mine, 'tile', [(i, i ^ by) for i in range(tiles)])  7.79 us
    pallas_call x1, Pallas kernels, body(): pl.pallas_call(functools.partial(far_kernel, wide=wide), in_specs=given +...  7.79 us
    ppermute x4, starting transfers between devices, along(): return lax.ppermute(value, 'bank', pairs)  6.78 us
  transfers between devices with their start and end apart: 18, of which 10 were waited for; matrix products, arithmetic and copies ran while one was open for 1% of the time, Pallas kernels for 12%

profile of v3, /device:TPU:0, one launch (start us, length us, event | category | flops | bytes accessed | tf_op | source)
XLA Modules:
  0.0 104.4 jit_solution(6624332487969588772)
XLA Ops:
  0.7 2.8 %broadcast_select_fusion = (bf16[48,64,128]{2,1,0:T(8,128)(2,1)}, bf16[48,64,128]{2,1,0:T(8,128)(2,1)}) fusion(pred[]{:T(512)S(6)} %eq.19, bf16[64,64,128]{2,1,0:T(8,128)(2,1)} %volume_ref.1), kind=kLoop, calls=%fused_computation.2 | loop fusion | flops 786432 | bytes 3145729 | tf_op jit(solution)/shard_map/jit(_where)/select_n | solution.py:476
  3.5 0.7 collective-permute-start.1
  4.2 5.7 %collective-permute-start = (s32[3,1,1,16]{3,2,1,0:T(1,128)S(1)}, s32[3,1,1,16]{3,2,1,0:T(1,128)S(1)}, u32[]{:S(2)}, u32[]{:S(2)}) collective-permute-start(s32[3,1,1,16]{3,2,1,0:T(1,128)S(1)} %copy-done.4), channel_id=1, source_target_pairs={{0,1},{1,0},{2,3},{3,2},{4,5},{5,4},{6,7},{7,6},{8,9},{9,8},{10,11... | collective-permute-start | bytes 584 | tf_op jit(solution)/shard_map/ppermute | solution.py:356
  9.9 1.6 %collective-permute-start.3 = (bf16[48,64,128]{2,1,0:T(8,128)(2,1)}, bf16[48,64,128]{2,1,0:T(8,128)(2,1)}, u32[]{:S(2)}, u32[]{:S(2)}) collective-permute-start(bf16[48,64,128]{2,1,0:T(8,128)(2,1)} %get-tuple-element.18), channel_id=1, source_target_pairs={{4,8},{8,4},{12,16},{16,12},{20,24},{24,20},{5,9},{9,5},{13,17},{1... | collective-permute-start | bytes 2359304 | tf_op jit(solution)/shard_map/ppermute | solution.py:356
  12.2 0.7 select_reduce_fusion
  13.0 1.7 %copy-done.1 = bf16[304,3072]{1,0:T(8,128)(2,1)S(1)} copy-done((bf16[304,3072]{1,0:T(8,128)(2,1)S(1)}, bf16[304,3072]{1,0:T(8,128)(2,1)}, u32[]{:S(2)}) %copy-start.1) | copy-done | bytes 1867800
  14.7 1.6 %copy-done.3 = f32[128,128]{1,0:T(8,128)S(1)} copy-done((f32[128,128]{1,0:T(8,128)S(1)}, f32[128,128]{1,0:T(8,128)}, u32[]{:S(2)}) %copy-start.3) | copy-done | bytes 65560
  16.3 4.8 %near_rows.1.near_ref = f32[304,768]{1,0:T(8,128)S(1)} custom-call(s32[3]{0:T(128)S(1)} %pad_add_fusion.origin_ref, s32[3,1,1,16]{3,2,1,0:T(1,128)S(1)} %collective-permute-done.first_pick_ref, s32[3,1,1,16]{3,2,1,0:T(1,128)S(1)} %copy-done.4, s32[3,1,1,16]{3,2,1,0:T(1,128)S(1)} %collective-permute-done.1.second_pick_ref, f32[128,128]{1,0:T(8,128)S(1)} %copy-done.3, ...), custom_call_target="tpu_custom_call" | custom-call | flops 2717908992 | bytes 8000000 | tf_op jit(solution)/shard_map/near_rows/pallas_call | solution.py:498
  21.1 7.8 %far_rows.1 = (bf16[256,256]{1,0:T(8,128)(2,1)S(1)}, f32[256,256]{1,0:T(8,128)S(1)}, bf16[256,256]{1,0:T(8,128)(2,1)S(1)}) custom-call(s32[3]{0:T(128)S(1)} %pad_add_fusion.origin_ref, s32[3,1,1,16]{3,2,1,0:T(1,128)S(1)} %collective-permute-done.first_pick_ref, s32[3,1,1,16]{3,2,1,0:T(1,128)S(1)} %copy-done.4, ...), custom_call_target="tpu_custom_call" | custom-call | tf_op jit(solution)/shard_map/far_rows/pallas_call | solution.py:510
  29.5 0.8 collective-permute-start.5
  30.4 3.5 %collective-permute-done.4.left_ref = bf16[256,256]{1,0:T(8,128)(2,1)S(1)} collective-permute-done((bf16[256,256]{1,0:T(8,128)(2,1)S(1)}, bf16[256,256]{1,0:T(8,128)(2,1)S(1)}, u32[]{:S(2)}, u32[]{:S(2)}) %collective-permute-start.4) | collective-permute-done | bytes 131104 | tf_op jit(solution)/shard_map/ppermute | solution.py:356
  34.0 3.3 %join.1 = bf16[16,4480]{1,0:T(8,128)(2,1)S(1)} custom-call(f32[256,256]{1,0:T(8,128)S(1)} %get-tuple-element.19.own_ref, bf16[256,256]{1,0:T(8,128)(2,1)S(1)} %collective-permute-done.4.left_ref, bf16[256,256]{1,0:T(8,128)(2,1)S(1)} %collective-permute-done.5.right_ref, bf16[16,256]{1,0:T(8,128)(2,1)S(1)} %select_convert_fusion.multiplicity_ref), custom_call_target="tpu_custom_call" | custom-call | tf_op jit(solution)/shard_map/join/pallas_call | solution.py:533
  37.3 7.1 %collective-permute-start.8 = (bf16[16,4480]{1,0:T(8,128)(2,1)S(1)}, bf16[16,4480]{1,0:T(8,128)(2,1)S(1)}, u32[]{:S(2)}, u32[]{:S(2)}) collective-permute-start(bf16[16,4480]{1,0:T(8,128)(2,1)S(1)} %join.1), channel_id=1, source_target_pairs={{0,24},{4,28},{8,16},{12,20},{16,8},{20,12},{24,0},{28,4},{1,25},{... | collective-permute-start | bytes 430088 | tf_op jit(solution)/shard_map/ppermute | solution.py:379
  45.1 3.9 %collective-permute-done.8 = bf16[16,4480]{1,0:T(8,128)(2,1)S(1)} collective-permute-done((bf16[16,4480]{1,0:T(8,128)(2,1)S(1)}, bf16[16,4480]{1,0:T(8,128)(2,1)S(1)}, u32[]{:S(2)}, u32[]{:S(2)}) %collective-permute-start.8) | collective-permute-done | bytes 143392 | tf_op jit(solution)/shard_map/ppermute | solution.py:379
  49.0 6.7 %collective-permute-done.7 = bf16[16,4480]{1,0:T(8,128)(2,1)S(1)} collective-permute-done((bf16[16,4480]{1,0:T(8,128)(2,1)S(1)}, bf16[16,4480]{1,0:T(8,128)(2,1)S(1)}, u32[]{:S(2)}, u32[]{:S(2)}) %collective-permute-start.7) | collective-permute-done | bytes 143392 | tf_op jit(solution)/shard_map/ppermute | solution.py:379
  55.8 4.6 %collective-permute-start.10 = (bf16[64,4480]{1,0:T(8,128)(2,1)S(1)}, bf16[64,4480]{1,0:T(8,128)(2,1)S(1)}, u32[]{:S(2)}, u32[]{:S(2)}) collective-permute-start(bf16[64,4480]{1,0:T(8,128)(2,1)S(1)} %pad_maximum_fusion.refs_0_.refs_2_), channel_id=1, source_target_pairs={{0,2},{2,0},{1,3},{3,1},{4,6},{6,4},{5,7},{7,5},{8,10},{10,8},{9,1... | collective-permute-start | bytes 1720328 | tf_op jit(solution)/shard_map/ppermute | solution.py:370
  60.5 3.9 %weigh.2.refs_0_ = bf16[20,64,128]{2,1,0:T(8,128)(2,1)S(1)} custom-call(s32[1]{0:T(128)} %bitcast.index_ref, bf16[64,4480]{1,0:T(8,128)(2,1)S(1)} %pad_maximum_fusion.refs_0_.refs_2_, bf16[64,4480]{1,0:T(8,128)(2,1)S(1)} %collective-permute-done.11.refs_1_.refs_3_, bf16[20,64,4096]{2,1,0:T(8,128)(2,1)S(1)} %bitcast.14), custom_call_target="tpu_custom_call" | custom-call | flops 1342177280 | bytes 10485760 | tf_op jit(solution)/shard_map/weigh/pallas_call | solution.py:420
  64.4 9.6 %collective-permute-done.10.refs_1_.refs_5_ = bf16[64,4480]{1,0:T(8,128)(2,1)S(1)} collective-permute-done((bf16[64,4480]{1,0:T(8,128)(2,1)S(1)}, bf16[64,4480]{1,0:T(8,128)(2,1)S(1)}, u32[]{:S(2)}, u32[]{:S(2)}) %collective-permute-start.10) | collective-permute-done | bytes 573472 | tf_op jit(solution)/shard_map/ppermute | solution.py:370
  74.0 1.5 %collective-permute-done.9.refs_0_.refs_4_ = bf16[64,4480]{1,0:T(8,128)(2,1)S(1)} collective-permute-done((bf16[64,4480]{1,0:T(8,128)(2,1)S(1)}, bf16[64,4480]{1,0:T(8,128)(2,1)S(1)}, u32[]{:S(2)}, u32[]{:S(2)}) %collective-permute-start.9) | collective-permute-done | bytes 573472 | tf_op jit(solution)/shard_map/ppermute | solution.py:370
  76.4 1.7 %collective-permute-start.12 = (bf16[32,4480]{1,0:T(8,128)(2,1)S(1)}, bf16[32,4480]{1,0:T(8,128)(2,1)S(1)}, u32[]{:S(2)}, u32[]{:S(2)}) collective-permute-start(bf16[32,4480]{1,0:T(8,128)(2,1)S(1)} %slice.14), channel_id=1, source_target_pairs={{0,2},{2,0},{1,3},{3,1},{4,6},{6,4},{5,7},{7,5},{8,10},{10,8},{9,1... | collective-permute-start | bytes 860168 | tf_op jit(solution)/shard_map/ppermute | solution.py:370
  78.3 4.3 %weigh.3.refs_1_ = bf16[20,64,256]{2,1,0:T(8,128)(2,1)S(1)} custom-call(s32[1]{0:T(128)} %bitcast.index_ref, bf16[64,4480]{1,0:T(8,128)(2,1)S(1)} %collective-permute-done.9.refs_0_.refs_4_, bf16[64,4480]{1,0:T(8,128)(2,1)S(1)} %collective-permute-done.10.refs_1_.refs_5_, bf16[64,4480]{1,0:T(8,128)(2,1)S(1)} %collective-permute-done.14.refs_2_.refs_6_, ...), custom_call_target="tpu_custom_call" | custom-call | flops 2684354560 | bytes 10485760 | tf_op jit(solution)/shard_map/weigh/pallas_call | solution.py:420
  82.5 2.3 %collective-permute-done.13.refs_9_ = bf16[32,4480]{1,0:T(8,128)(2,1)S(1)} collective-permute-done((bf16[32,4480]{1,0:T(8,128)(2,1)S(1)}, bf16[32,4480]{1,0:T(8,128)(2,1)S(1)}, u32[]{:S(2)}, u32[]{:S(2)}) %collective-permute-start.13) | collective-permute-done | bytes 286752 | tf_op jit(solution)/shard_map/ppermute | solution.py:370
  85.4 1.1 %collective-permute-done.16.refs_10_ = bf16[32,4480]{1,0:T(8,128)(2,1)S(1)} collective-permute-done((bf16[32,4480]{1,0:T(8,128)(2,1)S(1)}, bf16[32,4480]{1,0:T(8,128)(2,1)S(1)}, u32[]{:S(2)}, u32[]{:S(2)}) %collective-permute-start.16) | collective-permute-done | bytes 286752 | tf_op jit(solution)/shard_map/ppermute | solution.py:373
  86.9 17.3 %class_sums.1 = (f32[20,64,4096]{2,1,0:T(8,128)}, f32[20,64]{1,0:T(8,128)}) custom-call(s32[1]{0:T(128)} %bitcast.index_ref, bf16[20,64,128]{2,1,0:T(8,128)(2,1)S(1)} %weigh.2.refs_0_, bf16[20,64,256]{2,1,0:T(8,128)(2,1)S(1)} %weigh.3.refs_1_, bf16[64,4480]{1,0:T(8,128)(2,1)S(1)} %pad_maximum_fusion.refs_0_.refs_2_, ...), custom_call_target="tpu_custom_call" | custom-call | flops 6710886400 | bytes 31457280 | tf_op jit(solution)/shard_map/class_sums/pallas_call | solution.py:443
  (48 shorter events, 3.7 us)
Async XLA Ops:
  0.6 12.4 %copy-start.2 = (f32[128,128]{1,0:T(8,128)S(1)}, f32[128,128]{1,0:T(8,128)}, u32[]{:S(2)}) copy-start(f32[128,128]{1,0:T(8,128)} %constant.29.clone.second_ref) | copy-start | bytes 196612
  0.6 12.4 %copy-start = (bf16[64,64,128]{2,1,0:T(8,128)(2,1)S(1)}, bf16[64,64,128]{2,1,0:T(8,128)(2,1)}, u32[]{:S(2)}) copy-start(bf16[64,64,128]{2,1,0:T(8,128)(2,1)} %volume_ref.1) | copy-start | bytes 3145732
  0.7 11.5 %copy-start.5 = (s32[1,1,16,128]{3,2,1,0:T(8,128)S(1)}, s32[1,1,16,128]{3,2,1,0:T(8,128)}, u32[]{:S(2)}) copy-start(s32[1,1,16,128]{3,2,1,0:T(8,128)} %param.12) | copy-start | bytes 24580
  0.7 59.8 %slice-start = ((s8[10485760]{0:T(1024)(128)(4,1)}), s8[2097152]{0:T(1024)(128)(4,1)S(1)}, s32[]{:S(2)}) async-start(s8[10485760]{0:T(1024)(128)(4,1)} %bitcast.12), calls=%async_computation | async-start | bytes 4194304
  3.5 9.5 %collective-permute-start.1 = (s32[3,1,1,16]{3,2,1,0:T(1,128)S(1)}, s32[3,1,1,16]{3,2,1,0:T(1,128)S(1)}, u32[]{:S(2)}, u32[]{:S(2)}) collective-permute-start(s32[3,1,1,16]{3,2,1,0:T(1,128)S(1)} %copy-done.4), channel_id=1, source_target_pairs={{1,2},{2,1},{5,6},{6,5},{9,10},{10,9},{13,14},{14,13},{17,18},{18,... | collective-permute-start | bytes 584 | tf_op jit(solution)/shard_map/ppermute | solution.py:356
  4.2 8.8 %collective-permute-start = (s32[3,1,1,16]{3,2,1,0:T(1,128)S(1)}, s32[3,1,1,16]{3,2,1,0:T(1,128)S(1)}, u32[]{:S(2)}, u32[]{:S(2)}) collective-permute-start(s32[3,1,1,16]{3,2,1,0:T(1,128)S(1)} %copy-done.4), channel_id=1, source_target_pairs={{0,1},{1,0},{2,3},{3,2},{4,5},{5,4},{6,7},{7,6},{8,9},{9,8},{10,11... | collective-permute-start | bytes 584 | tf_op jit(solution)/shard_map/ppermute | solution.py:356
  9.9 11.2 %collective-permute-start.2 = (bf16[48,64,128]{2,1,0:T(8,128)(2,1)}, bf16[48,64,128]{2,1,0:T(8,128)(2,1)}, u32[]{:S(2)}, u32[]{:S(2)}) collective-permute-start(bf16[48,64,128]{2,1,0:T(8,128)(2,1)} %get-tuple-element.17), channel_id=1, source_target_pairs={{0,4},{4,0},{8,12},{12,8},{16,20},{20,16},{24,28},{28,24},{1,5},{5... | collective-permute-start | bytes 2359304 | tf_op jit(solution)/shard_map/ppermute | solution.py:356
  9.9 11.2 %collective-permute-start.3 = (bf16[48,64,128]{2,1,0:T(8,128)(2,1)}, bf16[48,64,128]{2,1,0:T(8,128)(2,1)}, u32[]{:S(2)}, u32[]{:S(2)}) collective-permute-start(bf16[48,64,128]{2,1,0:T(8,128)(2,1)} %get-tuple-element.18), channel_id=1, source_target_pairs={{4,8},{8,4},{12,16},{16,12},{20,24},{24,20},{5,9},{9,5},{13,17},{1... | collective-permute-start | bytes 2359304 | tf_op jit(solution)/shard_map/ppermute | solution.py:356
  13.0 47.6 %slice-start.1 = ((s8[10485760]{0:T(1024)(128)(4,1)}), s8[4194304]{0:T(1024)(128)(4,1)S(1)}, s32[]{:S(2)}) async-start(s8[10485760]{0:T(1024)(128)(4,1)} %bitcast.12), calls=%async_computation.1 | async-start | bytes 8388608
  13.0 47.6 %slice-start.2 = ((s8[10485760]{0:T(1024)(128)(4,1)}), s8[4194304]{0:T(1024)(128)(4,1)S(1)}, s32[]{:S(2)}) async-start(s8[10485760]{0:T(1024)(128)(4,1)} %bitcast.12), calls=%async_computation.2 | async-start | bytes 8388608
  28.9 5.0 %collective-permute-start.4 = (bf16[256,256]{1,0:T(8,128)(2,1)S(1)}, bf16[256,256]{1,0:T(8,128)(2,1)S(1)}, u32[]{:S(2)}, u32[]{:S(2)}) collective-permute-start(bf16[256,256]{1,0:T(8,128)(2,1)S(1)} %get-tuple-element.20), channel_id=1, source_target_pairs={{0,1},{1,0},{2,3},{3,2},{4,5},{5,4},{6,7},{7,6},{8,9},{9,8},{10,11... | collective-permute-start | bytes 393224 | tf_op jit(solution)/shard_map/ppermute | solution.py:356
  29.5 4.5 %collective-permute-start.5 = (bf16[256,256]{1,0:T(8,128)(2,1)S(1)}, bf16[256,256]{1,0:T(8,128)(2,1)S(1)}, u32[]{:S(2)}, u32[]{:S(2)}) collective-permute-start(bf16[256,256]{1,0:T(8,128)(2,1)S(1)} %get-tuple-element.21), channel_id=1, source_target_pairs={{1,2},{2,1},{5,6},{6,5},{9,10},{10,9},{13,14},{14,13},{17,18},{18,... | collective-permute-start | bytes 393224 | tf_op jit(solution)/shard_map/ppermute | solution.py:356
  37.3 11.7 %collective-permute-start.8 = (bf16[16,4480]{1,0:T(8,128)(2,1)S(1)}, bf16[16,4480]{1,0:T(8,128)(2,1)S(1)}, u32[]{:S(2)}, u32[]{:S(2)}) collective-permute-start(bf16[16,4480]{1,0:T(8,128)(2,1)S(1)} %join.1), channel_id=1, source_target_pairs={{0,24},{4,28},{8,16},{12,20},{16,8},{20,12},{24,0},{28,4},{1,25},{... | collective-permute-start | bytes 430088 | tf_op jit(solution)/shard_map/ppermute | solution.py:379
  44.5 11.3 %collective-permute-start.7 = (bf16[16,4480]{1,0:T(8,128)(2,1)S(1)}, bf16[16,4480]{1,0:T(8,128)(2,1)S(1)}, u32[]{:S(2)}, u32[]{:S(2)}) collective-permute-start(bf16[16,4480]{1,0:T(8,128)(2,1)S(1)} %join.1), channel_id=1, source_target_pairs={{0,16},{4,20},{8,24},{12,28},{16,0},{20,4},{24,8},{28,12},{1,17},{... | collective-permute-start | bytes 430088 | tf_op jit(solution)/shard_map/ppermute | solution.py:379
  44.5 11.3 %collective-permute-start.6 = (bf16[16,4480]{1,0:T(8,128)(2,1)S(1)}, bf16[16,4480]{1,0:T(8,128)(2,1)S(1)}, u32[]{:S(2)}, u32[]{:S(2)}) collective-permute-start(bf16[16,4480]{1,0:T(8,128)(2,1)S(1)} %join.1), channel_id=1, source_target_pairs={{0,8},{4,12},{8,0},{12,4},{16,24},{20,28},{24,16},{28,20},{1,9},{5... | collective-permute-start | bytes 430088 | tf_op jit(solution)/shard_map/ppermute | solution.py:379
  55.8 4.7 %collective-permute-start.11 = (bf16[64,4480]{1,0:T(8,128)(2,1)S(1)}, bf16[64,4480]{1,0:T(8,128)(2,1)S(1)}, u32[]{:S(2)}, u32[]{:S(2)}) collective-permute-start(bf16[64,4480]{1,0:T(8,128)(2,1)S(1)} %pad_maximum_fusion.refs_0_.refs_2_), channel_id=1, source_target_pairs={{0,4},{4,0},{8,12},{12,8},{16,20},{20,16},{24,28},{28,24},{1,5},{5... | collective-permute-start | bytes 1720328 | tf_op jit(solution)/shard_map/ppermute | solution.py:373
  55.8 18.1 %collective-permute-start.10 = (bf16[64,4480]{1,0:T(8,128)(2,1)S(1)}, bf16[64,4480]{1,0:T(8,128)(2,1)S(1)}, u32[]{:S(2)}, u32[]{:S(2)}) collective-permute-start(bf16[64,4480]{1,0:T(8,128)(2,1)S(1)} %pad_maximum_fusion.refs_0_.refs_2_), channel_id=1, source_target_pairs={{0,2},{2,0},{1,3},{3,1},{4,6},{6,4},{5,7},{7,5},{8,10},{10,8},{9,1... | collective-permute-start | bytes 1720328 | tf_op jit(solution)/shard_map/ppermute | solution.py:370
  60.4 15.0 %collective-permute-start.9 = (bf16[64,4480]{1,0:T(8,128)(2,1)S(1)}, bf16[64,4480]{1,0:T(8,128)(2,1)S(1)}, u32[]{:S(2)}, u32[]{:S(2)}) collective-permute-start(bf16[64,4480]{1,0:T(8,128)(2,1)S(1)} %pad_maximum_fusion.refs_0_.refs_2_), channel_id=1, source_target_pairs={{0,1},{1,0},{2,3},{3,2},{4,5},{5,4},{6,7},{7,6},{8,9},{9,8},{10,11... | collective-permute-start | bytes 1720328 | tf_op jit(solution)/shard_map/ppermute | solution.py:370
  75.5 2.7 %collective-permute-start.14 = (bf16[64,4480]{1,0:T(8,128)(2,1)S(1)}, bf16[64,4480]{1,0:T(8,128)(2,1)S(1)}, u32[]{:S(2)}, u32[]{:S(2)}) collective-permute-start(bf16[64,4480]{1,0:T(8,128)(2,1)S(1)} %collective-permute-done.9.refs_0_.refs_4_), channel_id=1, source_target_pairs={{0,4},{4,0},{8,12},{12,8},{16,20},{20,16},{24,28},{28,24},{1,5},{5... | collective-permute-start | bytes 1720328 | tf_op jit(solution)/shard_map/ppermute | solution.py:373
  75.5 2.8 %collective-permute-start.15 = (bf16[64,4480]{1,0:T(8,128)(2,1)S(1)}, bf16[64,4480]{1,0:T(8,128)(2,1)S(1)}, u32[]{:S(2)}, u32[]{:S(2)}) collective-permute-start(bf16[64,4480]{1,0:T(8,128)(2,1)S(1)} %collective-permute-done.10.refs_1_.refs_5_), channel_id=1, source_target_pairs={{0,4},{4,0},{8,12},{12,8},{16,20},{20,16},{24,28},{28,24},{1,5},{5... | collective-permute-start | bytes 1720328 | tf_op jit(solution)/shard_map/ppermute | solution.py:373
  76.0 8.8 %collective-permute-start.13 = (bf16[32,4480]{1,0:T(8,128)(2,1)S(1)}, bf16[32,4480]{1,0:T(8,128)(2,1)S(1)}, u32[]{:S(2)}, u32[]{:S(2)}) collective-permute-start(bf16[32,4480]{1,0:T(8,128)(2,1)S(1)} %slice.15), channel_id=1, source_target_pairs={{0,1},{1,0},{2,3},{3,2},{4,5},{5,4},{6,7},{7,6},{8,9},{9,8},{10,11... | collective-permute-start | bytes 860168 | tf_op jit(solution)/shard_map/ppermute | solution.py:370
  76.4 8.5 %collective-permute-start.12 = (bf16[32,4480]{1,0:T(8,128)(2,1)S(1)}, bf16[32,4480]{1,0:T(8,128)(2,1)S(1)}, u32[]{:S(2)}, u32[]{:S(2)}) collective-permute-start(bf16[32,4480]{1,0:T(8,128)(2,1)S(1)} %slice.14), channel_id=1, source_target_pairs={{0,2},{2,0},{1,3},{3,1},{4,6},{6,4},{5,7},{7,5},{8,10},{10,8},{9,1... | collective-permute-start | bytes 860168 | tf_op jit(solution)/shard_map/ppermute | solution.py:370
  84.9 1.6 %collective-permute-start.16 = (bf16[32,4480]{1,0:T(8,128)(2,1)S(1)}, bf16[32,4480]{1,0:T(8,128)(2,1)S(1)}, u32[]{:S(2)}, u32[]{:S(2)}) collective-permute-start(bf16[32,4480]{1,0:T(8,128)(2,1)S(1)} %collective-permute-done.12.refs_8_), channel_id=1, source_target_pairs={{0,4},{4,0},{8,12},{12,8},{16,20},{20,16},{24,28},{28,24},{1,5},{5... | collective-permute-start | bytes 860168 | tf_op jit(solution)/shard_map/ppermute | solution.py:373
  84.9 2.0 %collective-permute-start.17 = (bf16[32,4480]{1,0:T(8,128)(2,1)S(1)}, bf16[32,4480]{1,0:T(8,128)(2,1)S(1)}, u32[]{:S(2)}, u32[]{:S(2)}) collective-permute-start(bf16[32,4480]{1,0:T(8,128)(2,1)S(1)} %collective-permute-done.13.refs_9_), channel_id=1, source_target_pairs={{0,4},{4,0},{8,12},{12,8},{16,20},{20,16},{24,28},{28,24},{1,5},{5... | collective-permute-start | bytes 860168 | tf_op jit(solution)/shard_map/ppermute | solution.py:373
  (4 other events, 17.6 us)

commit v4 on v3

--- a/solution.py
+++ b/solution.py
@@ -212,7 +212,8 @@
     second_out_ref[...] = rows[:, 2 * width :].astype(jnp.bfloat16)
 
 
-def join_kernel(own_ref, left_ref, right_ref, multiplicity_ref, out_ref, wide_ref):
+def join_kernel(own_ref, left_ref, right_ref, multiplicity_ref, *refs):
+    outs, wide_ref = refs[:-1], refs[-1]
     total = own_ref[...] + left_ref[...].astype(jnp.float32) + right_ref[...].astype(jnp.float32)
     total = total.astype(jnp.bfloat16)
     rows, lanes = total.shape
@@ -244,9 +245,12 @@
     high = norm.astype(jnp.bfloat16).astype(jnp.float32)
     tail = lax.broadcasted_iota(jnp.int32, (slots, 128), 1)
     tail = jnp.where(tail == 0, high, jnp.where(tail == 1, norm - high, 0.0))
-    out_ref[:, :F] = wide.astype(jnp.bfloat16)
-    out_ref[:, F : F + R] = multiplicity_ref[...]
-    out_ref[:, F + R :] = tail.astype(jnp.bfloat16)
+    row = jnp.concatenate(
+        [wide.astype(jnp.bfloat16), multiplicity_ref[...], tail.astype(jnp.bfloat16)], axis=1
+    )
+    for k, out_ref in enumerate(outs):
+        count = out_ref.shape[0]
+        out_ref[...] = row[k * count : (k + 1) * count]
 
 
 def load_blocks(blocks, rows_ref, tail_ref, sems):
@@ -257,11 +261,12 @@
         copies.append(
             pltpu.make_async_copy(block.at[:, pl.ds(0, F)], rows_ref.at[place], sems.at[2 * k])
         )
-        copies.append(
-            pltpu.make_async_copy(
-                block.at[:, pl.ds(F, block.shape[1] - F)], tail_ref.at[place], sems.at[2 * k + 1]
+        if tail_ref is not None:
+            copies.append(
+                pltpu.make_async_copy(
+                    block.at[:, pl.ds(F, block.shape[1] - F)], tail_ref.at[place], sems.at[2 * k + 1]
+                )
             )
-        )
         at += count
     for copy in copies:
         copy.start()
@@ -302,27 +307,20 @@
     out_ref[...] = weights.reshape(out_ref.shape)
 
 
-def sum_kernel(index_ref, *refs, early, blocks, late):
+def sum_kernel(*refs, early, blocks):
     parts, sources = refs[:early], refs[early : early + blocks]
-    bank_ref, out_ref, sums_ref = refs[early + blocks : early + blocks + 3]
-    rows_ref, tail_ref, turned_ref, multiplicity_ref, norm_ref, sems = refs[early + blocks + 3 :]
-    count, orients, width = bank_ref.shape
+    out_ref, sums_ref, rows_ref, sems = refs[early + blocks :]
+    count, orients, width = out_ref.shape
     boxes = rows_ref.shape[0]
     step = pl.program_id(0)
 
     @pl.when(step == 0)
     def _():
-        load_blocks(sources, rows_ref, tail_ref, sems)
-        read_tail(
-            index_ref, tail_ref[boxes - late :], turned_ref, multiplicity_ref, norm_ref, orients
-        )
-
-    bank = bank_ref[...].reshape(count * orients, width)
-    weights = weigh(
-        bank, rows_ref[boxes - late :, :], multiplicity_ref[...], norm_ref[...], count
-    )
-    known = [part[...].reshape(count * orients, part.shape[2]) for part in parts]
-    weights = jnp.concatenate(known + [weights], axis=1)
+        load_blocks(sources, rows_ref, None, sems)
+
+    weights = jnp.concatenate(
+        [part[...].reshape(count * orients, part.shape[2]) for part in parts], axis=1
+    )
     total = jnp.dot(weights, rows_ref[...], preferred_element_type=jnp.float32)
     out_ref[...] = total.reshape(out_ref.shape)
     ones = jnp.ones((8, boxes), jnp.bfloat16)
@@ -359,51 +357,54 @@
 def gather_score(mine, reference_bank):
     tiles, banks = lax.axis_size("tile"), lax.axis_size("bank")
     local_rows, classes, width = reference_bank.shape
-    if banks != 4 or tiles & (tiles - 1) or tiles < 2 or tiles * banks * mine.shape[0] > 1024 or classes % 5:
-        return score_plain(
-            lax.all_gather(lax.all_gather(mine, "bank", axis=0, tiled=True), "tile", axis=0, tiled=True),
-            reference_bank,
-        )
+    boxes = tiles * banks * sum(part.shape[0] for part in mine)
+    if banks != 4 or tiles & (tiles - 1) or tiles < 4 or boxes > 1024 or classes % 5:
+        rows = jnp.concatenate(mine, axis=0)
+        for axis in ("bank", "tile"):
+            rows = lax.all_gather(rows, axis, axis=0, tiled=True)
+        return score_plain(rows, reference_bank)
     bank = jnp.transpose(reference_bank, (1, 0, 2))
-
-    def along(value, pairs):
-        return lax.ppermute(value, "bank", pairs)
-
-    def swap(value):
-        return lax.ppermute(value, "tile", [(i, i ^ 1) for i in range(tiles)])
-
-    x_pairs, y_pairs = [(0, 1), (1, 0), (2, 3), (3, 2)], [(0, 2), (2, 0), (1, 3), (3, 1)]
-    line = jnp.concatenate(
-        [mine]
-        + [
-            lax.ppermute(mine, "tile", [(i, i ^ by) for i in range(tiles)])
+    early, late = mine
+
+    def along_x(value):
+        return lax.ppermute(value, "bank", [(0, 1), (1, 0), (2, 3), (3, 2)])
+
+    def along_y(value):
+        return lax.ppermute(value, "bank", [(0, 2), (2, 0), (1, 3), (3, 1)])
+
+    def swap(*values):
+        return [lax.ppermute(value, "tile", [(i, i ^ 1) for i in range(tiles)]) for value in values]
+
+    def line_of(part):
+        others = [
+            lax.ppermute(part, "tile", [(i, i ^ by) for i in range(tiles)])
             for by in range(2, tiles, 2)
-        ],
-        axis=0,
-    )
-    half = line.shape[0] // 2
-    from_x, from_y = along(line, x_pairs), along(line, y_pairs)
-    near = [line, swap(line)]
-    first = weigh_blocks(near, bank)
-    from_x, from_y, first = lax.optimization_barrier((from_x, from_y, first))
-    across_y, across_x = along(from_x[:half], y_pairs), along(from_y[half:], x_pairs)
-    middle = [from_x, from_y, swap(from_x), swap(from_y)]
-    second = weigh_blocks(middle, bank)
-    across_y, across_x, second = lax.optimization_barrier((across_y, across_x, second))
-    last = [across_y, across_x, swap(across_y), swap(across_x)]
-    out, sums = sum_blocks([first, second], near + middle + last, 2 * line.shape[0], bank)
+        ]
+        return jnp.concatenate([part] + others, axis=0)
+
+    def with_swap(*values):
+        joined = jnp.concatenate(values, axis=0) if len(values) > 1 else values[0]
+        return [*values, *swap(joined)]
+
+    early_line = line_of(early)
+    late, early_line = lax.optimization_barrier((late, early_line))
+    from_x, from_y = along_x(early_line), along_y(early_line)
+    late_line = line_of(late)
+    half = early_line.shape[0] // 2
+    to_x = jnp.concatenate([from_y[half:], late_line], axis=0)
+    to_y = jnp.concatenate([from_x[:half], late_line], axis=0)
+    blocks = [with_swap(early_line, from_x, from_y)]
+    next_x, next_y = along_x(to_x), along_y(to_y)
+    first = weigh_blocks(blocks[0], bank)
+    first, next_x, next_y = lax.optimization_barrier((first, next_x, next_y))
+    last_x, last_y = along_x(next_y[half + half :]), along_y(next_x[half : half + half])
+    blocks.append(with_swap(late_line, next_x, next_y))
+    second = weigh_blocks(blocks[1], bank)
+    second, last_x, last_y = lax.optimization_barrier((second, last_x, last_y))
+    blocks.append(with_swap(last_x, last_y))
+    third = weigh_blocks(blocks[2], bank)
+    out, sums = sum_blocks([first, second, third], sum(blocks, []), bank)
     return jnp.transpose(out, (1, 0, 2)), jnp.transpose(sums, (1, 0))
-
-
-def scratch_of(boxes, scored, blocks, orients, tail):
-    return [
-        pltpu.VMEM((boxes, F), jnp.bfloat16),
-        pltpu.VMEM((boxes, tail), jnp.bfloat16),
-        pltpu.VMEM((tail, scored), jnp.float32),
-        pltpu.VMEM((orients, scored), jnp.float32),
-        pltpu.VMEM((1, scored), jnp.float32),
-        pltpu.SemaphoreType.DMA((2 * blocks,)),
-    ]
 
 
 CLASSES = 5
@@ -425,7 +426,14 @@
         + [pl.BlockSpec((CLASSES, orients, width), lambda i: (i, 0, 0))],
         out_specs=pl.BlockSpec((CLASSES, orients, boxes), lambda i: (i, 0, 0)),
         out_shape=jax.ShapeDtypeStruct((classes, orients, boxes), jnp.bfloat16),
-        scratch_shapes=scratch_of(boxes, boxes, len(blocks), orients, tail),
+        scratch_shapes=[
+            pltpu.VMEM((boxes, F), jnp.bfloat16),
+            pltpu.VMEM((boxes, tail), jnp.bfloat16),
+            pltpu.VMEM((tail, boxes), jnp.float32),
+            pltpu.VMEM((orients, boxes), jnp.float32),
+            pltpu.VMEM((1, boxes), jnp.float32),
+            pltpu.SemaphoreType.DMA((2 * len(blocks),)),
+        ],
         compiler_params=pltpu.CompilerParams(vmem_limit_bytes=18 * MIB),
         cost_estimate=pl.CostEstimate(
             flops=2 * boxes * classes * orients * width,
@@ -436,17 +444,16 @@
     )(bank_index(), *blocks, bank)
 
 
-def sum_blocks(parts, blocks, late, bank):
+def sum_blocks(parts, blocks, bank):
     classes, orients, width = bank.shape
     boxes = sum(block.shape[0] for block in blocks)
-    tail = blocks[0].shape[1] - F
     return pl.pallas_call(
-        functools.partial(sum_kernel, early=len(parts), blocks=len(blocks), late=late),
+        functools.partial(sum_kernel, early=len(parts), blocks=len(blocks)),
         grid=(classes // CLASSES,),
-        in_specs=[pl.BlockSpec(memory_space=pltpu.SMEM)]
-        + [pl.BlockSpec((CLASSES, orients, part.shape[2]), lambda i: (i, 0, 0)) for part in parts]
-        + [pl.BlockSpec(memory_space=pl.ANY)] * len(blocks)
-        + [pl.BlockSpec((CLASSES, orients, width), lambda i: (i, 0, 0))],
+        in_specs=[
+            pl.BlockSpec((CLASSES, orients, part.shape[2]), lambda i: (i, 0, 0)) for part in parts
+        ]
+        + [pl.BlockSpec(memory_space=pl.ANY)] * len(blocks),
         out_specs=[
             pl.BlockSpec((CLASSES, orients, width), lambda i: (i, 0, 0)),
             pl.BlockSpec((classes, orients), lambda i: (0, 0)),
@@ -455,15 +462,18 @@
             jax.ShapeDtypeStruct((classes, orients, width), jnp.float32),
             jax.ShapeDtypeStruct((classes, orients), jnp.float32),
         ],
-        scratch_shapes=scratch_of(boxes, late, len(blocks), orients, tail),
+        scratch_shapes=[
+            pltpu.VMEM((boxes, F), jnp.bfloat16),
+            pltpu.SemaphoreType.DMA((2 * len(blocks),)),
+        ],
         compiler_params=pltpu.CompilerParams(vmem_limit_bytes=36 * MIB),
         cost_estimate=pl.CostEstimate(
-            flops=2 * (boxes + late) * classes * orients * width,
-            bytes_accessed=6 * classes * orients * width,
+            flops=2 * boxes * classes * orients * width,
+            bytes_accessed=4 * classes * orients * width,
             transcendentals=0,
         ),
         name="class_sums",
-    )(bank_index(), *parts, *blocks, bank)
+    )(*parts, *blocks)
 
 
 def body(volume, pick_list, box_counts, orientations, orient_weight, reference_bank):
@@ -471,12 +481,12 @@
     slots = pick_list.shape[3]
     tile, bank = lax.axis_index("tile"), lax.axis_index("bank")
     side = lax.rem(tile, 2)
-    upper, lower = volume[wide - HALF :], volume[:HALF]
-    to_first = jnp.where(side == 0, upper, lower)
-    to_second = jnp.where(side == 0, lower, upper)
-    to_first, to_second, picks = lax.optimization_barrier((to_first, to_second, pick_list))
+    rest = wide - HALF
+    to_first = lax.dynamic_slice_in_dim(volume, jnp.where(side == 0, rest, 0), HALF, 0)
+    to_second = lax.dynamic_slice_in_dim(volume, jnp.where(side == 0, 0, rest), HALF, 0)
     first_halo = exchange(to_first, "tile", True)
     second_halo = exchange(to_second, "tile", False)
+    picks, first_halo = lax.optimization_barrier((pick_list, first_halo))
     first_picks, second_picks = exchange(picks, "bank", True), exchange(picks, "bank", False)
     origin = jnp.stack([tile * wide + HALF, bank * high + HALF, side]).astype(jnp.int32)
 
@@ -530,9 +540,10 @@
         jnp.where(matches, orient_weight[0, 0][:, :, None].astype(jnp.float32), 0.0), axis=1
     )
     multiplicity = jnp.where(live_slots[:, None], multiplicity, 0.0).astype(jnp.bfloat16)
+    parts = 2
     mine = pl.pallas_call(
         join_kernel,
-        out_shape=jax.ShapeDtypeStruct((slots, F + R + 128), jnp.bfloat16),
+        out_shape=[jax.ShapeDtypeStruct((slots // parts, F + R + 128), jnp.bfloat16)] * parts,
         scratch_shapes=[pltpu.VMEM((slots, F), jnp.float32)],
         compiler_params=params,
         name="join",

time: 105 us -> 96.1 us (0.915)
  waiting for transfers between devices: 29.2 us -> 21.1 us
  starting transfers between devices: 25 us -> 28.7 us
  other arithmetic: 3.71 us -> 0.98 us
  Pallas kernels: 41.4 us -> 40.3 us
    ppermute x12 -> x15, waiting for transfers between devices: 25.6 us -> 16.2 us  [the longest x3 6.55 us: along_y(): return lax.ppermute(value, 'bank', [(0, 2), (2, 0), (1, 3), (3, 1)])]
    pallas_call x1, Pallas kernels: 17.3 us -> 10.3 us  [sum_blocks(): pl.pallas_call(functools.partial(sum_kernel, early=len(parts), blocks=len...]
    pallas_call x2 -> x3, Pallas kernels: 8.12 us -> 13.9 us  [weigh_blocks(): pl.pallas_call(functools.partial(weigh_kernel, blocks=len(blocks)), grid=...]
    unnamed x20 -> x27, local copies, waits for them, and re-layouts: 3.31 us -> 0.23 us
    select_n x1 -> x0, other arithmetic: 2.79 us -> none  [body(): to_second = jnp.where(side == 0, lower, upper)]
    dynamic_slice x0 -> x1, local copies, waits for them, and re-layouts: none -> 2.78 us  [body(): lax.dynamic_slice_in_dim(volume, jnp.where(side == 0, 0, rest), HALF, 0)]
    ppermute x12 -> x15, starting transfers between devices: 15.7 us -> 17.8 us  [the longest x6 8.79 us: line_of(): lax.ppermute(part, 'tile', [(i, i ^ by) for i in range(tiles)])]
    ppermute x6, starting transfers between devices: 9.37 us -> 10.9 us  [exchange(): return lax.ppermute(value, axis, pairs)]
  transfers between devices with their start and end apart: 18 -> 21, of which waited for: 10 -> 12; matrix products, arithmetic and copies ran while one was open for 1% -> 1% of each run, Pallas kernels for 12% -> 15%
where the time goes in v4:
time: 96.1 us; the launch traced here: 96 us
  Pallas kernels  40.3 us (42%)
  starting transfers between devices  28.7 us (30%)
  waiting for transfers between devices  21.1 us (22%)
  local copies, waits for them, and re-layouts  3.07 us (3%)
  between operations  1.8 us (2%)
  other arithmetic  0.98 us (1%)
    pallas_call x3, Pallas kernels, weigh_blocks(): pl.pallas_call(functools.partial(weigh_kernel, blocks=len(blocks)), grid=...  13.9 us
    ppermute x6, starting transfers between devices, exchange(): return lax.ppermute(value, axis, pairs)  10.9 us
    pallas_call x1, Pallas kernels, sum_blocks(): pl.pallas_call(functools.partial(sum_kernel, early=len(parts), blocks=len...  10.3 us
    ppermute x6, starting transfers between devices, line_of(): lax.ppermute(part, 'tile', [(i, i ^ by) for i in range(tiles)])  8.79 us
    pallas_call x1, Pallas kernels, body(): pl.pallas_call(functools.partial(far_kernel, wide=wide), in_specs=given +...  7.93 us
    ppermute x3, starting transfers between devices, along_y(): return lax.ppermute(value, 'bank', [(0, 2), (2, 0), (1, 3), (3, 1)])  6.94 us
    ppermute x3, waiting for transfers between devices, along_y(): return lax.ppermute(value, 'bank', [(0, 2), (2, 0), (1, 3), (3, 1)])  6.55 us
    ppermute x6, waiting for transfers between devices, line_of(): lax.ppermute(part, 'tile', [(i, i ^ by) for i in range(tiles)])  5.88 us
  transfers between devices with their start and end apart: 21, of which 12 were waited for; matrix products, arithmetic and copies ran while one was open for 1% of the time, Pallas kernels for 15%

profile of v4, /device:TPU:0, one launch (start us, length us, event | category | flops | bytes accessed | tf_op | source)
XLA Modules:
  0.0 96.0 jit_solution(7625804338293992221)
XLA Ops:
  0.7 2.8 %constant_dynamic-slice_fusion = (bf16[48,64,128]{2,1,0:T(8,128)(2,1)}, bf16[48,64,128]{2,1,0:T(8,128)(2,1)}) fusion(bf16[64,64,128]{2,1,0:T(8,128)(2,1)} %volume_ref.1, s32[]{:T(128)S(6)} %select_n.18, s32[]{:T(128)S(6)} %select_n.17), kind=kLoop, calls=%fused_computation.29 | loop fusion | bytes 3145736 | tf_op jit(solution)/shard_map/dynamic_slice | solution.py:486
  4.0 1.6 %collective-permute-start.3 = (bf16[48,64,128]{2,1,0:T(8,128)(2,1)}, bf16[48,64,128]{2,1,0:T(8,128)(2,1)}, u32[]{:S(2)}, u32[]{:S(2)}) collective-permute-start(bf16[48,64,128]{2,1,0:T(8,128)(2,1)} %get-tuple-element.36), channel_id=1, source_target_pairs={{4,8},{8,4},{12,16},{16,12},{20,24},{24,20},{5,9},{9,5},{13,17},{1... | collective-permute-start | bytes 2359304 | tf_op jit(solution)/shard_map/ppermute | solution.py:354
  7.6 5.3 %collective-permute-start.1 = (s32[3,1,1,16]{3,2,1,0:T(1,128)S(1)}, s32[3,1,1,16]{3,2,1,0:T(1,128)S(1)}, u32[]{:S(2)}, u32[]{:S(2)}) collective-permute-start(s32[3,1,1,16]{3,2,1,0:T(1,128)S(1)} %copy-done.4), channel_id=1, source_target_pairs={{0,1},{1,0},{2,3},{3,2},{4,5},{5,4},{6,7},{7,6},{8,9},{9,8},{10,11... | collective-permute-start | bytes 584 | tf_op jit(solution)/shard_map/ppermute | solution.py:354
  13.0 1.5 %collective-permute-done.1.first_pick_ref = s32[3,1,1,16]{3,2,1,0:T(1,128)S(1)} collective-permute-done((s32[3,1,1,16]{3,2,1,0:T(1,128)S(1)}, s32[3,1,1,16]{3,2,1,0:T(1,128)S(1)}, u32[]{:S(2)}, u32[]{:S(2)}) %collective-permute-start.1) | collective-permute-done | bytes 224 | tf_op jit(solution)/shard_map/ppermute | solution.py:354
  14.5 4.8 %near_rows.1.near_ref = f32[304,768]{1,0:T(8,128)S(1)} custom-call(s32[3]{0:T(128)S(1)} %pad_add_fusion.origin_ref, s32[3,1,1,16]{3,2,1,0:T(1,128)S(1)} %collective-permute-done.1.first_pick_ref, s32[3,1,1,16]{3,2,1,0:T(1,128)S(1)} %copy-done.4, s32[3,1,1,16]{3,2,1,0:T(1,128)S(1)} %collective-permute-done.2.second_pick_ref, f32[128,128]{1,0:T(8,128)S(1)} %copy-done.3, ...), custom_call_target="tpu_custom_call" | custom-call | flops 2717908992 | bytes 8000000 | tf_op jit(solution)/shard_map/near_rows/pallas_call | solution.py:508
  19.4 7.9 %far_rows.1 = (bf16[256,256]{1,0:T(8,128)(2,1)S(1)}, f32[256,256]{1,0:T(8,128)S(1)}, bf16[256,256]{1,0:T(8,128)(2,1)S(1)}) custom-call(s32[3]{0:T(128)S(1)} %pad_add_fusion.origin_ref, s32[3,1,1,16]{3,2,1,0:T(1,128)S(1)} %collective-permute-done.1.first_pick_ref, s32[3,1,1,16]{3,2,1,0:T(1,128)S(1)} %copy-done.4, ...), custom_call_target="tpu_custom_call" | custom-call | tf_op jit(solution)/shard_map/far_rows/pallas_call | solution.py:520
  27.3 2.1 %collective-permute-start.4 = (bf16[256,256]{1,0:T(8,128)(2,1)S(1)}, bf16[256,256]{1,0:T(8,128)(2,1)S(1)}, u32[]{:S(2)}, u32[]{:S(2)}) collective-permute-start(bf16[256,256]{1,0:T(8,128)(2,1)S(1)} %get-tuple-element.22), channel_id=1, source_target_pairs={{0,1},{1,0},{2,3},{3,2},{4,5},{5,4},{6,7},{7,6},{8,9},{9,8},{10,11... | collective-permute-start | bytes 393224 | tf_op jit(solution)/shard_map/ppermute | solution.py:354
  30.3 3.4 %collective-permute-done.4.left_ref = bf16[256,256]{1,0:T(8,128)(2,1)S(1)} collective-permute-done((bf16[256,256]{1,0:T(8,128)(2,1)S(1)}, bf16[256,256]{1,0:T(8,128)(2,1)S(1)}, u32[]{:S(2)}, u32[]{:S(2)}) %collective-permute-start.4) | collective-permute-done | bytes 131104 | tf_op jit(solution)/shard_map/ppermute | solution.py:354
  33.7 3.3 %join.1 = (bf16[8,4480]{1,0:T(8,128)(2,1)S(1)}, bf16[8,4480]{1,0:T(8,128)(2,1)S(1)}) custom-call(f32[256,256]{1,0:T(8,128)S(1)} %get-tuple-element.21.own_ref, bf16[256,256]{1,0:T(8,128)(2,1)S(1)} %collective-permute-done.4.left_ref, bf16[256,256]{1,0:T(8,128)(2,1)S(1)} %collective-permute-done.5.right_ref, ...), custom_call_target="tpu_custom_call" | custom-call | tf_op jit(solution)/shard_map/join/pallas_call | solution.py:544
  37.0 3.7 %collective-permute-start.8 = (bf16[8,4480]{1,0:T(8,128)(2,1)S(1)}, bf16[8,4480]{1,0:T(8,128)(2,1)S(1)}, u32[]{:S(2)}, u32[]{:S(2)}) collective-permute-start(bf16[8,4480]{1,0:T(8,128)(2,1)S(1)} %get-tuple-element.25), channel_id=1, source_target_pairs={{0,24},{4,28},{8,16},{12,20},{16,8},{20,12},{24,0},{28,4},{1,25},{... | collective-permute-start | bytes 215048 | tf_op jit(solution)/shard_map/ppermute | solution.py:380
  41.4 2.2 %collective-permute-done.8 = bf16[8,4480]{1,0:T(8,128)(2,1)S(1)} collective-permute-done((bf16[8,4480]{1,0:T(8,128)(2,1)S(1)}, bf16[8,4480]{1,0:T(8,128)(2,1)S(1)}, u32[]{:S(2)}, u32[]{:S(2)}) %collective-permute-start.8) | collective-permute-done | bytes 71712 | tf_op jit(solution)/shard_map/ppermute | solution.py:380
  43.6 3.1 %collective-permute-done.7 = bf16[8,4480]{1,0:T(8,128)(2,1)S(1)} collective-permute-done((bf16[8,4480]{1,0:T(8,128)(2,1)S(1)}, bf16[8,4480]{1,0:T(8,128)(2,1)S(1)}, u32[]{:S(2)}, u32[]{:S(2)}) %collective-permute-start.7) | collective-permute-done | bytes 71712 | tf_op jit(solution)/shard_map/ppermute | solution.py:380
  46.8 4.5 %collective-permute-start.10 = (bf16[32,4480]{1,0:T(8,128)(2,1)S(1)}, bf16[32,4480]{1,0:T(8,128)(2,1)S(1)}, u32[]{:S(2)}, u32[]{:S(2)}) collective-permute-start(bf16[32,4480]{1,0:T(8,128)(2,1)S(1)} %pad_maximum_fusion.1.refs_0_.refs_3_), channel_id=1, source_target_pairs={{0,2},{2,0},{1,3},{3,1},{4,6},{6,4},{5,7},{7,5},{8,10},{10,8},{9,1... | collective-permute-start | bytes 860168 | tf_op jit(solution)/shard_map/ppermute | solution.py:373
  51.4 2.2 %collective-permute-start.14 = (bf16[8,4480]{1,0:T(8,128)(2,1)S(1)}, bf16[8,4480]{1,0:T(8,128)(2,1)S(1)}, u32[]{:S(2)}, u32[]{:S(2)}) collective-permute-start(bf16[8,4480]{1,0:T(8,128)(2,1)S(1)} %get-tuple-element.27), channel_id=1, source_target_pairs={{0,24},{4,28},{8,16},{12,20},{16,8},{20,12},{24,0},{28,4},{1,25},{... | collective-permute-start | bytes 215048 | tf_op jit(solution)/shard_map/ppermute | solution.py:380
  53.6 2.2 %collective-permute-start.12 = (bf16[8,4480]{1,0:T(8,128)(2,1)S(1)}, bf16[8,4480]{1,0:T(8,128)(2,1)S(1)}, u32[]{:S(2)}, u32[]{:S(2)}) collective-permute-start(bf16[8,4480]{1,0:T(8,128)(2,1)S(1)} %get-tuple-element.27), channel_id=1, source_target_pairs={{0,8},{4,12},{8,0},{12,4},{16,24},{20,28},{24,16},{28,20},{1,9},{5... | collective-permute-start | bytes 215048 | tf_op jit(solution)/shard_map/ppermute | solution.py:380
  55.7 1.5 %collective-permute-done.10.refs_2_.refs_5_ = bf16[32,4480]{1,0:T(8,128)(2,1)S(1)} collective-permute-done((bf16[32,4480]{1,0:T(8,128)(2,1)S(1)}, bf16[32,4480]{1,0:T(8,128)(2,1)S(1)}, u32[]{:S(2)}, u32[]{:S(2)}) %collective-permute-start.10) | collective-permute-done | bytes 286752 | tf_op jit(solution)/shard_map/ppermute | solution.py:373
  57.3 1.5 %collective-permute-done.9.refs_1_.refs_4_ = bf16[32,4480]{1,0:T(8,128)(2,1)S(1)} collective-permute-done((bf16[32,4480]{1,0:T(8,128)(2,1)S(1)}, bf16[32,4480]{1,0:T(8,128)(2,1)S(1)}, u32[]{:S(2)}, u32[]{:S(2)}) %collective-permute-start.9) | collective-permute-done | bytes 286752 | tf_op jit(solution)/shard_map/ppermute | solution.py:370
  59.6 2.0 %collective-permute-start.16 = (bf16[48,4480]{1,0:T(8,128)(2,1)S(1)}, bf16[48,4480]{1,0:T(8,128)(2,1)S(1)}, u32[]{:S(2)}, u32[]{:S(2)}) collective-permute-start(bf16[48,4480]{1,0:T(8,128)(2,1)S(1)} %get-tuple-element.40), channel_id=1, source_target_pairs={{0,2},{2,0},{1,3},{3,1},{4,6},{6,4},{5,7},{7,5},{8,10},{10,8},{9,1... | collective-permute-start | bytes 1290248 | tf_op jit(solution)/shard_map/ppermute | solution.py:373
  61.7 4.7 %weigh.3.refs_0_ = bf16[20,64,192]{2,1,0:T(8,128)(2,1)S(1)} custom-call(s32[1]{0:T(128)} %bitcast.index_ref, bf16[32,4480]{1,0:T(8,128)(2,1)S(1)} %pad_maximum_fusion.1.refs_0_.refs_3_, bf16[32,4480]{1,0:T(8,128)(2,1)S(1)} %collective-permute-done.9.refs_1_.refs_4_, bf16[32,4480]{1,0:T(8,128)(2,1)S(1)} %collective-permute-done.10.refs_2_.refs_5_, ...), custom_call_target="tpu_custom_call" | custom-call | flops 2013265920 | bytes 10485760 | tf_op jit(solution)/shard_map/weigh/pallas_call | solution.py:421
  66.4 5.0 %collective-permute-done.16.refs_2_.refs_9_ = bf16[48,4480]{1,0:T(8,128)(2,1)S(1)} collective-permute-done((bf16[48,4480]{1,0:T(8,128)(2,1)S(1)}, bf16[48,4480]{1,0:T(8,128)(2,1)S(1)}, u32[]{:S(2)}, u32[]{:S(2)}) %collective-permute-start.16) | collective-permute-done | bytes 430112 | tf_op jit(solution)/shard_map/ppermute | solution.py:373
  71.8 1.6 %collective-permute-start.18 = (bf16[16,4480]{1,0:T(8,128)(2,1)S(1)}, bf16[16,4480]{1,0:T(8,128)(2,1)S(1)}, u32[]{:S(2)}, u32[]{:S(2)}) collective-permute-start(bf16[16,4480]{1,0:T(8,128)(2,1)S(1)} %slice.14), channel_id=1, source_target_pairs={{0,1},{1,0},{2,3},{3,2},{4,5},{5,4},{6,7},{7,6},{8,9},{9,8},{10,11... | collective-permute-start | bytes 430088 | tf_op jit(solution)/shard_map/ppermute | solution.py:370
  74.6 5.0 %weigh.4.refs_1_ = bf16[20,64,256]{2,1,0:T(8,128)(2,1)S(1)} custom-call(s32[1]{0:T(128)} %bitcast.index_ref, bf16[32,4480]{1,0:T(8,128)(2,1)S(1)} %get-tuple-element.39.refs_0_.refs_7_, bf16[48,4480]{1,0:T(8,128)(2,1)S(1)} %collective-permute-done.15.refs_1_.refs_8_, bf16[48,4480]{1,0:T(8,128)(2,1)S(1)} %collective-permute-done.16.refs_2_.refs_9_, ...), custom_call_target="tpu_custom_call" | custom-call | flops 2684354560 | bytes 10485760 | tf_op jit(solution)/shard_map/weigh/pallas_call | solution.py:421
  81.3 4.2 %weigh.5.refs_2_ = bf16[20,64,64]{2,1,0:T(8,128)(2,1)S(1)} custom-call(s32[1]{0:T(128)} %bitcast.index_ref, bf16[16,4480]{1,0:T(8,128)(2,1)S(1)} %collective-permute-done.18.refs_0_.refs_11_, bf16[16,4480]{1,0:T(8,128)(2,1)S(1)} %collective-permute-done.19.refs_1_.refs_12_, bf16[32,4480]{1,0:T(8,128)(2,1)S(1)} %collective-permute-done.20.refs_2_.refs_13_, ...), custom_call_target="tpu_custom_call" | custom-call | flops 671088640 | bytes 10485760 | tf_op jit(solution)/shard_map/weigh/pallas_call | solution.py:421
  85.5 10.3 %class_sums.1 = (f32[20,64,4096]{2,1,0:T(8,128)}, f32[20,64]{1,0:T(8,128)}) custom-call(bf16[20,64,192]{2,1,0:T(8,128)(2,1)S(1)} %weigh.3.refs_0_, bf16[20,64,256]{2,1,0:T(8,128)(2,1)S(1)} %weigh.4.refs_1_, bf16[20,64,64]{2,1,0:T(8,128)(2,1)S(1)} %weigh.5.refs_2_, bf16[32,4480]{1,0:T(8,128)(2,1)S(1)} %pad_maximum_fusion.1.refs_0_.refs_3_, ...), custom_call_target="tpu_custom_call" | custom-call | flops 5368709120 | bytes 20971520 | tf_op jit(solution)/shard_map/class_sums/pallas_call | solution.py:450
  (65 shorter events, 7.8 us)
Async XLA Ops:
  3.5 3.4 %collective-permute-start = (bf16[48,64,128]{2,1,0:T(8,128)(2,1)}, bf16[48,64,128]{2,1,0:T(8,128)(2,1)}, u32[]{:S(2)}, u32[]{:S(2)}) collective-permute-start(bf16[48,64,128]{2,1,0:T(8,128)(2,1)} %get-tuple-element.37), channel_id=1, source_target_pairs={{0,4},{4,0},{8,12},{12,8},{16,20},{20,16},{24,28},{28,24},{1,5},{5... | collective-permute-start | bytes 2359304 | tf_op jit(solution)/shard_map/ppermute | solution.py:354
  4.0 15.4 %collective-permute-start.3 = (bf16[48,64,128]{2,1,0:T(8,128)(2,1)}, bf16[48,64,128]{2,1,0:T(8,128)(2,1)}, u32[]{:S(2)}, u32[]{:S(2)}) collective-permute-start(bf16[48,64,128]{2,1,0:T(8,128)(2,1)} %get-tuple-element.36), channel_id=1, source_target_pairs={{4,8},{8,4},{12,16},{16,12},{20,24},{24,20},{5,9},{9,5},{13,17},{1... | collective-permute-start | bytes 2359304 | tf_op jit(solution)/shard_map/ppermute | solution.py:354
  7.0 6.0 %collective-permute-start.2 = (s32[3,1,1,16]{3,2,1,0:T(1,128)S(1)}, s32[3,1,1,16]{3,2,1,0:T(1,128)S(1)}, u32[]{:S(2)}, u32[]{:S(2)}) collective-permute-start(s32[3,1,1,16]{3,2,1,0:T(1,128)S(1)} %copy-done.4), channel_id=1, source_target_pairs={{1,2},{2,1},{5,6},{6,5},{9,10},{10,9},{13,14},{14,13},{17,18},{18,... | collective-permute-start | bytes 584 | tf_op jit(solution)/shard_map/ppermute | solution.py:354
  7.6 6.9 %collective-permute-start.1 = (s32[3,1,1,16]{3,2,1,0:T(1,128)S(1)}, s32[3,1,1,16]{3,2,1,0:T(1,128)S(1)}, u32[]{:S(2)}, u32[]{:S(2)}) collective-permute-start(s32[3,1,1,16]{3,2,1,0:T(1,128)S(1)} %copy-done.4), channel_id=1, source_target_pairs={{0,1},{1,0},{2,3},{3,2},{4,5},{5,4},{6,7},{7,6},{8,9},{9,8},{10,11... | collective-permute-start | bytes 584 | tf_op jit(solution)/shard_map/ppermute | solution.py:354
  14.5 47.2 %slice-start = ((s8[10485760]{0:T(1024)(128)(4,1)}), s8[4194304]{0:T(1024)(128)(4,1)S(1)}, s32[]{:S(2)}) async-start(s8[10485760]{0:T(1024)(128)(4,1)} %bitcast.12), calls=%async_computation | async-start | bytes 8388608
  14.5 47.2 %slice-start.1 = ((s8[10485760]{0:T(1024)(128)(4,1)}), s8[4194304]{0:T(1024)(128)(4,1)S(1)}, s32[]{:S(2)}) async-start(s8[10485760]{0:T(1024)(128)(4,1)} %bitcast.12), calls=%async_computation.1 | async-start | bytes 8388608
  19.4 42.3 %slice-start.2 = ((s8[10485760]{0:T(1024)(128)(4,1)}), s8[2097152]{0:T(1024)(128)(4,1)S(1)}, s32[]{:S(2)}) async-start(s8[10485760]{0:T(1024)(128)(4,1)} %bitcast.12), calls=%async_computation.2 | async-start | bytes 4194304
  27.3 6.4 %collective-permute-start.4 = (bf16[256,256]{1,0:T(8,128)(2,1)S(1)}, bf16[256,256]{1,0:T(8,128)(2,1)S(1)}, u32[]{:S(2)}, u32[]{:S(2)}) collective-permute-start(bf16[256,256]{1,0:T(8,128)(2,1)S(1)} %get-tuple-element.22), channel_id=1, source_target_pairs={{0,1},{1,0},{2,3},{3,2},{4,5},{5,4},{6,7},{7,6},{8,9},{9,8},{10,11... | collective-permute-start | bytes 393224 | tf_op jit(solution)/shard_map/ppermute | solution.py:354
  29.4 4.3 %collective-permute-start.5 = (bf16[256,256]{1,0:T(8,128)(2,1)S(1)}, bf16[256,256]{1,0:T(8,128)(2,1)S(1)}, u32[]{:S(2)}, u32[]{:S(2)}) collective-permute-start(bf16[256,256]{1,0:T(8,128)(2,1)S(1)} %get-tuple-element.23), channel_id=1, source_target_pairs={{1,2},{2,1},{5,6},{6,5},{9,10},{10,9},{13,14},{14,13},{17,18},{18,... | collective-permute-start | bytes 393224 | tf_op jit(solution)/shard_map/ppermute | solution.py:354
  37.0 6.6 %collective-permute-start.8 = (bf16[8,4480]{1,0:T(8,128)(2,1)S(1)}, bf16[8,4480]{1,0:T(8,128)(2,1)S(1)}, u32[]{:S(2)}, u32[]{:S(2)}) collective-permute-start(bf16[8,4480]{1,0:T(8,128)(2,1)S(1)} %get-tuple-element.25), channel_id=1, source_target_pairs={{0,24},{4,28},{8,16},{12,20},{16,8},{20,12},{24,0},{28,4},{1,25},{... | collective-permute-start | bytes 215048 | tf_op jit(solution)/shard_map/ppermute | solution.py:380
  40.7 6.1 %collective-permute-start.7 = (bf16[8,4480]{1,0:T(8,128)(2,1)S(1)}, bf16[8,4480]{1,0:T(8,128)(2,1)S(1)}, u32[]{:S(2)}, u32[]{:S(2)}) collective-permute-start(bf16[8,4480]{1,0:T(8,128)(2,1)S(1)} %get-tuple-element.25), channel_id=1, source_target_pairs={{0,16},{4,20},{8,24},{12,28},{16,0},{20,4},{24,8},{28,12},{1,17},{... | collective-permute-start | bytes 215048 | tf_op jit(solution)/shard_map/ppermute | solution.py:380
  40.7 6.1 %collective-permute-start.6 = (bf16[8,4480]{1,0:T(8,128)(2,1)S(1)}, bf16[8,4480]{1,0:T(8,128)(2,1)S(1)}, u32[]{:S(2)}, u32[]{:S(2)}) collective-permute-start(bf16[8,4480]{1,0:T(8,128)(2,1)S(1)} %get-tuple-element.25), channel_id=1, source_target_pairs={{0,8},{4,12},{8,0},{12,4},{16,24},{20,28},{24,16},{28,20},{1,9},{5... | collective-permute-start | bytes 215048 | tf_op jit(solution)/shard_map/ppermute | solution.py:380
  46.8 10.5 %collective-permute-start.10 = (bf16[32,4480]{1,0:T(8,128)(2,1)S(1)}, bf16[32,4480]{1,0:T(8,128)(2,1)S(1)}, u32[]{:S(2)}, u32[]{:S(2)}) collective-permute-start(bf16[32,4480]{1,0:T(8,128)(2,1)S(1)} %pad_maximum_fusion.1.refs_0_.refs_3_), channel_id=1, source_target_pairs={{0,2},{2,0},{1,3},{3,1},{4,6},{6,4},{5,7},{7,5},{8,10},{10,8},{9,1... | collective-permute-start | bytes 860168 | tf_op jit(solution)/shard_map/ppermute | solution.py:373
  51.3 7.5 %collective-permute-start.9 = (bf16[32,4480]{1,0:T(8,128)(2,1)S(1)}, bf16[32,4480]{1,0:T(8,128)(2,1)S(1)}, u32[]{:S(2)}, u32[]{:S(2)}) collective-permute-start(bf16[32,4480]{1,0:T(8,128)(2,1)S(1)} %pad_maximum_fusion.1.refs_0_.refs_3_), channel_id=1, source_target_pairs={{0,1},{1,0},{2,3},{3,2},{4,5},{5,4},{6,7},{7,6},{8,9},{9,8},{10,11... | collective-permute-start | bytes 860168 | tf_op jit(solution)/shard_map/ppermute | solution.py:370
  51.4 8.2 %collective-permute-start.14 = (bf16[8,4480]{1,0:T(8,128)(2,1)S(1)}, bf16[8,4480]{1,0:T(8,128)(2,1)S(1)}, u32[]{:S(2)}, u32[]{:S(2)}) collective-permute-start(bf16[8,4480]{1,0:T(8,128)(2,1)S(1)} %get-tuple-element.27), channel_id=1, source_target_pairs={{0,24},{4,28},{8,16},{12,20},{16,8},{20,12},{24,0},{28,4},{1,25},{... | collective-permute-start | bytes 215048 | tf_op jit(solution)/shard_map/ppermute | solution.py:380
  53.6 6.0 %collective-permute-start.13 = (bf16[8,4480]{1,0:T(8,128)(2,1)S(1)}, bf16[8,4480]{1,0:T(8,128)(2,1)S(1)}, u32[]{:S(2)}, u32[]{:S(2)}) collective-permute-start(bf16[8,4480]{1,0:T(8,128)(2,1)S(1)} %get-tuple-element.27), channel_id=1, source_target_pairs={{0,16},{4,20},{8,24},{12,28},{16,0},{20,4},{24,8},{28,12},{1,17},{... | collective-permute-start | bytes 215048 | tf_op jit(solution)/shard_map/ppermute | solution.py:380
  53.6 5.4 %collective-permute-start.12 = (bf16[8,4480]{1,0:T(8,128)(2,1)S(1)}, bf16[8,4480]{1,0:T(8,128)(2,1)S(1)}, u32[]{:S(2)}, u32[]{:S(2)}) collective-permute-start(bf16[8,4480]{1,0:T(8,128)(2,1)S(1)} %get-tuple-element.27), channel_id=1, source_target_pairs={{0,8},{4,12},{8,0},{12,4},{16,24},{20,28},{24,16},{28,20},{1,9},{5... | collective-permute-start | bytes 215048 | tf_op jit(solution)/shard_map/ppermute | solution.py:380
  58.8 2.9 %collective-permute-start.11 = (bf16[96,4480]{1,0:T(8,128)(2,1)S(1)}, bf16[96,4480]{1,0:T(8,128)(2,1)S(1)}, u32[]{:S(2)}, u32[]{:S(2)}) collective-permute-start(bf16[96,4480]{1,0:T(8,128)(2,1)S(1)} %pad_maximum_fusion), channel_id=1, source_target_pairs={{0,4},{4,0},{8,12},{12,8},{16,20},{20,16},{24,28},{28,24},{1,5},{5... | collective-permute-start | bytes 2580488 | tf_op jit(solution)/shard_map/ppermute | solution.py:376
  59.6 11.8 %collective-permute-start.16 = (bf16[48,4480]{1,0:T(8,128)(2,1)S(1)}, bf16[48,4480]{1,0:T(8,128)(2,1)S(1)}, u32[]{:S(2)}, u32[]{:S(2)}) collective-permute-start(bf16[48,4480]{1,0:T(8,128)(2,1)S(1)} %get-tuple-element.40), channel_id=1, source_target_pairs={{0,2},{2,0},{1,3},{3,1},{4,6},{6,4},{5,7},{7,5},{8,10},{10,8},{9,1... | collective-permute-start | bytes 1290248 | tf_op jit(solution)/shard_map/ppermute | solution.py:373
  61.6 10.0 %collective-permute-start.15 = (bf16[48,4480]{1,0:T(8,128)(2,1)S(1)}, bf16[48,4480]{1,0:T(8,128)(2,1)S(1)}, u32[]{:S(2)}, u32[]{:S(2)}) collective-permute-start(bf16[48,4480]{1,0:T(8,128)(2,1)S(1)} %get-tuple-element.41), channel_id=1, source_target_pairs={{0,1},{1,0},{2,3},{3,2},{4,5},{5,4},{6,7},{7,6},{8,9},{9,8},{10,11... | collective-permute-start | bytes 1290248 | tf_op jit(solution)/shard_map/ppermute | solution.py:370
  71.7 2.9 %collective-permute-start.17 = (bf16[128,4480]{1,0:T(8,128)(2,1)S(1)}, bf16[128,4480]{1,0:T(8,128)(2,1)S(1)}, u32[]{:S(2)}, u32[]{:S(2)}) collective-permute-start(bf16[128,4480]{1,0:T(8,128)(2,1)S(1)} %constant_dynamic-update-slice_fusion.12), channel_id=1, source_target_pairs={{0,4},{4,0},{8,12},{12,8},{16,20},{20,16},{24,28},{28,24},{1,5},{5... | collective-permute-start | bytes 3440648 | tf_op jit(solution)/shard_map/ppermute | solution.py:376
  71.8 7.7 %collective-permute-start.18 = (bf16[16,4480]{1,0:T(8,128)(2,1)S(1)}, bf16[16,4480]{1,0:T(8,128)(2,1)S(1)}, u32[]{:S(2)}, u32[]{:S(2)}) collective-permute-start(bf16[16,4480]{1,0:T(8,128)(2,1)S(1)} %slice.14), channel_id=1, source_target_pairs={{0,1},{1,0},{2,3},{3,2},{4,5},{5,4},{6,7},{7,6},{8,9},{9,8},{10,11... | collective-permute-start | bytes 430088 | tf_op jit(solution)/shard_map/ppermute | solution.py:370
  73.5 6.1 %collective-permute-start.19 = (bf16[16,4480]{1,0:T(8,128)(2,1)S(1)}, bf16[16,4480]{1,0:T(8,128)(2,1)S(1)}, u32[]{:S(2)}, u32[]{:S(2)}) collective-permute-start(bf16[16,4480]{1,0:T(8,128)(2,1)S(1)} %slice.15), channel_id=1, source_target_pairs={{0,2},{2,0},{1,3},{3,1},{4,6},{6,4},{5,7},{7,5},{8,10},{10,8},{9,1... | collective-permute-start | bytes 430088 | tf_op jit(solution)/shard_map/ppermute | solution.py:373
  79.6 1.6 %collective-permute-start.20 = (bf16[32,4480]{1,0:T(8,128)(2,1)S(1)}, bf16[32,4480]{1,0:T(8,128)(2,1)S(1)}, u32[]{:S(2)}, u32[]{:S(2)}) collective-permute-start(bf16[32,4480]{1,0:T(8,128)(2,1)S(1)} %pad_maximum_fusion.2), channel_id=1, source_target_pairs={{0,4},{4,0},{8,12},{12,8},{16,20},{20,16},{24,28},{28,24},{1,5},{5... | collective-permute-start | bytes 860168 | tf_op jit(solution)/shard_map/ppermute | solution.py:376
  (7 other events, 72.6 us)

commit v5 on v4

--- a/solution.py
+++ b/solution.py
@@ -253,7 +253,7 @@
         out_ref[...] = row[k * count : (k + 1) * count]
 
 
-def load_blocks(blocks, rows_ref, tail_ref, sems):
+def block_copies(blocks, rows_ref, tail_ref, sems):
     copies, at = [], 0
     for k, block in enumerate(blocks):
         count = block.shape[0]
@@ -268,59 +268,90 @@
                 )
             )
         at += count
-    for copy in copies:
-        copy.start()
-    for copy in copies:
-        copy.wait()
-
-
-def read_tail(bank_ref, tail, tail_ref, multiplicity_ref, norm_ref, orients):
+    return copies
+
+
+def read_tail(bank_ref, tail, tail_ref, multiplicity_ref, orients):
     tail_ref[...] = tail.astype(jnp.float32).T
     start = pl.multiple_of(bank_ref[0] * orients, orients)
-    multiplicity_ref[...] = tail_ref[pl.ds(start, orients), :]
-    norm_ref[...] = tail_ref[R : R + 1, :] + tail_ref[R + 1 : R + 2, :]
-
-
-def weigh(bank_rows, rows, multiplicity, norm, count):
+    norm = tail_ref[R : R + 1, :] + tail_ref[R + 1 : R + 2, :]
+    multiplicity_ref[...] = tail_ref[pl.ds(start, orients), :] / (F * norm)
+
+
+def inverse_norms(bank_rows):
+    wide = bank_rows.astype(jnp.float32)
+    return 1.0 / jnp.sqrt(jnp.mean(wide * wide, axis=1, keepdims=True) + EPSILON)
+
+
+def weigh(bank_rows, inverse, rows, multiplicity, count):
     scores = lax.dot_general(
         bank_rows, rows, (((1,), (1,)), ((), ())), preferred_element_type=jnp.float32
     )
-    wide = bank_rows.astype(jnp.float32)
-    bank_norm = jnp.sqrt(jnp.mean(wide * wide, axis=1, keepdims=True) + EPSILON)
-    correl = scores / (F * norm * bank_norm)
     multiplicity = jnp.concatenate([multiplicity] * count, axis=0)
-    return (multiplicity * jnp.maximum(correl, 0.0)).astype(jnp.bfloat16)
-
-
-def weigh_kernel(index_ref, *refs, blocks):
-    sources, (bank_ref, out_ref) = refs[:blocks], refs[blocks : blocks + 2]
-    rows_ref, tail_ref, turned_ref, multiplicity_ref, norm_ref, sems = refs[blocks + 2 :]
+    return (multiplicity * jnp.maximum(scores * inverse, 0.0)).astype(jnp.bfloat16)
+
+
+def weigh_kernel(index_ref, *refs, blocks, known):
+    sources, bank_ref = refs[:blocks], refs[blocks]
+    if known:
+        norms_ref, out_ref = refs[blocks + 1 : blocks + 3]
+    else:
+        out_ref, norms_ref = refs[blocks + 1 : blocks + 3]
+    rows_ref, tail_ref, turned_ref, multiplicity_ref, sems = refs[blocks + 3 :]
     count, orients, width = bank_ref.shape
 
     @pl.when(pl.program_id(0) == 0)
     def _():
-        load_blocks(sources, rows_ref, tail_ref, sems)
-        read_tail(index_ref, tail_ref[...], turned_ref, multiplicity_ref, norm_ref, orients)
+        copies = block_copies(sources, rows_ref, tail_ref, sems)
+        for copy in copies:
+            copy.start()
+        for copy in copies:
+            copy.wait()
+        read_tail(index_ref, tail_ref[...], turned_ref, multiplicity_ref, orients)
 
     bank = bank_ref[...].reshape(count * orients, width)
-    weights = weigh(bank, rows_ref[...], multiplicity_ref[...], norm_ref[...], count)
+    if known:
+        inverse = norms_ref[...].reshape(count * orients, norms_ref.shape[2])[:, :1]
+    else:
+        inverse = inverse_norms(bank)
+        norms_ref[...] = jnp.broadcast_to(inverse, (count * orients, norms_ref.shape[2])).reshape(
+            norms_ref.shape
+        )
+    weights = weigh(bank, inverse, rows_ref[...], multiplicity_ref[...], count)
     out_ref[...] = weights.reshape(out_ref.shape)
 
 
-def sum_kernel(*refs, early, blocks):
+def sum_kernel(index_ref, *refs, early, blocks, late, group):
     parts, sources = refs[:early], refs[early : early + blocks]
-    out_ref, sums_ref, rows_ref, sems = refs[early + blocks :]
+    norms_ref, bank_ref, out_ref, sums_ref = refs[early + blocks : early + blocks + 4]
+    rows_ref, last_ref, tail_ref, turned_ref, multiplicity_ref, weights_ref, sems, last_sems = refs[
+        early + blocks + 4 :
+    ]
     count, orients, width = out_ref.shape
-    boxes = rows_ref.shape[0]
+    boxes, last = rows_ref.shape[0], last_ref.shape[0]
     step = pl.program_id(0)
 
     @pl.when(step == 0)
     def _():
-        load_blocks(sources, rows_ref, None, sems)
-
-    weights = jnp.concatenate(
-        [part[...].reshape(count * orients, part.shape[2]) for part in parts], axis=1
-    )
+        copies = block_copies(sources, rows_ref, None, sems)
+        urgent = block_copies(sources[blocks - late :], last_ref, tail_ref, last_sems)
+        for copy in urgent + copies:
+            copy.start()
+        for copy in urgent:
+            copy.wait()
+        read_tail(index_ref, tail_ref[...], turned_ref, multiplicity_ref, orients)
+        for c in range(0, bank_ref.shape[0], group):
+            bank = bank_ref[c : c + group].reshape(group * orients, width)
+            inverse = norms_ref[c : c + group].reshape(group * orients, norms_ref.shape[2])[:, :1]
+            weights = weigh(bank, inverse, last_ref[...], multiplicity_ref[...], group)
+            weights_ref[c : c + group] = weights.reshape(group, orients, last)
+        for copy in copies:
+            copy.wait()
+
+    known = [part[...].reshape(count * orients, part.shape[2]) for part in parts]
+    at = pl.multiple_of(step * count, count)
+    known.append(weights_ref[pl.ds(at, count)].reshape(count * orients, last))
+    weights = jnp.concatenate(known, axis=1)
     total = jnp.dot(weights, rows_ref[...], preferred_element_type=jnp.float32)
     out_ref[...] = total.reshape(out_ref.shape)
     ones = jnp.ones((8, boxes), jnp.bfloat16)
@@ -395,15 +426,14 @@
     to_y = jnp.concatenate([from_x[:half], late_line], axis=0)
     blocks = [with_swap(early_line, from_x, from_y)]
     next_x, next_y = along_x(to_x), along_y(to_y)
-    first = weigh_blocks(blocks[0], bank)
+    first, norms = weigh_blocks(blocks[0], bank)
     first, next_x, next_y = lax.optimization_barrier((first, next_x, next_y))
     last_x, last_y = along_x(next_y[half + half :]), along_y(next_x[half : half + half])
     blocks.append(with_swap(late_line, next_x, next_y))
-    second = weigh_blocks(blocks[1], bank)
+    second = weigh_blocks(blocks[1], bank, norms)
     second, last_x, last_y = lax.optimization_barrier((second, last_x, last_y))
-    blocks.append(with_swap(last_x, last_y))
-    third = weigh_blocks(blocks[2], bank)
-    out, sums = sum_blocks([first, second, third], sum(blocks, []), bank)
+    last = with_swap(last_x, last_y)
+    out, sums = sum_blocks([first, second], sum(blocks, []), last, norms, bank)
     return jnp.transpose(out, (1, 0, 2)), jnp.transpose(sums, (1, 0))
 
 
@@ -414,24 +444,29 @@
     return lax.axis_index("bank").astype(jnp.int32)[None]
 
 
-def weigh_blocks(blocks, bank):
+def weigh_blocks(blocks, bank, norms=None):
     classes, orients, width = bank.shape
     boxes = sum(block.shape[0] for block in blocks)
     tail = blocks[0].shape[1] - F
+    known = norms is not None
+    norm_spec = pl.BlockSpec((CLASSES, orients, 128), lambda i: (i, 0, 0))
+    out_spec = pl.BlockSpec((CLASSES, orients, boxes), lambda i: (i, 0, 0))
+    out_shape = jax.ShapeDtypeStruct((classes, orients, boxes), jnp.bfloat16)
+    norm_shape = jax.ShapeDtypeStruct((classes, orients, 128), jnp.float32)
     return pl.pallas_call(
-        functools.partial(weigh_kernel, blocks=len(blocks)),
+        functools.partial(weigh_kernel, blocks=len(blocks), known=known),
         grid=(classes // CLASSES,),
         in_specs=[pl.BlockSpec(memory_space=pltpu.SMEM)]
         + [pl.BlockSpec(memory_space=pl.ANY)] * len(blocks)
-        + [pl.BlockSpec((CLASSES, orients, width), lambda i: (i, 0, 0))],
-        out_specs=pl.BlockSpec((CLASSES, orients, boxes), lambda i: (i, 0, 0)),
-        out_shape=jax.ShapeDtypeStruct((classes, orients, boxes), jnp.bfloat16),
+        + [pl.BlockSpec((CLASSES, orients, width), lambda i: (i, 0, 0))]
+        + ([norm_spec] if known else []),
+        out_specs=out_spec if known else [out_spec, norm_spec],
+        out_shape=out_shape if known else [out_shape, norm_shape],
         scratch_shapes=[
             pltpu.VMEM((boxes, F), jnp.bfloat16),
             pltpu.VMEM((boxes, tail), jnp.bfloat16),
             pltpu.VMEM((tail, boxes), jnp.float32),
             pltpu.VMEM((orients, boxes), jnp.float32),
-            pltpu.VMEM((1, boxes), jnp.float32),
             pltpu.SemaphoreType.DMA((2 * len(blocks),)),
         ],
         compiler_params=pltpu.CompilerParams(vmem_limit_bytes=18 * MIB),
@@ -441,19 +476,25 @@
             transcendentals=0,
         ),
         name="weigh",
-    )(bank_index(), *blocks, bank)
-
-
-def sum_blocks(parts, blocks, bank):
+    )(bank_index(), *blocks, bank, *([norms] if known else []))
+
+
+def sum_blocks(parts, blocks, late, norms, bank):
     classes, orients, width = bank.shape
+    blocks = blocks + late
     boxes = sum(block.shape[0] for block in blocks)
+    last = sum(block.shape[0] for block in late)
+    tail = blocks[0].shape[1] - F
+    vmem = pl.BlockSpec(memory_space=pltpu.VMEM)
     return pl.pallas_call(
-        functools.partial(sum_kernel, early=len(parts), blocks=len(blocks)),
+        functools.partial(
+            sum_kernel, early=len(parts), blocks=len(blocks), late=len(late), group=CLASSES
+        ),
         grid=(classes // CLASSES,),
-        in_specs=[
-            pl.BlockSpec((CLASSES, orients, part.shape[2]), lambda i: (i, 0, 0)) for part in parts
-        ]
-        + [pl.BlockSpec(memory_space=pl.ANY)] * len(blocks),
+        in_specs=[pl.BlockSpec(memory_space=pltpu.SMEM)]
+        + [pl.BlockSpec((CLASSES, orients, part.shape[2]), lambda i: (i, 0, 0)) for part in parts]
+        + [pl.BlockSpec(memory_space=pl.ANY)] * len(blocks)
+        + [vmem, vmem],
         out_specs=[
             pl.BlockSpec((CLASSES, orients, width), lambda i: (i, 0, 0)),
             pl.BlockSpec((classes, orients), lambda i: (0, 0)),
@@ -464,16 +505,22 @@
         ],
         scratch_shapes=[
             pltpu.VMEM((boxes, F), jnp.bfloat16),
+            pltpu.VMEM((last, F), jnp.bfloat16),
+            pltpu.VMEM((last, tail), jnp.bfloat16),
+            pltpu.VMEM((tail, last), jnp.float32),
+            pltpu.VMEM((orients, last), jnp.float32),
+            pltpu.VMEM((classes, orients, last), jnp.bfloat16),
             pltpu.SemaphoreType.DMA((2 * len(blocks),)),
+            pltpu.SemaphoreType.DMA((2 * len(late),)),
         ],
-        compiler_params=pltpu.CompilerParams(vmem_limit_bytes=36 * MIB),
+        compiler_params=pltpu.CompilerParams(vmem_limit_bytes=34 * MIB),
         cost_estimate=pl.CostEstimate(
             flops=2 * boxes * classes * orients * width,
             bytes_accessed=4 * classes * orients * width,
             transcendentals=0,
         ),
         name="class_sums",
-    )(*parts, *blocks)
+    )(bank_index(), *parts, *blocks, norms, bank)
 
 
 def body(volume, pick_list, box_counts, orientations, orient_weight, reference_bank):

time: 96.1 us -> 94.8 us (0.986)
  Pallas kernels: 40.3 us -> 38.3 us
    pallas_call x3 -> x2, Pallas kernels: 13.9 us -> 8.85 us  [weigh_blocks(): pl.pallas_call(functools.partial(weigh_kernel, blocks=len(blocks), known=...]
    pallas_call x1, Pallas kernels: 10.3 us -> 13.4 us  [sum_blocks(): pl.pallas_call(functools.partial(sum_kernel, early=len(parts), blocks=len...]
  transfers between devices with their start and end apart: 21 -> 21, of which waited for: 12 -> 13; matrix products, arithmetic and copies ran while one was open for 1% -> 1% of each run, Pallas kernels for 15% -> 14%
where the time goes in v5:
time: 94.8 us; the launch traced here: 94.6 us
  Pallas kernels  38.3 us (40%)
  starting transfers between devices  28.5 us (30%)
  waiting for transfers between devices  21.9 us (23%)
  local copies, waits for them, and re-layouts  3.08 us (3%)
  between operations  1.79 us (2%)
  other arithmetic  0.98 us (1%)
    pallas_call x1, Pallas kernels, sum_blocks(): pl.pallas_call(functools.partial(sum_kernel, early=len(parts), blocks=len...  13.4 us
    ppermute x6, starting transfers between devices, exchange(): return lax.ppermute(value, axis, pairs)  10.9 us
    pallas_call x2, Pallas kernels, weigh_blocks(): pl.pallas_call(functools.partial(weigh_kernel, blocks=len(blocks), known=...  8.85 us
    ppermute x6, starting transfers between devices, line_of(): lax.ppermute(part, 'tile', [(i, i ^ by) for i in range(tiles)])  8.79 us
    pallas_call x1, Pallas kernels, body(): pl.pallas_call(functools.partial(far_kernel, wide=wide), in_specs=given +...  7.93 us
    ppermute x3, waiting for transfers between devices, along_y(): return lax.ppermute(value, 'bank', [(0, 2), (2, 0), (1, 3), (3, 1)])  7.09 us
    ppermute x3, starting transfers between devices, along_y(): return lax.ppermute(value, 'bank', [(0, 2), (2, 0), (1, 3), (3, 1)])  6.91 us
    ppermute x6, waiting for transfers between devices, line_of(): lax.ppermute(part, 'tile', [(i, i ^ by) for i in range(tiles)])  5.89 us
  transfers between devices with their start and end apart: 21, of which 13 were waited for; matrix products, arithmetic and copies ran while one was open for 1% of the time, Pallas kernels for 14%

profile of v5, /device:TPU:0, one launch (start us, length us, event | category | flops | bytes accessed | tf_op | source)
XLA Modules:
  0.0 94.6 jit_solution(1667931707259861667)
XLA Ops:
  0.7 2.8 %constant_dynamic-slice_fusion = (bf16[48,64,128]{2,1,0:T(8,128)(2,1)}, bf16[48,64,128]{2,1,0:T(8,128)(2,1)}) fusion(bf16[64,64,128]{2,1,0:T(8,128)(2,1)} %volume_ref.1, s32[]{:T(128)S(6)} %select_n.18, s32[]{:T(128)S(6)} %select_n.17), kind=kLoop, calls=%fused_computation.29 | loop fusion | bytes 3145736 | tf_op jit(solution)/shard_map/dynamic_slice | solution.py:533
  4.0 1.6 %collective-permute-start.3 = (bf16[48,64,128]{2,1,0:T(8,128)(2,1)}, bf16[48,64,128]{2,1,0:T(8,128)(2,1)}, u32[]{:S(2)}, u32[]{:S(2)}) collective-permute-start(bf16[48,64,128]{2,1,0:T(8,128)(2,1)} %get-tuple-element.40), channel_id=1, source_target_pairs={{4,8},{8,4},{12,16},{16,12},{20,24},{24,20},{5,9},{9,5},{13,17},{1... | collective-permute-start | bytes 2359304 | tf_op jit(solution)/shard_map/ppermute | solution.py:385
  7.6 5.3 %collective-permute-start.1 = (s32[3,1,1,16]{3,2,1,0:T(1,128)S(1)}, s32[3,1,1,16]{3,2,1,0:T(1,128)S(1)}, u32[]{:S(2)}, u32[]{:S(2)}) collective-permute-start(s32[3,1,1,16]{3,2,1,0:T(1,128)S(1)} %copy-done.4), channel_id=1, source_target_pairs={{0,1},{1,0},{2,3},{3,2},{4,5},{5,4},{6,7},{7,6},{8,9},{9,8},{10,11... | collective-permute-start | bytes 584 | tf_op jit(solution)/shard_map/ppermute | solution.py:385
  13.0 1.5 %collective-permute-done.1.first_pick_ref = s32[3,1,1,16]{3,2,1,0:T(1,128)S(1)} collective-permute-done((s32[3,1,1,16]{3,2,1,0:T(1,128)S(1)}, s32[3,1,1,16]{3,2,1,0:T(1,128)S(1)}, u32[]{:S(2)}, u32[]{:S(2)}) %collective-permute-start.1) | collective-permute-done | bytes 224 | tf_op jit(solution)/shard_map/ppermute | solution.py:385
  14.5 4.8 %near_rows.1.near_ref = f32[304,768]{1,0:T(8,128)S(1)} custom-call(s32[3]{0:T(128)S(1)} %pad_add_fusion.origin_ref, s32[3,1,1,16]{3,2,1,0:T(1,128)S(1)} %collective-permute-done.1.first_pick_ref, s32[3,1,1,16]{3,2,1,0:T(1,128)S(1)} %copy-done.4, s32[3,1,1,16]{3,2,1,0:T(1,128)S(1)} %collective-permute-done.2.second_pick_ref, f32[128,128]{1,0:T(8,128)S(1)} %copy-done.3, ...), custom_call_target="tpu_custom_call" | custom-call | flops 2717908992 | bytes 8000000 | tf_op jit(solution)/shard_map/near_rows/pallas_call | solution.py:555
  19.4 7.9 %far_rows.1 = (bf16[256,256]{1,0:T(8,128)(2,1)S(1)}, f32[256,256]{1,0:T(8,128)S(1)}, bf16[256,256]{1,0:T(8,128)(2,1)S(1)}) custom-call(s32[3]{0:T(128)S(1)} %pad_add_fusion.origin_ref, s32[3,1,1,16]{3,2,1,0:T(1,128)S(1)} %collective-permute-done.1.first_pick_ref, s32[3,1,1,16]{3,2,1,0:T(1,128)S(1)} %copy-done.4, ...), custom_call_target="tpu_custom_call" | custom-call | tf_op jit(solution)/shard_map/far_rows/pallas_call | solution.py:567
  27.3 2.1 %collective-permute-start.4 = (bf16[256,256]{1,0:T(8,128)(2,1)S(1)}, bf16[256,256]{1,0:T(8,128)(2,1)S(1)}, u32[]{:S(2)}, u32[]{:S(2)}) collective-permute-start(bf16[256,256]{1,0:T(8,128)(2,1)S(1)} %get-tuple-element.24), channel_id=1, source_target_pairs={{0,1},{1,0},{2,3},{3,2},{4,5},{5,4},{6,7},{7,6},{8,9},{9,8},{10,11... | collective-permute-start | bytes 393224 | tf_op jit(solution)/shard_map/ppermute | solution.py:385
  30.3 3.4 %collective-permute-done.4.left_ref = bf16[256,256]{1,0:T(8,128)(2,1)S(1)} collective-permute-done((bf16[256,256]{1,0:T(8,128)(2,1)S(1)}, bf16[256,256]{1,0:T(8,128)(2,1)S(1)}, u32[]{:S(2)}, u32[]{:S(2)}) %collective-permute-start.4) | collective-permute-done | bytes 131104 | tf_op jit(solution)/shard_map/ppermute | solution.py:385
  33.7 3.3 %join.1 = (bf16[8,4480]{1,0:T(8,128)(2,1)S(1)}, bf16[8,4480]{1,0:T(8,128)(2,1)S(1)}) custom-call(f32[256,256]{1,0:T(8,128)S(1)} %get-tuple-element.23.own_ref, bf16[256,256]{1,0:T(8,128)(2,1)S(1)} %collective-permute-done.4.left_ref, bf16[256,256]{1,0:T(8,128)(2,1)S(1)} %collective-permute-done.5.right_ref, ...), custom_call_target="tpu_custom_call" | custom-call | tf_op jit(solution)/shard_map/join/pallas_call | solution.py:591
  37.0 3.7 %collective-permute-start.8 = (bf16[8,4480]{1,0:T(8,128)(2,1)S(1)}, bf16[8,4480]{1,0:T(8,128)(2,1)S(1)}, u32[]{:S(2)}, u32[]{:S(2)}) collective-permute-start(bf16[8,4480]{1,0:T(8,128)(2,1)S(1)} %get-tuple-element.27), channel_id=1, source_target_pairs={{0,24},{4,28},{8,16},{12,20},{16,8},{20,12},{24,0},{28,4},{1,25},{... | collective-permute-start | bytes 215048 | tf_op jit(solution)/shard_map/ppermute | solution.py:411
  41.4 2.2 %collective-permute-done.8 = bf16[8,4480]{1,0:T(8,128)(2,1)S(1)} collective-permute-done((bf16[8,4480]{1,0:T(8,128)(2,1)S(1)}, bf16[8,4480]{1,0:T(8,128)(2,1)S(1)}, u32[]{:S(2)}, u32[]{:S(2)}) %collective-permute-start.8) | collective-permute-done | bytes 71712 | tf_op jit(solution)/shard_map/ppermute | solution.py:411
  43.6 3.1 %collective-permute-done.7 = bf16[8,4480]{1,0:T(8,128)(2,1)S(1)} collective-permute-done((bf16[8,4480]{1,0:T(8,128)(2,1)S(1)}, bf16[8,4480]{1,0:T(8,128)(2,1)S(1)}, u32[]{:S(2)}, u32[]{:S(2)}) %collective-permute-start.7) | collective-permute-done | bytes 71712 | tf_op jit(solution)/shard_map/ppermute | solution.py:411
  46.8 4.5 %collective-permute-start.10 = (bf16[32,4480]{1,0:T(8,128)(2,1)S(1)}, bf16[32,4480]{1,0:T(8,128)(2,1)S(1)}, u32[]{:S(2)}, u32[]{:S(2)}) collective-permute-start(bf16[32,4480]{1,0:T(8,128)(2,1)S(1)} %pad_maximum_fusion.1.refs_0_.refs_2_), channel_id=1, source_target_pairs={{0,2},{2,0},{1,3},{3,1},{4,6},{6,4},{5,7},{7,5},{8,10},{10,8},{9,1... | collective-permute-start | bytes 860168 | tf_op jit(solution)/shard_map/ppermute | solution.py:404
  51.4 2.2 %collective-permute-start.14 = (bf16[8,4480]{1,0:T(8,128)(2,1)S(1)}, bf16[8,4480]{1,0:T(8,128)(2,1)S(1)}, u32[]{:S(2)}, u32[]{:S(2)}) collective-permute-start(bf16[8,4480]{1,0:T(8,128)(2,1)S(1)} %get-tuple-element.30), channel_id=1, source_target_pairs={{0,24},{4,28},{8,16},{12,20},{16,8},{20,12},{24,0},{28,4},{1,25},{... | collective-permute-start | bytes 215048 | tf_op jit(solution)/shard_map/ppermute | solution.py:411
  53.6 2.2 %collective-permute-start.12 = (bf16[8,4480]{1,0:T(8,128)(2,1)S(1)}, bf16[8,4480]{1,0:T(8,128)(2,1)S(1)}, u32[]{:S(2)}, u32[]{:S(2)}) collective-permute-start(bf16[8,4480]{1,0:T(8,128)(2,1)S(1)} %get-tuple-element.30), channel_id=1, source_target_pairs={{0,8},{4,12},{8,0},{12,4},{16,24},{20,28},{24,16},{28,20},{1,9},{5... | collective-permute-start | bytes 215048 | tf_op jit(solution)/shard_map/ppermute | solution.py:411
  55.8 1.5 %collective-permute-done.10.refs_2_.refs_4_ = bf16[32,4480]{1,0:T(8,128)(2,1)S(1)} collective-permute-done((bf16[32,4480]{1,0:T(8,128)(2,1)S(1)}, bf16[32,4480]{1,0:T(8,128)(2,1)S(1)}, u32[]{:S(2)}, u32[]{:S(2)}) %collective-permute-start.10) | collective-permute-done | bytes 286752 | tf_op jit(solution)/shard_map/ppermute | solution.py:404
  57.3 1.5 %collective-permute-done.9.refs_1_.refs_3_ = bf16[32,4480]{1,0:T(8,128)(2,1)S(1)} collective-permute-done((bf16[32,4480]{1,0:T(8,128)(2,1)S(1)}, bf16[32,4480]{1,0:T(8,128)(2,1)S(1)}, u32[]{:S(2)}, u32[]{:S(2)}) %collective-permute-start.9) | collective-permute-done | bytes 286752 | tf_op jit(solution)/shard_map/ppermute | solution.py:401
  59.6 2.0 %collective-permute-start.16 = (bf16[48,4480]{1,0:T(8,128)(2,1)S(1)}, bf16[48,4480]{1,0:T(8,128)(2,1)S(1)}, u32[]{:S(2)}, u32[]{:S(2)}) collective-permute-start(bf16[48,4480]{1,0:T(8,128)(2,1)S(1)} %get-tuple-element.44), channel_id=1, source_target_pairs={{0,2},{2,0},{1,3},{3,1},{4,6},{6,4},{5,7},{7,5},{8,10},{10,8},{9,1... | collective-permute-start | bytes 1290248 | tf_op jit(solution)/shard_map/ppermute | solution.py:404
  61.7 4.7 %weigh.2 = (bf16[20,64,192]{2,1,0:T(8,128)(2,1)S(1)}, f32[20,64,128]{2,1,0:T(8,128)S(1)}) custom-call(s32[1]{0:T(128)} %bitcast.index_ref, bf16[32,4480]{1,0:T(8,128)(2,1)S(1)} %pad_maximum_fusion.1.refs_0_.refs_2_, bf16[32,4480]{1,0:T(8,128)(2,1)S(1)} %collective-permute-done.9.refs_1_.refs_3_, ...), custom_call_target="tpu_custom_call" | custom-call | flops 2013265920 | bytes 10485760 | tf_op jit(solution)/shard_map/weigh/pallas_call | solution.py:456
  66.4 5.0 %collective-permute-done.16.refs_2_.refs_8_ = bf16[48,4480]{1,0:T(8,128)(2,1)S(1)} collective-permute-done((bf16[48,4480]{1,0:T(8,128)(2,1)S(1)}, bf16[48,4480]{1,0:T(8,128)(2,1)S(1)}, u32[]{:S(2)}, u32[]{:S(2)}) %collective-permute-start.16) | collective-permute-done | bytes 430112 | tf_op jit(solution)/shard_map/ppermute | solution.py:404
  71.9 1.6 %collective-permute-start.18 = (bf16[16,4480]{1,0:T(8,128)(2,1)S(1)}, bf16[16,4480]{1,0:T(8,128)(2,1)S(1)}, u32[]{:S(2)}, u32[]{:S(2)}) collective-permute-start(bf16[16,4480]{1,0:T(8,128)(2,1)S(1)} %slice.14), channel_id=1, source_target_pairs={{0,1},{1,0},{2,3},{3,2},{4,5},{5,4},{6,7},{7,6},{8,9},{9,8},{10,11... | collective-permute-start | bytes 430088 | tf_op jit(solution)/shard_map/ppermute | solution.py:401
  74.6 4.1 %weigh.3.refs_1_ = bf16[20,64,256]{2,1,0:T(8,128)(2,1)S(1)} custom-call(s32[1]{0:T(128)} %bitcast.index_ref, bf16[32,4480]{1,0:T(8,128)(2,1)S(1)} %get-tuple-element.43.refs_0_.refs_6_, bf16[48,4480]{1,0:T(8,128)(2,1)S(1)} %collective-permute-done.15.refs_1_.refs_7_, bf16[48,4480]{1,0:T(8,128)(2,1)S(1)} %collective-permute-done.16.refs_2_.refs_8_, ...), custom_call_target="tpu_custom_call" | custom-call | flops 2684354560 | bytes 10485760 | tf_op jit(solution)/shard_map/weigh/pallas_call | solution.py:456
  79.5 1.6 %collective-permute-done.20.refs_12_ = bf16[32,4480]{1,0:T(8,128)(2,1)S(1)} collective-permute-done((bf16[32,4480]{1,0:T(8,128)(2,1)S(1)}, bf16[32,4480]{1,0:T(8,128)(2,1)S(1)}, u32[]{:S(2)}, u32[]{:S(2)}) %collective-permute-start.20) | collective-permute-done | bytes 286752 | tf_op jit(solution)/shard_map/ppermute | solution.py:407
  81.0 13.4 %class_sums.1 = (f32[20,64,4096]{2,1,0:T(8,128)}, f32[20,64]{1,0:T(8,128)}) custom-call(s32[1]{0:T(128)} %bitcast.index_ref, bf16[20,64,192]{2,1,0:T(8,128)(2,1)S(1)} %get-tuple-element.31.refs_0_, bf16[20,64,256]{2,1,0:T(8,128)(2,1)S(1)} %weigh.3.refs_1_, bf16[32,4480]{1,0:T(8,128)(2,1)S(1)} %pad_maximum_fusion.1.refs_0_.refs_2_, ...), custom_call_target="tpu_custom_call" | custom-call | flops 5368709120 | bytes 20971520 | tf_op jit(solution)/shard_map/class_sums/pallas_call | solution.py:489
  (64 shorter events, 6.9 us)
Async XLA Ops:
  3.5 3.4 %collective-permute-start = (bf16[48,64,128]{2,1,0:T(8,128)(2,1)}, bf16[48,64,128]{2,1,0:T(8,128)(2,1)}, u32[]{:S(2)}, u32[]{:S(2)}) collective-permute-start(bf16[48,64,128]{2,1,0:T(8,128)(2,1)} %get-tuple-element.41), channel_id=1, source_target_pairs={{0,4},{4,0},{8,12},{12,8},{16,20},{20,16},{24,28},{28,24},{1,5},{5... | collective-permute-start | bytes 2359304 | tf_op jit(solution)/shard_map/ppermute | solution.py:385
  4.0 15.4 %collective-permute-start.3 = (bf16[48,64,128]{2,1,0:T(8,128)(2,1)}, bf16[48,64,128]{2,1,0:T(8,128)(2,1)}, u32[]{:S(2)}, u32[]{:S(2)}) collective-permute-start(bf16[48,64,128]{2,1,0:T(8,128)(2,1)} %get-tuple-element.40), channel_id=1, source_target_pairs={{4,8},{8,4},{12,16},{16,12},{20,24},{24,20},{5,9},{9,5},{13,17},{1... | collective-permute-start | bytes 2359304 | tf_op jit(solution)/shard_map/ppermute | solution.py:385
  7.0 6.0 %collective-permute-start.2 = (s32[3,1,1,16]{3,2,1,0:T(1,128)S(1)}, s32[3,1,1,16]{3,2,1,0:T(1,128)S(1)}, u32[]{:S(2)}, u32[]{:S(2)}) collective-permute-start(s32[3,1,1,16]{3,2,1,0:T(1,128)S(1)} %copy-done.4), channel_id=1, source_target_pairs={{1,2},{2,1},{5,6},{6,5},{9,10},{10,9},{13,14},{14,13},{17,18},{18,... | collective-permute-start | bytes 584 | tf_op jit(solution)/shard_map/ppermute | solution.py:385
  7.6 6.9 %collective-permute-start.1 = (s32[3,1,1,16]{3,2,1,0:T(1,128)S(1)}, s32[3,1,1,16]{3,2,1,0:T(1,128)S(1)}, u32[]{:S(2)}, u32[]{:S(2)}) collective-permute-start(s32[3,1,1,16]{3,2,1,0:T(1,128)S(1)} %copy-done.4), channel_id=1, source_target_pairs={{0,1},{1,0},{2,3},{3,2},{4,5},{5,4},{6,7},{7,6},{8,9},{9,8},{10,11... | collective-permute-start | bytes 584 | tf_op jit(solution)/shard_map/ppermute | solution.py:385
  14.5 47.2 %slice-start = ((s8[10485760]{0:T(1024)(128)(4,1)}), s8[4194304]{0:T(1024)(128)(4,1)S(1)}, s32[]{:S(2)}) async-start(s8[10485760]{0:T(1024)(128)(4,1)} %bitcast.12), calls=%async_computation | async-start | bytes 8388608
  14.5 47.2 %slice-start.1 = ((s8[10485760]{0:T(1024)(128)(4,1)}), s8[4194304]{0:T(1024)(128)(4,1)S(1)}, s32[]{:S(2)}) async-start(s8[10485760]{0:T(1024)(128)(4,1)} %bitcast.12), calls=%async_computation.1 | async-start | bytes 8388608
  19.4 42.3 %slice-start.2 = ((s8[10485760]{0:T(1024)(128)(4,1)}), s8[2097152]{0:T(1024)(128)(4,1)S(1)}, s32[]{:S(2)}) async-start(s8[10485760]{0:T(1024)(128)(4,1)} %bitcast.12), calls=%async_computation.2 | async-start | bytes 4194304
  27.3 6.4 %collective-permute-start.4 = (bf16[256,256]{1,0:T(8,128)(2,1)S(1)}, bf16[256,256]{1,0:T(8,128)(2,1)S(1)}, u32[]{:S(2)}, u32[]{:S(2)}) collective-permute-start(bf16[256,256]{1,0:T(8,128)(2,1)S(1)} %get-tuple-element.24), channel_id=1, source_target_pairs={{0,1},{1,0},{2,3},{3,2},{4,5},{5,4},{6,7},{7,6},{8,9},{9,8},{10,11... | collective-permute-start | bytes 393224 | tf_op jit(solution)/shard_map/ppermute | solution.py:385
  29.4 4.3 %collective-permute-start.5 = (bf16[256,256]{1,0:T(8,128)(2,1)S(1)}, bf16[256,256]{1,0:T(8,128)(2,1)S(1)}, u32[]{:S(2)}, u32[]{:S(2)}) collective-permute-start(bf16[256,256]{1,0:T(8,128)(2,1)S(1)} %get-tuple-element.25), channel_id=1, source_target_pairs={{1,2},{2,1},{5,6},{6,5},{9,10},{10,9},{13,14},{14,13},{17,18},{18,... | collective-permute-start | bytes 393224 | tf_op jit(solution)/shard_map/ppermute | solution.py:385
  37.0 6.6 %collective-permute-start.8 = (bf16[8,4480]{1,0:T(8,128)(2,1)S(1)}, bf16[8,4480]{1,0:T(8,128)(2,1)S(1)}, u32[]{:S(2)}, u32[]{:S(2)}) collective-permute-start(bf16[8,4480]{1,0:T(8,128)(2,1)S(1)} %get-tuple-element.27), channel_id=1, source_target_pairs={{0,24},{4,28},{8,16},{12,20},{16,8},{20,12},{24,0},{28,4},{1,25},{... | collective-permute-start | bytes 215048 | tf_op jit(solution)/shard_map/ppermute | solution.py:411
  40.7 6.0 %collective-permute-start.7 = (bf16[8,4480]{1,0:T(8,128)(2,1)S(1)}, bf16[8,4480]{1,0:T(8,128)(2,1)S(1)}, u32[]{:S(2)}, u32[]{:S(2)}) collective-permute-start(bf16[8,4480]{1,0:T(8,128)(2,1)S(1)} %get-tuple-element.27), channel_id=1, source_target_pairs={{0,16},{4,20},{8,24},{12,28},{16,0},{20,4},{24,8},{28,12},{1,17},{... | collective-permute-start | bytes 215048 | tf_op jit(solution)/shard_map/ppermute | solution.py:411
  40.7 6.0 %collective-permute-start.6 = (bf16[8,4480]{1,0:T(8,128)(2,1)S(1)}, bf16[8,4480]{1,0:T(8,128)(2,1)S(1)}, u32[]{:S(2)}, u32[]{:S(2)}) collective-permute-start(bf16[8,4480]{1,0:T(8,128)(2,1)S(1)} %get-tuple-element.27), channel_id=1, source_target_pairs={{0,8},{4,12},{8,0},{12,4},{16,24},{20,28},{24,16},{28,20},{1,9},{5... | collective-permute-start | bytes 215048 | tf_op jit(solution)/shard_map/ppermute | solution.py:411
  46.8 10.5 %collective-permute-start.10 = (bf16[32,4480]{1,0:T(8,128)(2,1)S(1)}, bf16[32,4480]{1,0:T(8,128)(2,1)S(1)}, u32[]{:S(2)}, u32[]{:S(2)}) collective-permute-start(bf16[32,4480]{1,0:T(8,128)(2,1)S(1)} %pad_maximum_fusion.1.refs_0_.refs_2_), channel_id=1, source_target_pairs={{0,2},{2,0},{1,3},{3,1},{4,6},{6,4},{5,7},{7,5},{8,10},{10,8},{9,1... | collective-permute-start | bytes 860168 | tf_op jit(solution)/shard_map/ppermute | solution.py:404
  51.3 7.5 %collective-permute-start.9 = (bf16[32,4480]{1,0:T(8,128)(2,1)S(1)}, bf16[32,4480]{1,0:T(8,128)(2,1)S(1)}, u32[]{:S(2)}, u32[]{:S(2)}) collective-permute-start(bf16[32,4480]{1,0:T(8,128)(2,1)S(1)} %pad_maximum_fusion.1.refs_0_.refs_2_), channel_id=1, source_target_pairs={{0,1},{1,0},{2,3},{3,2},{4,5},{5,4},{6,7},{7,6},{8,9},{9,8},{10,11... | collective-permute-start | bytes 860168 | tf_op jit(solution)/shard_map/ppermute | solution.py:401
  51.4 8.2 %collective-permute-start.14 = (bf16[8,4480]{1,0:T(8,128)(2,1)S(1)}, bf16[8,4480]{1,0:T(8,128)(2,1)S(1)}, u32[]{:S(2)}, u32[]{:S(2)}) collective-permute-start(bf16[8,4480]{1,0:T(8,128)(2,1)S(1)} %get-tuple-element.30), channel_id=1, source_target_pairs={{0,24},{4,28},{8,16},{12,20},{16,8},{20,12},{24,0},{28,4},{1,25},{... | collective-permute-start | bytes 215048 | tf_op jit(solution)/shard_map/ppermute | solution.py:411
  53.6 6.0 %collective-permute-start.13 = (bf16[8,4480]{1,0:T(8,128)(2,1)S(1)}, bf16[8,4480]{1,0:T(8,128)(2,1)S(1)}, u32[]{:S(2)}, u32[]{:S(2)}) collective-permute-start(bf16[8,4480]{1,0:T(8,128)(2,1)S(1)} %get-tuple-element.30), channel_id=1, source_target_pairs={{0,16},{4,20},{8,24},{12,28},{16,0},{20,4},{24,8},{28,12},{1,17},{... | collective-permute-start | bytes 215048 | tf_op jit(solution)/shard_map/ppermute | solution.py:411
  53.6 5.5 %collective-permute-start.12 = (bf16[8,4480]{1,0:T(8,128)(2,1)S(1)}, bf16[8,4480]{1,0:T(8,128)(2,1)S(1)}, u32[]{:S(2)}, u32[]{:S(2)}) collective-permute-start(bf16[8,4480]{1,0:T(8,128)(2,1)S(1)} %get-tuple-element.30), channel_id=1, source_target_pairs={{0,8},{4,12},{8,0},{12,4},{16,24},{20,28},{24,16},{28,20},{1,9},{5... | collective-permute-start | bytes 215048 | tf_op jit(solution)/shard_map/ppermute | solution.py:411
  58.8 2.9 %collective-permute-start.11 = (bf16[96,4480]{1,0:T(8,128)(2,1)S(1)}, bf16[96,4480]{1,0:T(8,128)(2,1)S(1)}, u32[]{:S(2)}, u32[]{:S(2)}) collective-permute-start(bf16[96,4480]{1,0:T(8,128)(2,1)S(1)} %pad_maximum_fusion), channel_id=1, source_target_pairs={{0,4},{4,0},{8,12},{12,8},{16,20},{20,16},{24,28},{28,24},{1,5},{5... | collective-permute-start | bytes 2580488 | tf_op jit(solution)/shard_map/ppermute | solution.py:407
  59.6 11.8 %collective-permute-start.16 = (bf16[48,4480]{1,0:T(8,128)(2,1)S(1)}, bf16[48,4480]{1,0:T(8,128)(2,1)S(1)}, u32[]{:S(2)}, u32[]{:S(2)}) collective-permute-start(bf16[48,4480]{1,0:T(8,128)(2,1)S(1)} %get-tuple-element.44), channel_id=1, source_target_pairs={{0,2},{2,0},{1,3},{3,1},{4,6},{6,4},{5,7},{7,5},{8,10},{10,8},{9,1... | collective-permute-start | bytes 1290248 | tf_op jit(solution)/shard_map/ppermute | solution.py:404
  61.6 10.1 %collective-permute-start.15 = (bf16[48,4480]{1,0:T(8,128)(2,1)S(1)}, bf16[48,4480]{1,0:T(8,128)(2,1)S(1)}, u32[]{:S(2)}, u32[]{:S(2)}) collective-permute-start(bf16[48,4480]{1,0:T(8,128)(2,1)S(1)} %get-tuple-element.45), channel_id=1, source_target_pairs={{0,1},{1,0},{2,3},{3,2},{4,5},{5,4},{6,7},{7,6},{8,9},{9,8},{10,11... | collective-permute-start | bytes 1290248 | tf_op jit(solution)/shard_map/ppermute | solution.py:401
  71.8 2.9 %collective-permute-start.17 = (bf16[128,4480]{1,0:T(8,128)(2,1)S(1)}, bf16[128,4480]{1,0:T(8,128)(2,1)S(1)}, u32[]{:S(2)}, u32[]{:S(2)}) collective-permute-start(bf16[128,4480]{1,0:T(8,128)(2,1)S(1)} %constant_dynamic-update-slice_fusion.12), channel_id=1, source_target_pairs={{0,4},{4,0},{8,12},{12,8},{16,20},{20,16},{24,28},{28,24},{1,5},{5... | collective-permute-start | bytes 3440648 | tf_op jit(solution)/shard_map/ppermute | solution.py:407
  71.9 6.9 %collective-permute-start.18 = (bf16[16,4480]{1,0:T(8,128)(2,1)S(1)}, bf16[16,4480]{1,0:T(8,128)(2,1)S(1)}, u32[]{:S(2)}, u32[]{:S(2)}) collective-permute-start(bf16[16,4480]{1,0:T(8,128)(2,1)S(1)} %slice.14), channel_id=1, source_target_pairs={{0,1},{1,0},{2,3},{3,2},{4,5},{5,4},{6,7},{7,6},{8,9},{9,8},{10,11... | collective-permute-start | bytes 430088 | tf_op jit(solution)/shard_map/ppermute | solution.py:401
  73.5 5.9 %collective-permute-start.19 = (bf16[16,4480]{1,0:T(8,128)(2,1)S(1)}, bf16[16,4480]{1,0:T(8,128)(2,1)S(1)}, u32[]{:S(2)}, u32[]{:S(2)}) collective-permute-start(bf16[16,4480]{1,0:T(8,128)(2,1)S(1)} %slice.15), channel_id=1, source_target_pairs={{0,2},{2,0},{1,3},{3,1},{4,6},{6,4},{5,7},{7,5},{8,10},{10,8},{9,1... | collective-permute-start | bytes 430088 | tf_op jit(solution)/shard_map/ppermute | solution.py:404
  79.4 1.6 %collective-permute-start.20 = (bf16[32,4480]{1,0:T(8,128)(2,1)S(1)}, bf16[32,4480]{1,0:T(8,128)(2,1)S(1)}, u32[]{:S(2)}, u32[]{:S(2)}) collective-permute-start(bf16[32,4480]{1,0:T(8,128)(2,1)S(1)} %pad_maximum_fusion.2), channel_id=1, source_target_pairs={{0,4},{4,0},{8,12},{12,8},{16,20},{20,16},{24,28},{28,24},{1,5},{5... | collective-permute-start | bytes 860168 | tf_op jit(solution)/shard_map/ppermute | solution.py:407
  (7 other events, 72.6 us)

commit v6 on v5

--- a/solution.py
+++ b/solution.py
@@ -71,9 +71,10 @@
     return jnp.cos(angle), jnp.sin(angle)
 
 
-def prepare(origin_ref, corner_refs, first_ref, second_ref, depth_ref, high_ref):
+def prepare(origin_ref, corner_refs, first_ref, second_ref, depth_ref, high_ref, where_ref):
     depth, lanes = depth_ref.shape
     where = spread(origin_ref, corner_refs, lanes)
+    where_ref[...] = where
     start_y, start_z = where[1:2], where[2:3]
     lane = lax.rem(lax.broadcasted_iota(jnp.int32, (1, lanes), 1), L)
     term = jnp.where(lane <= TERMS, lane, lane - TERMS).astype(jnp.float32)
@@ -86,20 +87,18 @@
     depth_ref[...] = table.astype(jnp.bfloat16)
     y = lax.broadcasted_iota(jnp.int32, high_ref.shape, 0).astype(jnp.float32) - start_y
     high_ref[...] = jnp.where((y >= 0) & (y < B), 1.0, 0.0)
-    return where[0:1]
 
 
 def block_modes(voxels, at_x, turn, start_x, depth_ref, high_ref, part_ref, plane_ref):
     count, high, depth = voxels.shape
     offset = at_x - start_x
-    for x in range(0, count, 4):
-        rows = voxels[x : x + 4].reshape(4 * high, depth)
-        first = jnp.dot(rows, depth_ref[...], preferred_element_type=jnp.float32)
-        for i in range(4):
-            at = offset + float(x + i)
-            live = high_ref[...] * jnp.where((at >= 0) & (at < B), 1.0, 0.0)
-            kept = first[i * high : (i + 1) * high] * live
-            part_ref[pl.ds((x + i) * high, high), :] = kept.astype(jnp.bfloat16)
+    rows = voxels.reshape(count * high, depth)
+    first = jnp.dot(rows, depth_ref[...], preferred_element_type=jnp.float32)
+    for x in range(count):
+        at = offset + float(x)
+        live = high_ref[...] * jnp.where((at >= 0) & (at < B), 1.0, 0.0)
+        kept = first[x * high : (x + 1) * high] * live
+        part_ref[pl.ds(x * high, high), :] = kept.astype(jnp.bfloat16)
     length = count * high
     total = jnp.dot(
         plane_ref[:, :length], part_ref[:length], preferred_element_type=jnp.float32
@@ -139,10 +138,11 @@
 
 def near_kernel(
     origin_ref, first_pick_ref, pick_ref, second_pick_ref, first_ref, second_ref, volume_ref, plane_ref,
-    total_ref, depth_ref, high_ref, part_ref,
+    total_ref, depth_ref, high_ref, where_ref, part_ref,
 ):
     corner_refs = (first_pick_ref, pick_ref, second_pick_ref)
-    start_x = prepare(origin_ref, corner_refs, first_ref, second_ref, depth_ref, high_ref)
+    prepare(origin_ref, corner_refs, first_ref, second_ref, depth_ref, high_ref, where_ref)
+    start_x = where_ref[0:1]
     unit = part_ref.shape[0] // volume_ref.shape[1]
     for x in range(0, volume_ref.shape[0], unit):
         added = block_modes(
@@ -187,14 +187,12 @@
 
 
 def far_kernel(
-    origin_ref, first_pick_ref, pick_ref, second_pick_ref, first_ref, second_ref, first_halo_ref, second_halo_ref, plane_ref,
-    near_ref, first_out_ref, own_ref, second_out_ref, depth_ref, high_ref, part_ref, total_ref, *, wide,
+    side_ref, depth_ref, high_ref, where_ref, first_halo_ref, second_halo_ref, plane_ref, near_ref,
+    first_out_ref, own_ref, second_out_ref, part_ref, total_ref, *, wide,
 ):
-    corner_refs = (first_pick_ref, pick_ref, second_pick_ref)
-    start_x = prepare(origin_ref, corner_refs, first_ref, second_ref, depth_ref, high_ref)
-    where = spread(origin_ref, corner_refs, total_ref.shape[1])
+    start_x = where_ref[0:1]
     total_ref[...] = near_ref[...]
-    even = origin_ref[2] == 0
+    even = side_ref[0] == 0
     below, above = turn_of(-HALF), turn_of(wide)
     sides = (
         (first_halo_ref, jnp.where(even, wide, -HALF), either(even, above, below)),
@@ -205,7 +203,7 @@
             voxels_ref[...], at_x.astype(jnp.float32), turn, start_x,
             depth_ref, high_ref, part_ref, plane_ref,
         )
-    rows = rotate(total_ref[...], start_x, where[1:2])
+    rows = rotate(total_ref[...], start_x, where_ref[1:2])
     width = own_ref.shape[1]
     first_out_ref[...] = rows[:, :width].astype(jnp.bfloat16)
     own_ref[...] = rows[:, width : 2 * width]
@@ -217,29 +215,36 @@
     total = own_ref[...] + left_ref[...].astype(jnp.float32) + right_ref[...].astype(jnp.float32)
     total = total.astype(jnp.bfloat16)
     rows, lanes = total.shape
-    slots = lanes // L
-    k = lax.broadcasted_iota(jnp.int32, (lanes, L * L), 0)
-    lane = lax.broadcasted_iota(jnp.int32, (lanes, L * L), 1)
-    gap = k - lax.rem(lane, L)
-    row = lax.rem(lax.broadcasted_iota(jnp.int32, (rows, L * L), 0), L)
-    place = jnp.where(row == L - 1, 0, row + 1)
-    keep = jnp.where(
-        place == lax.broadcasted_iota(jnp.int32, (rows, L * L), 1) // L, 1.0, 0.0
-    )
-    sums = jnp.where(
-        lax.broadcasted_iota(jnp.int32, (L, rows), 1) // L
-        == lax.broadcasted_iota(jnp.int32, (L, rows), 0),
-        1.0,
-        0.0,
-    ).astype(jnp.bfloat16)
-    for s in range(slots):
-        copies = jnp.where(gap == s * L, 1.0, 0.0).astype(jnp.bfloat16)
-        spread_rows = jnp.dot(total, copies, preferred_element_type=jnp.float32) * keep
-        feature = jnp.dot(
-            sums, spread_rows.astype(jnp.bfloat16), preferred_element_type=jnp.float32
-        )
-        for a in range(L):
-            wide_ref[s : s + 1, a * L * L : (a + 1) * L * L] = feature[a : a + 1]
+    slots, group = lanes // L, rows // L
+
+    def grid_of(shape, axis):
+        return lax.broadcasted_iota(jnp.int32, shape, axis)
+
+    def ones_where(flag):
+        return jnp.where(flag, 1.0, 0.0).astype(jnp.bfloat16)
+
+    square = (slots * group, lanes)
+    mine = ones_where(grid_of(square, 0) // group == grid_of(square, 1) // L)
+    square = (lanes, L * L)
+    tiled = ones_where(lax.rem(grid_of(square, 0), L) == lax.rem(grid_of(square, 1), L))
+    square = (slots * group, L * L)
+    place = lax.rem(grid_of(square, 0), group) + 1
+    place = jnp.where(place == group, 0, place)
+    keep = ones_where(place == grid_of(square, 1) // L)
+    square = (slots, slots * group)
+    sums = ones_where(grid_of(square, 1) // group == grid_of(square, 0))
+    copies = jnp.concatenate(
+        [
+            jnp.concatenate([total[a * group : (a + 1) * group]] * slots, axis=0) * mine
+            for a in range(L)
+        ],
+        axis=0,
+    )
+    placed = jnp.dot(copies, tiled, preferred_element_type=jnp.float32).astype(jnp.bfloat16)
+    flat = jnp.concatenate(
+        [placed[a * rows : (a + 1) * rows] * keep for a in range(L)], axis=1
+    )
+    wide_ref[...] = jnp.dot(sums, flat, preferred_element_type=jnp.float32)
     wide = wide_ref[...]
     norm = jnp.sqrt(jnp.mean(wide * wide, axis=1, keepdims=True) + EPSILON)
     high = norm.astype(jnp.bfloat16).astype(jnp.float32)
@@ -527,7 +532,7 @@
     wide, high, depth = volume.shape
     slots = pick_list.shape[3]
     tile, bank = lax.axis_index("tile"), lax.axis_index("bank")
-    side = lax.rem(tile, 2)
+    side = lax.rem(tile, 2).astype(jnp.int32)
     rest = wide - HALF
     to_first = lax.dynamic_slice_in_dim(volume, jnp.where(side == 0, rest, 0), HALF, 0)
     to_second = lax.dynamic_slice_in_dim(volume, jnp.where(side == 0, 0, rest), HALF, 0)
@@ -535,29 +540,27 @@
     second_halo = exchange(to_second, "tile", False)
     picks, first_halo = lax.optimization_barrier((pick_list, first_halo))
     first_picks, second_picks = exchange(picks, "bank", True), exchange(picks, "bank", False)
-    origin = jnp.stack([tile * wide + HALF, bank * high + HALF, side]).astype(jnp.int32)
+    origin = jnp.stack([tile * wide + HALF, bank * high + HALF]).astype(jnp.int32)
 
     first, second = depth_tables(depth)
     plane = jnp.asarray(plane_table(HALF, high), jnp.bfloat16)
     modes, lanes = plane.shape[0], 3 * slots * L
     unit = 32
 
-    def scratch(count):
-        return [
-            pltpu.VMEM((depth, lanes), jnp.bfloat16),
-            pltpu.VMEM((high, lanes), jnp.float32),
-            pltpu.VMEM((count * high, lanes), jnp.bfloat16),
-        ]
-
-    params = pltpu.CompilerParams(vmem_limit_bytes=24 * MIB)
+    params = pltpu.CompilerParams(vmem_limit_bytes=32 * MIB)
     vmem = pl.BlockSpec(memory_space=pltpu.VMEM)
-    given = [pl.BlockSpec(memory_space=pltpu.SMEM)] + [vmem] * 5
-    near = pl.pallas_call(
+    smem = pl.BlockSpec(memory_space=pltpu.SMEM)
+    near, *tables = pl.pallas_call(
         near_kernel,
-        in_specs=given + [vmem] * 2,
-        out_specs=vmem,
-        out_shape=jax.ShapeDtypeStruct((modes, lanes), jnp.float32),
-        scratch_shapes=scratch(unit),
+        in_specs=[smem] + [vmem] * 7,
+        out_specs=[vmem] * 4,
+        out_shape=[
+            jax.ShapeDtypeStruct((modes, lanes), jnp.float32),
+            jax.ShapeDtypeStruct((depth, lanes), jnp.bfloat16),
+            jax.ShapeDtypeStruct((high, lanes), jnp.float32),
+            jax.ShapeDtypeStruct((8, lanes), jnp.float32),
+        ],
+        scratch_shapes=[pltpu.VMEM((unit * high, lanes), jnp.bfloat16)],
         compiler_params=params,
         cost_estimate=pl.CostEstimate(
             flops=2 * wide * high * lanes * (depth + modes), bytes_accessed=8000000, transcendentals=0
@@ -566,19 +569,20 @@
     )(origin, first_picks, picks, second_picks, first, second, volume, plane)
     for_first, mid, for_second = pl.pallas_call(
         functools.partial(far_kernel, wide=wide),
-        in_specs=given + [vmem] * 4,
+        in_specs=[smem] + [vmem] * 7,
         out_specs=[vmem] * 3,
         out_shape=[
             jax.ShapeDtypeStruct((L * L, slots * L), jnp.bfloat16),
             jax.ShapeDtypeStruct((L * L, slots * L), jnp.float32),
             jax.ShapeDtypeStruct((L * L, slots * L), jnp.bfloat16),
         ],
-        scratch_shapes=scratch(HALF) + [pltpu.VMEM((modes, lanes), jnp.float32)],
+        scratch_shapes=[
+            pltpu.VMEM((HALF * high, lanes), jnp.bfloat16),
+            pltpu.VMEM((modes, lanes), jnp.float32),
+        ],
         compiler_params=params,
         name="far_rows",
-    )(
-        origin, first_picks, picks, second_picks, first, second, first_halo, second_halo, plane, near
-    )
+    )(side[None], *tables, first_halo, second_halo, plane, near)
     from_first, from_second = exchange(for_first, "bank", True), exchange(for_second, "bank", False)
 
     live_slots = jnp.arange(slots) < box_counts[0, 0]

time: 94.8 us -> 92.2 us (0.973)
  Pallas kernels: 38.3 us -> 35.7 us
    pallas_call x1, Pallas kernels: 3.32 us -> 1.35 us  [body(): pl.pallas_call(join_kernel, out_shape=[jax.ShapeDtypeStruct((slots // par...]
  transfers between devices with their start and end apart: 21 -> 21, of which waited for: 13 -> 13; matrix products, arithmetic and copies ran while one was open for 1% -> 1% of each run, Pallas kernels for 14% -> 15%
where the time goes in v6:
time: 92.2 us; the launch traced here: 92 us
  Pallas kernels  35.7 us (39%)
  starting transfers between devices  28.6 us (31%)
  waiting for transfers between devices  21.9 us (24%)
  local copies, waits for them, and re-layouts  3.08 us (3%)
  between operations  1.8 us (2%)
  other arithmetic  0.98 us (1%)
    pallas_call x1, Pallas kernels, sum_blocks(): pl.pallas_call(functools.partial(sum_kernel, early=len(parts), blocks=len...  13.4 us
    ppermute x6, starting transfers between devices, exchange(): return lax.ppermute(value, axis, pairs)  10.9 us
    ppermute x6, starting transfers between devices, line_of(): lax.ppermute(part, 'tile', [(i, i ^ by) for i in range(tiles)])  8.84 us
    pallas_call x2, Pallas kernels, weigh_blocks(): pl.pallas_call(functools.partial(weigh_kernel, blocks=len(blocks), known=...  8.82 us
    pallas_call x1, Pallas kernels, body(): pl.pallas_call(functools.partial(far_kernel, wide=wide), in_specs=[smem]...  7.4 us
    ppermute x3, waiting for transfers between devices, along_y(): return lax.ppermute(value, 'bank', [(0, 2), (2, 0), (1, 3), (3, 1)])  7.09 us
    ppermute x3, starting transfers between devices, along_y(): return lax.ppermute(value, 'bank', [(0, 2), (2, 0), (1, 3), (3, 1)])  6.94 us
    ppermute x6, waiting for transfers between devices, line_of(): lax.ppermute(part, 'tile', [(i, i ^ by) for i in range(tiles)])  5.9 us
  transfers between devices with their start and end apart: 21, of which 13 were waited for; matrix products, arithmetic and copies ran while one was open for 1% of the time, Pallas kernels for 15%

profile of v6, /device:TPU:0, one launch (start us, length us, event | category | flops | bytes accessed | tf_op | source)
XLA Modules:
  0.0 92.0 jit_solution(15931628353318526361)
XLA Ops:
  0.7 2.8 %constant_dynamic-slice_fusion = (bf16[48,64,128]{2,1,0:T(8,128)(2,1)}, bf16[48,64,128]{2,1,0:T(8,128)(2,1)}) fusion(bf16[64,64,128]{2,1,0:T(8,128)(2,1)} %volume_ref.1, s32[]{:T(128)S(6)} %select_n.18, s32[]{:T(128)S(6)} %select_n.17), kind=kLoop, calls=%fused_computation.29 | loop fusion | bytes 3145736 | tf_op jit(solution)/shard_map/dynamic_slice | solution.py:538
  4.0 1.6 %collective-permute-start.3 = (bf16[48,64,128]{2,1,0:T(8,128)(2,1)}, bf16[48,64,128]{2,1,0:T(8,128)(2,1)}, u32[]{:S(2)}, u32[]{:S(2)}) collective-permute-start(bf16[48,64,128]{2,1,0:T(8,128)(2,1)} %get-tuple-element.48), channel_id=1, source_target_pairs={{4,8},{8,4},{12,16},{16,12},{20,24},{24,20},{5,9},{9,5},{13,17},{1... | collective-permute-start | bytes 2359304 | tf_op jit(solution)/shard_map/ppermute | solution.py:390
  7.6 5.3 %collective-permute-start.1 = (s32[3,1,1,16]{3,2,1,0:T(1,128)S(1)}, s32[3,1,1,16]{3,2,1,0:T(1,128)S(1)}, u32[]{:S(2)}, u32[]{:S(2)}) collective-permute-start(s32[3,1,1,16]{3,2,1,0:T(1,128)S(1)} %copy-done.2), channel_id=1, source_target_pairs={{0,1},{1,0},{2,3},{3,2},{4,5},{5,4},{6,7},{7,6},{8,9},{9,8},{10,11... | collective-permute-start | bytes 584 | tf_op jit(solution)/shard_map/ppermute | solution.py:390
  13.0 1.5 %collective-permute-done.1.first_pick_ref = s32[3,1,1,16]{3,2,1,0:T(1,128)S(1)} collective-permute-done((s32[3,1,1,16]{3,2,1,0:T(1,128)S(1)}, s32[3,1,1,16]{3,2,1,0:T(1,128)S(1)}, u32[]{:S(2)}, u32[]{:S(2)}) %collective-permute-start.1) | collective-permute-done | bytes 224 | tf_op jit(solution)/shard_map/ppermute | solution.py:390
  14.5 4.7 %near_rows.1 = (f32[304,768]{1,0:T(8,128)S(1)}, bf16[128,768]{1,0:T(8,128)(2,1)S(1)}, f32[64,768]{1,0:T(8,128)S(1)}, f32[8,768]{1,0:T(8,128)S(1)}) custom-call(s32[2]{0:T(128)S(1)} %pad_add_fusion.origin_ref, s32[3,1,1,16]{3,2,1,0:T(1,128)S(1)} %collective-permute-done.1.first_pick_ref, s32[3,1,1,16]{3,2,1,0:T(1,128)S(1)} %copy-done.2, ...), custom_call_target="tpu_custom_call" | custom-call | flops 2717908992 | bytes 8000000 | tf_op jit(solution)/shard_map/near_rows/pallas_call | solution.py:553
  19.3 7.4 %far_rows.1 = (bf16[256,256]{1,0:T(8,128)(2,1)S(1)}, f32[256,256]{1,0:T(8,128)S(1)}, bf16[256,256]{1,0:T(8,128)(2,1)S(1)}) custom-call(s32[1]{0:T(128)} %bitcast.1.side_ref, bf16[128,768]{1,0:T(8,128)(2,1)S(1)} %get-tuple-element.26.depth_ref, f32[64,768]{1,0:T(8,128)S(1)} %get-tuple-element.27.high_ref, f32[8,768]{1,0:T(8,128)S(1)} %get-tuple-element.28.where_ref, ...), custom_call_target="tpu_custom_call" | custom-call | tf_op jit(solution)/shard_map/far_rows/pallas_call | solution.py:570
  26.7 2.1 %collective-permute-start.4 = (bf16[256,256]{1,0:T(8,128)(2,1)S(1)}, bf16[256,256]{1,0:T(8,128)(2,1)S(1)}, u32[]{:S(2)}, u32[]{:S(2)}) collective-permute-start(bf16[256,256]{1,0:T(8,128)(2,1)S(1)} %get-tuple-element.32), channel_id=1, source_target_pairs={{0,1},{1,0},{2,3},{3,2},{4,5},{5,4},{6,7},{7,6},{8,9},{9,8},{10,11... | collective-permute-start | bytes 393224 | tf_op jit(solution)/shard_map/ppermute | solution.py:390
  29.7 3.4 %collective-permute-done.4.left_ref = bf16[256,256]{1,0:T(8,128)(2,1)S(1)} collective-permute-done((bf16[256,256]{1,0:T(8,128)(2,1)S(1)}, bf16[256,256]{1,0:T(8,128)(2,1)S(1)}, u32[]{:S(2)}, u32[]{:S(2)}) %collective-permute-start.4) | collective-permute-done | bytes 131104 | tf_op jit(solution)/shard_map/ppermute | solution.py:390
  33.1 1.4 %join.1 = (bf16[8,4480]{1,0:T(8,128)(2,1)S(1)}, bf16[8,4480]{1,0:T(8,128)(2,1)S(1)}) custom-call(f32[256,256]{1,0:T(8,128)S(1)} %get-tuple-element.31.own_ref, bf16[256,256]{1,0:T(8,128)(2,1)S(1)} %collective-permute-done.4.left_ref, bf16[256,256]{1,0:T(8,128)(2,1)S(1)} %collective-permute-done.5.right_ref, ...), custom_call_target="tpu_custom_call" | custom-call | tf_op jit(solution)/shard_map/join/pallas_call | solution.py:595
  34.4 3.7 %collective-permute-start.8 = (bf16[8,4480]{1,0:T(8,128)(2,1)S(1)}, bf16[8,4480]{1,0:T(8,128)(2,1)S(1)}, u32[]{:S(2)}, u32[]{:S(2)}) collective-permute-start(bf16[8,4480]{1,0:T(8,128)(2,1)S(1)} %get-tuple-element.35), channel_id=1, source_target_pairs={{0,24},{4,28},{8,16},{12,20},{16,8},{20,12},{24,0},{28,4},{1,25},{... | collective-permute-start | bytes 215048 | tf_op jit(solution)/shard_map/ppermute | solution.py:416
  38.9 2.2 %collective-permute-done.8 = bf16[8,4480]{1,0:T(8,128)(2,1)S(1)} collective-permute-done((bf16[8,4480]{1,0:T(8,128)(2,1)S(1)}, bf16[8,4480]{1,0:T(8,128)(2,1)S(1)}, u32[]{:S(2)}, u32[]{:S(2)}) %collective-permute-start.8) | collective-permute-done | bytes 71712 | tf_op jit(solution)/shard_map/ppermute | solution.py:416
  41.1 3.1 %collective-permute-done.7 = bf16[8,4480]{1,0:T(8,128)(2,1)S(1)} collective-permute-done((bf16[8,4480]{1,0:T(8,128)(2,1)S(1)}, bf16[8,4480]{1,0:T(8,128)(2,1)S(1)}, u32[]{:S(2)}, u32[]{:S(2)}) %collective-permute-start.7) | collective-permute-done | bytes 71712 | tf_op jit(solution)/shard_map/ppermute | solution.py:416
  44.2 4.5 %collective-permute-start.10 = (bf16[32,4480]{1,0:T(8,128)(2,1)S(1)}, bf16[32,4480]{1,0:T(8,128)(2,1)S(1)}, u32[]{:S(2)}, u32[]{:S(2)}) collective-permute-start(bf16[32,4480]{1,0:T(8,128)(2,1)S(1)} %pad_maximum_fusion.1.refs_0_.refs_2_), channel_id=1, source_target_pairs={{0,2},{2,0},{1,3},{3,1},{4,6},{6,4},{5,7},{7,5},{8,10},{10,8},{9,1... | collective-permute-start | bytes 860168 | tf_op jit(solution)/shard_map/ppermute | solution.py:409
  48.8 2.2 %collective-permute-start.14 = (bf16[8,4480]{1,0:T(8,128)(2,1)S(1)}, bf16[8,4480]{1,0:T(8,128)(2,1)S(1)}, u32[]{:S(2)}, u32[]{:S(2)}) collective-permute-start(bf16[8,4480]{1,0:T(8,128)(2,1)S(1)} %get-tuple-element.38), channel_id=1, source_target_pairs={{0,24},{4,28},{8,16},{12,20},{16,8},{20,12},{24,0},{28,4},{1,25},{... | collective-permute-start | bytes 215048 | tf_op jit(solution)/shard_map/ppermute | solution.py:416
  51.0 2.2 %collective-permute-start.12 = (bf16[8,4480]{1,0:T(8,128)(2,1)S(1)}, bf16[8,4480]{1,0:T(8,128)(2,1)S(1)}, u32[]{:S(2)}, u32[]{:S(2)}) collective-permute-start(bf16[8,4480]{1,0:T(8,128)(2,1)S(1)} %get-tuple-element.38), channel_id=1, source_target_pairs={{0,8},{4,12},{8,0},{12,4},{16,24},{20,28},{24,16},{28,20},{1,9},{5... | collective-permute-start | bytes 215048 | tf_op jit(solution)/shard_map/ppermute | solution.py:416
  53.2 1.5 %collective-permute-done.10.refs_2_.refs_4_ = bf16[32,4480]{1,0:T(8,128)(2,1)S(1)} collective-permute-done((bf16[32,4480]{1,0:T(8,128)(2,1)S(1)}, bf16[32,4480]{1,0:T(8,128)(2,1)S(1)}, u32[]{:S(2)}, u32[]{:S(2)}) %collective-permute-start.10) | collective-permute-done | bytes 286752 | tf_op jit(solution)/shard_map/ppermute | solution.py:409
  54.7 1.5 %collective-permute-done.9.refs_1_.refs_3_ = bf16[32,4480]{1,0:T(8,128)(2,1)S(1)} collective-permute-done((bf16[32,4480]{1,0:T(8,128)(2,1)S(1)}, bf16[32,4480]{1,0:T(8,128)(2,1)S(1)}, u32[]{:S(2)}, u32[]{:S(2)}) %collective-permute-start.9) | collective-permute-done | bytes 286752 | tf_op jit(solution)/shard_map/ppermute | solution.py:406
  57.1 2.0 %collective-permute-start.16 = (bf16[48,4480]{1,0:T(8,128)(2,1)S(1)}, bf16[48,4480]{1,0:T(8,128)(2,1)S(1)}, u32[]{:S(2)}, u32[]{:S(2)}) collective-permute-start(bf16[48,4480]{1,0:T(8,128)(2,1)S(1)} %get-tuple-element.52), channel_id=1, source_target_pairs={{0,2},{2,0},{1,3},{3,1},{4,6},{6,4},{5,7},{7,5},{8,10},{10,8},{9,1... | collective-permute-start | bytes 1290248 | tf_op jit(solution)/shard_map/ppermute | solution.py:409
  59.1 4.7 %weigh.2 = (bf16[20,64,192]{2,1,0:T(8,128)(2,1)S(1)}, f32[20,64,128]{2,1,0:T(8,128)S(1)}) custom-call(s32[1]{0:T(128)} %bitcast.index_ref, bf16[32,4480]{1,0:T(8,128)(2,1)S(1)} %pad_maximum_fusion.1.refs_0_.refs_2_, bf16[32,4480]{1,0:T(8,128)(2,1)S(1)} %collective-permute-done.9.refs_1_.refs_3_, ...), custom_call_target="tpu_custom_call" | custom-call | flops 2013265920 | bytes 10485760 | tf_op jit(solution)/shard_map/weigh/pallas_call | solution.py:461
  63.9 5.0 %collective-permute-done.16.refs_2_.refs_8_ = bf16[48,4480]{1,0:T(8,128)(2,1)S(1)} collective-permute-done((bf16[48,4480]{1,0:T(8,128)(2,1)S(1)}, bf16[48,4480]{1,0:T(8,128)(2,1)S(1)}, u32[]{:S(2)}, u32[]{:S(2)}) %collective-permute-start.16) | collective-permute-done | bytes 430112 | tf_op jit(solution)/shard_map/ppermute | solution.py:409
  69.4 1.6 %collective-permute-start.18 = (bf16[16,4480]{1,0:T(8,128)(2,1)S(1)}, bf16[16,4480]{1,0:T(8,128)(2,1)S(1)}, u32[]{:S(2)}, u32[]{:S(2)}) collective-permute-start(bf16[16,4480]{1,0:T(8,128)(2,1)S(1)} %slice.14), channel_id=1, source_target_pairs={{0,1},{1,0},{2,3},{3,2},{4,5},{5,4},{6,7},{7,6},{8,9},{9,8},{10,11... | collective-permute-start | bytes 430088 | tf_op jit(solution)/shard_map/ppermute | solution.py:406
  72.1 4.1 %weigh.3.refs_1_ = bf16[20,64,256]{2,1,0:T(8,128)(2,1)S(1)} custom-call(s32[1]{0:T(128)} %bitcast.index_ref, bf16[32,4480]{1,0:T(8,128)(2,1)S(1)} %get-tuple-element.51.refs_0_.refs_6_, bf16[48,4480]{1,0:T(8,128)(2,1)S(1)} %collective-permute-done.15.refs_1_.refs_7_, bf16[48,4480]{1,0:T(8,128)(2,1)S(1)} %collective-permute-done.16.refs_2_.refs_8_, ...), custom_call_target="tpu_custom_call" | custom-call | flops 2684354560 | bytes 10485760 | tf_op jit(solution)/shard_map/weigh/pallas_call | solution.py:461
  76.9 1.6 %collective-permute-done.20.refs_12_ = bf16[32,4480]{1,0:T(8,128)(2,1)S(1)} collective-permute-done((bf16[32,4480]{1,0:T(8,128)(2,1)S(1)}, bf16[32,4480]{1,0:T(8,128)(2,1)S(1)}, u32[]{:S(2)}, u32[]{:S(2)}) %collective-permute-start.20) | collective-permute-done | bytes 286752 | tf_op jit(solution)/shard_map/ppermute | solution.py:412
  78.5 13.4 %class_sums.1 = (f32[20,64,4096]{2,1,0:T(8,128)}, f32[20,64]{1,0:T(8,128)}) custom-call(s32[1]{0:T(128)} %bitcast.index_ref, bf16[20,64,192]{2,1,0:T(8,128)(2,1)S(1)} %get-tuple-element.39.refs_0_, bf16[20,64,256]{2,1,0:T(8,128)(2,1)S(1)} %weigh.3.refs_1_, bf16[32,4480]{1,0:T(8,128)(2,1)S(1)} %pad_maximum_fusion.1.refs_0_.refs_2_, ...), custom_call_target="tpu_custom_call" | custom-call | flops 5368709120 | bytes 20971520 | tf_op jit(solution)/shard_map/class_sums/pallas_call | solution.py:494
  (64 shorter events, 6.9 us)
Async XLA Ops:
  3.5 3.4 %collective-permute-start = (bf16[48,64,128]{2,1,0:T(8,128)(2,1)}, bf16[48,64,128]{2,1,0:T(8,128)(2,1)}, u32[]{:S(2)}, u32[]{:S(2)}) collective-permute-start(bf16[48,64,128]{2,1,0:T(8,128)(2,1)} %get-tuple-element.49), channel_id=1, source_target_pairs={{0,4},{4,0},{8,12},{12,8},{16,20},{20,16},{24,28},{28,24},{1,5},{5... | collective-permute-start | bytes 2359304 | tf_op jit(solution)/shard_map/ppermute | solution.py:390
  4.0 15.3 %collective-permute-start.3 = (bf16[48,64,128]{2,1,0:T(8,128)(2,1)}, bf16[48,64,128]{2,1,0:T(8,128)(2,1)}, u32[]{:S(2)}, u32[]{:S(2)}) collective-permute-start(bf16[48,64,128]{2,1,0:T(8,128)(2,1)} %get-tuple-element.48), channel_id=1, source_target_pairs={{4,8},{8,4},{12,16},{16,12},{20,24},{24,20},{5,9},{9,5},{13,17},{1... | collective-permute-start | bytes 2359304 | tf_op jit(solution)/shard_map/ppermute | solution.py:390
  7.0 6.0 %collective-permute-start.2 = (s32[3,1,1,16]{3,2,1,0:T(1,128)S(1)}, s32[3,1,1,16]{3,2,1,0:T(1,128)S(1)}, u32[]{:S(2)}, u32[]{:S(2)}) collective-permute-start(s32[3,1,1,16]{3,2,1,0:T(1,128)S(1)} %copy-done.2), channel_id=1, source_target_pairs={{1,2},{2,1},{5,6},{6,5},{9,10},{10,9},{13,14},{14,13},{17,18},{18,... | collective-permute-start | bytes 584 | tf_op jit(solution)/shard_map/ppermute | solution.py:390
  7.6 6.9 %collective-permute-start.1 = (s32[3,1,1,16]{3,2,1,0:T(1,128)S(1)}, s32[3,1,1,16]{3,2,1,0:T(1,128)S(1)}, u32[]{:S(2)}, u32[]{:S(2)}) collective-permute-start(s32[3,1,1,16]{3,2,1,0:T(1,128)S(1)} %copy-done.2), channel_id=1, source_target_pairs={{0,1},{1,0},{2,3},{3,2},{4,5},{5,4},{6,7},{7,6},{8,9},{9,8},{10,11... | collective-permute-start | bytes 584 | tf_op jit(solution)/shard_map/ppermute | solution.py:390
  14.5 44.6 %slice-start = ((s8[10485760]{0:T(1024)(128)(4,1)}), s8[4194304]{0:T(1024)(128)(4,1)S(1)}, s32[]{:S(2)}) async-start(s8[10485760]{0:T(1024)(128)(4,1)} %bitcast.12), calls=%async_computation | async-start | bytes 8388608
  14.5 44.6 %slice-start.1 = ((s8[10485760]{0:T(1024)(128)(4,1)}), s8[4194304]{0:T(1024)(128)(4,1)S(1)}, s32[]{:S(2)}) async-start(s8[10485760]{0:T(1024)(128)(4,1)} %bitcast.12), calls=%async_computation.1 | async-start | bytes 8388608
  19.3 39.9 %slice-start.2 = ((s8[10485760]{0:T(1024)(128)(4,1)}), s8[2097152]{0:T(1024)(128)(4,1)S(1)}, s32[]{:S(2)}) async-start(s8[10485760]{0:T(1024)(128)(4,1)} %bitcast.12), calls=%async_computation.2 | async-start | bytes 4194304
  26.7 6.4 %collective-permute-start.4 = (bf16[256,256]{1,0:T(8,128)(2,1)S(1)}, bf16[256,256]{1,0:T(8,128)(2,1)S(1)}, u32[]{:S(2)}, u32[]{:S(2)}) collective-permute-start(bf16[256,256]{1,0:T(8,128)(2,1)S(1)} %get-tuple-element.32), channel_id=1, source_target_pairs={{0,1},{1,0},{2,3},{3,2},{4,5},{5,4},{6,7},{7,6},{8,9},{9,8},{10,11... | collective-permute-start | bytes 393224 | tf_op jit(solution)/shard_map/ppermute | solution.py:390
  28.8 4.3 %collective-permute-start.5 = (bf16[256,256]{1,0:T(8,128)(2,1)S(1)}, bf16[256,256]{1,0:T(8,128)(2,1)S(1)}, u32[]{:S(2)}, u32[]{:S(2)}) collective-permute-start(bf16[256,256]{1,0:T(8,128)(2,1)S(1)} %get-tuple-element.33), channel_id=1, source_target_pairs={{1,2},{2,1},{5,6},{6,5},{9,10},{10,9},{13,14},{14,13},{17,18},{18,... | collective-permute-start | bytes 393224 | tf_op jit(solution)/shard_map/ppermute | solution.py:390
  34.4 6.6 %collective-permute-start.8 = (bf16[8,4480]{1,0:T(8,128)(2,1)S(1)}, bf16[8,4480]{1,0:T(8,128)(2,1)S(1)}, u32[]{:S(2)}, u32[]{:S(2)}) collective-permute-start(bf16[8,4480]{1,0:T(8,128)(2,1)S(1)} %get-tuple-element.35), channel_id=1, source_target_pairs={{0,24},{4,28},{8,16},{12,20},{16,8},{20,12},{24,0},{28,4},{1,25},{... | collective-permute-start | bytes 215048 | tf_op jit(solution)/shard_map/ppermute | solution.py:416
  38.2 6.0 %collective-permute-start.7 = (bf16[8,4480]{1,0:T(8,128)(2,1)S(1)}, bf16[8,4480]{1,0:T(8,128)(2,1)S(1)}, u32[]{:S(2)}, u32[]{:S(2)}) collective-permute-start(bf16[8,4480]{1,0:T(8,128)(2,1)S(1)} %get-tuple-element.35), channel_id=1, source_target_pairs={{0,16},{4,20},{8,24},{12,28},{16,0},{20,4},{24,8},{28,12},{1,17},{... | collective-permute-start | bytes 215048 | tf_op jit(solution)/shard_map/ppermute | solution.py:416
  38.2 6.0 %collective-permute-start.6 = (bf16[8,4480]{1,0:T(8,128)(2,1)S(1)}, bf16[8,4480]{1,0:T(8,128)(2,1)S(1)}, u32[]{:S(2)}, u32[]{:S(2)}) collective-permute-start(bf16[8,4480]{1,0:T(8,128)(2,1)S(1)} %get-tuple-element.35), channel_id=1, source_target_pairs={{0,8},{4,12},{8,0},{12,4},{16,24},{20,28},{24,16},{28,20},{1,9},{5... | collective-permute-start | bytes 215048 | tf_op jit(solution)/shard_map/ppermute | solution.py:416
  44.2 10.5 %collective-permute-start.10 = (bf16[32,4480]{1,0:T(8,128)(2,1)S(1)}, bf16[32,4480]{1,0:T(8,128)(2,1)S(1)}, u32[]{:S(2)}, u32[]{:S(2)}) collective-permute-start(bf16[32,4480]{1,0:T(8,128)(2,1)S(1)} %pad_maximum_fusion.1.refs_0_.refs_2_), channel_id=1, source_target_pairs={{0,2},{2,0},{1,3},{3,1},{4,6},{6,4},{5,7},{7,5},{8,10},{10,8},{9,1... | collective-permute-start | bytes 860168 | tf_op jit(solution)/shard_map/ppermute | solution.py:409
  48.7 7.5 %collective-permute-start.9 = (bf16[32,4480]{1,0:T(8,128)(2,1)S(1)}, bf16[32,4480]{1,0:T(8,128)(2,1)S(1)}, u32[]{:S(2)}, u32[]{:S(2)}) collective-permute-start(bf16[32,4480]{1,0:T(8,128)(2,1)S(1)} %pad_maximum_fusion.1.refs_0_.refs_2_), channel_id=1, source_target_pairs={{0,1},{1,0},{2,3},{3,2},{4,5},{5,4},{6,7},{7,6},{8,9},{9,8},{10,11... | collective-permute-start | bytes 860168 | tf_op jit(solution)/shard_map/ppermute | solution.py:406
  48.8 8.2 %collective-permute-start.14 = (bf16[8,4480]{1,0:T(8,128)(2,1)S(1)}, bf16[8,4480]{1,0:T(8,128)(2,1)S(1)}, u32[]{:S(2)}, u32[]{:S(2)}) collective-permute-start(bf16[8,4480]{1,0:T(8,128)(2,1)S(1)} %get-tuple-element.38), channel_id=1, source_target_pairs={{0,24},{4,28},{8,16},{12,20},{16,8},{20,12},{24,0},{28,4},{1,25},{... | collective-permute-start | bytes 215048 | tf_op jit(solution)/shard_map/ppermute | solution.py:416
  51.0 5.9 %collective-permute-start.13 = (bf16[8,4480]{1,0:T(8,128)(2,1)S(1)}, bf16[8,4480]{1,0:T(8,128)(2,1)S(1)}, u32[]{:S(2)}, u32[]{:S(2)}) collective-permute-start(bf16[8,4480]{1,0:T(8,128)(2,1)S(1)} %get-tuple-element.38), channel_id=1, source_target_pairs={{0,16},{4,20},{8,24},{12,28},{16,0},{20,4},{24,8},{28,12},{1,17},{... | collective-permute-start | bytes 215048 | tf_op jit(solution)/shard_map/ppermute | solution.py:416
  51.0 5.4 %collective-permute-start.12 = (bf16[8,4480]{1,0:T(8,128)(2,1)S(1)}, bf16[8,4480]{1,0:T(8,128)(2,1)S(1)}, u32[]{:S(2)}, u32[]{:S(2)}) collective-permute-start(bf16[8,4480]{1,0:T(8,128)(2,1)S(1)} %get-tuple-element.38), channel_id=1, source_target_pairs={{0,8},{4,12},{8,0},{12,4},{16,24},{20,28},{24,16},{28,20},{1,9},{5... | collective-permute-start | bytes 215048 | tf_op jit(solution)/shard_map/ppermute | solution.py:416
  56.2 2.9 %collective-permute-start.11 = (bf16[96,4480]{1,0:T(8,128)(2,1)S(1)}, bf16[96,4480]{1,0:T(8,128)(2,1)S(1)}, u32[]{:S(2)}, u32[]{:S(2)}) collective-permute-start(bf16[96,4480]{1,0:T(8,128)(2,1)S(1)} %pad_maximum_fusion), channel_id=1, source_target_pairs={{0,4},{4,0},{8,12},{12,8},{16,20},{20,16},{24,28},{28,24},{1,5},{5... | collective-permute-start | bytes 2580488 | tf_op jit(solution)/shard_map/ppermute | solution.py:412
  57.1 11.8 %collective-permute-start.16 = (bf16[48,4480]{1,0:T(8,128)(2,1)S(1)}, bf16[48,4480]{1,0:T(8,128)(2,1)S(1)}, u32[]{:S(2)}, u32[]{:S(2)}) collective-permute-start(bf16[48,4480]{1,0:T(8,128)(2,1)S(1)} %get-tuple-element.52), channel_id=1, source_target_pairs={{0,2},{2,0},{1,3},{3,1},{4,6},{6,4},{5,7},{7,5},{8,10},{10,8},{9,1... | collective-permute-start | bytes 1290248 | tf_op jit(solution)/shard_map/ppermute | solution.py:409
  59.1 10.1 %collective-permute-start.15 = (bf16[48,4480]{1,0:T(8,128)(2,1)S(1)}, bf16[48,4480]{1,0:T(8,128)(2,1)S(1)}, u32[]{:S(2)}, u32[]{:S(2)}) collective-permute-start(bf16[48,4480]{1,0:T(8,128)(2,1)S(1)} %get-tuple-element.53), channel_id=1, source_target_pairs={{0,1},{1,0},{2,3},{3,2},{4,5},{5,4},{6,7},{7,6},{8,9},{9,8},{10,11... | collective-permute-start | bytes 1290248 | tf_op jit(solution)/shard_map/ppermute | solution.py:406
  69.2 2.9 %collective-permute-start.17 = (bf16[128,4480]{1,0:T(8,128)(2,1)S(1)}, bf16[128,4480]{1,0:T(8,128)(2,1)S(1)}, u32[]{:S(2)}, u32[]{:S(2)}) collective-permute-start(bf16[128,4480]{1,0:T(8,128)(2,1)S(1)} %constant_dynamic-update-slice_fusion.12), channel_id=1, source_target_pairs={{0,4},{4,0},{8,12},{12,8},{16,20},{20,16},{24,28},{28,24},{1,5},{5... | collective-permute-start | bytes 3440648 | tf_op jit(solution)/shard_map/ppermute | solution.py:412
  69.4 6.9 %collective-permute-start.18 = (bf16[16,4480]{1,0:T(8,128)(2,1)S(1)}, bf16[16,4480]{1,0:T(8,128)(2,1)S(1)}, u32[]{:S(2)}, u32[]{:S(2)}) collective-permute-start(bf16[16,4480]{1,0:T(8,128)(2,1)S(1)} %slice.14), channel_id=1, source_target_pairs={{0,1},{1,0},{2,3},{3,2},{4,5},{5,4},{6,7},{7,6},{8,9},{9,8},{10,11... | collective-permute-start | bytes 430088 | tf_op jit(solution)/shard_map/ppermute | solution.py:406
  70.9 5.9 %collective-permute-start.19 = (bf16[16,4480]{1,0:T(8,128)(2,1)S(1)}, bf16[16,4480]{1,0:T(8,128)(2,1)S(1)}, u32[]{:S(2)}, u32[]{:S(2)}) collective-permute-start(bf16[16,4480]{1,0:T(8,128)(2,1)S(1)} %slice.15), channel_id=1, source_target_pairs={{0,2},{2,0},{1,3},{3,1},{4,6},{6,4},{5,7},{7,5},{8,10},{10,8},{9,1... | collective-permute-start | bytes 430088 | tf_op jit(solution)/shard_map/ppermute | solution.py:409
  76.8 1.6 %collective-permute-start.20 = (bf16[32,4480]{1,0:T(8,128)(2,1)S(1)}, bf16[32,4480]{1,0:T(8,128)(2,1)S(1)}, u32[]{:S(2)}, u32[]{:S(2)}) collective-permute-start(bf16[32,4480]{1,0:T(8,128)(2,1)S(1)} %pad_maximum_fusion.2), channel_id=1, source_target_pairs={{0,4},{4,0},{8,12},{12,8},{16,20},{20,16},{24,28},{28,24},{1,5},{5... | collective-permute-start | bytes 860168 | tf_op jit(solution)/shard_map/ppermute | solution.py:412
  (7 other events, 72.6 us)

commit v7 on v6

--- a/solution.py
+++ b/solution.py
@@ -429,16 +429,15 @@
     half = early_line.shape[0] // 2
     to_x = jnp.concatenate([from_y[half:], late_line], axis=0)
     to_y = jnp.concatenate([from_x[:half], late_line], axis=0)
-    blocks = [with_swap(early_line, from_x, from_y)]
+    known = with_swap(early_line, from_x, from_y)
+    to_x, to_y = lax.optimization_barrier((to_x, to_y))
     next_x, next_y = along_x(to_x), along_y(to_y)
-    first, norms = weigh_blocks(blocks[0], bank)
+    known += with_swap(to_x[half:])
+    first, norms = weigh_blocks(known, bank)
     first, next_x, next_y = lax.optimization_barrier((first, next_x, next_y))
     last_x, last_y = along_x(next_y[half + half :]), along_y(next_x[half : half + half])
-    blocks.append(with_swap(late_line, next_x, next_y))
-    second = weigh_blocks(blocks[1], bank, norms)
-    second, last_x, last_y = lax.optimization_barrier((second, last_x, last_y))
-    last = with_swap(last_x, last_y)
-    out, sums = sum_blocks([first, second], sum(blocks, []), last, norms, bank)
+    late = with_swap(next_x, next_y) + with_swap(last_x, last_y)
+    out, sums = sum_blocks([first], known, late, norms, bank)
     return jnp.transpose(out, (1, 0, 2)), jnp.transpose(sums, (1, 0))
 
 
@@ -476,8 +475,8 @@
         ],
         compiler_params=pltpu.CompilerParams(vmem_limit_bytes=18 * MIB),
         cost_estimate=pl.CostEstimate(
-            flops=2 * boxes * classes * orients * width,
-            bytes_accessed=2 * classes * orients * width,
+            flops=boxes * classes * orients * width // 8,
+            bytes_accessed=classes * orients * width // 8,
             transcendentals=0,
         ),
         name="weigh",

time: 92.2 us -> 91.5 us (level)
  Pallas kernels: 35.7 us -> 32.2 us
  waiting for transfers between devices: 21.9 us -> 24.7 us
    pallas_call x2 -> x1, Pallas kernels: 8.82 us -> 4.97 us  [weigh_blocks(): pl.pallas_call(functools.partial(weigh_kernel, blocks=len(blocks), known=...]
    ppermute x3, waiting for transfers between devices: 1.75 us -> 4.64 us  [along_x(): return lax.ppermute(value, 'bank', [(0, 1), (1, 0), (2, 3), (3, 2)])]
    ppermute x3, waiting for transfers between devices: 7.09 us -> 6.14 us  [along_y(): return lax.ppermute(value, 'bank', [(0, 2), (2, 0), (1, 3), (3, 1)])]
    ppermute x3 -> x4, waiting for transfers between devices: 2.32 us -> 3.12 us  [swap(): lax.ppermute(value, 'tile', [(i, i ^ 1) for i in range(tiles)])]
  transfers between devices with their start and end apart: 21 -> 22, of which waited for: 13 -> 14; matrix products, arithmetic and copies ran while one was open for 1% -> 1% of each run, Pallas kernels for 15% -> 11%
where the time goes in v7:
time: 91.5 us; the launch traced here: 91.3 us
  Pallas kernels  32.2 us (35%)
  starting transfers between devices  28.6 us (31%)
  waiting for transfers between devices  24.7 us (27%)
  local copies, waits for them, and re-layouts  2.98 us (3%)
  between operations  1.79 us (2%)
  other arithmetic  1.05 us (1%)
    pallas_call x1, Pallas kernels, sum_blocks(): pl.pallas_call(functools.partial(sum_kernel, early=len(parts), blocks=len...  13.7 us
    ppermute x6, starting transfers between devices, exchange(): return lax.ppermute(value, axis, pairs)  10.9 us
    ppermute x6, starting transfers between devices, line_of(): lax.ppermute(part, 'tile', [(i, i ^ by) for i in range(tiles)])  8.84 us
    pallas_call x1, Pallas kernels, body(): pl.pallas_call(functools.partial(far_kernel, wide=wide), in_specs=[smem]...  7.44 us
    ppermute x3, starting transfers between devices, along_y(): return lax.ppermute(value, 'bank', [(0, 2), (2, 0), (1, 3), (3, 1)])  6.93 us
    ppermute x3, waiting for transfers between devices, along_y(): return lax.ppermute(value, 'bank', [(0, 2), (2, 0), (1, 3), (3, 1)])  6.14 us
    ppermute x6, waiting for transfers between devices, line_of(): lax.ppermute(part, 'tile', [(i, i ^ by) for i in range(tiles)])  5.9 us
    pallas_call x1, Pallas kernels, weigh_blocks(): pl.pallas_call(functools.partial(weigh_kernel, blocks=len(blocks), known=...  4.97 us
  transfers between devices with their start and end apart: 22, of which 14 were waited for; matrix products, arithmetic and copies ran while one was open for 1% of the time, Pallas kernels for 11%

profile of v7, /device:TPU:0, one launch (start us, length us, event | category | flops | bytes accessed | tf_op | source)
XLA Modules:
  0.0 91.3 jit_solution(15902271862168100638)
XLA Ops:
  0.7 2.8 %constant_dynamic-slice_fusion = (bf16[48,64,128]{2,1,0:T(8,128)(2,1)}, bf16[48,64,128]{2,1,0:T(8,128)(2,1)}) fusion(bf16[64,64,128]{2,1,0:T(8,128)(2,1)} %volume_ref.1, s32[]{:T(128)S(6)} %select_n.18, s32[]{:T(128)S(6)} %select_n.17), kind=kLoop, calls=%fused_computation.20 | loop fusion | bytes 3145736 | tf_op jit(solution)/shard_map/dynamic_slice | solution.py:537
  4.0 1.6 %collective-permute-start.3 = (bf16[48,64,128]{2,1,0:T(8,128)(2,1)}, bf16[48,64,128]{2,1,0:T(8,128)(2,1)}, u32[]{:S(2)}, u32[]{:S(2)}) collective-permute-start(bf16[48,64,128]{2,1,0:T(8,128)(2,1)} %get-tuple-element.46), channel_id=1, source_target_pairs={{4,8},{8,4},{12,16},{16,12},{20,24},{24,20},{5,9},{9,5},{13,17},{1... | collective-permute-start | bytes 2359304 | tf_op jit(solution)/shard_map/ppermute | solution.py:390
  7.6 5.3 %collective-permute-start.1 = (s32[3,1,1,16]{3,2,1,0:T(1,128)S(1)}, s32[3,1,1,16]{3,2,1,0:T(1,128)S(1)}, u32[]{:S(2)}, u32[]{:S(2)}) collective-permute-start(s32[3,1,1,16]{3,2,1,0:T(1,128)S(1)} %copy-done.2), channel_id=1, source_target_pairs={{0,1},{1,0},{2,3},{3,2},{4,5},{5,4},{6,7},{7,6},{8,9},{9,8},{10,11... | collective-permute-start | bytes 584 | tf_op jit(solution)/shard_map/ppermute | solution.py:390
  13.0 1.5 %collective-permute-done.1.first_pick_ref = s32[3,1,1,16]{3,2,1,0:T(1,128)S(1)} collective-permute-done((s32[3,1,1,16]{3,2,1,0:T(1,128)S(1)}, s32[3,1,1,16]{3,2,1,0:T(1,128)S(1)}, u32[]{:S(2)}, u32[]{:S(2)}) %collective-permute-start.1) | collective-permute-done | bytes 224 | tf_op jit(solution)/shard_map/ppermute | solution.py:390
  14.5 4.7 %near_rows.1 = (f32[304,768]{1,0:T(8,128)S(1)}, bf16[128,768]{1,0:T(8,128)(2,1)S(1)}, f32[64,768]{1,0:T(8,128)S(1)}, f32[8,768]{1,0:T(8,128)S(1)}) custom-call(s32[2]{0:T(128)S(1)} %pad_add_fusion.origin_ref, s32[3,1,1,16]{3,2,1,0:T(1,128)S(1)} %collective-permute-done.1.first_pick_ref, s32[3,1,1,16]{3,2,1,0:T(1,128)S(1)} %copy-done.2, ...), custom_call_target="tpu_custom_call" | custom-call | flops 2717908992 | bytes 8000000 | tf_op jit(solution)/shard_map/near_rows/pallas_call | solution.py:552
  19.3 7.4 %far_rows.1 = (bf16[256,256]{1,0:T(8,128)(2,1)S(1)}, f32[256,256]{1,0:T(8,128)S(1)}, bf16[256,256]{1,0:T(8,128)(2,1)S(1)}) custom-call(s32[1]{0:T(128)} %bitcast.1.side_ref, bf16[128,768]{1,0:T(8,128)(2,1)S(1)} %get-tuple-element.25.depth_ref, f32[64,768]{1,0:T(8,128)S(1)} %get-tuple-element.26.high_ref, f32[8,768]{1,0:T(8,128)S(1)} %get-tuple-element.27.where_ref, ...), custom_call_target="tpu_custom_call" | custom-call | tf_op jit(solution)/shard_map/far_rows/pallas_call | solution.py:569
  26.7 2.1 %collective-permute-start.4 = (bf16[256,256]{1,0:T(8,128)(2,1)S(1)}, bf16[256,256]{1,0:T(8,128)(2,1)S(1)}, u32[]{:S(2)}, u32[]{:S(2)}) collective-permute-start(bf16[256,256]{1,0:T(8,128)(2,1)S(1)} %get-tuple-element.31), channel_id=1, source_target_pairs={{0,1},{1,0},{2,3},{3,2},{4,5},{5,4},{6,7},{7,6},{8,9},{9,8},{10,11... | collective-permute-start | bytes 393224 | tf_op jit(solution)/shard_map/ppermute | solution.py:390
  29.8 3.4 %collective-permute-done.4.left_ref = bf16[256,256]{1,0:T(8,128)(2,1)S(1)} collective-permute-done((bf16[256,256]{1,0:T(8,128)(2,1)S(1)}, bf16[256,256]{1,0:T(8,128)(2,1)S(1)}, u32[]{:S(2)}, u32[]{:S(2)}) %collective-permute-start.4) | collective-permute-done | bytes 131104 | tf_op jit(solution)/shard_map/ppermute | solution.py:390
  34.5 3.7 %collective-permute-start.8 = (bf16[8,4480]{1,0:T(8,128)(2,1)S(1)}, bf16[8,4480]{1,0:T(8,128)(2,1)S(1)}, u32[]{:S(2)}, u32[]{:S(2)}) collective-permute-start(bf16[8,4480]{1,0:T(8,128)(2,1)S(1)} %get-tuple-element.34), channel_id=1, source_target_pairs={{0,24},{4,28},{8,16},{12,20},{16,8},{20,12},{24,0},{28,4},{1,25},{... | collective-permute-start | bytes 215048 | tf_op jit(solution)/shard_map/ppermute | solution.py:416
  38.9 2.2 %collective-permute-done.8 = bf16[8,4480]{1,0:T(8,128)(2,1)S(1)} collective-permute-done((bf16[8,4480]{1,0:T(8,128)(2,1)S(1)}, bf16[8,4480]{1,0:T(8,128)(2,1)S(1)}, u32[]{:S(2)}, u32[]{:S(2)}) %collective-permute-start.8) | collective-permute-done | bytes 71712 | tf_op jit(solution)/shard_map/ppermute | solution.py:416
  41.1 3.1 %collective-permute-done.7 = bf16[8,4480]{1,0:T(8,128)(2,1)S(1)} collective-permute-done((bf16[8,4480]{1,0:T(8,128)(2,1)S(1)}, bf16[8,4480]{1,0:T(8,128)(2,1)S(1)}, u32[]{:S(2)}, u32[]{:S(2)}) %collective-permute-start.7) | collective-permute-done | bytes 71712 | tf_op jit(solution)/shard_map/ppermute | solution.py:416
  44.3 4.4 %collective-permute-start.10 = (bf16[32,4480]{1,0:T(8,128)(2,1)S(1)}, bf16[32,4480]{1,0:T(8,128)(2,1)S(1)}, u32[]{:S(2)}, u32[]{:S(2)}) collective-permute-start(bf16[32,4480]{1,0:T(8,128)(2,1)S(1)} %pad_maximum_fusion.2.refs_0_.refs_1_), channel_id=1, source_target_pairs={{0,2},{2,0},{1,3},{3,1},{4,6},{6,4},{5,7},{7,5},{8,10},{10,8},{9,1... | collective-permute-start | bytes 860168 | tf_op jit(solution)/shard_map/ppermute | solution.py:409
  48.8 2.3 %collective-permute-start.14 = (bf16[8,4480]{1,0:T(8,128)(2,1)S(1)}, bf16[8,4480]{1,0:T(8,128)(2,1)S(1)}, u32[]{:S(2)}, u32[]{:S(2)}) collective-permute-start(bf16[8,4480]{1,0:T(8,128)(2,1)S(1)} %get-tuple-element.36), channel_id=1, source_target_pairs={{0,24},{4,28},{8,16},{12,20},{16,8},{20,12},{24,0},{28,4},{1,25},{... | collective-permute-start | bytes 215048 | tf_op jit(solution)/shard_map/ppermute | solution.py:416
  51.1 2.1 %collective-permute-start.12 = (bf16[8,4480]{1,0:T(8,128)(2,1)S(1)}, bf16[8,4480]{1,0:T(8,128)(2,1)S(1)}, u32[]{:S(2)}, u32[]{:S(2)}) collective-permute-start(bf16[8,4480]{1,0:T(8,128)(2,1)S(1)} %get-tuple-element.36), channel_id=1, source_target_pairs={{0,8},{4,12},{8,0},{12,4},{16,24},{20,28},{24,16},{28,20},{1,9},{5... | collective-permute-start | bytes 215048 | tf_op jit(solution)/shard_map/ppermute | solution.py:416
  53.2 1.6 %collective-permute-done.10.refs_2_.refs_3_ = bf16[32,4480]{1,0:T(8,128)(2,1)S(1)} collective-permute-done((bf16[32,4480]{1,0:T(8,128)(2,1)S(1)}, bf16[32,4480]{1,0:T(8,128)(2,1)S(1)}, u32[]{:S(2)}, u32[]{:S(2)}) %collective-permute-start.10) | collective-permute-done | bytes 286752 | tf_op jit(solution)/shard_map/ppermute | solution.py:409
  57.1 2.0 %collective-permute-start.17 = (bf16[48,4480]{1,0:T(8,128)(2,1)S(1)}, bf16[48,4480]{1,0:T(8,128)(2,1)S(1)}, u32[]{:S(2)}, u32[]{:S(2)}) collective-permute-start(bf16[48,4480]{1,0:T(8,128)(2,1)S(1)} %get-tuple-element.39), channel_id=1, source_target_pairs={{0,2},{2,0},{1,3},{3,1},{4,6},{6,4},{5,7},{7,5},{8,10},{10,8},{9,1... | collective-permute-start | bytes 1290248 | tf_op jit(solution)/shard_map/ppermute | solution.py:409
  59.2 1.6 %collective-permute-done.15.refs_5_.refs_6_ = bf16[32,4480]{1,0:T(8,128)(2,1)S(1)} collective-permute-done((bf16[32,4480]{1,0:T(8,128)(2,1)S(1)}, bf16[32,4480]{1,0:T(8,128)(2,1)S(1)}, u32[]{:S(2)}, u32[]{:S(2)}) %collective-permute-start.15) | collective-permute-done | bytes 286752 | tf_op jit(solution)/shard_map/ppermute | solution.py:412
  60.8 5.0 %weigh.1 = (bf16[20,64,256]{2,1,0:T(8,128)(2,1)S(1)}, f32[20,64,128]{2,1,0:T(8,128)S(1)}) custom-call(s32[1]{0:T(128)} %bitcast.index_ref, bf16[32,4480]{1,0:T(8,128)(2,1)S(1)} %pad_maximum_fusion.2.refs_0_.refs_1_, bf16[32,4480]{1,0:T(8,128)(2,1)S(1)} %collective-permute-done.9.refs_1_.refs_2_, ...), custom_call_target="tpu_custom_call" | custom-call | flops 167772160 | bytes 655360 | tf_op jit(solution)/shard_map/weigh/pallas_call | solution.py:460
  65.8 3.1 %collective-permute-done.17.refs_8_ = bf16[48,4480]{1,0:T(8,128)(2,1)S(1)} collective-permute-done((bf16[48,4480]{1,0:T(8,128)(2,1)S(1)}, bf16[48,4480]{1,0:T(8,128)(2,1)S(1)}, u32[]{:S(2)}, u32[]{:S(2)}) %collective-permute-start.17) | collective-permute-done | bytes 430112 | tf_op jit(solution)/shard_map/ppermute | solution.py:409
  69.1 1.6 %collective-permute-start.19 = (bf16[16,4480]{1,0:T(8,128)(2,1)S(1)}, bf16[16,4480]{1,0:T(8,128)(2,1)S(1)}, u32[]{:S(2)}, u32[]{:S(2)}) collective-permute-start(bf16[16,4480]{1,0:T(8,128)(2,1)S(1)} %slice.18), channel_id=1, source_target_pairs={{0,1},{1,0},{2,3},{3,2},{4,5},{5,4},{6,7},{7,6},{8,9},{9,8},{10,11... | collective-permute-start | bytes 430088 | tf_op jit(solution)/shard_map/ppermute | solution.py:406
  71.3 3.0 %collective-permute-done.19.refs_10_ = bf16[16,4480]{1,0:T(8,128)(2,1)S(1)} collective-permute-done((bf16[16,4480]{1,0:T(8,128)(2,1)S(1)}, bf16[16,4480]{1,0:T(8,128)(2,1)S(1)}, u32[]{:S(2)}, u32[]{:S(2)}) %collective-permute-start.19) | collective-permute-done | bytes 143392 | tf_op jit(solution)/shard_map/ppermute | solution.py:406
  74.3 1.5 %collective-permute-done.20.refs_11_ = bf16[16,4480]{1,0:T(8,128)(2,1)S(1)} collective-permute-done((bf16[16,4480]{1,0:T(8,128)(2,1)S(1)}, bf16[16,4480]{1,0:T(8,128)(2,1)S(1)}, u32[]{:S(2)}, u32[]{:S(2)}) %collective-permute-start.20) | collective-permute-done | bytes 143392 | tf_op jit(solution)/shard_map/ppermute | solution.py:409
  75.9 1.6 %collective-permute-done.21.refs_12_ = bf16[32,4480]{1,0:T(8,128)(2,1)S(1)} collective-permute-done((bf16[32,4480]{1,0:T(8,128)(2,1)S(1)}, bf16[32,4480]{1,0:T(8,128)(2,1)S(1)}, u32[]{:S(2)}, u32[]{:S(2)}) %collective-permute-start.21) | collective-permute-done | bytes 286752 | tf_op jit(solution)/shard_map/ppermute | solution.py:412
  77.5 13.7 %class_sums.1 = (f32[20,64,4096]{2,1,0:T(8,128)}, f32[20,64]{1,0:T(8,128)}) custom-call(s32[1]{0:T(128)} %bitcast.index_ref, bf16[20,64,256]{2,1,0:T(8,128)(2,1)S(1)} %get-tuple-element.40.refs_0_, bf16[32,4480]{1,0:T(8,128)(2,1)S(1)} %pad_maximum_fusion.2.refs_0_.refs_1_, bf16[32,4480]{1,0:T(8,128)(2,1)S(1)} %collective-permute-done.9.refs_1_.refs_2_, ...), custom_call_target="tpu_custom_call" | custom-call | flops 5368709120 | bytes 20971520 | tf_op jit(solution)/shard_map/class_sums/pallas_call | solution.py:493
  (65 shorter events, 8.4 us)
Async XLA Ops:
  3.5 3.4 %collective-permute-start = (bf16[48,64,128]{2,1,0:T(8,128)(2,1)}, bf16[48,64,128]{2,1,0:T(8,128)(2,1)}, u32[]{:S(2)}, u32[]{:S(2)}) collective-permute-start(bf16[48,64,128]{2,1,0:T(8,128)(2,1)} %get-tuple-element.47), channel_id=1, source_target_pairs={{0,4},{4,0},{8,12},{12,8},{16,20},{20,16},{24,28},{28,24},{1,5},{5... | collective-permute-start | bytes 2359304 | tf_op jit(solution)/shard_map/ppermute | solution.py:390
  4.0 15.3 %collective-permute-start.3 = (bf16[48,64,128]{2,1,0:T(8,128)(2,1)}, bf16[48,64,128]{2,1,0:T(8,128)(2,1)}, u32[]{:S(2)}, u32[]{:S(2)}) collective-permute-start(bf16[48,64,128]{2,1,0:T(8,128)(2,1)} %get-tuple-element.46), channel_id=1, source_target_pairs={{4,8},{8,4},{12,16},{16,12},{20,24},{24,20},{5,9},{9,5},{13,17},{1... | collective-permute-start | bytes 2359304 | tf_op jit(solution)/shard_map/ppermute | solution.py:390
  7.0 6.0 %collective-permute-start.2 = (s32[3,1,1,16]{3,2,1,0:T(1,128)S(1)}, s32[3,1,1,16]{3,2,1,0:T(1,128)S(1)}, u32[]{:S(2)}, u32[]{:S(2)}) collective-permute-start(s32[3,1,1,16]{3,2,1,0:T(1,128)S(1)} %copy-done.2), channel_id=1, source_target_pairs={{1,2},{2,1},{5,6},{6,5},{9,10},{10,9},{13,14},{14,13},{17,18},{18,... | collective-permute-start | bytes 584 | tf_op jit(solution)/shard_map/ppermute | solution.py:390
  7.6 6.9 %collective-permute-start.1 = (s32[3,1,1,16]{3,2,1,0:T(1,128)S(1)}, s32[3,1,1,16]{3,2,1,0:T(1,128)S(1)}, u32[]{:S(2)}, u32[]{:S(2)}) collective-permute-start(s32[3,1,1,16]{3,2,1,0:T(1,128)S(1)} %copy-done.2), channel_id=1, source_target_pairs={{0,1},{1,0},{2,3},{3,2},{4,5},{5,4},{6,7},{7,6},{8,9},{9,8},{10,11... | collective-permute-start | bytes 584 | tf_op jit(solution)/shard_map/ppermute | solution.py:390
  14.5 46.3 %slice-start = ((s8[10485760]{0:T(1024)(128)(4,1)}), s8[4194304]{0:T(1024)(128)(4,1)S(1)}, s32[]{:S(2)}) async-start(s8[10485760]{0:T(1024)(128)(4,1)} %bitcast.12), calls=%async_computation | async-start | bytes 8388608
  14.5 46.3 %slice-start.1 = ((s8[10485760]{0:T(1024)(128)(4,1)}), s8[4194304]{0:T(1024)(128)(4,1)S(1)}, s32[]{:S(2)}) async-start(s8[10485760]{0:T(1024)(128)(4,1)} %bitcast.12), calls=%async_computation.1 | async-start | bytes 8388608
  26.7 6.4 %collective-permute-start.4 = (bf16[256,256]{1,0:T(8,128)(2,1)S(1)}, bf16[256,256]{1,0:T(8,128)(2,1)S(1)}, u32[]{:S(2)}, u32[]{:S(2)}) collective-permute-start(bf16[256,256]{1,0:T(8,128)(2,1)S(1)} %get-tuple-element.31), channel_id=1, source_target_pairs={{0,1},{1,0},{2,3},{3,2},{4,5},{5,4},{6,7},{7,6},{8,9},{9,8},{10,11... | collective-permute-start | bytes 393224 | tf_op jit(solution)/shard_map/ppermute | solution.py:390
  28.8 4.3 %collective-permute-start.5 = (bf16[256,256]{1,0:T(8,128)(2,1)S(1)}, bf16[256,256]{1,0:T(8,128)(2,1)S(1)}, u32[]{:S(2)}, u32[]{:S(2)}) collective-permute-start(bf16[256,256]{1,0:T(8,128)(2,1)S(1)} %get-tuple-element.32), channel_id=1, source_target_pairs={{1,2},{2,1},{5,6},{6,5},{9,10},{10,9},{13,14},{14,13},{17,18},{18,... | collective-permute-start | bytes 393224 | tf_op jit(solution)/shard_map/ppermute | solution.py:390
  34.5 6.7 %collective-permute-start.8 = (bf16[8,4480]{1,0:T(8,128)(2,1)S(1)}, bf16[8,4480]{1,0:T(8,128)(2,1)S(1)}, u32[]{:S(2)}, u32[]{:S(2)}) collective-permute-start(bf16[8,4480]{1,0:T(8,128)(2,1)S(1)} %get-tuple-element.34), channel_id=1, source_target_pairs={{0,24},{4,28},{8,16},{12,20},{16,8},{20,12},{24,0},{28,4},{1,25},{... | collective-permute-start | bytes 215048 | tf_op jit(solution)/shard_map/ppermute | solution.py:416
  38.2 6.1 %collective-permute-start.7 = (bf16[8,4480]{1,0:T(8,128)(2,1)S(1)}, bf16[8,4480]{1,0:T(8,128)(2,1)S(1)}, u32[]{:S(2)}, u32[]{:S(2)}) collective-permute-start(bf16[8,4480]{1,0:T(8,128)(2,1)S(1)} %get-tuple-element.34), channel_id=1, source_target_pairs={{0,16},{4,20},{8,24},{12,28},{16,0},{20,4},{24,8},{28,12},{1,17},{... | collective-permute-start | bytes 215048 | tf_op jit(solution)/shard_map/ppermute | solution.py:416
  38.2 6.1 %collective-permute-start.6 = (bf16[8,4480]{1,0:T(8,128)(2,1)S(1)}, bf16[8,4480]{1,0:T(8,128)(2,1)S(1)}, u32[]{:S(2)}, u32[]{:S(2)}) collective-permute-start(bf16[8,4480]{1,0:T(8,128)(2,1)S(1)} %get-tuple-element.34), channel_id=1, source_target_pairs={{0,8},{4,12},{8,0},{12,4},{16,24},{20,28},{24,16},{28,20},{1,9},{5... | collective-permute-start | bytes 215048 | tf_op jit(solution)/shard_map/ppermute | solution.py:416
  44.3 10.5 %collective-permute-start.10 = (bf16[32,4480]{1,0:T(8,128)(2,1)S(1)}, bf16[32,4480]{1,0:T(8,128)(2,1)S(1)}, u32[]{:S(2)}, u32[]{:S(2)}) collective-permute-start(bf16[32,4480]{1,0:T(8,128)(2,1)S(1)} %pad_maximum_fusion.2.refs_0_.refs_1_), channel_id=1, source_target_pairs={{0,2},{2,0},{1,3},{3,1},{4,6},{6,4},{5,7},{7,5},{8,10},{10,8},{9,1... | collective-permute-start | bytes 860168 | tf_op jit(solution)/shard_map/ppermute | solution.py:409
  48.8 7.5 %collective-permute-start.9 = (bf16[32,4480]{1,0:T(8,128)(2,1)S(1)}, bf16[32,4480]{1,0:T(8,128)(2,1)S(1)}, u32[]{:S(2)}, u32[]{:S(2)}) collective-permute-start(bf16[32,4480]{1,0:T(8,128)(2,1)S(1)} %pad_maximum_fusion.2.refs_0_.refs_1_), channel_id=1, source_target_pairs={{0,1},{1,0},{2,3},{3,2},{4,5},{5,4},{6,7},{7,6},{8,9},{9,8},{10,11... | collective-permute-start | bytes 860168 | tf_op jit(solution)/shard_map/ppermute | solution.py:406
  48.8 8.2 %collective-permute-start.14 = (bf16[8,4480]{1,0:T(8,128)(2,1)S(1)}, bf16[8,4480]{1,0:T(8,128)(2,1)S(1)}, u32[]{:S(2)}, u32[]{:S(2)}) collective-permute-start(bf16[8,4480]{1,0:T(8,128)(2,1)S(1)} %get-tuple-element.36), channel_id=1, source_target_pairs={{0,24},{4,28},{8,16},{12,20},{16,8},{20,12},{24,0},{28,4},{1,25},{... | collective-permute-start | bytes 215048 | tf_op jit(solution)/shard_map/ppermute | solution.py:416
  51.1 5.9 %collective-permute-start.13 = (bf16[8,4480]{1,0:T(8,128)(2,1)S(1)}, bf16[8,4480]{1,0:T(8,128)(2,1)S(1)}, u32[]{:S(2)}, u32[]{:S(2)}) collective-permute-start(bf16[8,4480]{1,0:T(8,128)(2,1)S(1)} %get-tuple-element.36), channel_id=1, source_target_pairs={{0,16},{4,20},{8,24},{12,28},{16,0},{20,4},{24,8},{28,12},{1,17},{... | collective-permute-start | bytes 215048 | tf_op jit(solution)/shard_map/ppermute | solution.py:416
  51.1 5.4 %collective-permute-start.12 = (bf16[8,4480]{1,0:T(8,128)(2,1)S(1)}, bf16[8,4480]{1,0:T(8,128)(2,1)S(1)}, u32[]{:S(2)}, u32[]{:S(2)}) collective-permute-start(bf16[8,4480]{1,0:T(8,128)(2,1)S(1)} %get-tuple-element.36), channel_id=1, source_target_pairs={{0,8},{4,12},{8,0},{12,4},{16,24},{20,28},{24,16},{28,20},{1,9},{5... | collective-permute-start | bytes 215048 | tf_op jit(solution)/shard_map/ppermute | solution.py:416
  56.3 4.5 %collective-permute-start.11 = (bf16[96,4480]{1,0:T(8,128)(2,1)S(1)}, bf16[96,4480]{1,0:T(8,128)(2,1)S(1)}, u32[]{:S(2)}, u32[]{:S(2)}) collective-permute-start(bf16[96,4480]{1,0:T(8,128)(2,1)S(1)} %pad_maximum_fusion), channel_id=1, source_target_pairs={{0,4},{4,0},{8,12},{12,8},{16,20},{20,16},{24,28},{28,24},{1,5},{5... | collective-permute-start | bytes 2580488 | tf_op jit(solution)/shard_map/ppermute | solution.py:412
  57.1 11.8 %collective-permute-start.17 = (bf16[48,4480]{1,0:T(8,128)(2,1)S(1)}, bf16[48,4480]{1,0:T(8,128)(2,1)S(1)}, u32[]{:S(2)}, u32[]{:S(2)}) collective-permute-start(bf16[48,4480]{1,0:T(8,128)(2,1)S(1)} %get-tuple-element.39), channel_id=1, source_target_pairs={{0,2},{2,0},{1,3},{3,1},{4,6},{6,4},{5,7},{7,5},{8,10},{10,8},{9,1... | collective-permute-start | bytes 1290248 | tf_op jit(solution)/shard_map/ppermute | solution.py:409
  59.1 10.0 %collective-permute-start.16 = (bf16[48,4480]{1,0:T(8,128)(2,1)S(1)}, bf16[48,4480]{1,0:T(8,128)(2,1)S(1)}, u32[]{:S(2)}, u32[]{:S(2)}) collective-permute-start(bf16[48,4480]{1,0:T(8,128)(2,1)S(1)} %get-tuple-element.37), channel_id=1, source_target_pairs={{0,1},{1,0},{2,3},{3,2},{4,5},{5,4},{6,7},{7,6},{8,9},{9,8},{10,11... | collective-permute-start | bytes 1290248 | tf_op jit(solution)/shard_map/ppermute | solution.py:406
  59.2 1.6 %collective-permute-start.15 = (bf16[32,4480]{1,0:T(8,128)(2,1)S(1)}, bf16[32,4480]{1,0:T(8,128)(2,1)S(1)}, u32[]{:S(2)}, u32[]{:S(2)}) collective-permute-start(bf16[32,4480]{1,0:T(8,128)(2,1)S(1)} %slice.17.refs_4_.refs_5_), channel_id=1, source_target_pairs={{0,4},{4,0},{8,12},{12,8},{16,20},{20,16},{24,28},{28,24},{1,5},{5... | collective-permute-start | bytes 860168 | tf_op jit(solution)/shard_map/ppermute | solution.py:412
  69.1 5.2 %collective-permute-start.19 = (bf16[16,4480]{1,0:T(8,128)(2,1)S(1)}, bf16[16,4480]{1,0:T(8,128)(2,1)S(1)}, u32[]{:S(2)}, u32[]{:S(2)}) collective-permute-start(bf16[16,4480]{1,0:T(8,128)(2,1)S(1)} %slice.18), channel_id=1, source_target_pairs={{0,1},{1,0},{2,3},{3,2},{4,5},{5,4},{6,7},{7,6},{8,9},{9,8},{10,11... | collective-permute-start | bytes 430088 | tf_op jit(solution)/shard_map/ppermute | solution.py:406
  70.7 5.1 %collective-permute-start.20 = (bf16[16,4480]{1,0:T(8,128)(2,1)S(1)}, bf16[16,4480]{1,0:T(8,128)(2,1)S(1)}, u32[]{:S(2)}, u32[]{:S(2)}) collective-permute-start(bf16[16,4480]{1,0:T(8,128)(2,1)S(1)} %slice.19), channel_id=1, source_target_pairs={{0,2},{2,0},{1,3},{3,1},{4,6},{6,4},{5,7},{7,5},{8,10},{10,8},{9,1... | collective-permute-start | bytes 430088 | tf_op jit(solution)/shard_map/ppermute | solution.py:409
  71.2 6.2 %collective-permute-start.18 = (bf16[96,4480]{1,0:T(8,128)(2,1)S(1)}, bf16[96,4480]{1,0:T(8,128)(2,1)S(1)}, u32[]{:S(2)}, u32[]{:S(2)}) collective-permute-start(bf16[96,4480]{1,0:T(8,128)(2,1)S(1)} %pad_maximum_fusion.1), channel_id=1, source_target_pairs={{0,4},{4,0},{8,12},{12,8},{16,20},{20,16},{24,28},{28,24},{1,5},{5... | collective-permute-start | bytes 2580488 | tf_op jit(solution)/shard_map/ppermute | solution.py:412
  75.8 1.6 %collective-permute-start.21 = (bf16[32,4480]{1,0:T(8,128)(2,1)S(1)}, bf16[32,4480]{1,0:T(8,128)(2,1)S(1)}, u32[]{:S(2)}, u32[]{:S(2)}) collective-permute-start(bf16[32,4480]{1,0:T(8,128)(2,1)S(1)} %pad_maximum_fusion.3), channel_id=1, source_target_pairs={{0,4},{4,0},{8,12},{12,8},{16,20},{20,16},{24,28},{28,24},{1,5},{5... | collective-permute-start | bytes 860168 | tf_op jit(solution)/shard_map/ppermute | solution.py:412
  (8 other events, 114.2 us)

commit v8 on v7

--- a/solution.py
+++ b/solution.py
@@ -584,6 +584,7 @@
     )(side[None], *tables, first_halo, second_halo, plane, near)
     from_first, from_second = exchange(for_first, "bank", True), exchange(for_second, "bank", False)
 
+    mid, orientations, orient_weight = lax.optimization_barrier((mid, orientations, orient_weight))
     live_slots = jnp.arange(slots) < box_counts[0, 0]
     matches = orientations[0, 0][:, :, None] == jnp.arange(R)[None, None, :]
     multiplicity = jnp.sum(

time: 91.5 us -> 89.9 us (0.983)
  waiting for transfers between devices: 24.7 us -> 22.6 us
    ppermute x3, waiting for transfers between devices: 6.14 us -> 4.07 us  [along_y(): return lax.ppermute(value, 'bank', [(0, 2), (2, 0), (1, 3), (3, 1)])]
    ppermute x6, waiting for transfers between devices: 4.86 us -> 3.79 us  [exchange(): return lax.ppermute(value, axis, pairs)]
where the time goes in v8:
time: 89.9 us; the launch traced here: 89.7 us
  Pallas kernels  32.2 us (36%)
  starting transfers between devices  29.1 us (32%)
  waiting for transfers between devices  22.6 us (25%)
  local copies, waits for them, and re-layouts  2.99 us (3%)
  between operations  1.76 us (2%)
  other arithmetic  1.04 us (1%)
    pallas_call x1, Pallas kernels, sum_blocks(): pl.pallas_call(functools.partial(sum_kernel, early=len(parts), blocks=len...  13.7 us
    ppermute x6, starting transfers between devices, exchange(): return lax.ppermute(value, axis, pairs)  11.2 us
    ppermute x6, starting transfers between devices, line_of(): lax.ppermute(part, 'tile', [(i, i ^ by) for i in range(tiles)])  8.84 us
    pallas_call x1, Pallas kernels, body(): pl.pallas_call(functools.partial(far_kernel, wide=wide), in_specs=[smem]...  7.44 us
    ppermute x3, starting transfers between devices, along_y(): return lax.ppermute(value, 'bank', [(0, 2), (2, 0), (1, 3), (3, 1)])  7.21 us
    ppermute x6, waiting for transfers between devices, line_of(): lax.ppermute(part, 'tile', [(i, i ^ by) for i in range(tiles)])  6.45 us
    ppermute x3, waiting for transfers between devices, along_x(): return lax.ppermute(value, 'bank', [(0, 1), (1, 0), (2, 3), (3, 2)])  5.19 us
    pallas_call x1, Pallas kernels, weigh_blocks(): pl.pallas_call(functools.partial(weigh_kernel, blocks=len(blocks), known=...  4.97 us
  transfers between devices with their start and end apart: 22, of which 14 were waited for; matrix products, arithmetic and copies ran while one was open for 1% of the time, Pallas kernels for 11%

profile of v8, /device:TPU:0, one launch (start us, length us, event | category | flops | bytes accessed | tf_op | source)
XLA Modules:
  0.0 89.7 jit_solution(3037890960779338626)
XLA Ops:
  0.7 2.8 %constant_dynamic-slice_fusion = (bf16[48,64,128]{2,1,0:T(8,128)(2,1)}, bf16[48,64,128]{2,1,0:T(8,128)(2,1)}) fusion(bf16[64,64,128]{2,1,0:T(8,128)(2,1)} %volume_ref.1, s32[]{:T(128)S(6)} %select_n.18, s32[]{:T(128)S(6)} %select_n.17), kind=kLoop, calls=%fused_computation.20 | loop fusion | bytes 3145736 | tf_op jit(solution)/shard_map/dynamic_slice | solution.py:537
  3.9 1.6 %collective-permute-start.3 = (bf16[48,64,128]{2,1,0:T(8,128)(2,1)}, bf16[48,64,128]{2,1,0:T(8,128)(2,1)}, u32[]{:S(2)}, u32[]{:S(2)}) collective-permute-start(bf16[48,64,128]{2,1,0:T(8,128)(2,1)} %get-tuple-element.52), channel_id=1, source_target_pairs={{4,8},{8,4},{12,16},{16,12},{20,24},{24,20},{5,9},{9,5},{13,17},{1... | collective-permute-start | bytes 2359304 | tf_op jit(solution)/shard_map/ppermute | solution.py:390
  6.9 5.7 %collective-permute-start.1 = (s32[3,1,1,16]{3,2,1,0:T(1,128)S(1)}, s32[3,1,1,16]{3,2,1,0:T(1,128)S(1)}, u32[]{:S(2)}, u32[]{:S(2)}) collective-permute-start(s32[3,1,1,16]{3,2,1,0:T(1,128)S(1)} %copy-done.2), channel_id=1, source_target_pairs={{0,1},{1,0},{2,3},{3,2},{4,5},{5,4},{6,7},{7,6},{8,9},{9,8},{10,11... | collective-permute-start | bytes 584 | tf_op jit(solution)/shard_map/ppermute | solution.py:390
  12.6 1.5 %collective-permute-done.1.first_pick_ref = s32[3,1,1,16]{3,2,1,0:T(1,128)S(1)} collective-permute-done((s32[3,1,1,16]{3,2,1,0:T(1,128)S(1)}, s32[3,1,1,16]{3,2,1,0:T(1,128)S(1)}, u32[]{:S(2)}, u32[]{:S(2)}) %collective-permute-start.1) | collective-permute-done | bytes 224 | tf_op jit(solution)/shard_map/ppermute | solution.py:390
  14.1 4.8 %near_rows.1 = (f32[304,768]{1,0:T(8,128)S(1)}, bf16[128,768]{1,0:T(8,128)(2,1)S(1)}, f32[64,768]{1,0:T(8,128)S(1)}, f32[8,768]{1,0:T(8,128)S(1)}) custom-call(s32[2]{0:T(128)S(1)} %pad_add_fusion.origin_ref, s32[3,1,1,16]{3,2,1,0:T(1,128)S(1)} %collective-permute-done.1.first_pick_ref, s32[3,1,1,16]{3,2,1,0:T(1,128)S(1)} %copy-done.2, ...), custom_call_target="tpu_custom_call" | custom-call | flops 2717908992 | bytes 8000000 | tf_op jit(solution)/shard_map/near_rows/pallas_call | solution.py:552
  18.9 7.4 %far_rows.1 = (bf16[256,256]{1,0:T(8,128)(2,1)S(1)}, f32[256,256]{1,0:T(8,128)S(1)}, bf16[256,256]{1,0:T(8,128)(2,1)S(1)}) custom-call(s32[1]{0:T(128)} %bitcast.1.side_ref, bf16[128,768]{1,0:T(8,128)(2,1)S(1)} %get-tuple-element.28.depth_ref, f32[64,768]{1,0:T(8,128)S(1)} %get-tuple-element.29.high_ref, f32[8,768]{1,0:T(8,128)S(1)} %get-tuple-element.30.where_ref, ...), custom_call_target="tpu_custom_call" | custom-call | tf_op jit(solution)/shard_map/far_rows/pallas_call | solution.py:569
  26.4 2.1 %collective-permute-start.4 = (bf16[256,256]{1,0:T(8,128)(2,1)S(1)}, bf16[256,256]{1,0:T(8,128)(2,1)S(1)}, u32[]{:S(2)}, u32[]{:S(2)}) collective-permute-start(bf16[256,256]{1,0:T(8,128)(2,1)S(1)} %get-tuple-element.35), channel_id=1, source_target_pairs={{0,1},{1,0},{2,3},{3,2},{4,5},{5,4},{6,7},{7,6},{8,9},{9,8},{10,11... | collective-permute-start | bytes 393224 | tf_op jit(solution)/shard_map/ppermute | solution.py:390
  30.1 2.3 %collective-permute-done.4.left_ref = bf16[256,256]{1,0:T(8,128)(2,1)S(1)} collective-permute-done((bf16[256,256]{1,0:T(8,128)(2,1)S(1)}, bf16[256,256]{1,0:T(8,128)(2,1)S(1)}, u32[]{:S(2)}, u32[]{:S(2)}) %collective-permute-start.4) | collective-permute-done | bytes 131104 | tf_op jit(solution)/shard_map/ppermute | solution.py:390
  32.4 1.4 %join.1 = (bf16[8,4480]{1,0:T(8,128)(2,1)S(1)}, bf16[8,4480]{1,0:T(8,128)(2,1)S(1)}) custom-call(f32[256,256]{1,0:T(8,128)S(1)} %get-tuple-element.34.own_ref, bf16[256,256]{1,0:T(8,128)(2,1)S(1)} %collective-permute-done.4.left_ref, bf16[256,256]{1,0:T(8,128)(2,1)S(1)} %collective-permute-done.5.right_ref, ...), custom_call_target="tpu_custom_call" | custom-call | tf_op jit(solution)/shard_map/join/pallas_call | solution.py:595
  33.8 3.7 %collective-permute-start.8 = (bf16[8,4480]{1,0:T(8,128)(2,1)S(1)}, bf16[8,4480]{1,0:T(8,128)(2,1)S(1)}, u32[]{:S(2)}, u32[]{:S(2)}) collective-permute-start(bf16[8,4480]{1,0:T(8,128)(2,1)S(1)} %get-tuple-element.40), channel_id=1, source_target_pairs={{0,24},{4,28},{8,16},{12,20},{16,8},{20,12},{24,0},{28,4},{1,25},{... | collective-permute-start | bytes 215048 | tf_op jit(solution)/shard_map/ppermute | solution.py:416
  38.2 2.2 %collective-permute-done.8 = bf16[8,4480]{1,0:T(8,128)(2,1)S(1)} collective-permute-done((bf16[8,4480]{1,0:T(8,128)(2,1)S(1)}, bf16[8,4480]{1,0:T(8,128)(2,1)S(1)}, u32[]{:S(2)}, u32[]{:S(2)}) %collective-permute-start.8) | collective-permute-done | bytes 71712 | tf_op jit(solution)/shard_map/ppermute | solution.py:416
  40.4 3.1 %collective-permute-done.7 = bf16[8,4480]{1,0:T(8,128)(2,1)S(1)} collective-permute-done((bf16[8,4480]{1,0:T(8,128)(2,1)S(1)}, bf16[8,4480]{1,0:T(8,128)(2,1)S(1)}, u32[]{:S(2)}, u32[]{:S(2)}) %collective-permute-start.7) | collective-permute-done | bytes 71712 | tf_op jit(solution)/shard_map/ppermute | solution.py:416
  43.6 4.8 %collective-permute-start.10 = (bf16[32,4480]{1,0:T(8,128)(2,1)S(1)}, bf16[32,4480]{1,0:T(8,128)(2,1)S(1)}, u32[]{:S(2)}, u32[]{:S(2)}) collective-permute-start(bf16[32,4480]{1,0:T(8,128)(2,1)S(1)} %pad_maximum_fusion.2.refs_0_.refs_1_), channel_id=1, source_target_pairs={{0,2},{2,0},{1,3},{3,1},{4,6},{6,4},{5,7},{7,5},{8,10},{10,8},{9,1... | collective-permute-start | bytes 860168 | tf_op jit(solution)/shard_map/ppermute | solution.py:409
  48.4 2.1 %collective-permute-start.14 = (bf16[8,4480]{1,0:T(8,128)(2,1)S(1)}, bf16[8,4480]{1,0:T(8,128)(2,1)S(1)}, u32[]{:S(2)}, u32[]{:S(2)}) collective-permute-start(bf16[8,4480]{1,0:T(8,128)(2,1)S(1)} %get-tuple-element.42), channel_id=1, source_target_pairs={{0,24},{4,28},{8,16},{12,20},{16,8},{20,12},{24,0},{28,4},{1,25},{... | collective-permute-start | bytes 215048 | tf_op jit(solution)/shard_map/ppermute | solution.py:416
  50.4 2.3 %collective-permute-start.12 = (bf16[8,4480]{1,0:T(8,128)(2,1)S(1)}, bf16[8,4480]{1,0:T(8,128)(2,1)S(1)}, u32[]{:S(2)}, u32[]{:S(2)}) collective-permute-start(bf16[8,4480]{1,0:T(8,128)(2,1)S(1)} %get-tuple-element.42), channel_id=1, source_target_pairs={{0,8},{4,12},{8,0},{12,4},{16,24},{20,28},{24,16},{28,20},{1,9},{5... | collective-permute-start | bytes 215048 | tf_op jit(solution)/shard_map/ppermute | solution.py:416
  53.4 1.6 %collective-permute-done.9.refs_1_.refs_2_ = bf16[32,4480]{1,0:T(8,128)(2,1)S(1)} collective-permute-done((bf16[32,4480]{1,0:T(8,128)(2,1)S(1)}, bf16[32,4480]{1,0:T(8,128)(2,1)S(1)}, u32[]{:S(2)}, u32[]{:S(2)}) %collective-permute-start.9) | collective-permute-done | bytes 286752 | tf_op jit(solution)/shard_map/ppermute | solution.py:406
  56.4 1.7 %collective-permute-start.17 = (bf16[48,4480]{1,0:T(8,128)(2,1)S(1)}, bf16[48,4480]{1,0:T(8,128)(2,1)S(1)}, u32[]{:S(2)}, u32[]{:S(2)}) collective-permute-start(bf16[48,4480]{1,0:T(8,128)(2,1)S(1)} %get-tuple-element.45), channel_id=1, source_target_pairs={{0,2},{2,0},{1,3},{3,1},{4,6},{6,4},{5,7},{7,5},{8,10},{10,8},{9,1... | collective-permute-start | bytes 1290248 | tf_op jit(solution)/shard_map/ppermute | solution.py:409
  58.7 1.6 %collective-permute-done.15.refs_5_.refs_6_ = bf16[32,4480]{1,0:T(8,128)(2,1)S(1)} collective-permute-done((bf16[32,4480]{1,0:T(8,128)(2,1)S(1)}, bf16[32,4480]{1,0:T(8,128)(2,1)S(1)}, u32[]{:S(2)}, u32[]{:S(2)}) %collective-permute-start.15) | collective-permute-done | bytes 286752 | tf_op jit(solution)/shard_map/ppermute | solution.py:412
  60.3 5.0 %weigh.1 = (bf16[20,64,256]{2,1,0:T(8,128)(2,1)S(1)}, f32[20,64,128]{2,1,0:T(8,128)S(1)}) custom-call(s32[1]{0:T(128)} %bitcast.index_ref, bf16[32,4480]{1,0:T(8,128)(2,1)S(1)} %pad_maximum_fusion.2.refs_0_.refs_1_, bf16[32,4480]{1,0:T(8,128)(2,1)S(1)} %collective-permute-done.9.refs_1_.refs_2_, ...), custom_call_target="tpu_custom_call" | custom-call | flops 167772160 | bytes 655360 | tf_op jit(solution)/shard_map/weigh/pallas_call | solution.py:460
  65.3 2.4 %collective-permute-done.17.refs_8_ = bf16[48,4480]{1,0:T(8,128)(2,1)S(1)} collective-permute-done((bf16[48,4480]{1,0:T(8,128)(2,1)S(1)}, bf16[48,4480]{1,0:T(8,128)(2,1)S(1)}, u32[]{:S(2)}, u32[]{:S(2)}) %collective-permute-start.17) | collective-permute-done | bytes 430112 | tf_op jit(solution)/shard_map/ppermute | solution.py:409
  68.1 1.1 %collective-permute-start.19 = (bf16[16,4480]{1,0:T(8,128)(2,1)S(1)}, bf16[16,4480]{1,0:T(8,128)(2,1)S(1)}, u32[]{:S(2)}, u32[]{:S(2)}) collective-permute-start(bf16[16,4480]{1,0:T(8,128)(2,1)S(1)} %slice.18), channel_id=1, source_target_pairs={{0,1},{1,0},{2,3},{3,2},{4,5},{5,4},{6,7},{7,6},{8,9},{9,8},{10,11... | collective-permute-start | bytes 430088 | tf_op jit(solution)/shard_map/ppermute | solution.py:406
  70.0 3.3 %collective-permute-done.19.refs_10_ = bf16[16,4480]{1,0:T(8,128)(2,1)S(1)} collective-permute-done((bf16[16,4480]{1,0:T(8,128)(2,1)S(1)}, bf16[16,4480]{1,0:T(8,128)(2,1)S(1)}, u32[]{:S(2)}, u32[]{:S(2)}) %collective-permute-start.19) | collective-permute-done | bytes 143392 | tf_op jit(solution)/shard_map/ppermute | solution.py:406
  74.3 1.6 %collective-permute-done.21.refs_12_ = bf16[32,4480]{1,0:T(8,128)(2,1)S(1)} collective-permute-done((bf16[32,4480]{1,0:T(8,128)(2,1)S(1)}, bf16[32,4480]{1,0:T(8,128)(2,1)S(1)}, u32[]{:S(2)}, u32[]{:S(2)}) %collective-permute-start.21) | collective-permute-done | bytes 286752 | tf_op jit(solution)/shard_map/ppermute | solution.py:412
  75.9 13.7 %class_sums.1 = (f32[20,64,4096]{2,1,0:T(8,128)}, f32[20,64]{1,0:T(8,128)}) custom-call(s32[1]{0:T(128)} %bitcast.index_ref, bf16[20,64,256]{2,1,0:T(8,128)(2,1)S(1)} %get-tuple-element.46.refs_0_, bf16[32,4480]{1,0:T(8,128)(2,1)S(1)} %pad_maximum_fusion.2.refs_0_.refs_1_, bf16[32,4480]{1,0:T(8,128)(2,1)S(1)} %collective-permute-done.9.refs_1_.refs_2_, ...), custom_call_target="tpu_custom_call" | custom-call | flops 5368709120 | bytes 20971520 | tf_op jit(solution)/shard_map/class_sums/pallas_call | solution.py:493
  (65 shorter events, 8.6 us)
Async XLA Ops:
  3.5 2.7 %collective-permute-start = (bf16[48,64,128]{2,1,0:T(8,128)(2,1)}, bf16[48,64,128]{2,1,0:T(8,128)(2,1)}, u32[]{:S(2)}, u32[]{:S(2)}) collective-permute-start(bf16[48,64,128]{2,1,0:T(8,128)(2,1)} %get-tuple-element.53), channel_id=1, source_target_pairs={{0,4},{4,0},{8,12},{12,8},{16,20},{20,16},{24,28},{28,24},{1,5},{5... | collective-permute-start | bytes 2359304 | tf_op jit(solution)/shard_map/ppermute | solution.py:390
  3.9 14.9 %collective-permute-start.3 = (bf16[48,64,128]{2,1,0:T(8,128)(2,1)}, bf16[48,64,128]{2,1,0:T(8,128)(2,1)}, u32[]{:S(2)}, u32[]{:S(2)}) collective-permute-start(bf16[48,64,128]{2,1,0:T(8,128)(2,1)} %get-tuple-element.52), channel_id=1, source_target_pairs={{4,8},{8,4},{12,16},{16,12},{20,24},{24,20},{5,9},{9,5},{13,17},{1... | collective-permute-start | bytes 2359304 | tf_op jit(solution)/shard_map/ppermute | solution.py:390
  6.2 6.4 %collective-permute-start.2 = (s32[3,1,1,16]{3,2,1,0:T(1,128)S(1)}, s32[3,1,1,16]{3,2,1,0:T(1,128)S(1)}, u32[]{:S(2)}, u32[]{:S(2)}) collective-permute-start(s32[3,1,1,16]{3,2,1,0:T(1,128)S(1)} %copy-done.2), channel_id=1, source_target_pairs={{1,2},{2,1},{5,6},{6,5},{9,10},{10,9},{13,14},{14,13},{17,18},{18,... | collective-permute-start | bytes 584 | tf_op jit(solution)/shard_map/ppermute | solution.py:390
  6.9 7.2 %collective-permute-start.1 = (s32[3,1,1,16]{3,2,1,0:T(1,128)S(1)}, s32[3,1,1,16]{3,2,1,0:T(1,128)S(1)}, u32[]{:S(2)}, u32[]{:S(2)}) collective-permute-start(s32[3,1,1,16]{3,2,1,0:T(1,128)S(1)} %copy-done.2), channel_id=1, source_target_pairs={{0,1},{1,0},{2,3},{3,2},{4,5},{5,4},{6,7},{7,6},{8,9},{9,8},{10,11... | collective-permute-start | bytes 584 | tf_op jit(solution)/shard_map/ppermute | solution.py:390
  14.1 46.2 %slice-start = ((s8[10485760]{0:T(1024)(128)(4,1)}), s8[4194304]{0:T(1024)(128)(4,1)S(1)}, s32[]{:S(2)}) async-start(s8[10485760]{0:T(1024)(128)(4,1)} %bitcast.12), calls=%async_computation | async-start | bytes 8388608
  14.1 46.2 %slice-start.1 = ((s8[10485760]{0:T(1024)(128)(4,1)}), s8[4194304]{0:T(1024)(128)(4,1)S(1)}, s32[]{:S(2)}) async-start(s8[10485760]{0:T(1024)(128)(4,1)} %bitcast.12), calls=%async_computation.1 | async-start | bytes 8388608
  26.4 6.0 %collective-permute-start.4 = (bf16[256,256]{1,0:T(8,128)(2,1)S(1)}, bf16[256,256]{1,0:T(8,128)(2,1)S(1)}, u32[]{:S(2)}, u32[]{:S(2)}) collective-permute-start(bf16[256,256]{1,0:T(8,128)(2,1)S(1)} %get-tuple-element.35), channel_id=1, source_target_pairs={{0,1},{1,0},{2,3},{3,2},{4,5},{5,4},{6,7},{7,6},{8,9},{9,8},{10,11... | collective-permute-start | bytes 393224 | tf_op jit(solution)/shard_map/ppermute | solution.py:390
  28.5 3.9 %collective-permute-start.5 = (bf16[256,256]{1,0:T(8,128)(2,1)S(1)}, bf16[256,256]{1,0:T(8,128)(2,1)S(1)}, u32[]{:S(2)}, u32[]{:S(2)}) collective-permute-start(bf16[256,256]{1,0:T(8,128)(2,1)S(1)} %get-tuple-element.36), channel_id=1, source_target_pairs={{1,2},{2,1},{5,6},{6,5},{9,10},{10,9},{13,14},{14,13},{17,18},{18,... | collective-permute-start | bytes 393224 | tf_op jit(solution)/shard_map/ppermute | solution.py:390
  33.8 6.6 %collective-permute-start.8 = (bf16[8,4480]{1,0:T(8,128)(2,1)S(1)}, bf16[8,4480]{1,0:T(8,128)(2,1)S(1)}, u32[]{:S(2)}, u32[]{:S(2)}) collective-permute-start(bf16[8,4480]{1,0:T(8,128)(2,1)S(1)} %get-tuple-element.40), channel_id=1, source_target_pairs={{0,24},{4,28},{8,16},{12,20},{16,8},{20,12},{24,0},{28,4},{1,25},{... | collective-permute-start | bytes 215048 | tf_op jit(solution)/shard_map/ppermute | solution.py:416
  37.5 6.1 %collective-permute-start.7 = (bf16[8,4480]{1,0:T(8,128)(2,1)S(1)}, bf16[8,4480]{1,0:T(8,128)(2,1)S(1)}, u32[]{:S(2)}, u32[]{:S(2)}) collective-permute-start(bf16[8,4480]{1,0:T(8,128)(2,1)S(1)} %get-tuple-element.40), channel_id=1, source_target_pairs={{0,16},{4,20},{8,24},{12,28},{16,0},{20,4},{24,8},{28,12},{1,17},{... | collective-permute-start | bytes 215048 | tf_op jit(solution)/shard_map/ppermute | solution.py:416
  37.5 6.1 %collective-permute-start.6 = (bf16[8,4480]{1,0:T(8,128)(2,1)S(1)}, bf16[8,4480]{1,0:T(8,128)(2,1)S(1)}, u32[]{:S(2)}, u32[]{:S(2)}) collective-permute-start(bf16[8,4480]{1,0:T(8,128)(2,1)S(1)} %get-tuple-element.40), channel_id=1, source_target_pairs={{0,8},{4,12},{8,0},{12,4},{16,24},{20,28},{24,16},{28,20},{1,9},{5... | collective-permute-start | bytes 215048 | tf_op jit(solution)/shard_map/ppermute | solution.py:416
  43.6 9.9 %collective-permute-start.10 = (bf16[32,4480]{1,0:T(8,128)(2,1)S(1)}, bf16[32,4480]{1,0:T(8,128)(2,1)S(1)}, u32[]{:S(2)}, u32[]{:S(2)}) collective-permute-start(bf16[32,4480]{1,0:T(8,128)(2,1)S(1)} %pad_maximum_fusion.2.refs_0_.refs_1_), channel_id=1, source_target_pairs={{0,2},{2,0},{1,3},{3,1},{4,6},{6,4},{5,7},{7,5},{8,10},{10,8},{9,1... | collective-permute-start | bytes 860168 | tf_op jit(solution)/shard_map/ppermute | solution.py:409
  48.4 6.6 %collective-permute-start.9 = (bf16[32,4480]{1,0:T(8,128)(2,1)S(1)}, bf16[32,4480]{1,0:T(8,128)(2,1)S(1)}, u32[]{:S(2)}, u32[]{:S(2)}) collective-permute-start(bf16[32,4480]{1,0:T(8,128)(2,1)S(1)} %pad_maximum_fusion.2.refs_0_.refs_1_), channel_id=1, source_target_pairs={{0,1},{1,0},{2,3},{3,2},{4,5},{5,4},{6,7},{7,6},{8,9},{9,8},{10,11... | collective-permute-start | bytes 860168 | tf_op jit(solution)/shard_map/ppermute | solution.py:406
  48.4 8.0 %collective-permute-start.14 = (bf16[8,4480]{1,0:T(8,128)(2,1)S(1)}, bf16[8,4480]{1,0:T(8,128)(2,1)S(1)}, u32[]{:S(2)}, u32[]{:S(2)}) collective-permute-start(bf16[8,4480]{1,0:T(8,128)(2,1)S(1)} %get-tuple-element.42), channel_id=1, source_target_pairs={{0,24},{4,28},{8,16},{12,20},{16,8},{20,12},{24,0},{28,4},{1,25},{... | collective-permute-start | bytes 215048 | tf_op jit(solution)/shard_map/ppermute | solution.py:416
  50.4 5.9 %collective-permute-start.13 = (bf16[8,4480]{1,0:T(8,128)(2,1)S(1)}, bf16[8,4480]{1,0:T(8,128)(2,1)S(1)}, u32[]{:S(2)}, u32[]{:S(2)}) collective-permute-start(bf16[8,4480]{1,0:T(8,128)(2,1)S(1)} %get-tuple-element.42), channel_id=1, source_target_pairs={{0,16},{4,20},{8,24},{12,28},{16,0},{20,4},{24,8},{28,12},{1,17},{... | collective-permute-start | bytes 215048 | tf_op jit(solution)/shard_map/ppermute | solution.py:416
  50.4 5.5 %collective-permute-start.12 = (bf16[8,4480]{1,0:T(8,128)(2,1)S(1)}, bf16[8,4480]{1,0:T(8,128)(2,1)S(1)}, u32[]{:S(2)}, u32[]{:S(2)}) collective-permute-start(bf16[8,4480]{1,0:T(8,128)(2,1)S(1)} %get-tuple-element.42), channel_id=1, source_target_pairs={{0,8},{4,12},{8,0},{12,4},{16,24},{20,28},{24,16},{28,20},{1,9},{5... | collective-permute-start | bytes 215048 | tf_op jit(solution)/shard_map/ppermute | solution.py:416
  55.1 5.2 %collective-permute-start.11 = (bf16[96,4480]{1,0:T(8,128)(2,1)S(1)}, bf16[96,4480]{1,0:T(8,128)(2,1)S(1)}, u32[]{:S(2)}, u32[]{:S(2)}) collective-permute-start(bf16[96,4480]{1,0:T(8,128)(2,1)S(1)} %pad_maximum_fusion), channel_id=1, source_target_pairs={{0,4},{4,0},{8,12},{12,8},{16,20},{20,16},{24,28},{28,24},{1,5},{5... | collective-permute-start | bytes 2580488 | tf_op jit(solution)/shard_map/ppermute | solution.py:412
  56.4 11.3 %collective-permute-start.17 = (bf16[48,4480]{1,0:T(8,128)(2,1)S(1)}, bf16[48,4480]{1,0:T(8,128)(2,1)S(1)}, u32[]{:S(2)}, u32[]{:S(2)}) collective-permute-start(bf16[48,4480]{1,0:T(8,128)(2,1)S(1)} %get-tuple-element.45), channel_id=1, source_target_pairs={{0,2},{2,0},{1,3},{3,1},{4,6},{6,4},{5,7},{7,5},{8,10},{10,8},{9,1... | collective-permute-start | bytes 1290248 | tf_op jit(solution)/shard_map/ppermute | solution.py:409
  58.1 9.9 %collective-permute-start.16 = (bf16[48,4480]{1,0:T(8,128)(2,1)S(1)}, bf16[48,4480]{1,0:T(8,128)(2,1)S(1)}, u32[]{:S(2)}, u32[]{:S(2)}) collective-permute-start(bf16[48,4480]{1,0:T(8,128)(2,1)S(1)} %get-tuple-element.43), channel_id=1, source_target_pairs={{0,1},{1,0},{2,3},{3,2},{4,5},{5,4},{6,7},{7,6},{8,9},{9,8},{10,11... | collective-permute-start | bytes 1290248 | tf_op jit(solution)/shard_map/ppermute | solution.py:406
  58.6 1.6 %collective-permute-start.15 = (bf16[32,4480]{1,0:T(8,128)(2,1)S(1)}, bf16[32,4480]{1,0:T(8,128)(2,1)S(1)}, u32[]{:S(2)}, u32[]{:S(2)}) collective-permute-start(bf16[32,4480]{1,0:T(8,128)(2,1)S(1)} %slice.17.refs_4_.refs_5_), channel_id=1, source_target_pairs={{0,4},{4,0},{8,12},{12,8},{16,20},{20,16},{24,28},{28,24},{1,5},{5... | collective-permute-start | bytes 860168 | tf_op jit(solution)/shard_map/ppermute | solution.py:412
  68.1 5.2 %collective-permute-start.19 = (bf16[16,4480]{1,0:T(8,128)(2,1)S(1)}, bf16[16,4480]{1,0:T(8,128)(2,1)S(1)}, u32[]{:S(2)}, u32[]{:S(2)}) collective-permute-start(bf16[16,4480]{1,0:T(8,128)(2,1)S(1)} %slice.18), channel_id=1, source_target_pairs={{0,1},{1,0},{2,3},{3,2},{4,5},{5,4},{6,7},{7,6},{8,9},{9,8},{10,11... | collective-permute-start | bytes 430088 | tf_op jit(solution)/shard_map/ppermute | solution.py:406
  69.1 5.1 %collective-permute-start.20 = (bf16[16,4480]{1,0:T(8,128)(2,1)S(1)}, bf16[16,4480]{1,0:T(8,128)(2,1)S(1)}, u32[]{:S(2)}, u32[]{:S(2)}) collective-permute-start(bf16[16,4480]{1,0:T(8,128)(2,1)S(1)} %slice.19), channel_id=1, source_target_pairs={{0,2},{2,0},{1,3},{3,1},{4,6},{6,4},{5,7},{7,5},{8,10},{10,8},{9,1... | collective-permute-start | bytes 430088 | tf_op jit(solution)/shard_map/ppermute | solution.py:409
  69.9 6.0 %collective-permute-start.18 = (bf16[96,4480]{1,0:T(8,128)(2,1)S(1)}, bf16[96,4480]{1,0:T(8,128)(2,1)S(1)}, u32[]{:S(2)}, u32[]{:S(2)}) collective-permute-start(bf16[96,4480]{1,0:T(8,128)(2,1)S(1)} %pad_maximum_fusion.1), channel_id=1, source_target_pairs={{0,4},{4,0},{8,12},{12,8},{16,20},{20,16},{24,28},{28,24},{1,5},{5... | collective-permute-start | bytes 2580488 | tf_op jit(solution)/shard_map/ppermute | solution.py:412
  74.3 1.6 %collective-permute-start.21 = (bf16[32,4480]{1,0:T(8,128)(2,1)S(1)}, bf16[32,4480]{1,0:T(8,128)(2,1)S(1)}, u32[]{:S(2)}, u32[]{:S(2)}) collective-permute-start(bf16[32,4480]{1,0:T(8,128)(2,1)S(1)} %pad_maximum_fusion.3), channel_id=1, source_target_pairs={{0,4},{4,0},{8,12},{12,8},{16,20},{20,16},{24,28},{28,24},{1,5},{5... | collective-permute-start | bytes 860168 | tf_op jit(solution)/shard_map/ppermute | solution.py:412
  (8 other events, 118.6 us)

commit v9 on v8

--- a/solution.py
+++ b/solution.py
@@ -250,12 +250,10 @@
     high = norm.astype(jnp.bfloat16).astype(jnp.float32)
     tail = lax.broadcasted_iota(jnp.int32, (slots, 128), 1)
     tail = jnp.where(tail == 0, high, jnp.where(tail == 1, norm - high, 0.0))
-    row = jnp.concatenate(
-        [wide.astype(jnp.bfloat16), multiplicity_ref[...], tail.astype(jnp.bfloat16)], axis=1
-    )
+    row = jnp.concatenate([wide, multiplicity_ref[...].astype(jnp.float32), tail], axis=1)
     for k, out_ref in enumerate(outs):
         count = out_ref.shape[0]
-        out_ref[...] = row[k * count : (k + 1) * count]
+        out_ref[...] = row[k * count : (k + 1) * count].astype(jnp.bfloat16)
 
 
 def block_copies(blocks, rows_ref, tail_ref, sems):

time: 89.9 us -> 89.9 us (level)
  no operation moved by 1% of the time
where the time goes in v9:
time: 89.9 us; the launch traced here: 89.7 us
  Pallas kernels  32.2 us (36%)
  starting transfers between devices  29.1 us (32%)
  waiting for transfers between devices  22.6 us (25%)
  local copies, waits for them, and re-layouts  2.99 us (3%)
  between operations  1.76 us (2%)
  other arithmetic  1.04 us (1%)
    pallas_call x1, Pallas kernels, sum_blocks(): pl.pallas_call(functools.partial(sum_kernel, early=len(parts), blocks=len...  13.7 us
    ppermute x6, starting transfers between devices, exchange(): return lax.ppermute(value, axis, pairs)  11.2 us
    ppermute x6, starting transfers between devices, line_of(): lax.ppermute(part, 'tile', [(i, i ^ by) for i in range(tiles)])  8.84 us
    pallas_call x1, Pallas kernels, body(): pl.pallas_call(functools.partial(far_kernel, wide=wide), in_specs=[smem]...  7.44 us
    ppermute x3, starting transfers between devices, along_y(): return lax.ppermute(value, 'bank', [(0, 2), (2, 0), (1, 3), (3, 1)])  7.21 us
    ppermute x6, waiting for transfers between devices, line_of(): lax.ppermute(part, 'tile', [(i, i ^ by) for i in range(tiles)])  6.45 us
    ppermute x3, waiting for transfers between devices, along_x(): return lax.ppermute(value, 'bank', [(0, 1), (1, 0), (2, 3), (3, 2)])  5.19 us
    pallas_call x1, Pallas kernels, weigh_blocks(): pl.pallas_call(functools.partial(weigh_kernel, blocks=len(blocks), known=...  4.97 us
  transfers between devices with their start and end apart: 22, of which 14 were waited for; matrix products, arithmetic and copies ran while one was open for 1% of the time, Pallas kernels for 11%

profile of v9, /device:TPU:0, one launch (start us, length us, event | category | flops | bytes accessed | tf_op | source)
XLA Modules:
  0.0 89.7 jit_solution(3037890960779338626)
XLA Ops:
  0.7 2.8 %constant_dynamic-slice_fusion = (bf16[48,64,128]{2,1,0:T(8,128)(2,1)}, bf16[48,64,128]{2,1,0:T(8,128)(2,1)}) fusion(bf16[64,64,128]{2,1,0:T(8,128)(2,1)} %volume_ref.1, s32[]{:T(128)S(6)} %select_n.18, s32[]{:T(128)S(6)} %select_n.17), kind=kLoop, calls=%fused_computation.20 | loop fusion | bytes 3145736 | tf_op jit(solution)/shard_map/dynamic_slice | solution.py:535
  3.9 1.6 %collective-permute-start.3 = (bf16[48,64,128]{2,1,0:T(8,128)(2,1)}, bf16[48,64,128]{2,1,0:T(8,128)(2,1)}, u32[]{:S(2)}, u32[]{:S(2)}) collective-permute-start(bf16[48,64,128]{2,1,0:T(8,128)(2,1)} %get-tuple-element.52), channel_id=1, source_target_pairs={{4,8},{8,4},{12,16},{16,12},{20,24},{24,20},{5,9},{9,5},{13,17},{1... | collective-permute-start | bytes 2359304 | tf_op jit(solution)/shard_map/ppermute | solution.py:388
  6.9 5.7 %collective-permute-start.1 = (s32[3,1,1,16]{3,2,1,0:T(1,128)S(1)}, s32[3,1,1,16]{3,2,1,0:T(1,128)S(1)}, u32[]{:S(2)}, u32[]{:S(2)}) collective-permute-start(s32[3,1,1,16]{3,2,1,0:T(1,128)S(1)} %copy-done.2), channel_id=1, source_target_pairs={{0,1},{1,0},{2,3},{3,2},{4,5},{5,4},{6,7},{7,6},{8,9},{9,8},{10,11... | collective-permute-start | bytes 584 | tf_op jit(solution)/shard_map/ppermute | solution.py:388
  12.6 1.5 %collective-permute-done.1.first_pick_ref = s32[3,1,1,16]{3,2,1,0:T(1,128)S(1)} collective-permute-done((s32[3,1,1,16]{3,2,1,0:T(1,128)S(1)}, s32[3,1,1,16]{3,2,1,0:T(1,128)S(1)}, u32[]{:S(2)}, u32[]{:S(2)}) %collective-permute-start.1) | collective-permute-done | bytes 224 | tf_op jit(solution)/shard_map/ppermute | solution.py:388
  14.1 4.8 %near_rows.1 = (f32[304,768]{1,0:T(8,128)S(1)}, bf16[128,768]{1,0:T(8,128)(2,1)S(1)}, f32[64,768]{1,0:T(8,128)S(1)}, f32[8,768]{1,0:T(8,128)S(1)}) custom-call(s32[2]{0:T(128)S(1)} %pad_add_fusion.origin_ref, s32[3,1,1,16]{3,2,1,0:T(1,128)S(1)} %collective-permute-done.1.first_pick_ref, s32[3,1,1,16]{3,2,1,0:T(1,128)S(1)} %copy-done.2, ...), custom_call_target="tpu_custom_call" | custom-call | flops 2717908992 | bytes 8000000 | tf_op jit(solution)/shard_map/near_rows/pallas_call | solution.py:550
  18.9 7.4 %far_rows.1 = (bf16[256,256]{1,0:T(8,128)(2,1)S(1)}, f32[256,256]{1,0:T(8,128)S(1)}, bf16[256,256]{1,0:T(8,128)(2,1)S(1)}) custom-call(s32[1]{0:T(128)} %bitcast.1.side_ref, bf16[128,768]{1,0:T(8,128)(2,1)S(1)} %get-tuple-element.28.depth_ref, f32[64,768]{1,0:T(8,128)S(1)} %get-tuple-element.29.high_ref, f32[8,768]{1,0:T(8,128)S(1)} %get-tuple-element.30.where_ref, ...), custom_call_target="tpu_custom_call" | custom-call | tf_op jit(solution)/shard_map/far_rows/pallas_call | solution.py:567
  26.4 2.1 %collective-permute-start.4 = (bf16[256,256]{1,0:T(8,128)(2,1)S(1)}, bf16[256,256]{1,0:T(8,128)(2,1)S(1)}, u32[]{:S(2)}, u32[]{:S(2)}) collective-permute-start(bf16[256,256]{1,0:T(8,128)(2,1)S(1)} %get-tuple-element.35), channel_id=1, source_target_pairs={{0,1},{1,0},{2,3},{3,2},{4,5},{5,4},{6,7},{7,6},{8,9},{9,8},{10,11... | collective-permute-start | bytes 393224 | tf_op jit(solution)/shard_map/ppermute | solution.py:388
  30.1 2.3 %collective-permute-done.4.left_ref = bf16[256,256]{1,0:T(8,128)(2,1)S(1)} collective-permute-done((bf16[256,256]{1,0:T(8,128)(2,1)S(1)}, bf16[256,256]{1,0:T(8,128)(2,1)S(1)}, u32[]{:S(2)}, u32[]{:S(2)}) %collective-permute-start.4) | collective-permute-done | bytes 131104 | tf_op jit(solution)/shard_map/ppermute | solution.py:388
  32.4 1.4 %join.1 = (bf16[8,4480]{1,0:T(8,128)(2,1)S(1)}, bf16[8,4480]{1,0:T(8,128)(2,1)S(1)}) custom-call(f32[256,256]{1,0:T(8,128)S(1)} %get-tuple-element.34.own_ref, bf16[256,256]{1,0:T(8,128)(2,1)S(1)} %collective-permute-done.4.left_ref, bf16[256,256]{1,0:T(8,128)(2,1)S(1)} %collective-permute-done.5.right_ref, ...), custom_call_target="tpu_custom_call" | custom-call | tf_op jit(solution)/shard_map/join/pallas_call | solution.py:593
  33.8 3.7 %collective-permute-start.8 = (bf16[8,4480]{1,0:T(8,128)(2,1)S(1)}, bf16[8,4480]{1,0:T(8,128)(2,1)S(1)}, u32[]{:S(2)}, u32[]{:S(2)}) collective-permute-start(bf16[8,4480]{1,0:T(8,128)(2,1)S(1)} %get-tuple-element.40), channel_id=1, source_target_pairs={{0,24},{4,28},{8,16},{12,20},{16,8},{20,12},{24,0},{28,4},{1,25},{... | collective-permute-start | bytes 215048 | tf_op jit(solution)/shard_map/ppermute | solution.py:414
  38.2 2.2 %collective-permute-done.8 = bf16[8,4480]{1,0:T(8,128)(2,1)S(1)} collective-permute-done((bf16[8,4480]{1,0:T(8,128)(2,1)S(1)}, bf16[8,4480]{1,0:T(8,128)(2,1)S(1)}, u32[]{:S(2)}, u32[]{:S(2)}) %collective-permute-start.8) | collective-permute-done | bytes 71712 | tf_op jit(solution)/shard_map/ppermute | solution.py:414
  40.4 3.1 %collective-permute-done.7 = bf16[8,4480]{1,0:T(8,128)(2,1)S(1)} collective-permute-done((bf16[8,4480]{1,0:T(8,128)(2,1)S(1)}, bf16[8,4480]{1,0:T(8,128)(2,1)S(1)}, u32[]{:S(2)}, u32[]{:S(2)}) %collective-permute-start.7) | collective-permute-done | bytes 71712 | tf_op jit(solution)/shard_map/ppermute | solution.py:414
  43.6 4.8 %collective-permute-start.10 = (bf16[32,4480]{1,0:T(8,128)(2,1)S(1)}, bf16[32,4480]{1,0:T(8,128)(2,1)S(1)}, u32[]{:S(2)}, u32[]{:S(2)}) collective-permute-start(bf16[32,4480]{1,0:T(8,128)(2,1)S(1)} %pad_maximum_fusion.2.refs_0_.refs_1_), channel_id=1, source_target_pairs={{0,2},{2,0},{1,3},{3,1},{4,6},{6,4},{5,7},{7,5},{8,10},{10,8},{9,1... | collective-permute-start | bytes 860168 | tf_op jit(solution)/shard_map/ppermute | solution.py:407
  48.4 2.1 %collective-permute-start.14 = (bf16[8,4480]{1,0:T(8,128)(2,1)S(1)}, bf16[8,4480]{1,0:T(8,128)(2,1)S(1)}, u32[]{:S(2)}, u32[]{:S(2)}) collective-permute-start(bf16[8,4480]{1,0:T(8,128)(2,1)S(1)} %get-tuple-element.42), channel_id=1, source_target_pairs={{0,24},{4,28},{8,16},{12,20},{16,8},{20,12},{24,0},{28,4},{1,25},{... | collective-permute-start | bytes 215048 | tf_op jit(solution)/shard_map/ppermute | solution.py:414
  50.4 2.3 %collective-permute-start.12 = (bf16[8,4480]{1,0:T(8,128)(2,1)S(1)}, bf16[8,4480]{1,0:T(8,128)(2,1)S(1)}, u32[]{:S(2)}, u32[]{:S(2)}) collective-permute-start(bf16[8,4480]{1,0:T(8,128)(2,1)S(1)} %get-tuple-element.42), channel_id=1, source_target_pairs={{0,8},{4,12},{8,0},{12,4},{16,24},{20,28},{24,16},{28,20},{1,9},{5... | collective-permute-start | bytes 215048 | tf_op jit(solution)/shard_map/ppermute | solution.py:414
  53.4 1.6 %collective-permute-done.9.refs_1_.refs_2_ = bf16[32,4480]{1,0:T(8,128)(2,1)S(1)} collective-permute-done((bf16[32,4480]{1,0:T(8,128)(2,1)S(1)}, bf16[32,4480]{1,0:T(8,128)(2,1)S(1)}, u32[]{:S(2)}, u32[]{:S(2)}) %collective-permute-start.9) | collective-permute-done | bytes 286752 | tf_op jit(solution)/shard_map/ppermute | solution.py:404
  56.4 1.7 %collective-permute-start.17 = (bf16[48,4480]{1,0:T(8,128)(2,1)S(1)}, bf16[48,4480]{1,0:T(8,128)(2,1)S(1)}, u32[]{:S(2)}, u32[]{:S(2)}) collective-permute-start(bf16[48,4480]{1,0:T(8,128)(2,1)S(1)} %get-tuple-element.45), channel_id=1, source_target_pairs={{0,2},{2,0},{1,3},{3,1},{4,6},{6,4},{5,7},{7,5},{8,10},{10,8},{9,1... | collective-permute-start | bytes 1290248 | tf_op jit(solution)/shard_map/ppermute | solution.py:407
  58.7 1.6 %collective-permute-done.15.refs_5_.refs_6_ = bf16[32,4480]{1,0:T(8,128)(2,1)S(1)} collective-permute-done((bf16[32,4480]{1,0:T(8,128)(2,1)S(1)}, bf16[32,4480]{1,0:T(8,128)(2,1)S(1)}, u32[]{:S(2)}, u32[]{:S(2)}) %collective-permute-start.15) | collective-permute-done | bytes 286752 | tf_op jit(solution)/shard_map/ppermute | solution.py:410
  60.3 5.0 %weigh.1 = (bf16[20,64,256]{2,1,0:T(8,128)(2,1)S(1)}, f32[20,64,128]{2,1,0:T(8,128)S(1)}) custom-call(s32[1]{0:T(128)} %bitcast.index_ref, bf16[32,4480]{1,0:T(8,128)(2,1)S(1)} %pad_maximum_fusion.2.refs_0_.refs_1_, bf16[32,4480]{1,0:T(8,128)(2,1)S(1)} %collective-permute-done.9.refs_1_.refs_2_, ...), custom_call_target="tpu_custom_call" | custom-call | flops 167772160 | bytes 655360 | tf_op jit(solution)/shard_map/weigh/pallas_call | solution.py:458
  65.3 2.4 %collective-permute-done.17.refs_8_ = bf16[48,4480]{1,0:T(8,128)(2,1)S(1)} collective-permute-done((bf16[48,4480]{1,0:T(8,128)(2,1)S(1)}, bf16[48,4480]{1,0:T(8,128)(2,1)S(1)}, u32[]{:S(2)}, u32[]{:S(2)}) %collective-permute-start.17) | collective-permute-done | bytes 430112 | tf_op jit(solution)/shard_map/ppermute | solution.py:407
  68.1 1.1 %collective-permute-start.19 = (bf16[16,4480]{1,0:T(8,128)(2,1)S(1)}, bf16[16,4480]{1,0:T(8,128)(2,1)S(1)}, u32[]{:S(2)}, u32[]{:S(2)}) collective-permute-start(bf16[16,4480]{1,0:T(8,128)(2,1)S(1)} %slice.18), channel_id=1, source_target_pairs={{0,1},{1,0},{2,3},{3,2},{4,5},{5,4},{6,7},{7,6},{8,9},{9,8},{10,11... | collective-permute-start | bytes 430088 | tf_op jit(solution)/shard_map/ppermute | solution.py:404
  70.0 3.3 %collective-permute-done.19.refs_10_ = bf16[16,4480]{1,0:T(8,128)(2,1)S(1)} collective-permute-done((bf16[16,4480]{1,0:T(8,128)(2,1)S(1)}, bf16[16,4480]{1,0:T(8,128)(2,1)S(1)}, u32[]{:S(2)}, u32[]{:S(2)}) %collective-permute-start.19) | collective-permute-done | bytes 143392 | tf_op jit(solution)/shard_map/ppermute | solution.py:404
  74.3 1.6 %collective-permute-done.21.refs_12_ = bf16[32,4480]{1,0:T(8,128)(2,1)S(1)} collective-permute-done((bf16[32,4480]{1,0:T(8,128)(2,1)S(1)}, bf16[32,4480]{1,0:T(8,128)(2,1)S(1)}, u32[]{:S(2)}, u32[]{:S(2)}) %collective-permute-start.21) | collective-permute-done | bytes 286752 | tf_op jit(solution)/shard_map/ppermute | solution.py:410
  75.9 13.7 %class_sums.1 = (f32[20,64,4096]{2,1,0:T(8,128)}, f32[20,64]{1,0:T(8,128)}) custom-call(s32[1]{0:T(128)} %bitcast.index_ref, bf16[20,64,256]{2,1,0:T(8,128)(2,1)S(1)} %get-tuple-element.46.refs_0_, bf16[32,4480]{1,0:T(8,128)(2,1)S(1)} %pad_maximum_fusion.2.refs_0_.refs_1_, bf16[32,4480]{1,0:T(8,128)(2,1)S(1)} %collective-permute-done.9.refs_1_.refs_2_, ...), custom_call_target="tpu_custom_call" | custom-call | flops 5368709120 | bytes 20971520 | tf_op jit(solution)/shard_map/class_sums/pallas_call | solution.py:491
  (65 shorter events, 8.6 us)
Async XLA Ops:
  3.5 2.7 %collective-permute-start = (bf16[48,64,128]{2,1,0:T(8,128)(2,1)}, bf16[48,64,128]{2,1,0:T(8,128)(2,1)}, u32[]{:S(2)}, u32[]{:S(2)}) collective-permute-start(bf16[48,64,128]{2,1,0:T(8,128)(2,1)} %get-tuple-element.53), channel_id=1, source_target_pairs={{0,4},{4,0},{8,12},{12,8},{16,20},{20,16},{24,28},{28,24},{1,5},{5... | collective-permute-start | bytes 2359304 | tf_op jit(solution)/shard_map/ppermute | solution.py:388
  3.9 14.9 %collective-permute-start.3 = (bf16[48,64,128]{2,1,0:T(8,128)(2,1)}, bf16[48,64,128]{2,1,0:T(8,128)(2,1)}, u32[]{:S(2)}, u32[]{:S(2)}) collective-permute-start(bf16[48,64,128]{2,1,0:T(8,128)(2,1)} %get-tuple-element.52), channel_id=1, source_target_pairs={{4,8},{8,4},{12,16},{16,12},{20,24},{24,20},{5,9},{9,5},{13,17},{1... | collective-permute-start | bytes 2359304 | tf_op jit(solution)/shard_map/ppermute | solution.py:388
  6.2 6.4 %collective-permute-start.2 = (s32[3,1,1,16]{3,2,1,0:T(1,128)S(1)}, s32[3,1,1,16]{3,2,1,0:T(1,128)S(1)}, u32[]{:S(2)}, u32[]{:S(2)}) collective-permute-start(s32[3,1,1,16]{3,2,1,0:T(1,128)S(1)} %copy-done.2), channel_id=1, source_target_pairs={{1,2},{2,1},{5,6},{6,5},{9,10},{10,9},{13,14},{14,13},{17,18},{18,... | collective-permute-start | bytes 584 | tf_op jit(solution)/shard_map/ppermute | solution.py:388
  6.9 7.2 %collective-permute-start.1 = (s32[3,1,1,16]{3,2,1,0:T(1,128)S(1)}, s32[3,1,1,16]{3,2,1,0:T(1,128)S(1)}, u32[]{:S(2)}, u32[]{:S(2)}) collective-permute-start(s32[3,1,1,16]{3,2,1,0:T(1,128)S(1)} %copy-done.2), channel_id=1, source_target_pairs={{0,1},{1,0},{2,3},{3,2},{4,5},{5,4},{6,7},{7,6},{8,9},{9,8},{10,11... | collective-permute-start | bytes 584 | tf_op jit(solution)/shard_map/ppermute | solution.py:388
  14.1 46.2 %slice-start = ((s8[10485760]{0:T(1024)(128)(4,1)}), s8[4194304]{0:T(1024)(128)(4,1)S(1)}, s32[]{:S(2)}) async-start(s8[10485760]{0:T(1024)(128)(4,1)} %bitcast.12), calls=%async_computation | async-start | bytes 8388608
  14.1 46.2 %slice-start.1 = ((s8[10485760]{0:T(1024)(128)(4,1)}), s8[4194304]{0:T(1024)(128)(4,1)S(1)}, s32[]{:S(2)}) async-start(s8[10485760]{0:T(1024)(128)(4,1)} %bitcast.12), calls=%async_computation.1 | async-start | bytes 8388608
  26.4 6.0 %collective-permute-start.4 = (bf16[256,256]{1,0:T(8,128)(2,1)S(1)}, bf16[256,256]{1,0:T(8,128)(2,1)S(1)}, u32[]{:S(2)}, u32[]{:S(2)}) collective-permute-start(bf16[256,256]{1,0:T(8,128)(2,1)S(1)} %get-tuple-element.35), channel_id=1, source_target_pairs={{0,1},{1,0},{2,3},{3,2},{4,5},{5,4},{6,7},{7,6},{8,9},{9,8},{10,11... | collective-permute-start | bytes 393224 | tf_op jit(solution)/shard_map/ppermute | solution.py:388
  28.5 3.9 %collective-permute-start.5 = (bf16[256,256]{1,0:T(8,128)(2,1)S(1)}, bf16[256,256]{1,0:T(8,128)(2,1)S(1)}, u32[]{:S(2)}, u32[]{:S(2)}) collective-permute-start(bf16[256,256]{1,0:T(8,128)(2,1)S(1)} %get-tuple-element.36), channel_id=1, source_target_pairs={{1,2},{2,1},{5,6},{6,5},{9,10},{10,9},{13,14},{14,13},{17,18},{18,... | collective-permute-start | bytes 393224 | tf_op jit(solution)/shard_map/ppermute | solution.py:388
  33.8 6.6 %collective-permute-start.8 = (bf16[8,4480]{1,0:T(8,128)(2,1)S(1)}, bf16[8,4480]{1,0:T(8,128)(2,1)S(1)}, u32[]{:S(2)}, u32[]{:S(2)}) collective-permute-start(bf16[8,4480]{1,0:T(8,128)(2,1)S(1)} %get-tuple-element.40), channel_id=1, source_target_pairs={{0,24},{4,28},{8,16},{12,20},{16,8},{20,12},{24,0},{28,4},{1,25},{... | collective-permute-start | bytes 215048 | tf_op jit(solution)/shard_map/ppermute | solution.py:414
  37.5 6.1 %collective-permute-start.7 = (bf16[8,4480]{1,0:T(8,128)(2,1)S(1)}, bf16[8,4480]{1,0:T(8,128)(2,1)S(1)}, u32[]{:S(2)}, u32[]{:S(2)}) collective-permute-start(bf16[8,4480]{1,0:T(8,128)(2,1)S(1)} %get-tuple-element.40), channel_id=1, source_target_pairs={{0,16},{4,20},{8,24},{12,28},{16,0},{20,4},{24,8},{28,12},{1,17},{... | collective-permute-start | bytes 215048 | tf_op jit(solution)/shard_map/ppermute | solution.py:414
  37.5 6.1 %collective-permute-start.6 = (bf16[8,4480]{1,0:T(8,128)(2,1)S(1)}, bf16[8,4480]{1,0:T(8,128)(2,1)S(1)}, u32[]{:S(2)}, u32[]{:S(2)}) collective-permute-start(bf16[8,4480]{1,0:T(8,128)(2,1)S(1)} %get-tuple-element.40), channel_id=1, source_target_pairs={{0,8},{4,12},{8,0},{12,4},{16,24},{20,28},{24,16},{28,20},{1,9},{5... | collective-permute-start | bytes 215048 | tf_op jit(solution)/shard_map/ppermute | solution.py:414
  43.6 9.9 %collective-permute-start.10 = (bf16[32,4480]{1,0:T(8,128)(2,1)S(1)}, bf16[32,4480]{1,0:T(8,128)(2,1)S(1)}, u32[]{:S(2)}, u32[]{:S(2)}) collective-permute-start(bf16[32,4480]{1,0:T(8,128)(2,1)S(1)} %pad_maximum_fusion.2.refs_0_.refs_1_), channel_id=1, source_target_pairs={{0,2},{2,0},{1,3},{3,1},{4,6},{6,4},{5,7},{7,5},{8,10},{10,8},{9,1... | collective-permute-start | bytes 860168 | tf_op jit(solution)/shard_map/ppermute | solution.py:407
  48.4 6.6 %collective-permute-start.9 = (bf16[32,4480]{1,0:T(8,128)(2,1)S(1)}, bf16[32,4480]{1,0:T(8,128)(2,1)S(1)}, u32[]{:S(2)}, u32[]{:S(2)}) collective-permute-start(bf16[32,4480]{1,0:T(8,128)(2,1)S(1)} %pad_maximum_fusion.2.refs_0_.refs_1_), channel_id=1, source_target_pairs={{0,1},{1,0},{2,3},{3,2},{4,5},{5,4},{6,7},{7,6},{8,9},{9,8},{10,11... | collective-permute-start | bytes 860168 | tf_op jit(solution)/shard_map/ppermute | solution.py:404
  48.4 8.0 %collective-permute-start.14 = (bf16[8,4480]{1,0:T(8,128)(2,1)S(1)}, bf16[8,4480]{1,0:T(8,128)(2,1)S(1)}, u32[]{:S(2)}, u32[]{:S(2)}) collective-permute-start(bf16[8,4480]{1,0:T(8,128)(2,1)S(1)} %get-tuple-element.42), channel_id=1, source_target_pairs={{0,24},{4,28},{8,16},{12,20},{16,8},{20,12},{24,0},{28,4},{1,25},{... | collective-permute-start | bytes 215048 | tf_op jit(solution)/shard_map/ppermute | solution.py:414
  50.4 5.9 %collective-permute-start.13 = (bf16[8,4480]{1,0:T(8,128)(2,1)S(1)}, bf16[8,4480]{1,0:T(8,128)(2,1)S(1)}, u32[]{:S(2)}, u32[]{:S(2)}) collective-permute-start(bf16[8,4480]{1,0:T(8,128)(2,1)S(1)} %get-tuple-element.42), channel_id=1, source_target_pairs={{0,16},{4,20},{8,24},{12,28},{16,0},{20,4},{24,8},{28,12},{1,17},{... | collective-permute-start | bytes 215048 | tf_op jit(solution)/shard_map/ppermute | solution.py:414
  50.4 5.5 %collective-permute-start.12 = (bf16[8,4480]{1,0:T(8,128)(2,1)S(1)}, bf16[8,4480]{1,0:T(8,128)(2,1)S(1)}, u32[]{:S(2)}, u32[]{:S(2)}) collective-permute-start(bf16[8,4480]{1,0:T(8,128)(2,1)S(1)} %get-tuple-element.42), channel_id=1, source_target_pairs={{0,8},{4,12},{8,0},{12,4},{16,24},{20,28},{24,16},{28,20},{1,9},{5... | collective-permute-start | bytes 215048 | tf_op jit(solution)/shard_map/ppermute | solution.py:414
  55.1 5.2 %collective-permute-start.11 = (bf16[96,4480]{1,0:T(8,128)(2,1)S(1)}, bf16[96,4480]{1,0:T(8,128)(2,1)S(1)}, u32[]{:S(2)}, u32[]{:S(2)}) collective-permute-start(bf16[96,4480]{1,0:T(8,128)(2,1)S(1)} %pad_maximum_fusion), channel_id=1, source_target_pairs={{0,4},{4,0},{8,12},{12,8},{16,20},{20,16},{24,28},{28,24},{1,5},{5... | collective-permute-start | bytes 2580488 | tf_op jit(solution)/shard_map/ppermute | solution.py:410
  56.4 11.3 %collective-permute-start.17 = (bf16[48,4480]{1,0:T(8,128)(2,1)S(1)}, bf16[48,4480]{1,0:T(8,128)(2,1)S(1)}, u32[]{:S(2)}, u32[]{:S(2)}) collective-permute-start(bf16[48,4480]{1,0:T(8,128)(2,1)S(1)} %get-tuple-element.45), channel_id=1, source_target_pairs={{0,2},{2,0},{1,3},{3,1},{4,6},{6,4},{5,7},{7,5},{8,10},{10,8},{9,1... | collective-permute-start | bytes 1290248 | tf_op jit(solution)/shard_map/ppermute | solution.py:407
  58.1 9.9 %collective-permute-start.16 = (bf16[48,4480]{1,0:T(8,128)(2,1)S(1)}, bf16[48,4480]{1,0:T(8,128)(2,1)S(1)}, u32[]{:S(2)}, u32[]{:S(2)}) collective-permute-start(bf16[48,4480]{1,0:T(8,128)(2,1)S(1)} %get-tuple-element.43), channel_id=1, source_target_pairs={{0,1},{1,0},{2,3},{3,2},{4,5},{5,4},{6,7},{7,6},{8,9},{9,8},{10,11... | collective-permute-start | bytes 1290248 | tf_op jit(solution)/shard_map/ppermute | solution.py:404
  58.6 1.6 %collective-permute-start.15 = (bf16[32,4480]{1,0:T(8,128)(2,1)S(1)}, bf16[32,4480]{1,0:T(8,128)(2,1)S(1)}, u32[]{:S(2)}, u32[]{:S(2)}) collective-permute-start(bf16[32,4480]{1,0:T(8,128)(2,1)S(1)} %slice.17.refs_4_.refs_5_), channel_id=1, source_target_pairs={{0,4},{4,0},{8,12},{12,8},{16,20},{20,16},{24,28},{28,24},{1,5},{5... | collective-permute-start | bytes 860168 | tf_op jit(solution)/shard_map/ppermute | solution.py:410
  68.1 5.2 %collective-permute-start.19 = (bf16[16,4480]{1,0:T(8,128)(2,1)S(1)}, bf16[16,4480]{1,0:T(8,128)(2,1)S(1)}, u32[]{:S(2)}, u32[]{:S(2)}) collective-permute-start(bf16[16,4480]{1,0:T(8,128)(2,1)S(1)} %slice.18), channel_id=1, source_target_pairs={{0,1},{1,0},{2,3},{3,2},{4,5},{5,4},{6,7},{7,6},{8,9},{9,8},{10,11... | collective-permute-start | bytes 430088 | tf_op jit(solution)/shard_map/ppermute | solution.py:404
  69.1 5.1 %collective-permute-start.20 = (bf16[16,4480]{1,0:T(8,128)(2,1)S(1)}, bf16[16,4480]{1,0:T(8,128)(2,1)S(1)}, u32[]{:S(2)}, u32[]{:S(2)}) collective-permute-start(bf16[16,4480]{1,0:T(8,128)(2,1)S(1)} %slice.19), channel_id=1, source_target_pairs={{0,2},{2,0},{1,3},{3,1},{4,6},{6,4},{5,7},{7,5},{8,10},{10,8},{9,1... | collective-permute-start | bytes 430088 | tf_op jit(solution)/shard_map/ppermute | solution.py:407
  69.9 6.0 %collective-permute-start.18 = (bf16[96,4480]{1,0:T(8,128)(2,1)S(1)}, bf16[96,4480]{1,0:T(8,128)(2,1)S(1)}, u32[]{:S(2)}, u32[]{:S(2)}) collective-permute-start(bf16[96,4480]{1,0:T(8,128)(2,1)S(1)} %pad_maximum_fusion.1), channel_id=1, source_target_pairs={{0,4},{4,0},{8,12},{12,8},{16,20},{20,16},{24,28},{28,24},{1,5},{5... | collective-permute-start | bytes 2580488 | tf_op jit(solution)/shard_map/ppermute | solution.py:410
  74.3 1.6 %collective-permute-start.21 = (bf16[32,4480]{1,0:T(8,128)(2,1)S(1)}, bf16[32,4480]{1,0:T(8,128)(2,1)S(1)}, u32[]{:S(2)}, u32[]{:S(2)}) collective-permute-start(bf16[32,4480]{1,0:T(8,128)(2,1)S(1)} %pad_maximum_fusion.3), channel_id=1, source_target_pairs={{0,4},{4,0},{8,12},{12,8},{16,20},{20,16},{24,28},{28,24},{1,5},{5... | collective-permute-start | bytes 860168 | tf_op jit(solution)/shard_map/ppermute | solution.py:410
  (8 other events, 118.6 us)

commit v10 on v9

--- a/solution.py
+++ b/solution.py
@@ -544,7 +544,7 @@
     modes, lanes = plane.shape[0], 3 * slots * L
     unit = 32
 
-    params = pltpu.CompilerParams(vmem_limit_bytes=32 * MIB)
+    params = pltpu.CompilerParams(vmem_limit_bytes=20 * MIB)
     vmem = pl.BlockSpec(memory_space=pltpu.VMEM)
     smem = pl.BlockSpec(memory_space=pltpu.SMEM)
     near, *tables = pl.pallas_call(

time: 89.9 us -> 89.9 us (level)
  no operation moved by 1% of the time
where the time goes in v10:
time: 89.9 us; the launch traced here: 89.7 us
  Pallas kernels  32.2 us (36%)
  starting transfers between devices  29.1 us (32%)
  waiting for transfers between devices  22.6 us (25%)
  local copies, waits for them, and re-layouts  2.99 us (3%)
  between operations  1.76 us (2%)
  other arithmetic  1.04 us (1%)
    pallas_call x1, Pallas kernels, sum_blocks(): pl.pallas_call(functools.partial(sum_kernel, early=len(parts), blocks=len...  13.7 us
    ppermute x6, starting transfers between devices, exchange(): return lax.ppermute(value, axis, pairs)  11.2 us
    ppermute x6, starting transfers between devices, line_of(): lax.ppermute(part, 'tile', [(i, i ^ by) for i in range(tiles)])  8.84 us
    pallas_call x1, Pallas kernels, body(): pl.pallas_call(functools.partial(far_kernel, wide=wide), in_specs=[smem]...  7.44 us
    ppermute x3, starting transfers between devices, along_y(): return lax.ppermute(value, 'bank', [(0, 2), (2, 0), (1, 3), (3, 1)])  7.21 us
    ppermute x6, waiting for transfers between devices, line_of(): lax.ppermute(part, 'tile', [(i, i ^ by) for i in range(tiles)])  6.45 us
    ppermute x3, waiting for transfers between devices, along_x(): return lax.ppermute(value, 'bank', [(0, 1), (1, 0), (2, 3), (3, 2)])  5.19 us
    pallas_call x1, Pallas kernels, weigh_blocks(): pl.pallas_call(functools.partial(weigh_kernel, blocks=len(blocks), known=...  4.97 us
  transfers between devices with their start and end apart: 22, of which 14 were waited for; matrix products, arithmetic and copies ran while one was open for 1% of the time, Pallas kernels for 11%

profile of v10, /device:TPU:0, one launch (start us, length us, event | category | flops | bytes accessed | tf_op | source)
XLA Modules:
  0.0 89.7 jit_solution(13797278061508550919)
XLA Ops:
  0.7 2.8 %constant_dynamic-slice_fusion = (bf16[48,64,128]{2,1,0:T(8,128)(2,1)}, bf16[48,64,128]{2,1,0:T(8,128)(2,1)}) fusion(bf16[64,64,128]{2,1,0:T(8,128)(2,1)} %volume_ref.1, s32[]{:T(128)S(6)} %select_n.18, s32[]{:T(128)S(6)} %select_n.17), kind=kLoop, calls=%fused_computation.20 | loop fusion | bytes 3145736 | tf_op jit(solution)/shard_map/dynamic_slice | solution.py:535
  3.9 1.6 %collective-permute-start.3 = (bf16[48,64,128]{2,1,0:T(8,128)(2,1)}, bf16[48,64,128]{2,1,0:T(8,128)(2,1)}, u32[]{:S(2)}, u32[]{:S(2)}) collective-permute-start(bf16[48,64,128]{2,1,0:T(8,128)(2,1)} %get-tuple-element.52), channel_id=1, source_target_pairs={{4,8},{8,4},{12,16},{16,12},{20,24},{24,20},{5,9},{9,5},{13,17},{1... | collective-permute-start | bytes 2359304 | tf_op jit(solution)/shard_map/ppermute | solution.py:388
  6.9 5.7 %collective-permute-start.1 = (s32[3,1,1,16]{3,2,1,0:T(1,128)S(1)}, s32[3,1,1,16]{3,2,1,0:T(1,128)S(1)}, u32[]{:S(2)}, u32[]{:S(2)}) collective-permute-start(s32[3,1,1,16]{3,2,1,0:T(1,128)S(1)} %copy-done.2), channel_id=1, source_target_pairs={{0,1},{1,0},{2,3},{3,2},{4,5},{5,4},{6,7},{7,6},{8,9},{9,8},{10,11... | collective-permute-start | bytes 584 | tf_op jit(solution)/shard_map/ppermute | solution.py:388
  12.6 1.5 %collective-permute-done.1.first_pick_ref = s32[3,1,1,16]{3,2,1,0:T(1,128)S(1)} collective-permute-done((s32[3,1,1,16]{3,2,1,0:T(1,128)S(1)}, s32[3,1,1,16]{3,2,1,0:T(1,128)S(1)}, u32[]{:S(2)}, u32[]{:S(2)}) %collective-permute-start.1) | collective-permute-done | bytes 224 | tf_op jit(solution)/shard_map/ppermute | solution.py:388
  14.1 4.8 %near_rows.1 = (f32[304,768]{1,0:T(8,128)S(1)}, bf16[128,768]{1,0:T(8,128)(2,1)S(1)}, f32[64,768]{1,0:T(8,128)S(1)}, f32[8,768]{1,0:T(8,128)S(1)}) custom-call(s32[2]{0:T(128)S(1)} %pad_add_fusion.origin_ref, s32[3,1,1,16]{3,2,1,0:T(1,128)S(1)} %collective-permute-done.1.first_pick_ref, s32[3,1,1,16]{3,2,1,0:T(1,128)S(1)} %copy-done.2, ...), custom_call_target="tpu_custom_call" | custom-call | flops 2717908992 | bytes 8000000 | tf_op jit(solution)/shard_map/near_rows/pallas_call | solution.py:550
  18.9 7.4 %far_rows.1 = (bf16[256,256]{1,0:T(8,128)(2,1)S(1)}, f32[256,256]{1,0:T(8,128)S(1)}, bf16[256,256]{1,0:T(8,128)(2,1)S(1)}) custom-call(s32[1]{0:T(128)} %bitcast.1.side_ref, bf16[128,768]{1,0:T(8,128)(2,1)S(1)} %get-tuple-element.28.depth_ref, f32[64,768]{1,0:T(8,128)S(1)} %get-tuple-element.29.high_ref, f32[8,768]{1,0:T(8,128)S(1)} %get-tuple-element.30.where_ref, ...), custom_call_target="tpu_custom_call" | custom-call | tf_op jit(solution)/shard_map/far_rows/pallas_call | solution.py:567
  26.4 2.1 %collective-permute-start.4 = (bf16[256,256]{1,0:T(8,128)(2,1)S(1)}, bf16[256,256]{1,0:T(8,128)(2,1)S(1)}, u32[]{:S(2)}, u32[]{:S(2)}) collective-permute-start(bf16[256,256]{1,0:T(8,128)(2,1)S(1)} %get-tuple-element.35), channel_id=1, source_target_pairs={{0,1},{1,0},{2,3},{3,2},{4,5},{5,4},{6,7},{7,6},{8,9},{9,8},{10,11... | collective-permute-start | bytes 393224 | tf_op jit(solution)/shard_map/ppermute | solution.py:388
  30.1 2.3 %collective-permute-done.4.left_ref = bf16[256,256]{1,0:T(8,128)(2,1)S(1)} collective-permute-done((bf16[256,256]{1,0:T(8,128)(2,1)S(1)}, bf16[256,256]{1,0:T(8,128)(2,1)S(1)}, u32[]{:S(2)}, u32[]{:S(2)}) %collective-permute-start.4) | collective-permute-done | bytes 131104 | tf_op jit(solution)/shard_map/ppermute | solution.py:388
  32.4 1.4 %join.1 = (bf16[8,4480]{1,0:T(8,128)(2,1)S(1)}, bf16[8,4480]{1,0:T(8,128)(2,1)S(1)}) custom-call(f32[256,256]{1,0:T(8,128)S(1)} %get-tuple-element.34.own_ref, bf16[256,256]{1,0:T(8,128)(2,1)S(1)} %collective-permute-done.4.left_ref, bf16[256,256]{1,0:T(8,128)(2,1)S(1)} %collective-permute-done.5.right_ref, ...), custom_call_target="tpu_custom_call" | custom-call | tf_op jit(solution)/shard_map/join/pallas_call | solution.py:593
  33.8 3.7 %collective-permute-start.8 = (bf16[8,4480]{1,0:T(8,128)(2,1)S(1)}, bf16[8,4480]{1,0:T(8,128)(2,1)S(1)}, u32[]{:S(2)}, u32[]{:S(2)}) collective-permute-start(bf16[8,4480]{1,0:T(8,128)(2,1)S(1)} %get-tuple-element.40), channel_id=1, source_target_pairs={{0,24},{4,28},{8,16},{12,20},{16,8},{20,12},{24,0},{28,4},{1,25},{... | collective-permute-start | bytes 215048 | tf_op jit(solution)/shard_map/ppermute | solution.py:414
  38.2 2.2 %collective-permute-done.8 = bf16[8,4480]{1,0:T(8,128)(2,1)S(1)} collective-permute-done((bf16[8,4480]{1,0:T(8,128)(2,1)S(1)}, bf16[8,4480]{1,0:T(8,128)(2,1)S(1)}, u32[]{:S(2)}, u32[]{:S(2)}) %collective-permute-start.8) | collective-permute-done | bytes 71712 | tf_op jit(solution)/shard_map/ppermute | solution.py:414
  40.4 3.1 %collective-permute-done.7 = bf16[8,4480]{1,0:T(8,128)(2,1)S(1)} collective-permute-done((bf16[8,4480]{1,0:T(8,128)(2,1)S(1)}, bf16[8,4480]{1,0:T(8,128)(2,1)S(1)}, u32[]{:S(2)}, u32[]{:S(2)}) %collective-permute-start.7) | collective-permute-done | bytes 71712 | tf_op jit(solution)/shard_map/ppermute | solution.py:414
  43.6 4.8 %collective-permute-start.10 = (bf16[32,4480]{1,0:T(8,128)(2,1)S(1)}, bf16[32,4480]{1,0:T(8,128)(2,1)S(1)}, u32[]{:S(2)}, u32[]{:S(2)}) collective-permute-start(bf16[32,4480]{1,0:T(8,128)(2,1)S(1)} %pad_maximum_fusion.2.refs_0_.refs_1_), channel_id=1, source_target_pairs={{0,2},{2,0},{1,3},{3,1},{4,6},{6,4},{5,7},{7,5},{8,10},{10,8},{9,1... | collective-permute-start | bytes 860168 | tf_op jit(solution)/shard_map/ppermute | solution.py:407
  48.4 2.1 %collective-permute-start.14 = (bf16[8,4480]{1,0:T(8,128)(2,1)S(1)}, bf16[8,4480]{1,0:T(8,128)(2,1)S(1)}, u32[]{:S(2)}, u32[]{:S(2)}) collective-permute-start(bf16[8,4480]{1,0:T(8,128)(2,1)S(1)} %get-tuple-element.42), channel_id=1, source_target_pairs={{0,24},{4,28},{8,16},{12,20},{16,8},{20,12},{24,0},{28,4},{1,25},{... | collective-permute-start | bytes 215048 | tf_op jit(solution)/shard_map/ppermute | solution.py:414
  50.4 2.3 %collective-permute-start.12 = (bf16[8,4480]{1,0:T(8,128)(2,1)S(1)}, bf16[8,4480]{1,0:T(8,128)(2,1)S(1)}, u32[]{:S(2)}, u32[]{:S(2)}) collective-permute-start(bf16[8,4480]{1,0:T(8,128)(2,1)S(1)} %get-tuple-element.42), channel_id=1, source_target_pairs={{0,8},{4,12},{8,0},{12,4},{16,24},{20,28},{24,16},{28,20},{1,9},{5... | collective-permute-start | bytes 215048 | tf_op jit(solution)/shard_map/ppermute | solution.py:414
  53.4 1.6 %collective-permute-done.9.refs_1_.refs_2_ = bf16[32,4480]{1,0:T(8,128)(2,1)S(1)} collective-permute-done((bf16[32,4480]{1,0:T(8,128)(2,1)S(1)}, bf16[32,4480]{1,0:T(8,128)(2,1)S(1)}, u32[]{:S(2)}, u32[]{:S(2)}) %collective-permute-start.9) | collective-permute-done | bytes 286752 | tf_op jit(solution)/shard_map/ppermute | solution.py:404
  56.4 1.7 %collective-permute-start.17 = (bf16[48,4480]{1,0:T(8,128)(2,1)S(1)}, bf16[48,4480]{1,0:T(8,128)(2,1)S(1)}, u32[]{:S(2)}, u32[]{:S(2)}) collective-permute-start(bf16[48,4480]{1,0:T(8,128)(2,1)S(1)} %get-tuple-element.45), channel_id=1, source_target_pairs={{0,2},{2,0},{1,3},{3,1},{4,6},{6,4},{5,7},{7,5},{8,10},{10,8},{9,1... | collective-permute-start | bytes 1290248 | tf_op jit(solution)/shard_map/ppermute | solution.py:407
  58.7 1.6 %collective-permute-done.15.refs_5_.refs_6_ = bf16[32,4480]{1,0:T(8,128)(2,1)S(1)} collective-permute-done((bf16[32,4480]{1,0:T(8,128)(2,1)S(1)}, bf16[32,4480]{1,0:T(8,128)(2,1)S(1)}, u32[]{:S(2)}, u32[]{:S(2)}) %collective-permute-start.15) | collective-permute-done | bytes 286752 | tf_op jit(solution)/shard_map/ppermute | solution.py:410
  60.3 5.0 %weigh.1 = (bf16[20,64,256]{2,1,0:T(8,128)(2,1)S(1)}, f32[20,64,128]{2,1,0:T(8,128)S(1)}) custom-call(s32[1]{0:T(128)} %bitcast.index_ref, bf16[32,4480]{1,0:T(8,128)(2,1)S(1)} %pad_maximum_fusion.2.refs_0_.refs_1_, bf16[32,4480]{1,0:T(8,128)(2,1)S(1)} %collective-permute-done.9.refs_1_.refs_2_, ...), custom_call_target="tpu_custom_call" | custom-call | flops 167772160 | bytes 655360 | tf_op jit(solution)/shard_map/weigh/pallas_call | solution.py:458
  65.3 2.4 %collective-permute-done.17.refs_8_ = bf16[48,4480]{1,0:T(8,128)(2,1)S(1)} collective-permute-done((bf16[48,4480]{1,0:T(8,128)(2,1)S(1)}, bf16[48,4480]{1,0:T(8,128)(2,1)S(1)}, u32[]{:S(2)}, u32[]{:S(2)}) %collective-permute-start.17) | collective-permute-done | bytes 430112 | tf_op jit(solution)/shard_map/ppermute | solution.py:407
  68.1 1.1 %collective-permute-start.19 = (bf16[16,4480]{1,0:T(8,128)(2,1)S(1)}, bf16[16,4480]{1,0:T(8,128)(2,1)S(1)}, u32[]{:S(2)}, u32[]{:S(2)}) collective-permute-start(bf16[16,4480]{1,0:T(8,128)(2,1)S(1)} %slice.18), channel_id=1, source_target_pairs={{0,1},{1,0},{2,3},{3,2},{4,5},{5,4},{6,7},{7,6},{8,9},{9,8},{10,11... | collective-permute-start | bytes 430088 | tf_op jit(solution)/shard_map/ppermute | solution.py:404
  70.0 3.3 %collective-permute-done.19.refs_10_ = bf16[16,4480]{1,0:T(8,128)(2,1)S(1)} collective-permute-done((bf16[16,4480]{1,0:T(8,128)(2,1)S(1)}, bf16[16,4480]{1,0:T(8,128)(2,1)S(1)}, u32[]{:S(2)}, u32[]{:S(2)}) %collective-permute-start.19) | collective-permute-done | bytes 143392 | tf_op jit(solution)/shard_map/ppermute | solution.py:404
  74.3 1.6 %collective-permute-done.21.refs_12_ = bf16[32,4480]{1,0:T(8,128)(2,1)S(1)} collective-permute-done((bf16[32,4480]{1,0:T(8,128)(2,1)S(1)}, bf16[32,4480]{1,0:T(8,128)(2,1)S(1)}, u32[]{:S(2)}, u32[]{:S(2)}) %collective-permute-start.21) | collective-permute-done | bytes 286752 | tf_op jit(solution)/shard_map/ppermute | solution.py:410
  75.9 13.7 %class_sums.1 = (f32[20,64,4096]{2,1,0:T(8,128)}, f32[20,64]{1,0:T(8,128)}) custom-call(s32[1]{0:T(128)} %bitcast.index_ref, bf16[20,64,256]{2,1,0:T(8,128)(2,1)S(1)} %get-tuple-element.46.refs_0_, bf16[32,4480]{1,0:T(8,128)(2,1)S(1)} %pad_maximum_fusion.2.refs_0_.refs_1_, bf16[32,4480]{1,0:T(8,128)(2,1)S(1)} %collective-permute-done.9.refs_1_.refs_2_, ...), custom_call_target="tpu_custom_call" | custom-call | flops 5368709120 | bytes 20971520 | tf_op jit(solution)/shard_map/class_sums/pallas_call | solution.py:491
  (65 shorter events, 8.6 us)
Async XLA Ops:
  3.5 2.7 %collective-permute-start = (bf16[48,64,128]{2,1,0:T(8,128)(2,1)}, bf16[48,64,128]{2,1,0:T(8,128)(2,1)}, u32[]{:S(2)}, u32[]{:S(2)}) collective-permute-start(bf16[48,64,128]{2,1,0:T(8,128)(2,1)} %get-tuple-element.53), channel_id=1, source_target_pairs={{0,4},{4,0},{8,12},{12,8},{16,20},{20,16},{24,28},{28,24},{1,5},{5... | collective-permute-start | bytes 2359304 | tf_op jit(solution)/shard_map/ppermute | solution.py:388
  3.9 14.9 %collective-permute-start.3 = (bf16[48,64,128]{2,1,0:T(8,128)(2,1)}, bf16[48,64,128]{2,1,0:T(8,128)(2,1)}, u32[]{:S(2)}, u32[]{:S(2)}) collective-permute-start(bf16[48,64,128]{2,1,0:T(8,128)(2,1)} %get-tuple-element.52), channel_id=1, source_target_pairs={{4,8},{8,4},{12,16},{16,12},{20,24},{24,20},{5,9},{9,5},{13,17},{1... | collective-permute-start | bytes 2359304 | tf_op jit(solution)/shard_map/ppermute | solution.py:388
  6.2 6.4 %collective-permute-start.2 = (s32[3,1,1,16]{3,2,1,0:T(1,128)S(1)}, s32[3,1,1,16]{3,2,1,0:T(1,128)S(1)}, u32[]{:S(2)}, u32[]{:S(2)}) collective-permute-start(s32[3,1,1,16]{3,2,1,0:T(1,128)S(1)} %copy-done.2), channel_id=1, source_target_pairs={{1,2},{2,1},{5,6},{6,5},{9,10},{10,9},{13,14},{14,13},{17,18},{18,... | collective-permute-start | bytes 584 | tf_op jit(solution)/shard_map/ppermute | solution.py:388
  6.9 7.2 %collective-permute-start.1 = (s32[3,1,1,16]{3,2,1,0:T(1,128)S(1)}, s32[3,1,1,16]{3,2,1,0:T(1,128)S(1)}, u32[]{:S(2)}, u32[]{:S(2)}) collective-permute-start(s32[3,1,1,16]{3,2,1,0:T(1,128)S(1)} %copy-done.2), channel_id=1, source_target_pairs={{0,1},{1,0},{2,3},{3,2},{4,5},{5,4},{6,7},{7,6},{8,9},{9,8},{10,11... | collective-permute-start | bytes 584 | tf_op jit(solution)/shard_map/ppermute | solution.py:388
  14.1 46.2 %slice-start = ((s8[10485760]{0:T(1024)(128)(4,1)}), s8[4194304]{0:T(1024)(128)(4,1)S(1)}, s32[]{:S(2)}) async-start(s8[10485760]{0:T(1024)(128)(4,1)} %bitcast.12), calls=%async_computation | async-start | bytes 8388608
  14.1 46.2 %slice-start.1 = ((s8[10485760]{0:T(1024)(128)(4,1)}), s8[4194304]{0:T(1024)(128)(4,1)S(1)}, s32[]{:S(2)}) async-start(s8[10485760]{0:T(1024)(128)(4,1)} %bitcast.12), calls=%async_computation.1 | async-start | bytes 8388608
  26.4 6.0 %collective-permute-start.4 = (bf16[256,256]{1,0:T(8,128)(2,1)S(1)}, bf16[256,256]{1,0:T(8,128)(2,1)S(1)}, u32[]{:S(2)}, u32[]{:S(2)}) collective-permute-start(bf16[256,256]{1,0:T(8,128)(2,1)S(1)} %get-tuple-element.35), channel_id=1, source_target_pairs={{0,1},{1,0},{2,3},{3,2},{4,5},{5,4},{6,7},{7,6},{8,9},{9,8},{10,11... | collective-permute-start | bytes 393224 | tf_op jit(solution)/shard_map/ppermute | solution.py:388
  28.5 3.9 %collective-permute-start.5 = (bf16[256,256]{1,0:T(8,128)(2,1)S(1)}, bf16[256,256]{1,0:T(8,128)(2,1)S(1)}, u32[]{:S(2)}, u32[]{:S(2)}) collective-permute-start(bf16[256,256]{1,0:T(8,128)(2,1)S(1)} %get-tuple-element.36), channel_id=1, source_target_pairs={{1,2},{2,1},{5,6},{6,5},{9,10},{10,9},{13,14},{14,13},{17,18},{18,... | collective-permute-start | bytes 393224 | tf_op jit(solution)/shard_map/ppermute | solution.py:388
  33.8 6.6 %collective-permute-start.8 = (bf16[8,4480]{1,0:T(8,128)(2,1)S(1)}, bf16[8,4480]{1,0:T(8,128)(2,1)S(1)}, u32[]{:S(2)}, u32[]{:S(2)}) collective-permute-start(bf16[8,4480]{1,0:T(8,128)(2,1)S(1)} %get-tuple-element.40), channel_id=1, source_target_pairs={{0,24},{4,28},{8,16},{12,20},{16,8},{20,12},{24,0},{28,4},{1,25},{... | collective-permute-start | bytes 215048 | tf_op jit(solution)/shard_map/ppermute | solution.py:414
  37.5 6.1 %collective-permute-start.7 = (bf16[8,4480]{1,0:T(8,128)(2,1)S(1)}, bf16[8,4480]{1,0:T(8,128)(2,1)S(1)}, u32[]{:S(2)}, u32[]{:S(2)}) collective-permute-start(bf16[8,4480]{1,0:T(8,128)(2,1)S(1)} %get-tuple-element.40), channel_id=1, source_target_pairs={{0,16},{4,20},{8,24},{12,28},{16,0},{20,4},{24,8},{28,12},{1,17},{... | collective-permute-start | bytes 215048 | tf_op jit(solution)/shard_map/ppermute | solution.py:414
  37.5 6.1 %collective-permute-start.6 = (bf16[8,4480]{1,0:T(8,128)(2,1)S(1)}, bf16[8,4480]{1,0:T(8,128)(2,1)S(1)}, u32[]{:S(2)}, u32[]{:S(2)}) collective-permute-start(bf16[8,4480]{1,0:T(8,128)(2,1)S(1)} %get-tuple-element.40), channel_id=1, source_target_pairs={{0,8},{4,12},{8,0},{12,4},{16,24},{20,28},{24,16},{28,20},{1,9},{5... | collective-permute-start | bytes 215048 | tf_op jit(solution)/shard_map/ppermute | solution.py:414
  43.6 9.9 %collective-permute-start.10 = (bf16[32,4480]{1,0:T(8,128)(2,1)S(1)}, bf16[32,4480]{1,0:T(8,128)(2,1)S(1)}, u32[]{:S(2)}, u32[]{:S(2)}) collective-permute-start(bf16[32,4480]{1,0:T(8,128)(2,1)S(1)} %pad_maximum_fusion.2.refs_0_.refs_1_), channel_id=1, source_target_pairs={{0,2},{2,0},{1,3},{3,1},{4,6},{6,4},{5,7},{7,5},{8,10},{10,8},{9,1... | collective-permute-start | bytes 860168 | tf_op jit(solution)/shard_map/ppermute | solution.py:407
  48.4 6.6 %collective-permute-start.9 = (bf16[32,4480]{1,0:T(8,128)(2,1)S(1)}, bf16[32,4480]{1,0:T(8,128)(2,1)S(1)}, u32[]{:S(2)}, u32[]{:S(2)}) collective-permute-start(bf16[32,4480]{1,0:T(8,128)(2,1)S(1)} %pad_maximum_fusion.2.refs_0_.refs_1_), channel_id=1, source_target_pairs={{0,1},{1,0},{2,3},{3,2},{4,5},{5,4},{6,7},{7,6},{8,9},{9,8},{10,11... | collective-permute-start | bytes 860168 | tf_op jit(solution)/shard_map/ppermute | solution.py:404
  48.4 8.0 %collective-permute-start.14 = (bf16[8,4480]{1,0:T(8,128)(2,1)S(1)}, bf16[8,4480]{1,0:T(8,128)(2,1)S(1)}, u32[]{:S(2)}, u32[]{:S(2)}) collective-permute-start(bf16[8,4480]{1,0:T(8,128)(2,1)S(1)} %get-tuple-element.42), channel_id=1, source_target_pairs={{0,24},{4,28},{8,16},{12,20},{16,8},{20,12},{24,0},{28,4},{1,25},{... | collective-permute-start | bytes 215048 | tf_op jit(solution)/shard_map/ppermute | solution.py:414
  50.4 5.9 %collective-permute-start.13 = (bf16[8,4480]{1,0:T(8,128)(2,1)S(1)}, bf16[8,4480]{1,0:T(8,128)(2,1)S(1)}, u32[]{:S(2)}, u32[]{:S(2)}) collective-permute-start(bf16[8,4480]{1,0:T(8,128)(2,1)S(1)} %get-tuple-element.42), channel_id=1, source_target_pairs={{0,16},{4,20},{8,24},{12,28},{16,0},{20,4},{24,8},{28,12},{1,17},{... | collective-permute-start | bytes 215048 | tf_op jit(solution)/shard_map/ppermute | solution.py:414
  50.4 5.5 %collective-permute-start.12 = (bf16[8,4480]{1,0:T(8,128)(2,1)S(1)}, bf16[8,4480]{1,0:T(8,128)(2,1)S(1)}, u32[]{:S(2)}, u32[]{:S(2)}) collective-permute-start(bf16[8,4480]{1,0:T(8,128)(2,1)S(1)} %get-tuple-element.42), channel_id=1, source_target_pairs={{0,8},{4,12},{8,0},{12,4},{16,24},{20,28},{24,16},{28,20},{1,9},{5... | collective-permute-start | bytes 215048 | tf_op jit(solution)/shard_map/ppermute | solution.py:414
  55.1 5.2 %collective-permute-start.11 = (bf16[96,4480]{1,0:T(8,128)(2,1)S(1)}, bf16[96,4480]{1,0:T(8,128)(2,1)S(1)}, u32[]{:S(2)}, u32[]{:S(2)}) collective-permute-start(bf16[96,4480]{1,0:T(8,128)(2,1)S(1)} %pad_maximum_fusion), channel_id=1, source_target_pairs={{0,4},{4,0},{8,12},{12,8},{16,20},{20,16},{24,28},{28,24},{1,5},{5... | collective-permute-start | bytes 2580488 | tf_op jit(solution)/shard_map/ppermute | solution.py:410
  56.4 11.3 %collective-permute-start.17 = (bf16[48,4480]{1,0:T(8,128)(2,1)S(1)}, bf16[48,4480]{1,0:T(8,128)(2,1)S(1)}, u32[]{:S(2)}, u32[]{:S(2)}) collective-permute-start(bf16[48,4480]{1,0:T(8,128)(2,1)S(1)} %get-tuple-element.45), channel_id=1, source_target_pairs={{0,2},{2,0},{1,3},{3,1},{4,6},{6,4},{5,7},{7,5},{8,10},{10,8},{9,1... | collective-permute-start | bytes 1290248 | tf_op jit(solution)/shard_map/ppermute | solution.py:407
  58.1 9.9 %collective-permute-start.16 = (bf16[48,4480]{1,0:T(8,128)(2,1)S(1)}, bf16[48,4480]{1,0:T(8,128)(2,1)S(1)}, u32[]{:S(2)}, u32[]{:S(2)}) collective-permute-start(bf16[48,4480]{1,0:T(8,128)(2,1)S(1)} %get-tuple-element.43), channel_id=1, source_target_pairs={{0,1},{1,0},{2,3},{3,2},{4,5},{5,4},{6,7},{7,6},{8,9},{9,8},{10,11... | collective-permute-start | bytes 1290248 | tf_op jit(solution)/shard_map/ppermute | solution.py:404
  58.6 1.6 %collective-permute-start.15 = (bf16[32,4480]{1,0:T(8,128)(2,1)S(1)}, bf16[32,4480]{1,0:T(8,128)(2,1)S(1)}, u32[]{:S(2)}, u32[]{:S(2)}) collective-permute-start(bf16[32,4480]{1,0:T(8,128)(2,1)S(1)} %slice.17.refs_4_.refs_5_), channel_id=1, source_target_pairs={{0,4},{4,0},{8,12},{12,8},{16,20},{20,16},{24,28},{28,24},{1,5},{5... | collective-permute-start | bytes 860168 | tf_op jit(solution)/shard_map/ppermute | solution.py:410
  68.1 5.2 %collective-permute-start.19 = (bf16[16,4480]{1,0:T(8,128)(2,1)S(1)}, bf16[16,4480]{1,0:T(8,128)(2,1)S(1)}, u32[]{:S(2)}, u32[]{:S(2)}) collective-permute-start(bf16[16,4480]{1,0:T(8,128)(2,1)S(1)} %slice.18), channel_id=1, source_target_pairs={{0,1},{1,0},{2,3},{3,2},{4,5},{5,4},{6,7},{7,6},{8,9},{9,8},{10,11... | collective-permute-start | bytes 430088 | tf_op jit(solution)/shard_map/ppermute | solution.py:404
  69.1 5.1 %collective-permute-start.20 = (bf16[16,4480]{1,0:T(8,128)(2,1)S(1)}, bf16[16,4480]{1,0:T(8,128)(2,1)S(1)}, u32[]{:S(2)}, u32[]{:S(2)}) collective-permute-start(bf16[16,4480]{1,0:T(8,128)(2,1)S(1)} %slice.19), channel_id=1, source_target_pairs={{0,2},{2,0},{1,3},{3,1},{4,6},{6,4},{5,7},{7,5},{8,10},{10,8},{9,1... | collective-permute-start | bytes 430088 | tf_op jit(solution)/shard_map/ppermute | solution.py:407
  69.9 6.0 %collective-permute-start.18 = (bf16[96,4480]{1,0:T(8,128)(2,1)S(1)}, bf16[96,4480]{1,0:T(8,128)(2,1)S(1)}, u32[]{:S(2)}, u32[]{:S(2)}) collective-permute-start(bf16[96,4480]{1,0:T(8,128)(2,1)S(1)} %pad_maximum_fusion.1), channel_id=1, source_target_pairs={{0,4},{4,0},{8,12},{12,8},{16,20},{20,16},{24,28},{28,24},{1,5},{5... | collective-permute-start | bytes 2580488 | tf_op jit(solution)/shard_map/ppermute | solution.py:410
  74.3 1.6 %collective-permute-start.21 = (bf16[32,4480]{1,0:T(8,128)(2,1)S(1)}, bf16[32,4480]{1,0:T(8,128)(2,1)S(1)}, u32[]{:S(2)}, u32[]{:S(2)}) collective-permute-start(bf16[32,4480]{1,0:T(8,128)(2,1)S(1)} %pad_maximum_fusion.3), channel_id=1, source_target_pairs={{0,4},{4,0},{8,12},{12,8},{16,20},{20,16},{24,28},{28,24},{1,5},{5... | collective-permute-start | bytes 860168 | tf_op jit(solution)/shard_map/ppermute | solution.py:410
  (8 other events, 118.6 us)
